TPU v7x, 32 devices: a whole 2x2x4 slice. The times are simulated.
32 devices in a mesh: groups: 2 (over x), tm: 16 (over z, y, core).
Axes of the slice: x: 2, y: 2, z: 4, core: 2. Of those that a mesh axis runs over, the one named last changes fastest.
Arguments:
- space_time: bfloat16 [32, 512, 1024], P(('groups', 'tm')), parts along dimension 0, may hold values from -16 to 16
- w_lin: bfloat16 [1024, 3072], replicated, may hold values from -0.1875 to 0.1875
- gain_lin: bfloat16 [1024], replicated, may hold values from 0.099609375 to 1.8984375
- w_query: bfloat16 [1024, 1024], replicated, may hold values from -4 to 4
- w_kv: bfloat16 [1024, 512], replicated, may hold values from -4 to 4
- frame_attention_gain: bfloat16 [1024], replicated, may hold values from 0.099609375 to 1.8984375
Outputs:
- attended: bfloat16 [32, 512, 1024], P(('groups', 'tm')), parts along dimension 0
There are 2 independent parts, one for each index of `groups`. A program takes and returns all parts, laid end to end along the dimension named above; an argument that names none is the same for every part. Nothing has to cross between parts.
All inputs are finite; a program needn't handle non-finite values.
Results may differ from a plain program's by a relative error of at most 0.028.
The roundings to bfloat16 on the way count: a program that leaves them out, or rounds other values in their place, can miss the bound.
Values may be sent and summed in bfloat16 or wider, within the bound.
No kernel may reach another device: no remote copies, remote signals or barrier semaphores. Data moves between devices by JAX's collectives and lax.ppermute only.
A program may use at most 64 MiB of HBM per device.

v0:
```python
import math

import jax
import jax.numpy as jnp
from jax import lax
from jax.sharding import PartitionSpec as P

HEADS = 8
HD = 128
KVH = 2
P_SIZE = 512
SB = 16
SPAN = 128
FA = 1


epsilon = 1e-06


def shifted(block, axis, distance):
    devices = range(lax.axis_size(axis))
    route = [(i - distance, i) for i in devices if i - distance in devices]
    return lax.ppermute(block, axis, route)


def partner(block, axis, apart):
    count = lax.axis_size(axis)
    route = []
    for low in range(count):
        high = low | 1 << apart
        if high != low and high < count:
            route += [(low, high), (high, low)]
    return lax.ppermute(block, axis, route)


def butterfly(pieces, position, mover):
    slot_order = jnp.arange(SB, dtype=jnp.int32)
    rest_shape = pieces.shape[1:]
    relative = jnp.take(pieces, jnp.bitwise_xor(position, slot_order), axis=0)
    for bit_index in range(SB.bit_length() - 1):
        shaped = relative.reshape((SB // (2 << bit_index), 2, 1 << bit_index) + rest_shape)
        arrived = mover(shaped[:, 1], bit_index)
        relative = jnp.stack([shaped[:, 0], arrived], axis=1).reshape((SB,) + rest_shape)
    return jnp.take(relative, jnp.bitwise_xor(position, slot_order), axis=0)


def frame_norm(rows, frame_attention_gain):
    widened = rows.astype(jnp.float32)
    mean_square = jnp.mean(widened * widened, axis=-1, keepdims=True)
    return (
        widened * lax.rsqrt(mean_square + epsilon) * frame_attention_gain.astype(jnp.float32)
    ).astype(jnp.bfloat16)


def body(space_time, w_lin, gain_lin, w_query, w_kv, frame_attention_gain):
    tokens = space_time[0]
    row_count = tokens.shape[0]
    model_width = tokens.shape[1]
    span_count = row_count // SPAN
    packed = jnp.dot(tokens, w_lin, preferred_element_type=jnp.float32).astype(jnp.bfloat16)
    query_rows = packed[:, :model_width].reshape(span_count, SPAN, HEADS, HD)
    key_rows = packed[:, model_width : 2 * model_width].reshape(span_count, SPAN, HEADS, HD)
    value_rows = packed[:, 2 * model_width :].reshape(span_count, SPAN, HEADS, HD)
    states = jnp.einsum("bnhd,bnhe->bhde", key_rows, value_rows, preferred_element_type=jnp.float32)
    block_total = jnp.sum(states, axis=0)
    time_ranges = lax.axis_size("tm") // SB
    device_index = lax.axis_index("tm")
    position = device_index % SB
    within = device_index // SB

    def advance_hop(turn_index, running_state_total):
        moved = shifted(running_state_total + block_total, "tm", SB)
        return jnp.where(within > 0, moved, 0.0)

    incoming = lax.fori_loop(0, time_ranges - 1, advance_hop, jnp.zeros_like(block_total))
    earlier_sums = jnp.cumsum(states[:-1], axis=0)
    before = jnp.concatenate([jnp.zeros_like(states[:1]), earlier_sums], axis=0) + incoming[None]
    readout = jnp.einsum(
        "bnhd,bhde->bnhe",
        query_rows,
        before.astype(jnp.bfloat16),
        preferred_element_type=jnp.float32,
    )
    attention_logits = jnp.einsum(
        "bnhd,bmhd->bhnm", query_rows, key_rows, preferred_element_type=jnp.float32
    )
    causal_mask = jnp.tril(jnp.ones((SPAN, SPAN), jnp.float32)) > 0
    local_weights = jnp.where(causal_mask, attention_logits, 0.0).astype(jnp.bfloat16)
    local_sum = jnp.einsum(
        "bhnm,bmhe->bnhe", local_weights, value_rows, preferred_element_type=jnp.float32
    )
    outputs = readout + local_sum
    mean_square = jnp.mean(outputs * outputs, axis=-1, keepdims=True)
    normed_heads = (
        outputs * lax.rsqrt(mean_square + epsilon) * gain_lin.astype(jnp.float32).reshape(HEADS, HD)
    )
    hidden = (tokens.astype(jnp.float32) + normed_heads.reshape(row_count, model_width)).astype(
        jnp.bfloat16
    )
    block_tokens = P_SIZE // SB
    pieces = hidden.reshape(SB, FA, block_tokens, model_width)

    def move_hidden(moving, bit_index):
        return partner(moving, "tm", bit_index)

    ordered = butterfly(pieces, position, move_hidden)
    frame_rows = ordered.transpose(1, 0, 2, 3).reshape(FA * P_SIZE, model_width)
    normed = frame_norm(frame_rows, frame_attention_gain)
    queries = jnp.dot(normed, w_query, preferred_element_type=jnp.float32).astype(jnp.bfloat16)
    key_value_product = jnp.dot(normed, w_kv, preferred_element_type=jnp.float32).astype(
        jnp.bfloat16
    )
    group_size = HEADS // KVH
    queries = queries.reshape(FA, P_SIZE, KVH, group_size, HD)
    earlier_pairs = shifted(key_value_product, "tm", 1)
    joined = jnp.concatenate([earlier_pairs, key_value_product], axis=0).reshape(
        FA + 1, P_SIZE, 2 * KVH * HD
    )
    windows = jnp.concatenate([joined[:-1], joined[1:]], axis=1)
    window_keys = windows[:, :, : KVH * HD].reshape(FA, 2 * P_SIZE, KVH, HD)
    window_values = windows[:, :, KVH * HD :].reshape(FA, 2 * P_SIZE, KVH, HD)
    frame_number = device_index * FA + jnp.arange(FA, dtype=jnp.int32)
    key_positions = jnp.arange(2 * P_SIZE)
    usable_key = (key_positions[None, :] >= P_SIZE) | (frame_number[:, None] > 0)
    attention_logits = jnp.einsum(
        "fpkgd,fmkd->fkgpm", queries, window_keys, preferred_element_type=jnp.float32
    )
    attention_logits = attention_logits * (1.0 / math.sqrt(HD))
    attention_logits = jnp.where(usable_key[:, None, None, None, :], attention_logits, -jnp.inf)
    largest = jnp.max(attention_logits, axis=-1, keepdims=True)
    raised = jnp.exp(attention_logits - largest)
    weights = (raised / jnp.sum(raised, axis=-1, keepdims=True)).astype(jnp.bfloat16)
    attended = jnp.einsum(
        "fkgpm,fmkd->fpkgd", weights, window_values, preferred_element_type=jnp.float32
    )
    return attended.astype(jnp.bfloat16).reshape(FA, P_SIZE, model_width)


def solution(mesh):
    placed = (P(("groups", "tm"), None, None), P(), P(), P(), P(), P())
    return jax.shard_map(
        body, mesh=mesh, in_specs=placed, out_specs=P(("groups", "tm"), None, None), check_vma=False
    )
```

profile of v0, /device:TPU:1, one launch (start us, length us, event | category | flops | bytes accessed | tf_op | source)
XLA Modules:
  0.0 128.0 jit_solution(5426737005679243072)
XLA Ops:
  0.9 6.5 %convolution_convert_fusion = bf16[512,3072]{1,0:T(8,128)(2,1)S(1)} fusion(bf16[1024,3072]{1,0:T(8,128)(2,1)} %param.9, bf16[1,512,1024]{2,1,0:T(8,128)(2,1)} %param.8), kind=kOutput, calls=%fused_computation.10 | convolution fusion | flops 3222798336 | bytes 10485760 | tf_op jit(solution)/shard_map/dot_general | solution.py:60
  7.4 1.7 %slice_bitcast_fusion = (bf16[64,8,8,128]{3,1,2,0:T(8,128)(2,1)S(1)}, bf16[64,8,8,128]{3,1,2,0:T(8,128)(2,1)S(1)}, bf16[64,8,8,128]{3,1,2,0:T(8,128)(2,1)}) fusion(bf16[512,3072]{1,0:T(8,128)(2,1)S(1)} %convolution_convert_fusion), kind=kLoop, calls=%fused_computation.29 | loop fusion | bytes 6291456
  9.1 1.3 copy.41
  10.6 1.5 %copy.18 = bf16[4,128,8,128]{1,3,2,0:T(8,128)(2,1)} copy(bf16[4,128,8,128]{3,2,1,0:T(8,128)(2,1)S(1)} %bitcast.135) | data formatting | bytes 2097152 | tf_op jit(solution)/shard_map/reshape | solution.py:63
  12.1 2.5 %copy.39 = bf16[64,8,8,128]{3,2,1,0:T(8,128)(2,1)} copy(bf16[64,8,8,128]{3,1,2,0:T(8,128)(2,1)} %get-tuple-element.8) | data formatting | bytes 2097152
  14.6 1.8 %copy.28 = bf16[4,128,8,128]{1,3,2,0:T(8,128)(2,1)S(1)} copy(bf16[4,128,8,128]{3,2,1,0:T(8,128)(2,1)} %bitcast.136) | data formatting | bytes 2097152 | tf_op jit(solution)/shard_map/reshape | solution.py:62
  16.3 1.9 %fusion.33 = f32[3,8,128,128]{2,3,1,0:T(8,128)S(1)} fusion(bf16[4,128,8,128]{1,3,2,0:T(8,128)(2,1)S(1)} %copy.28, bf16[4,128,8,128]{1,3,2,0:T(8,128)(2,1)} %copy.18), kind=kOutput, calls=%fused_computation.75 | convolution fusion | flops 100663296 | bytes 3670016 | tf_op jit(solution)/shard_map/slice | solution.py:76
  19.3 4.0 %fusion.12 = f32[4,8,128,128]{3,2,1,0:T(8,128)} fusion(bf16[4,128,8,128]{1,3,2,0:T(8,128)(2,1)} %copy.18, bf16[4,128,8,128]{1,3,2,0:T(8,128)(2,1)S(1)} %copy.28, pred[128,128]{1,0:T(8,128)(4,1)S(1)} %select_compare_fusion, bf16[4,128,8,128]{3,2,1,0:T(8,128)(2,1)} %bitcast.129), kind=kOutput, calls=%fused_computation.26 | convolution fusion | flops 269484032 | bytes 5259264 | tf_op jit(solution)/shard_map/bhnm,bmhe->bnhe/dot_general | solution.py:89
  23.3 3.0 %fusion.7 = (f32[4,128,8]{1,2,0:T(8,128)S(1)}, f32[4,8,128,128]{3,2,1,0:T(8,128)S(1)}) fusion(f32[4,8,128,128]{3,2,1,0:T(8,128)} %fusion.12, bf16[3,8,128,128]{2,3,1,0:T(8,128)(2,1)} %reduce-window_convert_fusion, bf16[4,128,8,128]{3,2,1,0:T(8,128)(2,1)} %bitcast.130), kind=kOutput, calls=%fused_computation.18 | convolution fusion | flops 102232064 | bytes 6045696 | tf_op jit(solution)/shard_map/bnhd,bhde->bnhe/dot_general | solution.py:78
  26.3 1.7 %fusion.8 = f32[4,128,8,128]{1,3,2,0:T(8,128)} fusion(f32[4,8,128,128]{3,2,1,0:T(8,128)S(1)} %get-tuple-element.20, f32[8,128]{1,0:T(8,128)S(1)} %bitcast_convert_fusion, f32[4,128,8]{1,2,0:T(8,128)S(1)} %add_rsqrt_fusion), kind=kLoop, calls=%fused_computation.19 | loop fusion | flops 1048576 | bytes 4214784 | tf_op jit(solution)/shard_map/mul | solution.py:95
  28.0 2.9 %copy.19 = f32[4,128,8,128]{3,2,1,0:T(8,128)} copy(f32[4,128,8,128]{1,3,2,0:T(8,128)} %fusion.8) | data formatting | bytes 4194304 | tf_op jit(solution)/shard_map/mul | solution.py:95
  30.9 2.8 %reshape.148 = f32[16,1,32,1024]{3,2,0,1:T(8,128)} reshape(f32[4,128,8,128]{3,2,1,0:T(8,128)} %copy.19) | data formatting | bytes 4194304 | tf_op jit(solution)/shard_map/reshape | solution.py:97
  33.7 2.9 %fusion.13 = bf16[16,32,1024]{2,1,0:T(8,128)(2,1)} fusion(f32[16,1,32,1024]{3,2,0,1:T(8,128)} %reshape.148, bf16[16,1,32,1024]{3,2,0,1:T(8,128)(2,1)S(1)} %bitcast.140), kind=kLoop, calls=%fused_computation.28 | loop fusion | flops 1572864 | bytes 4194304 | tf_op jit(solution)/shard_map/jit(_take)/Arg_0.17 | solution.py:39
  36.6 1.8 %gather_fusion = bf16[16,32,1024]{2,1,0:T(8,128)(2,1)S(1)} fusion(bf16[16,32,1024]{2,1,0:T(8,128)(2,1)} %fusion.13, s32[1024]{0:T(1024)S(1)} %pad_clamp_fusion), kind=kCustom, calls=%fused_computation.clone | custom fusion | bytes 2097216 | tf_op jit(solution)/shard_map/jit(_take)/gather | solution.py:39
  38.9 1.9 %collective-permute-done = bf16[8,1,1,32,1024]{4,3,0,2,1:T(8,128)(2,1)S(1)} collective-permute-done((bf16[8,1,1,32,1024]{4,3,0,2,1:T(8,128)(2,1)S(1)}, bf16[8,1,1,32,1024]{4,3,0,2,1:T(8,128)(2,1)S(1)}, u32[]{:S(2)}, u32[]{:S(2)}) %collective-permute-start) | collective-permute-done | bytes 524320 | tf_op jit(solution)/shard_map/ppermute | solution.py:33
  40.8 2.4 %collective-permute-start.1 = (bf16[4,2,1,32,1024]{4,3,0,1,2:T(8,128)(2,1)S(1)}, bf16[4,2,1,32,1024]{4,3,0,1,2:T(8,128)(2,1)S(1)}, u32[]{:S(2)}, u32[]{:S(2)}) collective-permute-start(bf16[4,2,1,32,1024]{4,3,0,1,2:T(8,128)(2,1)S(1)} %get-tuple-element.16), channel_id=1, source_target_pairs={{0,2},{2,0},{1,3},{3,1},{4,6},{6,4},{5,7},{7,5},{8,10},{10,8},{9,1... | collective-permute-start | bytes 1572872 | tf_op jit(solution)/shard_map/ppermute | solution.py:33
  43.3 12.0 %collective-permute-done.1 = bf16[4,2,1,32,1024]{4,3,0,1,2:T(8,128)(2,1)S(1)} collective-permute-done((bf16[4,2,1,32,1024]{4,3,0,1,2:T(8,128)(2,1)S(1)}, bf16[4,2,1,32,1024]{4,3,0,1,2:T(8,128)(2,1)S(1)}, u32[]{:S(2)}, u32[]{:S(2)}) %collective-permute-start.1) | collective-permute-done | bytes 524320 | tf_op jit(solution)/shard_map/ppermute | solution.py:33
  56.7 11.4 %collective-permute-done.2 = bf16[2,4,1,32,1024]{4,3,0,1,2:T(8,128)(2,1)S(1)} collective-permute-done((bf16[2,4,1,32,1024]{4,3,0,1,2:T(8,128)(2,1)S(1)}, bf16[2,4,1,32,1024]{4,3,0,1,2:T(8,128)(2,1)S(1)}, u32[]{:S(2)}, u32[]{:S(2)}) %collective-permute-start.2) | collective-permute-done | bytes 524320 | tf_op jit(solution)/shard_map/ppermute | solution.py:33
  68.3 1.9 %collective-permute-start.3 = (bf16[1,8,1,32,1024]{4,3,1,2,0:T(8,128)(2,1)S(1)}, bf16[1,8,1,32,1024]{4,3,1,2,0:T(8,128)(2,1)S(1)}, u32[]{:S(2)}, u32[]{:S(2)}) collective-permute-start(bf16[1,8,1,32,1024]{4,3,1,2,0:T(8,128)(2,1)S(1)} %get-tuple-element.12), channel_id=1, source_target_pairs={{0,8},{8,0},{1,9},{9,1},{2,10},{10,2},{3,11},{11,3},{4,12},{12,4},... | collective-permute-start | bytes 1572872 | tf_op jit(solution)/shard_map/ppermute | solution.py:33
  70.2 23.5 %collective-permute-done.3 = bf16[1,8,1,32,1024]{4,3,1,2,0:T(8,128)(2,1)S(1)} collective-permute-done((bf16[1,8,1,32,1024]{4,3,1,2,0:T(8,128)(2,1)S(1)}, bf16[1,8,1,32,1024]{4,3,1,2,0:T(8,128)(2,1)S(1)}, u32[]{:S(2)}, u32[]{:S(2)}) %collective-permute-start.3) | collective-permute-done | bytes 524320 | tf_op jit(solution)/shard_map/ppermute | solution.py:33
  94.7 1.8 %gather_fusion.1 = bf16[16,32,1024]{2,1,0:T(8,128)(2,1)S(1)} fusion(bf16[16,32,1024]{2,1,0:T(8,128)(2,1)} %bitcast.132, s32[1024]{0:T(1024)S(1)} %pad_clamp_fusion), kind=kCustom, calls=%fused_computation.1.clone | custom fusion | bytes 2097216 | tf_op jit(solution)/shard_map/jit(_take)/gather | solution.py:44
  97.0 1.5 %fusion.14 = f32[16,1,32,1024]{3,2,0,1:T(8,128)} fusion(bf16[16,32,1024]{2,1,0:T(8,128)(2,1)S(1)} %gather_fusion.1, pred[16]{0:T(512)(128)(4,1)S(1)} %compare_and_fusion), kind=kLoop, calls=%fused_computation.40 | loop fusion | flops 1048576 | bytes 3145744 | tf_op jit(solution)/shard_map/convert_element_type | solution.py:48
  98.6 1.8 %fusion.6 = bf16[512,1024]{1,0:T(8,128)(2,1)S(1)} fusion(f32[16,1,32,1024]{3,2,0,1:T(8,128)} %fusion.14, f32[1024]{0:T(1024)S(1)} %convert_element_type.72, f32[512]{0:T(512)S(1)} %rsqrt.21), kind=kLoop, calls=%fused_computation.15 | loop fusion | flops 1572864 | bytes 3151872 | tf_op jit(solution)/shard_map/convert_element_type | solution.py:52
  100.5 2.7 %convolution_convert_fusion.2 = bf16[512,512]{1,0:T(8,128)(2,1)} fusion(bf16[512,1024]{1,0:T(8,128)(2,1)S(1)} %fusion.6, bf16[1024,512]{1,0:T(8,128)(2,1)} %param.12), kind=kOutput, calls=%fused_computation.27 | convolution fusion | flops 537133056 | bytes 2621440 | tf_op jit(solution)/shard_map/dot_general | solution.py:110
  103.2 3.9 %collective-permute-start.4 = (bf16[512,512]{1,0:T(8,128)(2,1)}, bf16[512,512]{1,0:T(8,128)(2,1)}, u32[]{:S(2)}, u32[]{:S(2)}) collective-permute-start(bf16[512,512]{1,0:T(8,128)(2,1)} %convolution_convert_fusion.2), channel_id=1, source_target_pairs={{0,1},{1,2},{2,3},{3,4},{4,5},{5,6},{6,7},{7,8},{8,9},{9,10},{10,1... | collective-permute-start | bytes 1572872 | tf_op jit(solution)/shard_map/ppermute | solution.py:23
  107.1 2.2 %convolution_convert_fusion.1 = bf16[512,1024]{1,0:T(8,128)(2,1)} fusion(bf16[512,1024]{1,0:T(8,128)(2,1)S(1)} %fusion.6, bf16[1024,1024]{1,0:T(8,128)(2,1)S(1)} %copy-done), kind=kOutput, calls=%fused_computation.25 | convolution fusion | flops 1074266112 | bytes 4194304 | tf_op jit(solution)/shard_map/dot_general | solution.py:109
  109.4 1.8 %reshape.153 = bf16[512,2,4,128]{3,2,1,0:T(4,128)(2,1)S(1)} reshape(bf16[512,1024]{1,0:T(8,128)(2,1)} %convolution_convert_fusion.1) | data formatting | bytes 2097152 | tf_op jit(solution)/shard_map/reshape.6
  111.1 2.2 %collective-permute-done.4 = bf16[512,512]{1,0:T(8,128)(2,1)} collective-permute-done((bf16[512,512]{1,0:T(8,128)(2,1)}, bf16[512,512]{1,0:T(8,128)(2,1)}, u32[]{:S(2)}, u32[]{:S(2)}) %collective-permute-start.4) | collective-permute-done | bytes 524320 | tf_op jit(solution)/shard_map/ppermute | solution.py:23
  115.7 2.4 %bitcast_reduce_fusion = (f32[2,4,512]{2,1,0:T(4,128)S(1)}, f32[2,1024,512,4]{2,1,3,0:T(8,128)S(1)}) fusion(pred[1024]{0:T(1024)(128)(4,1)S(1)} %fusion.28, bf16[512,2,4,128]{3,2,1,0:T(4,128)(2,1)S(1)} %reshape.153, bf16[1024,2,128,1]{2,1,0,3:T(2,128)(2,1)S(1)} %bitcast.137), kind=kOutput, calls=%fused_computation.3 | convolution fusion | flops 1086320640 | bytes 18367488 | tf_op jit(solution)/shard_map/fpkgd,fmkd->fkgpm/dot_general | solution.py:125
  118.1 4.0 %fusion.1 = f32[2,4,512]{2,1,0:T(4,128)S(1)} fusion(f32[2,1024,512,4]{2,1,3,0:T(8,128)S(1)} %get-tuple-element.22, f32[2,4,512]{2,1,0:T(4,128)S(1)} %get-tuple-element.21, pred[1024]{0:T(1024)(128)(4,1)S(1)} %fusion.28), kind=kLoop, calls=%fused_computation.7 | loop fusion | flops 16773120 | bytes 16811008 | tf_op jit(solution)/shard_map/reduce_sum | solution.py:132
  122.2 4.6 %fusion.9 = bf16[2,128,4,512]{3,1,2,0:T(8,128)(2,1)S(1)} fusion(bf16[1024,2,128,1]{0,2,3,1:T(8,128)(2,1)S(1)} %bitcast.141, f32[2,4,512]{2,1,0:T(4,128)S(1)} %fusion.1, f32[2,4,512]{2,1,0:T(4,128)S(1)} %get-tuple-element.21, f32[2,1024,512,4]{2,1,3,0:T(8,128)S(1)} %get-tuple-element.22, pred[1024]{0:T(1024)(128)(4,1)S(1)} %fusion.28), kind=kOutput, calls=%fused_computation.24 | convolution fusion | flops 1095237632 | bytes 18383872 | tf_op jit(solution)/shard_map/fkgpm,fmkd->fpkgd/dot_general | solution.py:133
  126.7 1.3 %copy.27 = bf16[1,512,1024]{2,1,0:T(8,128)(2,1)} copy(bf16[1,512,1024]{1,2,0:T(8,128)(2,1)S(1)} %bitcast.139) | data formatting | bytes 2097152 | tf_op jit(solution)/shard_map/reshape | solution.py:136
  (36 shorter events, 8.3 us)
Async XLA Ops:
  0.0 107.1 %copy-start = (bf16[1024,1024]{1,0:T(8,128)(2,1)S(1)}, bf16[1024,1024]{1,0:T(8,128)(2,1)}, u32[]{:S(2)}) copy-start(bf16[1024,1024]{1,0:T(8,128)(2,1)} %param.11) | copy-start | bytes 6291460
  30.9 2.8 %copy-start.2 = (bf16[1,512,1024]{2,1,0:T(8,128)(2,1)S(1)}, bf16[1,512,1024]{2,1,0:T(8,128)(2,1)}, u32[]{:S(2)}) copy-start(bf16[1,512,1024]{2,1,0:T(8,128)(2,1)} %param.8) | copy-start | bytes 3145732
  38.7 2.0 %collective-permute-start = (bf16[8,1,1,32,1024]{4,3,0,2,1:T(8,128)(2,1)S(1)}, bf16[8,1,1,32,1024]{4,3,0,2,1:T(8,128)(2,1)S(1)}, u32[]{:S(2)}, u32[]{:S(2)}) collective-permute-start(bf16[8,1,1,32,1024]{4,3,0,2,1:T(8,128)(2,1)S(1)} %get-tuple-element.18), channel_id=1, source_target_pairs={{0,1},{1,0},{2,3},{3,2},{4,5},{5,4},{6,7},{7,6},{8,9},{9,8},{10,11... | collective-permute-start | bytes 1572872 | tf_op jit(solution)/shard_map/ppermute | solution.py:33
  40.8 14.4 %collective-permute-start.1 = (bf16[4,2,1,32,1024]{4,3,0,1,2:T(8,128)(2,1)S(1)}, bf16[4,2,1,32,1024]{4,3,0,1,2:T(8,128)(2,1)S(1)}, u32[]{:S(2)}, u32[]{:S(2)}) collective-permute-start(bf16[4,2,1,32,1024]{4,3,0,1,2:T(8,128)(2,1)S(1)} %get-tuple-element.16), channel_id=1, source_target_pairs={{0,2},{2,0},{1,3},{3,1},{4,6},{6,4},{5,7},{7,5},{8,10},{10,8},{9,1... | collective-permute-start | bytes 1572872 | tf_op jit(solution)/shard_map/ppermute | solution.py:33
  55.4 12.6 %collective-permute-start.2 = (bf16[2,4,1,32,1024]{4,3,0,1,2:T(8,128)(2,1)S(1)}, bf16[2,4,1,32,1024]{4,3,0,1,2:T(8,128)(2,1)S(1)}, u32[]{:S(2)}, u32[]{:S(2)}) collective-permute-start(bf16[2,4,1,32,1024]{4,3,0,1,2:T(8,128)(2,1)S(1)} %get-tuple-element.14), channel_id=1, source_target_pairs={{0,4},{4,0},{1,5},{5,1},{2,6},{6,2},{3,7},{7,3},{8,12},{12,8},{9,1... | collective-permute-start | bytes 1572872 | tf_op jit(solution)/shard_map/ppermute | solution.py:33
  68.1 2.1 %copy-start.4 = (bf16[1024]{0:T(1024)(128)(2,1)S(1)}, bf16[1024]{0:T(1024)(128)(2,1)}, u32[]{:S(2)}) copy-start(bf16[1024]{0:T(1024)(128)(2,1)} %param.13) | copy-start | bytes 6148
  68.3 25.4 %collective-permute-start.3 = (bf16[1,8,1,32,1024]{4,3,1,2,0:T(8,128)(2,1)S(1)}, bf16[1,8,1,32,1024]{4,3,1,2,0:T(8,128)(2,1)S(1)}, u32[]{:S(2)}, u32[]{:S(2)}) collective-permute-start(bf16[1,8,1,32,1024]{4,3,1,2,0:T(8,128)(2,1)S(1)} %get-tuple-element.12), channel_id=1, source_target_pairs={{0,8},{8,0},{1,9},{9,1},{2,10},{10,2},{3,11},{11,3},{4,12},{12,4},... | collective-permute-start | bytes 1572872 | tf_op jit(solution)/shard_map/ppermute | solution.py:33
  103.2 10.2 %collective-permute-start.4 = (bf16[512,512]{1,0:T(8,128)(2,1)}, bf16[512,512]{1,0:T(8,128)(2,1)}, u32[]{:S(2)}, u32[]{:S(2)}) collective-permute-start(bf16[512,512]{1,0:T(8,128)(2,1)} %convolution_convert_fusion.2), channel_id=1, source_target_pairs={{0,1},{1,2},{2,3},{3,4},{4,5},{5,6},{6,7},{7,8},{8,9},{9,10},{10,1... | collective-permute-start | bytes 1572872 | tf_op jit(solution)/shard_map/ppermute | solution.py:23
  118.1 4.0 %copy-start.3 = (bf16[1,1024,256]{1,2,0:T(8,128)(2,1)S(1)}, bf16[1,1024,256]{1,2,0:T(8,128)(2,1)}, u32[]{:S(2)}) copy-start(bf16[1,1024,256]{1,2,0:T(8,128)(2,1)} %copy.33) | copy-start | bytes 1572868
  122.2 5.9 %copy-start.1 = (bf16[1024,1024]{1,0:T(8,128)(2,1)S(1)}, bf16[1024,1024]{1,0:T(8,128)(2,1)}, u32[]{:S(2)}) copy-start(bf16[1024,1024]{1,0:T(8,128)(2,1)} %param.11) | copy-start | bytes 6291460
where the time goes:
time: 129 us; the launch traced here: 128 us
  waiting for transfers between devices  50.9 us (39%)
  matrix products  27.4 us (21%)
  local copies, waits for them, and re-layouts  22.9 us (18%)
  other arithmetic  17.1 us (13%)
  starting transfers between devices  9.66 us (7%)
    ppermute x4, waiting for transfers between devices, partner(): return lax.ppermute(block, axis, route)  48.7 us
    dot_general x1, matrix products, body(): jnp.dot(tokens, w_lin, preferred_element_type=jnp.float32)  6.54 us
    unnamed x16, local copies, waits for them, and re-layouts  5.87 us
    ppermute x4, starting transfers between devices, partner(): return lax.ppermute(block, axis, route)  5.76 us
    dot_general x1, matrix products, body(): jnp.einsum('fkgpm,fmkd->fpkgd', weights, window_values, preferred_element...  4.55 us
    dot_general x1, matrix products, body(): jnp.einsum('bhnm,bmhe->bnhe', local_weights, value_rows, preferred_elemen...  4.03 us
    reduce_sum x1, other arithmetic, body(): jnp.sum(raised, axis=-1, keepdims=True)  3.99 us
    ppermute x1, starting transfers between devices, shifted(): return lax.ppermute(block, axis, route)  3.91 us
  transfers between devices with their start and end apart: 5, of which 5 were waited for; matrix products, arithmetic and copies ran while one was open for 3% of the time, Pallas kernels for 0%

commit v1 on v0

v1 whole, which is shorter than its diff:
```python
import functools
import math

import jax
import jax.numpy as jnp
from jax import lax
from jax.experimental import pallas as pl
from jax.experimental.pallas import tpu as pltpu
from jax.sharding import PartitionSpec as P

HEADS = 8
HD = 128
KVH = 2
SB = 16
SPAN = 128
PAIR = 2

epsilon = 1e-06
MIB = 1 << 20


def shifted(block, axis, distance):
    devices = range(lax.axis_size(axis))
    route = [(i - distance, i) for i in devices if i - distance in devices]
    return lax.ppermute(block, axis, route)


def dot(a, b):
    return jnp.dot(a, b, preferred_element_type=jnp.float32)


def dot_nt(a, b):
    return lax.dot_general(a, b, (((1,), (1,)), ((), ())), preferred_element_type=jnp.float32)


def dot_tn(a, b):
    return lax.dot_general(a, b, (((0,), (0,)), ((), ())), preferred_element_type=jnp.float32)


def mixer_kernel(has_state, *refs):
    if has_state:
        tokens_ref, residual_ref, wq_ref, wk_ref, wv_ref, gain_ref, state_ref, out_ref = refs
    else:
        tokens_ref, residual_ref, wq_ref, wk_ref, wv_ref, gain_ref, out_ref = refs
    tokens = tokens_ref[...]
    rows = tokens.shape[0]
    query = dot(tokens, wq_ref[...]).astype(jnp.bfloat16)
    key = dot(tokens, wk_ref[...]).astype(jnp.bfloat16)
    value = dot(tokens, wv_ref[...]).astype(jnp.bfloat16)
    causal = lax.broadcasted_iota(jnp.int32, (SPAN, SPAN), 0) >= lax.broadcasted_iota(
        jnp.int32, (SPAN, SPAN), 1
    )
    for head in range(PAIR):
        lanes = slice(head * HD, (head + 1) * HD)
        gain = gain_ref[:, lanes].astype(jnp.float32)
        state = state_ref[head] if has_state else None
        for span in range(rows // SPAN):
            here = slice(span * SPAN, (span + 1) * SPAN)
            q, k, v = query[here, lanes], key[here, lanes], value[here, lanes]
            local = jnp.where(causal, dot_nt(q, k), 0.0).astype(jnp.bfloat16)
            if state is None:
                mixed = dot(local, v)
            else:
                mixed = dot(
                    jnp.concatenate([q, local], axis=1),
                    jnp.concatenate([state.astype(jnp.bfloat16), v], axis=0),
                )
            if (span + 1) * SPAN < rows:
                update = dot_tn(k, v)
                state = update if state is None else state + update
            mean_square = jnp.mean(mixed * mixed, axis=-1, keepdims=True)
            normed = mixed * lax.rsqrt(mean_square + epsilon) * gain
            out_ref[here, lanes] = (
                residual_ref[here, lanes].astype(jnp.float32) + normed
            ).astype(jnp.bfloat16)


def mixer(tokens, w_lin, gain_lin, state):
    rows, width = tokens.shape
    steps = HEADS // PAIR
    columns = PAIR * HD
    in_specs = [
        pl.BlockSpec((rows, width), lambda c: (0, 0)),
        pl.BlockSpec((rows, columns), lambda c: (0, c)),
        pl.BlockSpec((width, columns), lambda c: (0, c)),
        pl.BlockSpec((width, columns), lambda c: (0, steps + c)),
        pl.BlockSpec((width, columns), lambda c: (0, 2 * steps + c)),
        pl.BlockSpec((1, columns), lambda c: (0, c)),
    ]
    operands = [tokens, tokens, w_lin, w_lin, w_lin, gain_lin.reshape(1, width)]
    if state is not None:
        in_specs.append(pl.BlockSpec((PAIR, HD, HD), lambda c: (c, 0, 0)))
        operands.append(state)
    return pl.pallas_call(
        functools.partial(mixer_kernel, state is not None),
        grid=(steps,),
        in_specs=in_specs,
        out_specs=pl.BlockSpec((rows, columns), lambda c: (0, c)),
        out_shape=jax.ShapeDtypeStruct((rows, width), jnp.bfloat16),
        compiler_params=pltpu.CompilerParams(vmem_limit_bytes=24 * MIB),
        cost_estimate=pl.CostEstimate(
            flops=2 * rows * width * 3 * width + 8 * rows * SPAN * width,
            bytes_accessed=2 * (3 * width * width + 2 * rows * width),
            transcendentals=rows * HEADS,
        ),
        name="mixer",
    )(*operands)


def incoming_state(tokens, w_lin, time_ranges):
    rows, width = tokens.shape
    packed = dot(tokens, w_lin[:, width:]).astype(jnp.bfloat16).reshape(rows, 2, HEADS, HD)
    block_total = jnp.einsum(
        "nhd,nhe->hde", packed[:, 0], packed[:, 1], preferred_element_type=jnp.float32
    )
    within = lax.axis_index("tm") // SB

    def advance_hop(turn_index, running_total):
        moved = shifted(running_total + block_total, "tm", SB)
        return jnp.where(within > 0, moved, 0.0)

    return lax.fori_loop(0, time_ranges - 1, advance_hop, jnp.zeros_like(block_total))


def pairs_kernel(hidden_ref, gain_ref, w_ref, normed_ref, pairs_ref):
    widened = hidden_ref[...].astype(jnp.float32)
    mean_square = jnp.mean(widened * widened, axis=-1, keepdims=True)
    normed = (
        widened * lax.rsqrt(mean_square + epsilon) * gain_ref[...].astype(jnp.float32)
    ).astype(jnp.bfloat16)
    normed_ref[...] = normed
    pairs_ref[...] = dot(normed, w_ref[...]).astype(jnp.bfloat16)


def make_pairs(hidden, gain, w_kv):
    rows, width = hidden.shape
    wide = w_kv.shape[1]
    block = rows // 2
    return pl.pallas_call(
        pairs_kernel,
        grid=(rows // block,),
        in_specs=[
            pl.BlockSpec((block, width), lambda i: (i, 0)),
            pl.BlockSpec((1, width), lambda i: (0, 0)),
            pl.BlockSpec((width, wide), lambda i: (0, 0)),
        ],
        out_specs=[
            pl.BlockSpec((block, width), lambda i: (i, 0)),
            pl.BlockSpec((block, wide), lambda i: (i, 0)),
        ],
        out_shape=[
            jax.ShapeDtypeStruct((rows, width), jnp.bfloat16),
            jax.ShapeDtypeStruct((rows, wide), jnp.bfloat16),
        ],
        compiler_params=pltpu.CompilerParams(vmem_limit_bytes=16 * MIB),
        cost_estimate=pl.CostEstimate(
            flops=2 * rows * width * wide,
            bytes_accessed=2 * (2 * rows * width + width * wide + rows * wide),
            transcendentals=rows,
        ),
        name="pairs",
    )(hidden, gain.reshape(1, width), w_kv)


SCORE_SCALE = math.log2(math.e) / math.sqrt(HD)


def with_ones(value):
    return jnp.concatenate([value, jnp.ones_like(value)], axis=1)


def own_kernel(normed_ref, w_ref, key_ref, value_ref, query_ref, partial_ref, log_ref):
    query = dot(normed_ref[...], w_ref[...]).astype(jnp.bfloat16)
    query_ref[...] = query
    key = key_ref[...]
    value = with_ones(value_ref[...])
    for head in range(PAIR):
        lanes = slice(head * HD, (head + 1) * HD)
        scores = dot_nt(query[:, lanes], key)
        largest = jnp.max(scores, axis=-1, keepdims=True)
        raised = jnp.exp2((scores - largest) * SCORE_SCALE).astype(jnp.bfloat16)
        summed = dot(raised, value)
        total = summed[:, HD:]
        partial_ref[:, lanes] = summed[:, :HD] / total
        log_ref[0, :, head : head + 1] = largest * SCORE_SCALE + jnp.log2(total[:, :1])


def own_frame(normed, w_query, pairs):
    rows, width = normed.shape
    steps = HEADS // PAIR
    columns = PAIR * HD
    per_kv = HEADS // KVH // PAIR
    return pl.pallas_call(
        own_kernel,
        grid=(steps,),
        in_specs=[
            pl.BlockSpec((rows, width), lambda c: (0, 0)),
            pl.BlockSpec((width, columns), lambda c: (0, c)),
            pl.BlockSpec((rows, HD), lambda c: (0, c // per_kv)),
            pl.BlockSpec((rows, HD), lambda c: (0, KVH + c // per_kv)),
        ],
        out_specs=[
            pl.BlockSpec((rows, columns), lambda c: (0, c)),
            pl.BlockSpec((rows, columns), lambda c: (0, c)),
            pl.BlockSpec((1, rows, PAIR), lambda c: (c, 0, 0)),
        ],
        out_shape=[
            jax.ShapeDtypeStruct((rows, width), jnp.bfloat16),
            jax.ShapeDtypeStruct((rows, width), jnp.float32),
            jax.ShapeDtypeStruct((steps, rows, PAIR), jnp.float32),
        ],
        compiler_params=pltpu.CompilerParams(vmem_limit_bytes=32 * MIB),
        cost_estimate=pl.CostEstimate(
            flops=2 * rows * width * width + 4 * rows * rows * width,
            bytes_accessed=2 * width * width + 8 * rows * width,
            transcendentals=rows * rows * HEADS,
        ),
        name="own_frame",
    )(normed, w_query, pairs, pairs)


def earlier_kernel(query_ref, key_ref, value_ref, partial_ref, log_ref, usable_ref, out_ref):
    query = query_ref[...]
    key = key_ref[...]
    value = with_ones(value_ref[...])
    barred = jnp.where(usable_ref[0] > 0, 0.0, -jnp.inf)
    for head in range(PAIR):
        lanes = slice(head * HD, (head + 1) * HD)
        own = log_ref[0, :, head : head + 1]
        scores = dot_nt(query[:, lanes], key)
        here = jnp.max(scores, axis=-1, keepdims=True) * SCORE_SCALE + barred
        largest = jnp.maximum(here, own)
        raised = jnp.exp2(scores * SCORE_SCALE - (largest - barred)).astype(jnp.bfloat16)
        summed = dot(raised, value)
        share = jnp.exp2(own - largest)
        out_ref[:, lanes] = (
            (partial_ref[:, lanes] * share + summed[:, :HD]) / (share + summed[:, HD:])
        ).astype(jnp.bfloat16)


def earlier_frame(query, earlier_pairs, partial, log_total, usable):
    rows, width = query.shape
    steps = HEADS // PAIR
    columns = PAIR * HD
    per_kv = HEADS // KVH // PAIR
    return pl.pallas_call(
        earlier_kernel,
        grid=(steps,),
        in_specs=[
            pl.BlockSpec((rows, columns), lambda c: (0, c)),
            pl.BlockSpec((rows, HD), lambda c: (0, c // per_kv)),
            pl.BlockSpec((rows, HD), lambda c: (0, KVH + c // per_kv)),
            pl.BlockSpec((rows, columns), lambda c: (0, c)),
            pl.BlockSpec((1, rows, PAIR), lambda c: (c, 0, 0)),
            pl.BlockSpec(memory_space=pltpu.SMEM),
        ],
        out_specs=pl.BlockSpec((rows, columns), lambda c: (0, c)),
        out_shape=jax.ShapeDtypeStruct((rows, width), jnp.bfloat16),
        compiler_params=pltpu.CompilerParams(vmem_limit_bytes=32 * MIB),
        cost_estimate=pl.CostEstimate(
            flops=4 * rows * rows * width,
            bytes_accessed=10 * rows * width,
            transcendentals=rows * rows * HEADS,
        ),
        name="earlier_frame",
    )(query, earlier_pairs, earlier_pairs, partial, log_total, usable)


def body(space_time, w_lin, gain_lin, w_query, w_kv, frame_attention_gain):
    tokens = space_time[0]
    rows, width = tokens.shape
    devices = lax.axis_size("tm")
    time_ranges = devices // SB
    state = incoming_state(tokens, w_lin, time_ranges) if time_ranges > 1 else None
    hidden = mixer(tokens, w_lin, gain_lin, state)
    teams = [[t * SB + s for s in range(SB)] for t in range(time_ranges)]
    frame_rows = lax.all_to_all(
        hidden.reshape(SB, rows // SB, width),
        "tm",
        0,
        0,
        axis_index_groups=teams,
        tiled=True,
    ).reshape(rows, width)
    normed, pairs = make_pairs(frame_rows, frame_attention_gain, w_kv)
    earlier_pairs = shifted(pairs, "tm", 1)
    query, partial, log_total = own_frame(normed, w_query, pairs)
    usable = (lax.axis_index("tm") > 0).astype(jnp.int32).reshape(1)
    attended = earlier_frame(query, earlier_pairs, partial, log_total, usable)
    return attended[None]


def solution(mesh):
    placed = (P(("groups", "tm"), None, None), P(), P(), P(), P(), P())
    return jax.shard_map(
        body, mesh=mesh, in_specs=placed, out_specs=P(("groups", "tm"), None, None), check_vma=False
    )
```

time: 129 us -> 71.5 us (0.55)
  the two profiles are of different devices: /device:TPU:1 before, /device:TPU:13 now
where the time goes in v1:
time: 71.5 us; the launch traced here: 71.1 us
  Pallas kernels  29.6 us (41%)
  waiting for transfers between devices  24.9 us (35%)
  starting transfers between devices  10.3 us (14%)
  local copies, waits for them, and re-layouts  6.29 us (9%)
    all_to_all x1, waiting for transfers between devices, body(): lax.all_to_all(hidden.reshape(SB, rows // SB, width), 'tm', 0, 0, axis_in...  24.9 us
    pallas_call x1, Pallas kernels, mixer(): pl.pallas_call(functools.partial(mixer_kernel, state is not None), grid=(...  12.3 us
    pallas_call x1, Pallas kernels, own_frame(): pl.pallas_call(own_kernel, grid=(steps,), in_specs=[pl.BlockSpec((rows, w...  8.43 us
    pallas_call x1, Pallas kernels, earlier_frame(): pl.pallas_call(earlier_kernel, grid=(steps,), in_specs=[pl.BlockSpec((row...  7.06 us
    all_to_all x1, starting transfers between devices, body(): lax.all_to_all(hidden.reshape(SB, rows // SB, width), 'tm', 0, 0, axis_in...  6.69 us
    unnamed x10, local copies, waits for them, and re-layouts  5.6 us
    ppermute x1, starting transfers between devices, shifted(): return lax.ppermute(block, axis, route)  3.61 us
    pallas_call x1, Pallas kernels, make_pairs(): pl.pallas_call(pairs_kernel, grid=(rows // block,), in_specs=[pl.BlockSpe...  1.82 us
  transfers between devices with their start and end apart: 2, of which 1 were waited for; matrix products, arithmetic and copies ran while one was open for 0% of the time, Pallas kernels for 12%

profile of v1, /device:TPU:13, one launch (start us, length us, event | category | flops | bytes accessed | tf_op | source)
XLA Modules:
  0.0 71.1 jit_solution(2557612039081410824)
XLA Ops:
  0.0 0.7 reshape.17.refs_5_
  0.7 0.0 copy-start
  0.7 2.8 %copy-done = bf16[1024,3072]{1,0:T(8,128)(2,1)S(1)} copy-done((bf16[1024,3072]{1,0:T(8,128)(2,1)S(1)}, bf16[1024,3072]{1,0:T(8,128)(2,1)}, u32[]{:S(2)}) %copy-start) | copy-done | bytes 6291480
  3.5 0.0 copy-start.1
  3.5 1.2 %copy-done.1 = bf16[1,512,1024]{2,1,0:T(8,128)(2,1)S(1)} copy-done((bf16[1,512,1024]{2,1,0:T(8,128)(2,1)S(1)}, bf16[1,512,1024]{2,1,0:T(8,128)(2,1)}, u32[]{:S(2)}) %copy-start.1) | copy-done | bytes 1048600
  4.7 12.3 %mixer.1 = bf16[512,1024]{1,0:T(8,128)(2,1)} custom-call(bf16[512,1024]{1,0:T(8,128)(2,1)S(1)} %bitcast.5, bf16[512,1024]{1,0:T(8,128)(2,1)S(1)} %bitcast.6, bf16[1024,3072]{1,0:T(8,128)(2,1)S(1)} %copy-done, bf16[1024,3072]{1,0:T(8,128)(2,1)S(1)} %copy-done, bf16[1024,3072]{1,0:T(8,128)(2,1)S(1)} %copy-done, bf16[1,1024]{1,0:T(2,128)(2,1)S(1)} %reshape.17.refs_5_), custom_call_target="tpu_custom_call" | custom-call | flops 3758096384 | bytes 8388608 | tf_op jit(solution)/shard_map/mixer/pallas_call | solution.py:94
  17.0 0.0 copy-start.4
  17.0 0.0 copy-start.2
  17.0 6.7 %all-to-all-start = ((bf16[16,32,1024]{2,1,0:T(8,128)(2,1)}), bf16[16,32,1024]{2,1,0:T(8,128)(2,1)S(1)}, u32[]{:S(2)}, u32[]{:S(2)}) async-start(bf16[16,32,1024]{2,1,0:T(8,128)(2,1)} %bitcast.1), calls=%async_computation | async-start | bytes 2097152 | tf_op jit(solution)/shard_map/all_to_all | solution.py:277
  23.7 0.0 copy-done.4
  23.7 24.9 %all-to-all-done = bf16[16,32,1024]{2,1,0:T(8,128)(2,1)S(1)} async-done(((bf16[16,32,1024]{2,1,0:T(8,128)(2,1)}), bf16[16,32,1024]{2,1,0:T(8,128)(2,1)S(1)}, u32[]{:S(2)}, u32[]{:S(2)}) %all-to-all-start) | async-done | bytes 1048608 | tf_op jit(solution)/shard_map/all_to_all | solution.py:277
  48.6 0.0 copy-done.2
  48.6 1.8 %pairs.1 = (bf16[512,1024]{1,0:T(8,128)(2,1)S(1)}, bf16[512,512]{1,0:T(8,128)(2,1)}) custom-call(bf16[512,1024]{1,0:T(8,128)(2,1)S(1)} %bitcast.7, bf16[1,1024]{1,0:T(2,128)(2,1)S(1)} %reshape.20.gain_ref, bf16[1024,512]{1,0:T(8,128)(2,1)S(1)} %copy-done.2), custom_call_target="tpu_custom_call" | custom-call | flops 536870912 | bytes 3670016 | tf_op jit(solution)/shard_map/pairs/pallas_call | solution.py:139
  50.4 3.6 %collective-permute-start = (bf16[512,512]{1,0:T(8,128)(2,1)}, bf16[512,512]{1,0:T(8,128)(2,1)S(1)}, u32[]{:S(2)}, u32[]{:S(2)}) collective-permute-start(bf16[512,512]{1,0:T(8,128)(2,1)} %get-tuple-element.11.key_ref.value_ref), channel_id=1, source_target_pairs={{0,1},{1,2},{2,3},{3,4},{4,5},{5,6},{6,7},{7,8},{8,9},{9,10},{10,1... | collective-permute-start | bytes 1572872 | tf_op jit(solution)/shard_map/ppermute | solution.py:25
  54.0 0.0 copy-start.3
  54.0 1.6 %copy-done.3 = bf16[1024,1024]{1,0:T(8,128)(2,1)S(1)} copy-done((bf16[1024,1024]{1,0:T(8,128)(2,1)S(1)}, bf16[1024,1024]{1,0:T(8,128)(2,1)}, u32[]{:S(2)}) %copy-start.3) | copy-done | bytes 2097176
  55.6 8.4 %own_frame.1 = (bf16[512,1024]{1,0:T(8,128)(2,1)S(1)}, f32[512,1024]{1,0:T(8,128)S(1)}, f32[4,512,2]{2,1,0:T(8,128)S(1)}) custom-call(bf16[512,1024]{1,0:T(8,128)(2,1)S(1)} %get-tuple-element.10.normed_ref, bf16[1024,1024]{1,0:T(8,128)(2,1)S(1)} %copy-done.3, bf16[512,512]{1,0:T(8,128)(2,1)} %get-tuple-element.11.key_ref.value_ref, ...), custom_call_target="tpu_custom_call" | custom-call | flops 2147483648 | bytes 6291456 | tf_op jit(solution)/shard_map/own_frame/pallas_call | solution.py:193
  64.0 0.0 collective-permute-done.key_ref.value_ref
  64.1 7.1 %earlier_frame.1 = bf16[512,1024]{1,0:T(8,128)(2,1)} custom-call(bf16[512,1024]{1,0:T(8,128)(2,1)S(1)} %get-tuple-element.12.query_ref, bf16[512,512]{1,0:T(8,128)(2,1)S(1)} %collective-permute-done.key_ref.value_ref, bf16[512,512]{1,0:T(8,128)(2,1)S(1)} %collective-permute-done.key_ref.value_ref, f32[512,1024]{1,0:T(8,128)S(1)} %get-tuple-element.13.partial_ref, ...), custom_call_target="tpu_custom_call" | custom-call | flops 1073741824 | bytes 5242880 | tf_op jit(solution)/shard_map/earlier_frame/pallas_call | solution.py:246
  (1 shorter events, 0.0 us)
Async XLA Ops:
  0.7 2.8 %copy-start = (bf16[1024,3072]{1,0:T(8,128)(2,1)S(1)}, bf16[1024,3072]{1,0:T(8,128)(2,1)}, u32[]{:S(2)}) copy-start(bf16[1024,3072]{1,0:T(8,128)(2,1)} %refs_4_.1) | copy-start | bytes 18874372
  3.5 1.2 %copy-start.1 = (bf16[1,512,1024]{2,1,0:T(8,128)(2,1)S(1)}, bf16[1,512,1024]{2,1,0:T(8,128)(2,1)}, u32[]{:S(2)}) copy-start(bf16[1,512,1024]{2,1,0:T(8,128)(2,1)} %param.6) | copy-start | bytes 3145732
  17.0 6.7 %copy-start.4 = (bf16[1024]{0:T(1024)(128)(2,1)S(1)}, bf16[1024]{0:T(1024)(128)(2,1)}, u32[]{:S(2)}) copy-start(bf16[1024]{0:T(1024)(128)(2,1)} %param.11) | copy-start | bytes 6148
  17.0 31.6 %copy-start.2 = (bf16[1024,512]{1,0:T(8,128)(2,1)S(1)}, bf16[1024,512]{1,0:T(8,128)(2,1)}, u32[]{:S(2)}) copy-start(bf16[1024,512]{1,0:T(8,128)(2,1)} %w_ref.2) | copy-start | bytes 3145732
  17.0 31.6 %all-to-all-start = ((bf16[16,32,1024]{2,1,0:T(8,128)(2,1)}), bf16[16,32,1024]{2,1,0:T(8,128)(2,1)S(1)}, u32[]{:S(2)}, u32[]{:S(2)}) async-start(bf16[16,32,1024]{2,1,0:T(8,128)(2,1)} %bitcast.1), calls=%async_computation | async-start | bytes 2097152 | tf_op jit(solution)/shard_map/all_to_all | solution.py:277
  50.4 13.7 %collective-permute-start = (bf16[512,512]{1,0:T(8,128)(2,1)}, bf16[512,512]{1,0:T(8,128)(2,1)S(1)}, u32[]{:S(2)}, u32[]{:S(2)}) collective-permute-start(bf16[512,512]{1,0:T(8,128)(2,1)} %get-tuple-element.11.key_ref.value_ref), channel_id=1, source_target_pairs={{0,1},{1,2},{2,3},{3,4},{4,5},{5,6},{6,7},{7,8},{8,9},{9,10},{10,1... | collective-permute-start | bytes 1572872 | tf_op jit(solution)/shard_map/ppermute | solution.py:25
  54.0 1.6 %copy-start.3 = (bf16[1024,1024]{1,0:T(8,128)(2,1)S(1)}, bf16[1024,1024]{1,0:T(8,128)(2,1)}, u32[]{:S(2)}) copy-start(bf16[1024,1024]{1,0:T(8,128)(2,1)} %w_ref.3) | copy-start | bytes 6291460

commit v2 on v1

v2 whole, which is shorter than its diff:
```python
import functools
import math

import jax
import jax.numpy as jnp
from jax import lax
from jax.experimental import pallas as pl
from jax.experimental.pallas import tpu as pltpu
from jax.sharding import PartitionSpec as P

HEADS = 8
HD = 128
KVH = 2
SB = 16
SPAN = 128
PAIR = 2

APART = (0, 15, 14, 4, 10, 3, 9, 2, 8, 1, 7, 13, 6, 12, 5, 11)

epsilon = 1e-06
MIB = 1 << 20


def shifted(block, axis, distance):
    devices = range(lax.axis_size(axis))
    route = [(i - distance, i) for i in devices if i - distance in devices]
    return lax.ppermute(block, axis, route)


def dot(a, b):
    return jnp.dot(a, b, preferred_element_type=jnp.float32)


def dot_nt(a, b):
    return lax.dot_general(a, b, (((1,), (1,)), ((), ())), preferred_element_type=jnp.float32)


def dot_tn(a, b):
    return lax.dot_general(a, b, (((0,), (0,)), ((), ())), preferred_element_type=jnp.float32)


def mixer_kernel(has_state, place_ref, *refs):
    if has_state:
        state_ref, *refs = refs
    tokens_ref, residual_ref, wq_ref, wk_ref, wv_ref, gain_ref, *tiles, hidden_ref = refs
    tokens = tokens_ref[...]
    rows = tokens.shape[0]
    query = dot(tokens, wq_ref[...]).astype(jnp.bfloat16)
    key = dot(tokens, wk_ref[...]).astype(jnp.bfloat16)
    value = dot(tokens, wv_ref[...]).astype(jnp.bfloat16)
    causal = lax.broadcasted_iota(jnp.int32, (SPAN, SPAN), 0) >= lax.broadcasted_iota(
        jnp.int32, (SPAN, SPAN), 1
    )
    spans = rows // SPAN
    units = []
    for head in range(PAIR):
        for span in range(spans):
            here = slice(span * SPAN, (span + 1) * SPAN)
            lanes = slice(head * HD, (head + 1) * HD)
            units.append((head, span, here, lanes))
    local, before = {}, {}
    for head, span, here, lanes in units:
        scores = dot_nt(query[here, lanes], key[here, lanes])
        local[head, span] = jnp.where(causal, scores, 0.0).astype(jnp.bfloat16)
    for head in range(PAIR):
        state = state_ref[head] if has_state else None
        for span in range(spans):
            before[head, span] = state
            if span + 1 < spans:
                here = slice(span * SPAN, (span + 1) * SPAN)
                lanes = slice(head * HD, (head + 1) * HD)
                update = dot_tn(key[here, lanes], value[here, lanes])
                state = update if state is None else state + update
    mixed = {}
    for head, span, here, lanes in units:
        state = before[head, span]
        if state is None:
            mixed[head, span] = dot(local[head, span], value[here, lanes])
        else:
            mixed[head, span] = dot(
                jnp.concatenate([query[here, lanes], local[head, span]], axis=1),
                jnp.concatenate([state.astype(jnp.bfloat16), value[here, lanes]], axis=0),
            )
    for head, span, here, lanes in units:
        out = mixed[head, span]
        mean_square = jnp.mean(out * out, axis=-1, keepdims=True)
        normed = out * lax.rsqrt(mean_square + epsilon) * gain_ref[:, lanes].astype(jnp.float32)
        hidden_ref[here, lanes] = (
            residual_ref[here, lanes].astype(jnp.float32) + normed
        ).astype(jnp.bfloat16)
    size = rows // SB
    for apart, tile in zip(APART, tiles):
        start = pl.multiple_of((place_ref[0] ^ apart) * size, size)
        tile[...] = hidden_ref[pl.ds(start, size), :]


def mixer(place, tokens, w_lin, gain_lin, state):
    rows, width = tokens.shape
    steps = HEADS // PAIR
    columns = PAIR * HD
    in_specs = [pl.BlockSpec(memory_space=pltpu.SMEM)]
    operands = [place]
    if state is not None:
        in_specs.append(pl.BlockSpec((PAIR, HD, HD), lambda c: (c, 0, 0)))
        operands.append(state)
    in_specs += [
        pl.BlockSpec((rows, width), lambda c: (0, 0)),
        pl.BlockSpec((rows, columns), lambda c: (0, c)),
        pl.BlockSpec((width, columns), lambda c: (0, c)),
        pl.BlockSpec((width, columns), lambda c: (0, steps + c)),
        pl.BlockSpec((width, columns), lambda c: (0, 2 * steps + c)),
        pl.BlockSpec((1, columns), lambda c: (0, c)),
    ]
    operands += [tokens, tokens, w_lin, w_lin, w_lin, gain_lin.reshape(1, width)]
    return pl.pallas_call(
        functools.partial(mixer_kernel, state is not None),
        grid=(steps,),
        in_specs=in_specs,
        out_specs=[pl.BlockSpec((rows // SB, columns), lambda c: (0, c))] * SB,
        out_shape=[jax.ShapeDtypeStruct((rows // SB, width), jnp.bfloat16)] * SB,
        scratch_shapes=[pltpu.VMEM((rows, columns), jnp.bfloat16)],
        compiler_params=pltpu.CompilerParams(vmem_limit_bytes=56 * MIB),
        cost_estimate=pl.CostEstimate(
            flops=2 * rows * width * 3 * width + 8 * rows * SPAN * width,
            bytes_accessed=2 * (3 * width * width + 2 * rows * width),
            transcendentals=rows * HEADS,
        ),
        name="mixer",
    )(*operands)


def incoming_state(tokens, w_lin, time_ranges):
    rows, width = tokens.shape
    packed = dot(tokens, w_lin[:, width:]).astype(jnp.bfloat16).reshape(rows, 2, HEADS, HD)
    block_total = jnp.einsum(
        "nhd,nhe->hde", packed[:, 0], packed[:, 1], preferred_element_type=jnp.float32
    )
    within = lax.axis_index("tm") // SB

    def advance_hop(turn_index, running_total):
        moved = shifted(running_total + block_total, "tm", SB)
        return jnp.where(within > 0, moved, 0.0)

    return lax.fori_loop(0, time_ranges - 1, advance_hop, jnp.zeros_like(block_total))


def pairs_kernel(gain_ref, w_ref, *refs):
    tiles, normed_ref, pairs_ref = refs[:-2], refs[-2], refs[-1]
    widened = jnp.concatenate([tile[...] for tile in tiles], axis=0).astype(jnp.float32)
    mean_square = jnp.mean(widened * widened, axis=-1, keepdims=True)
    normed = (
        widened * lax.rsqrt(mean_square + epsilon) * gain_ref[...].astype(jnp.float32)
    ).astype(jnp.bfloat16)
    normed_ref[...] = normed
    pairs_ref[...] = dot(normed, w_ref[...]).astype(jnp.bfloat16)


def make_pairs(tiles, gain, w_kv):
    size, width = tiles[0].shape
    rows = size * len(tiles)
    wide = w_kv.shape[1]
    return pl.pallas_call(
        pairs_kernel,
        out_shape=[
            jax.ShapeDtypeStruct((rows, width), jnp.bfloat16),
            jax.ShapeDtypeStruct((rows, wide), jnp.bfloat16),
        ],
        compiler_params=pltpu.CompilerParams(vmem_limit_bytes=16 * MIB),
        cost_estimate=pl.CostEstimate(
            flops=2 * rows * width * wide,
            bytes_accessed=2 * (2 * rows * width + width * wide + rows * wide),
            transcendentals=rows,
        ),
        name="pairs",
    )(gain.reshape(1, width), w_kv, *tiles)


SCORE_SCALE = math.log2(math.e) / math.sqrt(HD)


def with_ones(value):
    return jnp.concatenate([value, jnp.ones_like(value)], axis=1)


def head_lanes(head):
    return slice(head * HD, (head + 1) * HD)


def own_kernel(normed_ref, w_ref, key_ref, value_ref, query_ref, partial_ref, log_ref):
    query = dot(normed_ref[...], w_ref[...]).astype(jnp.bfloat16)
    query_ref[...] = query
    key = key_ref[...]
    value = with_ones(value_ref[...])
    heads = query.shape[1] // HD
    scores = dot_nt(query[:, head_lanes(0)], key)
    for head in range(heads):
        upcoming = dot_nt(query[:, head_lanes(head + 1)], key) if head + 1 < heads else None
        largest = jnp.max(scores, axis=-1, keepdims=True)
        raised = jnp.exp2((scores - largest) * SCORE_SCALE).astype(jnp.bfloat16)
        summed = dot(raised, value)
        total = summed[:, HD:]
        partial_ref[:, head_lanes(head)] = summed[:, :HD] / total
        log_ref[0, :, head : head + 1] = largest * SCORE_SCALE + jnp.log2(total[:, :1])
        scores = upcoming


def own_frame(normed, w_query, pairs):
    rows, width = normed.shape
    group = HEADS // KVH
    columns = group * HD
    return pl.pallas_call(
        own_kernel,
        grid=(KVH,),
        in_specs=[
            pl.BlockSpec((rows, width), lambda c: (0, 0)),
            pl.BlockSpec((width, columns), lambda c: (0, c)),
            pl.BlockSpec((rows, HD), lambda c: (0, c)),
            pl.BlockSpec((rows, HD), lambda c: (0, KVH + c)),
        ],
        out_specs=[
            pl.BlockSpec((rows, columns), lambda c: (0, c)),
            pl.BlockSpec((rows, columns), lambda c: (0, c)),
            pl.BlockSpec((1, rows, group), lambda c: (c, 0, 0)),
        ],
        out_shape=[
            jax.ShapeDtypeStruct((rows, width), jnp.bfloat16),
            jax.ShapeDtypeStruct((rows, width), jnp.float32),
            jax.ShapeDtypeStruct((KVH, rows, group), jnp.float32),
        ],
        compiler_params=pltpu.CompilerParams(vmem_limit_bytes=32 * MIB),
        cost_estimate=pl.CostEstimate(
            flops=2 * rows * width * width + 4 * rows * rows * width,
            bytes_accessed=2 * width * width + 8 * rows * width,
            transcendentals=rows * rows * HEADS,
        ),
        name="own_frame",
    )(normed, w_query, pairs, pairs)


def earlier_kernel(place_ref, query_ref, key_ref, value_ref, partial_ref, log_ref, out_ref):
    rows = query_ref.shape[0]
    heads = query_ref.shape[1] // HD
    key = key_ref[...]
    value = with_ones(value_ref[...])
    barred = jnp.where(place_ref[1] > 0, 0.0, -jnp.inf)
    size = rows // SB
    scores = dot_nt(query_ref[:, head_lanes(0)], key)
    for head in range(heads):
        lanes = head_lanes(head)
        upcoming = dot_nt(query_ref[:, head_lanes(head + 1)], key) if head + 1 < heads else None
        own = log_ref[0, :, head : head + 1]
        here = jnp.max(scores, axis=-1, keepdims=True) * SCORE_SCALE + barred
        largest = jnp.maximum(here, own)
        raised = jnp.exp2(scores * SCORE_SCALE - (largest - barred)).astype(jnp.bfloat16)
        summed = dot(raised, value)
        share = jnp.exp2(own - largest)
        mixed = (
            (partial_ref[:, lanes] * share + summed[:, :HD]) / (share + summed[:, HD:])
        ).astype(jnp.bfloat16)
        for slot, apart in enumerate(APART):
            start = pl.multiple_of((place_ref[0] ^ apart) * size, size)
            out_ref[pl.ds(start, size), lanes] = mixed[slot * size : (slot + 1) * size]
        scores = upcoming


def earlier_frame(place, query, earlier_pairs, partial, log_total):
    rows, width = query.shape
    group = HEADS // KVH
    columns = group * HD
    return pl.pallas_call(
        earlier_kernel,
        grid=(KVH,),
        in_specs=[
            pl.BlockSpec(memory_space=pltpu.SMEM),
            pl.BlockSpec((rows, columns), lambda c: (0, c)),
            pl.BlockSpec((rows, HD), lambda c: (0, c)),
            pl.BlockSpec((rows, HD), lambda c: (0, KVH + c)),
            pl.BlockSpec((rows, columns), lambda c: (0, c)),
            pl.BlockSpec((1, rows, group), lambda c: (c, 0, 0)),
        ],
        out_specs=pl.BlockSpec((rows, columns), lambda c: (0, c)),
        out_shape=jax.ShapeDtypeStruct((rows, width), jnp.bfloat16),
        compiler_params=pltpu.CompilerParams(vmem_limit_bytes=32 * MIB),
        cost_estimate=pl.CostEstimate(
            flops=4 * rows * rows * width,
            bytes_accessed=10 * rows * width,
            transcendentals=rows * rows * HEADS,
        ),
        name="earlier_frame",
    )(place, query, earlier_pairs, earlier_pairs, partial, log_total)


def exchange(tiles):
    devices = lax.axis_size("tm")
    arrived = []
    for apart, tile in zip(APART, tiles):
        route = [(i, i - i % SB + (i % SB ^ apart)) for i in range(devices)]
        arrived.append(lax.ppermute(tile, "tm", route) if apart else tile)
    return arrived


def body(space_time, w_lin, gain_lin, w_query, w_kv, frame_attention_gain):
    tokens = space_time[0]
    time_ranges = lax.axis_size("tm") // SB
    index = lax.axis_index("tm")
    place = jnp.stack([index % SB, (index > 0).astype(jnp.int32)])
    state = incoming_state(tokens, w_lin, time_ranges) if time_ranges > 1 else None
    tiles = exchange(mixer(place, tokens, w_lin, gain_lin, state))
    normed, pairs = make_pairs(tiles, frame_attention_gain, w_kv)
    earlier_pairs = shifted(pairs, "tm", 1)
    query, partial, log_total = own_frame(normed, w_query, pairs)
    attended = earlier_frame(place, query, earlier_pairs, partial, log_total)
    return attended[None]


def solution(mesh):
    placed = (P(("groups", "tm"), None, None), P(), P(), P(), P(), P())
    return jax.shard_map(
        body, mesh=mesh, in_specs=placed, out_specs=P(("groups", "tm"), None, None), check_vma=False
    )
```

time: 71.5 us -> 61.9 us (0.87)
  the two profiles are of different devices: /device:TPU:13 before, /device:TPU:1 now
where the time goes in v2:
time: 61.9 us; the launch traced here: 61.4 us
  starting transfers between devices  27.6 us (45%)
  Pallas kernels  23.8 us (38%)
  waiting for transfers between devices  7.15 us (12%)
  local copies, waits for them, and re-layouts  2.13 us (3%)
  other arithmetic  0.65 us (1%)
    ppermute x15, starting transfers between devices, exchange(): arrived.append(lax.ppermute(tile, 'tm', route) if apart else tile)  25.7 us
    pallas_call x1, Pallas kernels, mixer(): pl.pallas_call(functools.partial(mixer_kernel, state is not None), grid=(...  10.4 us
    pallas_call x1, Pallas kernels, earlier_frame(): pl.pallas_call(earlier_kernel, grid=(KVH,), in_specs=[pl.BlockSpec(memory...  7.72 us
    ppermute x15, waiting for transfers between devices, exchange(): arrived.append(lax.ppermute(tile, 'tm', route) if apart else tile)  5.85 us
    pallas_call x1, Pallas kernels, own_frame(): pl.pallas_call(own_kernel, grid=(KVH,), in_specs=[pl.BlockSpec((rows, wid...  4.77 us
    ppermute x1, starting transfers between devices, shifted(): return lax.ppermute(block, axis, route)  1.93 us
    ppermute x1, waiting for transfers between devices, shifted(): return lax.ppermute(block, axis, route)  1.3 us
    reshape x1, local copies, waits for them, and re-layouts, mixer(): gain_lin.reshape(1, width)  1.27 us
  transfers between devices with their start and end apart: 16, of which 7 were waited for; matrix products, arithmetic and copies ran while one was open for 0% of the time, Pallas kernels for 8%

profile of v2, /device:TPU:1, one launch (start us, length us, event | category | flops | bytes accessed | tf_op | source)
XLA Modules:
  0.0 61.4 jit_solution(4315310855831540015)
XLA Ops:
  0.0 1.3 %reshape.7.refs_5_ = bf16[1,1024]{1,0:T(2,128)(2,1)} reshape(bf16[1024]{0:T(1024)(128)(2,1)} %param.8) | data formatting | bytes 4096 | tf_op jit(solution)/shard_map/reshape | solution.py:114
  1.3 0.7 %pad_add_fusion.place_ref = s32[2]{0:T(128)} fusion(s32[1]{0:T(128)} %bitcast.1, s32[1]{0:T(128)} %bitcast), kind=kLoop, calls=%fused_computation | loop fusion | flops 2 | bytes 16 | tf_op jit(solution)/shard_map/stack | solution.py:306
  1.9 10.4 %mixer.1 = (bf16[32,1024]{1,0:T(8,128)(2,1)}, bf16[32,1024]{1,0:T(8,128)(2,1)}, bf16[32,1024]{1,0:T(8,128)(2,1)}, bf16[32,1024]{1,0:T(8,128)(2,1)}, bf16[32,1024...) custom-call(s32[2]{0:T(128)} %pad_add_fusion.place_ref, ...), custom_call_target="tpu_custom_call" | custom-call | flops 3758096384 | bytes 8388608 | tf_op jit(solution)/shard_map/mixer/pallas_call | solution.py:115
  12.3 5.7 %collective-permute-start = (bf16[32,1024]{1,0:T(8,128)(2,1)}, bf16[32,1024]{1,0:T(8,128)(2,1)S(1)}, u32[]{:S(2)}, u32[]{:S(2)}) collective-permute-start(bf16[32,1024]{1,0:T(8,128)(2,1)} %get-tuple-element.27), channel_id=1, source_target_pairs={{0,15},{1,14},{2,13},{3,12},{4,11},{5,10},{6,9},{7,8},{8,7},{9,6},... | collective-permute-start | bytes 196616 | tf_op jit(solution)/shard_map/ppermute | solution.py:298
  18.0 0.0 collective-permute-start.1
  18.1 3.2 %collective-permute-start.10 = (bf16[32,1024]{1,0:T(8,128)(2,1)}, bf16[32,1024]{1,0:T(8,128)(2,1)S(1)}, u32[]{:S(2)}, u32[]{:S(2)}) collective-permute-start(bf16[32,1024]{1,0:T(8,128)(2,1)} %get-tuple-element.37), channel_id=1, source_target_pairs={{0,13},{1,12},{2,15},{3,14},{4,9},{5,8},{6,11},{7,10},{8,5},{9,4},... | collective-permute-start | bytes 196616 | tf_op jit(solution)/shard_map/ppermute | solution.py:298
  21.3 0.0 collective-permute-start.11
  21.3 0.4 collective-permute-start.12
  21.7 0.0 collective-permute-done.refs_1_
  21.7 2.6 %collective-permute-start.13 = (bf16[32,1024]{1,0:T(8,128)(2,1)}, bf16[32,1024]{1,0:T(8,128)(2,1)S(1)}, u32[]{:S(2)}, u32[]{:S(2)}) collective-permute-start(bf16[32,1024]{1,0:T(8,128)(2,1)} %get-tuple-element.40), channel_id=1, source_target_pairs={{0,5},{1,4},{2,7},{3,6},{4,1},{5,0},{6,3},{7,2},{8,13},{9,12},{10,... | collective-permute-start | bytes 196616 | tf_op jit(solution)/shard_map/ppermute | solution.py:298
  24.3 0.5 collective-permute-done.1.refs_2_
  24.8 3.7 %collective-permute-start.14 = (bf16[32,1024]{1,0:T(8,128)(2,1)}, bf16[32,1024]{1,0:T(8,128)(2,1)S(1)}, u32[]{:S(2)}, u32[]{:S(2)}) collective-permute-start(bf16[32,1024]{1,0:T(8,128)(2,1)} %get-tuple-element.41), channel_id=1, source_target_pairs={{0,11},{1,10},{2,9},{3,8},{4,15},{5,14},{6,13},{7,12},{8,3},{9,2},... | collective-permute-start | bytes 196616 | tf_op jit(solution)/shard_map/ppermute | solution.py:298
  28.6 0.2 collective-permute-start.2
  28.8 0.0 collective-permute-done.11.refs_12_
  28.8 0.3 collective-permute-start.3
  29.1 2.3 %collective-permute-start.4 = (bf16[32,1024]{1,0:T(8,128)(2,1)}, bf16[32,1024]{1,0:T(8,128)(2,1)S(1)}, u32[]{:S(2)}, u32[]{:S(2)}) collective-permute-start(bf16[32,1024]{1,0:T(8,128)(2,1)} %get-tuple-element.31), channel_id=1, source_target_pairs={{0,3},{1,2},{2,1},{3,0},{4,7},{5,6},{6,5},{7,4},{8,11},{9,10},{10,... | collective-permute-start | bytes 196616 | tf_op jit(solution)/shard_map/ppermute | solution.py:298
  31.5 1.2 %collective-permute-start.5 = (bf16[32,1024]{1,0:T(8,128)(2,1)}, bf16[32,1024]{1,0:T(8,128)(2,1)S(1)}, u32[]{:S(2)}, u32[]{:S(2)}) collective-permute-start(bf16[32,1024]{1,0:T(8,128)(2,1)} %get-tuple-element.32), channel_id=1, source_target_pairs={{0,9},{1,8},{2,11},{3,10},{4,13},{5,12},{6,15},{7,14},{8,1},{9,0},... | collective-permute-start | bytes 196616 | tf_op jit(solution)/shard_map/ppermute | solution.py:298
  32.7 0.3 collective-permute-done.14.refs_15_
  33.0 0.9 %collective-permute-start.6 = (bf16[32,1024]{1,0:T(8,128)(2,1)}, bf16[32,1024]{1,0:T(8,128)(2,1)S(1)}, u32[]{:S(2)}, u32[]{:S(2)}) collective-permute-start(bf16[32,1024]{1,0:T(8,128)(2,1)} %get-tuple-element.33), channel_id=1, source_target_pairs={{0,2},{1,3},{2,0},{3,1},{4,6},{5,7},{6,4},{7,5},{8,10},{9,11},{10,... | collective-permute-start | bytes 196616 | tf_op jit(solution)/shard_map/ppermute | solution.py:298
  33.9 0.2 collective-permute-done.2.refs_3_
  34.1 0.7 %collective-permute-start.7 = (bf16[32,1024]{1,0:T(8,128)(2,1)}, bf16[32,1024]{1,0:T(8,128)(2,1)S(1)}, u32[]{:S(2)}, u32[]{:S(2)}) collective-permute-start(bf16[32,1024]{1,0:T(8,128)(2,1)} %get-tuple-element.34), channel_id=1, source_target_pairs={{0,8},{1,9},{2,10},{3,11},{4,12},{5,13},{6,14},{7,15},{8,0},{9,1},... | collective-permute-start | bytes 196616 | tf_op jit(solution)/shard_map/ppermute | solution.py:298
  34.8 4.2 %collective-permute-start.8 = (bf16[32,1024]{1,0:T(8,128)(2,1)}, bf16[32,1024]{1,0:T(8,128)(2,1)S(1)}, u32[]{:S(2)}, u32[]{:S(2)}) collective-permute-start(bf16[32,1024]{1,0:T(8,128)(2,1)} %get-tuple-element.35), channel_id=1, source_target_pairs={{0,1},{1,0},{2,3},{3,2},{4,5},{5,4},{6,7},{7,6},{8,9},{9,8},{10,11... | collective-permute-start | bytes 196616 | tf_op jit(solution)/shard_map/ppermute | solution.py:298
  39.1 1.3 %collective-permute-done.5.refs_6_ = bf16[32,1024]{1,0:T(8,128)(2,1)S(1)} collective-permute-done((bf16[32,1024]{1,0:T(8,128)(2,1)}, bf16[32,1024]{1,0:T(8,128)(2,1)S(1)}, u32[]{:S(2)}, u32[]{:S(2)}) %collective-permute-start.5) | collective-permute-done | bytes 65568 | tf_op jit(solution)/shard_map/ppermute | solution.py:298
  40.4 0.0 collective-permute-done.6.refs_7_
  40.4 0.5 collective-permute-done.7.refs_8_
  40.9 3.0 %collective-permute-done.9.refs_10_ = bf16[32,1024]{1,0:T(8,128)(2,1)S(1)} collective-permute-done((bf16[32,1024]{1,0:T(8,128)(2,1)}, bf16[32,1024]{1,0:T(8,128)(2,1)S(1)}, u32[]{:S(2)}, u32[]{:S(2)}) %collective-permute-start.9) | collective-permute-done | bytes 65568 | tf_op jit(solution)/shard_map/ppermute | solution.py:298
  43.9 0.8 %copy-done.1 = bf16[32,1024]{1,0:T(8,128)(2,1)S(1)} copy-done((bf16[32,1024]{1,0:T(8,128)(2,1)S(1)}, bf16[32,1024]{1,0:T(8,128)(2,1)}, u32[]{:S(2)}) %copy-start.1) | copy-done | bytes 65560
  44.7 0.9 %pairs.1 = (bf16[512,1024]{1,0:T(8,128)(2,1)S(1)}, bf16[512,512]{1,0:T(8,128)(2,1)S(1)}) custom-call(bf16[1,1024]{1,0:T(2,128)(2,1)S(1)} %reshape.6.gain_ref, bf16[1024,512]{1,0:T(8,128)(2,1)S(1)} %copy-done, bf16[32,1024]{1,0:T(8,128)(2,1)S(1)} %copy-done.1, bf16[32,1024]{1,0:T(8,128)(2,1)S(1)} %collective-permute-done.refs_1_, ...), custom_call_target="tpu_custom_call" | custom-call | flops 536870912 | bytes 3670016 | tf_op jit(solution)/shard_map/pairs/pallas_call | solution.py:162
  45.7 1.9 %collective-permute-start.15 = (bf16[512,512]{1,0:T(8,128)(2,1)S(1)}, bf16[512,512]{1,0:T(8,128)(2,1)S(1)}, u32[]{:S(2)}, u32[]{:S(2)}) collective-permute-start(bf16[512,512]{1,0:T(8,128)(2,1)S(1)} %get-tuple-element.43.key_ref.value_ref), channel_id=1, source_target_pairs={{0,1},{1,2},{2,3},{3,4},{4,5},{5,6},{6,7},{7,8},{8,9},{9,10},{10,1... | collective-permute-start | bytes 1572872 | tf_op jit(solution)/shard_map/ppermute | solution.py:27
  47.6 4.8 %own_frame.1 = (bf16[512,1024]{1,0:T(8,128)(2,1)S(1)}, f32[512,1024]{1,0:T(8,128)S(1)}, f32[2,512,4]{2,1,0:T(8,128)S(1)}) custom-call(bf16[512,1024]{1,0:T(8,128)(2,1)S(1)} %get-tuple-element.42.normed_ref, bf16[1024,1024]{1,0:T(8,128)(2,1)S(1)} %copy-done.3, bf16[512,512]{1,0:T(8,128)(2,1)S(1)} %get-tuple-element.43.key_ref.value_ref, ...), custom_call_target="tpu_custom_call" | custom-call | flops 2147483648 | bytes 6291456 | tf_op jit(solution)/shard_map/own_frame/pallas_call | solution.py:211
  52.4 1.3 %collective-permute-done.15.key_ref.value_ref = bf16[512,512]{1,0:T(8,128)(2,1)S(1)} collective-permute-done((bf16[512,512]{1,0:T(8,128)(2,1)S(1)}, bf16[512,512]{1,0:T(8,128)(2,1)S(1)}, u32[]{:S(2)}, u32[]{:S(2)}) %collective-permute-start.15) | collective-permute-done | bytes 524320 | tf_op jit(solution)/shard_map/ppermute | solution.py:27
  53.7 7.7 %earlier_frame.1 = bf16[512,1024]{1,0:T(8,128)(2,1)} custom-call(s32[2]{0:T(128)S(1)} %copy-done.2, bf16[512,1024]{1,0:T(8,128)(2,1)S(1)} %get-tuple-element.44.query_ref, bf16[512,512]{1,0:T(8,128)(2,1)S(1)} %collective-permute-done.15.key_ref.value_ref, bf16[512,512]{1,0:T(8,128)(2,1)S(1)} %collective-permute-done.15.key_ref.value_ref, ...), custom_call_target="tpu_custom_call" | custom-call | flops 1073741824 | bytes 5242880 | tf_op jit(solution)/shard_map/earlier_frame/pallas_call | solution.py:270
  (17 shorter events, 0.0 us)
Async XLA Ops:
  1.9 37.1 %copy-start.4 = (bf16[1024]{0:T(1024)(128)(2,1)S(1)}, bf16[1024]{0:T(1024)(128)(2,1)}, u32[]{:S(2)}) copy-start(bf16[1024]{0:T(1024)(128)(2,1)} %param.11) | copy-start | bytes 6148
  1.9 42.0 %copy-start = (bf16[1024,512]{1,0:T(8,128)(2,1)S(1)}, bf16[1024,512]{1,0:T(8,128)(2,1)}, u32[]{:S(2)}) copy-start(bf16[1024,512]{1,0:T(8,128)(2,1)} %w_ref.2) | copy-start | bytes 3145732
  1.9 45.7 %copy-start.3 = (bf16[1024,1024]{1,0:T(8,128)(2,1)S(1)}, bf16[1024,1024]{1,0:T(8,128)(2,1)}, u32[]{:S(2)}) copy-start(bf16[1024,1024]{1,0:T(8,128)(2,1)} %w_ref.3) | copy-start | bytes 6291460
  12.3 9.4 %collective-permute-start = (bf16[32,1024]{1,0:T(8,128)(2,1)}, bf16[32,1024]{1,0:T(8,128)(2,1)S(1)}, u32[]{:S(2)}, u32[]{:S(2)}) collective-permute-start(bf16[32,1024]{1,0:T(8,128)(2,1)} %get-tuple-element.27), channel_id=1, source_target_pairs={{0,15},{1,14},{2,13},{3,12},{4,11},{5,10},{6,9},{7,8},{8,7},{9,6},... | collective-permute-start | bytes 196616 | tf_op jit(solution)/shard_map/ppermute | solution.py:298
  18.0 6.8 %collective-permute-start.1 = (bf16[32,1024]{1,0:T(8,128)(2,1)}, bf16[32,1024]{1,0:T(8,128)(2,1)S(1)}, u32[]{:S(2)}, u32[]{:S(2)}) collective-permute-start(bf16[32,1024]{1,0:T(8,128)(2,1)} %get-tuple-element.28), channel_id=1, source_target_pairs={{0,14},{1,15},{2,12},{3,13},{4,10},{5,11},{6,8},{7,9},{8,6},{9,7},... | collective-permute-start | bytes 196616 | tf_op jit(solution)/shard_map/ppermute | solution.py:298
  18.1 10.5 %collective-permute-start.10 = (bf16[32,1024]{1,0:T(8,128)(2,1)}, bf16[32,1024]{1,0:T(8,128)(2,1)S(1)}, u32[]{:S(2)}, u32[]{:S(2)}) collective-permute-start(bf16[32,1024]{1,0:T(8,128)(2,1)} %get-tuple-element.37), channel_id=1, source_target_pairs={{0,13},{1,12},{2,15},{3,14},{4,9},{5,8},{6,11},{7,10},{8,5},{9,4},... | collective-permute-start | bytes 196616 | tf_op jit(solution)/shard_map/ppermute | solution.py:298
  21.3 7.5 %collective-permute-start.11 = (bf16[32,1024]{1,0:T(8,128)(2,1)}, bf16[32,1024]{1,0:T(8,128)(2,1)S(1)}, u32[]{:S(2)}, u32[]{:S(2)}) collective-permute-start(bf16[32,1024]{1,0:T(8,128)(2,1)} %get-tuple-element.38), channel_id=1, source_target_pairs={{0,6},{1,7},{2,4},{3,5},{4,2},{5,3},{6,0},{7,1},{8,14},{9,15},{10,... | collective-permute-start | bytes 196616 | tf_op jit(solution)/shard_map/ppermute | solution.py:298
  21.3 7.8 %collective-permute-start.12 = (bf16[32,1024]{1,0:T(8,128)(2,1)}, bf16[32,1024]{1,0:T(8,128)(2,1)S(1)}, u32[]{:S(2)}, u32[]{:S(2)}) collective-permute-start(bf16[32,1024]{1,0:T(8,128)(2,1)} %get-tuple-element.39), channel_id=1, source_target_pairs={{0,12},{1,13},{2,14},{3,15},{4,8},{5,9},{6,10},{7,11},{8,4},{9,5},... | collective-permute-start | bytes 196616 | tf_op jit(solution)/shard_map/ppermute | solution.py:298
  21.7 9.8 %collective-permute-start.13 = (bf16[32,1024]{1,0:T(8,128)(2,1)}, bf16[32,1024]{1,0:T(8,128)(2,1)S(1)}, u32[]{:S(2)}, u32[]{:S(2)}) collective-permute-start(bf16[32,1024]{1,0:T(8,128)(2,1)} %get-tuple-element.40), channel_id=1, source_target_pairs={{0,5},{1,4},{2,7},{3,6},{4,1},{5,0},{6,3},{7,2},{8,13},{9,12},{10,... | collective-permute-start | bytes 196616 | tf_op jit(solution)/shard_map/ppermute | solution.py:298
  24.8 8.2 %collective-permute-start.14 = (bf16[32,1024]{1,0:T(8,128)(2,1)}, bf16[32,1024]{1,0:T(8,128)(2,1)S(1)}, u32[]{:S(2)}, u32[]{:S(2)}) collective-permute-start(bf16[32,1024]{1,0:T(8,128)(2,1)} %get-tuple-element.41), channel_id=1, source_target_pairs={{0,11},{1,10},{2,9},{3,8},{4,15},{5,14},{6,13},{7,12},{8,3},{9,2},... | collective-permute-start | bytes 196616 | tf_op jit(solution)/shard_map/ppermute | solution.py:298
  28.6 5.5 %collective-permute-start.2 = (bf16[32,1024]{1,0:T(8,128)(2,1)}, bf16[32,1024]{1,0:T(8,128)(2,1)S(1)}, u32[]{:S(2)}, u32[]{:S(2)}) collective-permute-start(bf16[32,1024]{1,0:T(8,128)(2,1)} %get-tuple-element.29), channel_id=1, source_target_pairs={{0,4},{1,5},{2,6},{3,7},{4,0},{5,1},{6,2},{7,3},{8,12},{9,13},{10,... | collective-permute-start | bytes 196616 | tf_op jit(solution)/shard_map/ppermute | solution.py:298
  28.8 6.0 %collective-permute-start.3 = (bf16[32,1024]{1,0:T(8,128)(2,1)}, bf16[32,1024]{1,0:T(8,128)(2,1)S(1)}, u32[]{:S(2)}, u32[]{:S(2)}) collective-permute-start(bf16[32,1024]{1,0:T(8,128)(2,1)} %get-tuple-element.30), channel_id=1, source_target_pairs={{0,10},{1,11},{2,8},{3,9},{4,14},{5,15},{6,12},{7,13},{8,2},{9,3},... | collective-permute-start | bytes 196616 | tf_op jit(solution)/shard_map/ppermute | solution.py:298
  29.1 9.9 %collective-permute-start.4 = (bf16[32,1024]{1,0:T(8,128)(2,1)}, bf16[32,1024]{1,0:T(8,128)(2,1)S(1)}, u32[]{:S(2)}, u32[]{:S(2)}) collective-permute-start(bf16[32,1024]{1,0:T(8,128)(2,1)} %get-tuple-element.31), channel_id=1, source_target_pairs={{0,3},{1,2},{2,1},{3,0},{4,7},{5,6},{6,5},{7,4},{8,11},{9,10},{10,... | collective-permute-start | bytes 196616 | tf_op jit(solution)/shard_map/ppermute | solution.py:298
  31.5 8.9 %collective-permute-start.5 = (bf16[32,1024]{1,0:T(8,128)(2,1)}, bf16[32,1024]{1,0:T(8,128)(2,1)S(1)}, u32[]{:S(2)}, u32[]{:S(2)}) collective-permute-start(bf16[32,1024]{1,0:T(8,128)(2,1)} %get-tuple-element.32), channel_id=1, source_target_pairs={{0,9},{1,8},{2,11},{3,10},{4,13},{5,12},{6,15},{7,14},{8,1},{9,0},... | collective-permute-start | bytes 196616 | tf_op jit(solution)/shard_map/ppermute | solution.py:298
  33.0 7.4 %collective-permute-start.6 = (bf16[32,1024]{1,0:T(8,128)(2,1)}, bf16[32,1024]{1,0:T(8,128)(2,1)S(1)}, u32[]{:S(2)}, u32[]{:S(2)}) collective-permute-start(bf16[32,1024]{1,0:T(8,128)(2,1)} %get-tuple-element.33), channel_id=1, source_target_pairs={{0,2},{1,3},{2,0},{3,1},{4,6},{5,7},{6,4},{7,5},{8,10},{9,11},{10,... | collective-permute-start | bytes 196616 | tf_op jit(solution)/shard_map/ppermute | solution.py:298
  34.1 6.8 %collective-permute-start.7 = (bf16[32,1024]{1,0:T(8,128)(2,1)}, bf16[32,1024]{1,0:T(8,128)(2,1)S(1)}, u32[]{:S(2)}, u32[]{:S(2)}) collective-permute-start(bf16[32,1024]{1,0:T(8,128)(2,1)} %get-tuple-element.34), channel_id=1, source_target_pairs={{0,8},{1,9},{2,10},{3,11},{4,12},{5,13},{6,14},{7,15},{8,0},{9,1},... | collective-permute-start | bytes 196616 | tf_op jit(solution)/shard_map/ppermute | solution.py:298
  34.8 6.0 %collective-permute-start.8 = (bf16[32,1024]{1,0:T(8,128)(2,1)}, bf16[32,1024]{1,0:T(8,128)(2,1)S(1)}, u32[]{:S(2)}, u32[]{:S(2)}) collective-permute-start(bf16[32,1024]{1,0:T(8,128)(2,1)} %get-tuple-element.35), channel_id=1, source_target_pairs={{0,1},{1,0},{2,3},{3,2},{4,5},{5,4},{6,7},{7,6},{8,9},{9,8},{10,11... | collective-permute-start | bytes 196616 | tf_op jit(solution)/shard_map/ppermute | solution.py:298
  39.1 4.8 %collective-permute-start.9 = (bf16[32,1024]{1,0:T(8,128)(2,1)}, bf16[32,1024]{1,0:T(8,128)(2,1)S(1)}, u32[]{:S(2)}, u32[]{:S(2)}) collective-permute-start(bf16[32,1024]{1,0:T(8,128)(2,1)} %get-tuple-element.36), channel_id=1, source_target_pairs={{0,7},{1,6},{2,5},{3,4},{4,3},{5,2},{6,1},{7,0},{8,15},{9,14},{10,... | collective-permute-start | bytes 196616 | tf_op jit(solution)/shard_map/ppermute | solution.py:298
  43.9 0.8 %copy-start.1 = (bf16[32,1024]{1,0:T(8,128)(2,1)S(1)}, bf16[32,1024]{1,0:T(8,128)(2,1)}, u32[]{:S(2)}) copy-start(bf16[32,1024]{1,0:T(8,128)(2,1)} %get-tuple-element.26.refs_0_) | copy-start | bytes 196612
  45.7 8.0 %collective-permute-start.15 = (bf16[512,512]{1,0:T(8,128)(2,1)S(1)}, bf16[512,512]{1,0:T(8,128)(2,1)S(1)}, u32[]{:S(2)}, u32[]{:S(2)}) collective-permute-start(bf16[512,512]{1,0:T(8,128)(2,1)S(1)} %get-tuple-element.43.key_ref.value_ref), channel_id=1, source_target_pairs={{0,1},{1,2},{2,3},{3,4},{4,5},{5,6},{6,7},{7,8},{8,9},{9,10},{10,1... | collective-permute-start | bytes 1572872 | tf_op jit(solution)/shard_map/ppermute | solution.py:27
  47.6 6.1 %copy-start.2 = (s32[2]{0:T(128)S(1)}, s32[2]{0:T(128)}, u32[]{:S(2)}) copy-start(s32[2]{0:T(128)} %pad_add_fusion.place_ref) | copy-start | bytes 28

commit v3 on v2

v3 whole, which is shorter than its diff:
```python
import functools
import math

import jax
import jax.numpy as jnp
from jax import lax
from jax.experimental import pallas as pl
from jax.experimental.pallas import tpu as pltpu
from jax.sharding import PartitionSpec as P

HEADS = 8
HD = 128
KVH = 2
SB = 16
SPAN = 128
PAIR = 2

epsilon = 1e-06
MIB = 1 << 20


def shifted(block, axis, distance):
    devices = range(lax.axis_size(axis))
    route = [(i - distance, i) for i in devices if i - distance in devices]
    return lax.ppermute(block, axis, route)


def dot(a, b):
    return jnp.dot(a, b, preferred_element_type=jnp.float32)


def dot_nt(a, b):
    return lax.dot_general(a, b, (((1,), (1,)), ((), ())), preferred_element_type=jnp.float32)


def dot_tn(a, b):
    return lax.dot_general(a, b, (((0,), (0,)), ((), ())), preferred_element_type=jnp.float32)


def head_lanes(head):
    return slice(head * HD, (head + 1) * HD)


def mixer_kernel(first, heads, has_state, *refs):
    if has_state:
        state_ref, *refs = refs
    tokens_ref, w_ref, gain_ref, out_ref, weights, arrived = refs
    rows, width = tokens_ref.shape
    spans = rows // SPAN
    columns = PAIR * HD
    pairs = heads // PAIR
    copies = []
    for pair in range(pairs):
        for part in range(3):
            start = part * width + first * HD + pair * columns
            copies.append(
                pltpu.make_async_copy(
                    w_ref.at[:, start : start + columns],
                    weights.at[pair, part],
                    arrived.at[pair, part],
                )
            )
    for copy in copies:
        copy.start()
    tokens = tokens_ref[...]
    gains = gain_ref[...].astype(jnp.float32).reshape(1, width)
    causal = lax.broadcasted_iota(jnp.int32, (SPAN, SPAN), 0) >= lax.broadcasted_iota(
        jnp.int32, (SPAN, SPAN), 1
    )

    def project(pair):
        packed = []
        for part in range(3):
            copies[3 * pair + part].wait()
            packed.append(dot(tokens, weights[pair, part]).astype(jnp.bfloat16))
        return packed

    def attend(pair, query, key, value):
        units = []
        for head in range(PAIR):
            for span in range(spans):
                here = slice(span * SPAN, (span + 1) * SPAN)
                units.append((head, span, here, head_lanes(head)))
        local, before, mixed = {}, {}, {}
        for head, span, here, lanes in units:
            scores = dot_nt(query[here, lanes], key[here, lanes])
            local[head, span] = jnp.where(causal, scores, 0.0).astype(jnp.bfloat16)
        for head, span, here, lanes in units:
            if span == 0:
                state = state_ref[pair * PAIR + head] if has_state else None
            before[head, span] = state
            if span + 1 < spans:
                update = dot_tn(key[here, lanes], value[here, lanes])
                state = update if state is None else state + update
        for head, span, here, lanes in units:
            if before[head, span] is None:
                mixed[head, span] = dot(local[head, span], value[here, lanes])
            else:
                mixed[head, span] = dot(
                    jnp.concatenate([query[here, lanes], local[head, span]], axis=1),
                    jnp.concatenate(
                        [before[head, span].astype(jnp.bfloat16), value[here, lanes]], axis=0
                    ),
                )
        for head, span, here, lanes in units:
            out = mixed[head, span]
            own = pair * PAIR + head
            mean_square = jnp.mean(out * out, axis=-1, keepdims=True)
            gain = gains[:, head_lanes(first + own)]
            normed = out * lax.rsqrt(mean_square + epsilon) * gain
            residual = tokens_ref[here, head_lanes(first + own)].astype(jnp.float32)
            out_ref[here, head_lanes(own)] = (residual + normed).astype(jnp.bfloat16)

    packed = project(0)
    for pair in range(pairs):
        upcoming = project(pair + 1) if pair + 1 < pairs else None
        attend(pair, *packed)
        packed = upcoming


def mixer(first, heads, tokens, w_lin, gain_lin, state):
    rows, width = tokens.shape
    columns = heads * HD
    operands = [tokens, w_lin, gain_lin]
    in_specs = [
        pl.BlockSpec(memory_space=pltpu.VMEM),
        pl.BlockSpec(memory_space=pl.ANY),
        pl.BlockSpec(memory_space=pltpu.VMEM),
    ]
    if state is not None:
        operands.insert(0, state[first : first + heads])
        in_specs.insert(0, pl.BlockSpec(memory_space=pltpu.VMEM))
    return pl.pallas_call(
        functools.partial(mixer_kernel, first, heads, state is not None),
        in_specs=in_specs,
        out_shape=jax.ShapeDtypeStruct((rows, columns), jnp.bfloat16),
        scratch_shapes=[
            pltpu.VMEM((heads // PAIR, 3, width, PAIR * HD), jnp.bfloat16),
            pltpu.SemaphoreType.DMA((heads // PAIR, 3)),
        ],
        compiler_params=pltpu.CompilerParams(vmem_limit_bytes=56 * MIB),
        cost_estimate=pl.CostEstimate(
            flops=2 * rows * width * 3 * columns + 8 * rows * SPAN * columns,
            bytes_accessed=2 * (3 * width * columns + rows * width + rows * columns),
            transcendentals=rows * heads,
        ),
        name="mixer",
    )(*operands)


def incoming_state(tokens, w_lin, time_ranges):
    rows, width = tokens.shape
    packed = dot(tokens, w_lin[:, width:]).astype(jnp.bfloat16).reshape(rows, 2, HEADS, HD)
    block_total = jnp.einsum(
        "nhd,nhe->hde", packed[:, 0], packed[:, 1], preferred_element_type=jnp.float32
    )
    within = lax.axis_index("tm") // SB

    def advance_hop(turn_index, running_total):
        moved = shifted(running_total + block_total, "tm", SB)
        return jnp.where(within > 0, moved, 0.0)

    return lax.fori_loop(0, time_ranges - 1, advance_hop, jnp.zeros_like(block_total))


def pairs_kernel(left_ref, right_ref, gain_ref, w_ref, normed_ref, pairs_ref):
    widened = jnp.concatenate([left_ref[...], right_ref[...]], axis=1).astype(jnp.float32)
    mean_square = jnp.mean(widened * widened, axis=-1, keepdims=True)
    normed = (
        widened * lax.rsqrt(mean_square + epsilon) * gain_ref[...].astype(jnp.float32).reshape(1, -1)
    ).astype(jnp.bfloat16)
    normed_ref[...] = normed
    pairs_ref[...] = dot(normed, w_ref[...]).astype(jnp.bfloat16)


def make_pairs(left, right, gain, w_kv):
    rows = left.shape[0]
    width, wide = w_kv.shape
    return pl.pallas_call(
        pairs_kernel,
        out_shape=[
            jax.ShapeDtypeStruct((rows, width), jnp.bfloat16),
            jax.ShapeDtypeStruct((rows, wide), jnp.bfloat16),
        ],
        compiler_params=pltpu.CompilerParams(vmem_limit_bytes=16 * MIB),
        cost_estimate=pl.CostEstimate(
            flops=2 * rows * width * wide,
            bytes_accessed=2 * (2 * rows * width + width * wide + rows * wide),
            transcendentals=rows,
        ),
        name="pairs",
    )(left, right, gain, w_kv)


SCORE_SCALE = math.log2(math.e) / math.sqrt(HD)


def with_ones(value):
    return jnp.concatenate([value, jnp.ones_like(value)], axis=1)


def own_kernel(normed_ref, w_ref, key_ref, value_ref, query_ref, partial_ref, log_ref):
    query = dot(normed_ref[...], w_ref[...]).astype(jnp.bfloat16)
    query_ref[...] = query
    key = key_ref[...]
    value = with_ones(value_ref[...])
    heads = query.shape[1] // HD
    scores = dot_nt(query[:, head_lanes(0)], key)
    for head in range(heads):
        upcoming = dot_nt(query[:, head_lanes(head + 1)], key) if head + 1 < heads else None
        largest = jnp.max(scores, axis=-1, keepdims=True)
        raised = jnp.exp2((scores - largest) * SCORE_SCALE).astype(jnp.bfloat16)
        summed = dot(raised, value)
        total = summed[:, HD:]
        partial_ref[:, head_lanes(head)] = summed[:, :HD] / total
        log_ref[:, head_lanes(head)] = largest * SCORE_SCALE + jnp.log2(total)
        scores = upcoming


def own_frame(normed, w_query, pairs):
    rows, width = normed.shape
    group = HEADS // KVH
    columns = group * HD
    return pl.pallas_call(
        own_kernel,
        grid=(KVH,),
        in_specs=[
            pl.BlockSpec((rows, width), lambda c: (0, 0)),
            pl.BlockSpec((width, columns), lambda c: (0, c)),
            pl.BlockSpec((rows, HD), lambda c: (0, c)),
            pl.BlockSpec((rows, HD), lambda c: (0, KVH + c)),
        ],
        out_specs=[
            pl.BlockSpec((rows, columns), lambda c: (0, c)),
            pl.BlockSpec((rows, columns), lambda c: (0, c)),
            pl.BlockSpec((rows, columns), lambda c: (0, c)),
        ],
        out_shape=[
            jax.ShapeDtypeStruct((rows, width), jnp.bfloat16),
            jax.ShapeDtypeStruct((rows, width), jnp.float32),
            jax.ShapeDtypeStruct((rows, width), jnp.float32),
        ],
        compiler_params=pltpu.CompilerParams(vmem_limit_bytes=32 * MIB),
        cost_estimate=pl.CostEstimate(
            flops=2 * rows * width * width + 4 * rows * rows * width,
            bytes_accessed=2 * width * width + 8 * rows * width,
            transcendentals=rows * rows * HEADS,
        ),
        name="own_frame",
    )(normed, w_query, pairs, pairs)


def earlier_kernel(query_ref, key_ref, value_ref, partial_ref, log_ref, out_ref):
    rows = query_ref.shape[0]
    heads = query_ref.shape[1] // HD
    key = key_ref[...]
    value = with_ones(value_ref[...])
    barred = jnp.where(lax.axis_index("tm") > 0, 0.0, -jnp.inf)
    scores = dot_nt(query_ref[:, head_lanes(0)], key)
    for head in range(heads):
        lanes = head_lanes(head)
        upcoming = dot_nt(query_ref[:, head_lanes(head + 1)], key) if head + 1 < heads else None
        own = log_ref[:, lanes]
        here = jnp.max(scores, axis=-1, keepdims=True) * SCORE_SCALE + barred
        largest = jnp.maximum(jnp.broadcast_to(here, own.shape), own)
        below = jnp.concatenate([largest - barred] * (rows // HD), axis=1)
        raised = jnp.exp2(scores * SCORE_SCALE - below).astype(jnp.bfloat16)
        summed = dot(raised, value)
        share = jnp.exp2(own - largest)
        out_ref[:, lanes] = (
            (partial_ref[:, lanes] * share + summed[:, :HD]) / (share + summed[:, HD:])
        ).astype(jnp.bfloat16)
        scores = upcoming


def earlier_frame(query, earlier_pairs, partial, log_total):
    rows, width = query.shape
    group = HEADS // KVH
    columns = group * HD
    return pl.pallas_call(
        earlier_kernel,
        grid=(KVH,),
        in_specs=[
            pl.BlockSpec((rows, columns), lambda c: (0, c)),
            pl.BlockSpec((rows, HD), lambda c: (0, c)),
            pl.BlockSpec((rows, HD), lambda c: (0, KVH + c)),
            pl.BlockSpec((rows, columns), lambda c: (0, c)),
            pl.BlockSpec((rows, columns), lambda c: (0, c)),
        ],
        out_specs=pl.BlockSpec((rows, columns), lambda c: (0, c)),
        out_shape=jax.ShapeDtypeStruct((rows, width), jnp.bfloat16),
        compiler_params=pltpu.CompilerParams(vmem_limit_bytes=32 * MIB),
        cost_estimate=pl.CostEstimate(
            flops=4 * rows * rows * width,
            bytes_accessed=10 * rows * width,
            transcendentals=rows * rows * HEADS,
        ),
        name="earlier_frame",
    )(query, earlier_pairs, earlier_pairs, partial, log_total)


def to_frames(part):
    rows, columns = part.shape
    teams = [[t * SB + s for s in range(SB)] for t in range(lax.axis_size("tm") // SB)]
    moved = lax.all_to_all(
        part.reshape(SB, rows // SB, columns), "tm", 0, 0, axis_index_groups=teams, tiled=True
    )
    return moved.reshape(rows, columns)


def body(space_time, w_lin, gain_lin, w_query, w_kv, frame_attention_gain):
    tokens = space_time[0]
    time_ranges = lax.axis_size("tm") // SB
    state = incoming_state(tokens, w_lin, time_ranges) if time_ranges > 1 else None
    half = HEADS // 2
    left = to_frames(mixer(0, half, tokens, w_lin, gain_lin, state))
    right = to_frames(mixer(half, half, tokens, w_lin, gain_lin, state))
    normed, pairs = make_pairs(left, right, frame_attention_gain, w_kv)
    earlier_pairs = shifted(pairs, "tm", 1)
    query, partial, log_total = own_frame(normed, w_query, pairs)
    attended = earlier_frame(query, earlier_pairs, partial, log_total)
    return attended[None]


def solution(mesh):
    placed = (P(("groups", "tm"), None, None), P(), P(), P(), P(), P())
    return jax.shard_map(
        body, mesh=mesh, in_specs=placed, out_specs=P(("groups", "tm"), None, None), check_vma=False
    )
```

time: 61.9 us -> 64.3 us (1.039)
  the two profiles are of different devices: /device:TPU:1 before, /device:TPU:16 now
where the time goes in v3:
time: 64.3 us; the launch traced here: 63.9 us
  Pallas kernels  26.7 us (42%)
  blocking collectives  18.7 us (29%)
  waiting for transfers between devices  10.3 us (16%)
  starting transfers between devices  8.12 us (13%)
    all_to_all x1, blocking collectives, to_frames(): lax.all_to_all(part.reshape(SB, rows // SB, columns), 'tm', 0, 0, axis_in...  18.7 us
    pallas_call x2, Pallas kernels, mixer(): pl.pallas_call(functools.partial(mixer_kernel, first, heads, state is not...  16.5 us
    all_to_all x1, starting transfers between devices, to_frames(): lax.all_to_all(part.reshape(SB, rows // SB, columns), 'tm', 0, 0, axis_in...  6.2 us
    all_to_all x1, waiting for transfers between devices, to_frames(): lax.all_to_all(part.reshape(SB, rows // SB, columns), 'tm', 0, 0, axis_in...  5.6 us
    pallas_call x1, Pallas kernels, own_frame(): pl.pallas_call(own_kernel, grid=(KVH,), in_specs=[pl.BlockSpec((rows, wid...  4.77 us
    ppermute x1, waiting for transfers between devices, shifted(): return lax.ppermute(block, axis, route)  4.68 us
    pallas_call x1, Pallas kernels, earlier_frame(): pl.pallas_call(earlier_kernel, grid=(KVH,), in_specs=[pl.BlockSpec((rows,...  4.56 us
    ppermute x1, starting transfers between devices, shifted(): return lax.ppermute(block, axis, route)  1.92 us
  transfers between devices with their start and end apart: 2, of which 2 were waited for; matrix products, arithmetic and copies ran while one was open for 0% of the time, Pallas kernels for 20%

profile of v3, /device:TPU:16, one launch (start us, length us, event | category | flops | bytes accessed | tf_op | source)
XLA Modules:
  0.0 63.9 jit_solution(647651977859200425)
XLA Ops:
  0.0 8.2 %mixer.2 = bf16[512,512]{1,0:T(8,128)(2,1)} custom-call(bf16[512,1024]{1,0:T(8,128)(2,1)} %bitcast.8, bf16[1024,3072]{1,0:T(8,128)(2,1)} %refs_1_.3, bf16[1024]{0:T(1024)(128)(2,1)} %refs_2_.3), custom_call_target="tpu_custom_call" | custom-call | flops 1879048192 | bytes 4718592 | tf_op jit(solution)/shard_map/mixer/pallas_call | solution.py:133
  8.2 6.2 %all-to-all-start = ((bf16[16,32,512]{2,1,0:T(8,128)(2,1)}), bf16[16,32,512]{2,1,0:T(8,128)(2,1)S(1)}, u32[]{:S(2)}, u32[]{:S(2)}) async-start(bf16[16,32,512]{2,1,0:T(8,128)(2,1)} %bitcast.10), calls=%async_computation | async-start | bytes 1048576 | tf_op jit(solution)/shard_map/all_to_all | solution.py:305
  14.4 0.0 copy-start
  14.4 0.0 copy-start.1
  14.4 8.3 %mixer.3 = bf16[512,512]{1,0:T(8,128)(2,1)} custom-call(bf16[512,1024]{1,0:T(8,128)(2,1)} %bitcast.9, bf16[1024,3072]{1,0:T(8,128)(2,1)} %refs_1_.3, bf16[1024]{0:T(1024)(128)(2,1)} %refs_2_.3), custom_call_target="tpu_custom_call" | custom-call | flops 1879048192 | bytes 4718592 | tf_op jit(solution)/shard_map/mixer/pallas_call | solution.py:133
  22.7 5.6 %all-to-all-done = bf16[16,32,512]{2,1,0:T(8,128)(2,1)S(1)} async-done(((bf16[16,32,512]{2,1,0:T(8,128)(2,1)}), bf16[16,32,512]{2,1,0:T(8,128)(2,1)S(1)}, u32[]{:S(2)}, u32[]{:S(2)}) %all-to-all-start) | async-done | bytes 524320 | tf_op jit(solution)/shard_map/all_to_all | solution.py:305
  28.3 0.0 copy-start.2
  28.3 18.7 %all_to_all.10 = bf16[16,32,512]{2,1,0:T(8,128)(2,1)S(1)} all-to-all(bf16[16,32,512]{2,1,0:T(8,128)(2,1)} %bitcast.11), channel_id=1, replica_groups={{0,1,2,3,4,5,6,7,8,9,10,11,12,13,14,15},{16,17,18,19,20,21,22,23,24,25,..., dimensions={0} | all-to-all | bytes 1048576 | tf_op jit(solution)/shard_map/all_to_all | solution.py:305
  47.0 0.0 copy-done
  47.0 0.0 copy-done.1
  47.0 0.9 %pairs.1 = (bf16[512,1024]{1,0:T(8,128)(2,1)S(1)}, bf16[512,512]{1,0:T(8,128)(2,1)S(1)}) custom-call(bf16[512,512]{1,0:T(8,128)(2,1)S(1)} %bitcast.6, bf16[512,512]{1,0:T(8,128)(2,1)S(1)} %bitcast.7, bf16[1024]{0:T(1024)(128)(2,1)S(1)} %copy-done.1, bf16[1024,512]{1,0:T(8,128)(2,1)S(1)} %copy-done), custom_call_target="tpu_custom_call" | custom-call | flops 536870912 | bytes 3670016 | tf_op jit(solution)/shard_map/pairs/pallas_call | solution.py:179
  48.0 1.9 %collective-permute-start = (bf16[512,512]{1,0:T(8,128)(2,1)S(1)}, bf16[512,512]{1,0:T(8,128)(2,1)S(1)}, u32[]{:S(2)}, u32[]{:S(2)}) collective-permute-start(bf16[512,512]{1,0:T(8,128)(2,1)S(1)} %get-tuple-element.11.key_ref.value_ref), channel_id=1, source_target_pairs={{0,1},{1,2},{2,3},{3,4},{4,5},{5,6},{6,7},{7,8},{8,9},{9,10},{10,1... | collective-permute-start | bytes 1572872 | tf_op jit(solution)/shard_map/ppermute | solution.py:25
  49.9 0.0 copy-done.2
  49.9 4.8 %own_frame.1 = (bf16[512,1024]{1,0:T(8,128)(2,1)S(1)}, f32[512,1024]{1,0:T(8,128)S(1)}, f32[512,1024]{1,0:T(8,128)S(1)}) custom-call(bf16[512,1024]{1,0:T(8,128)(2,1)S(1)} %get-tuple-element.10.normed_ref, bf16[1024,1024]{1,0:T(8,128)(2,1)S(1)} %copy-done.2, bf16[512,512]{1,0:T(8,128)(2,1)S(1)} %get-tuple-element.11.key_ref.value_ref, ...), custom_call_target="tpu_custom_call" | custom-call | flops 2147483648 | bytes 6291456 | tf_op jit(solution)/shard_map/own_frame/pallas_call | solution.py:224
  54.7 4.7 %collective-permute-done.key_ref.value_ref = bf16[512,512]{1,0:T(8,128)(2,1)S(1)} collective-permute-done((bf16[512,512]{1,0:T(8,128)(2,1)S(1)}, bf16[512,512]{1,0:T(8,128)(2,1)S(1)}, u32[]{:S(2)}, u32[]{:S(2)}) %collective-permute-start) | collective-permute-done | bytes 524320 | tf_op jit(solution)/shard_map/ppermute | solution.py:25
  59.3 4.6 %earlier_frame.1 = bf16[512,1024]{1,0:T(8,128)(2,1)} custom-call(bf16[512,1024]{1,0:T(8,128)(2,1)S(1)} %get-tuple-element.12.query_ref, bf16[512,512]{1,0:T(8,128)(2,1)S(1)} %collective-permute-done.key_ref.value_ref, bf16[512,512]{1,0:T(8,128)(2,1)S(1)} %collective-permute-done.key_ref.value_ref, f32[512,1024]{1,0:T(8,128)S(1)} %get-tuple-element.13.partial_ref, ...), custom_call_target="tpu_custom_call" | custom-call | flops 1073741824 | bytes 5242880 | tf_op jit(solution)/shard_map/earlier_frame/pallas_call | solution.py:280
Async XLA Ops:
  8.2 20.1 %all-to-all-start = ((bf16[16,32,512]{2,1,0:T(8,128)(2,1)}), bf16[16,32,512]{2,1,0:T(8,128)(2,1)S(1)}, u32[]{:S(2)}, u32[]{:S(2)}) async-start(bf16[16,32,512]{2,1,0:T(8,128)(2,1)} %bitcast.10), calls=%async_computation | async-start | bytes 1048576 | tf_op jit(solution)/shard_map/all_to_all | solution.py:305
  14.4 32.6 %copy-start = (bf16[1024,512]{1,0:T(8,128)(2,1)S(1)}, bf16[1024,512]{1,0:T(8,128)(2,1)}, u32[]{:S(2)}) copy-start(bf16[1024,512]{1,0:T(8,128)(2,1)} %w_ref.2) | copy-start | bytes 3145732
  14.4 32.6 %copy-start.1 = (bf16[1024]{0:T(1024)(128)(2,1)S(1)}, bf16[1024]{0:T(1024)(128)(2,1)}, u32[]{:S(2)}) copy-start(bf16[1024]{0:T(1024)(128)(2,1)} %gain_ref.1) | copy-start | bytes 6148
  28.3 21.6 %copy-start.2 = (bf16[1024,1024]{1,0:T(8,128)(2,1)S(1)}, bf16[1024,1024]{1,0:T(8,128)(2,1)}, u32[]{:S(2)}) copy-start(bf16[1024,1024]{1,0:T(8,128)(2,1)} %w_ref.3) | copy-start | bytes 6291460
  48.0 11.4 %collective-permute-start = (bf16[512,512]{1,0:T(8,128)(2,1)S(1)}, bf16[512,512]{1,0:T(8,128)(2,1)S(1)}, u32[]{:S(2)}, u32[]{:S(2)}) collective-permute-start(bf16[512,512]{1,0:T(8,128)(2,1)S(1)} %get-tuple-element.11.key_ref.value_ref), channel_id=1, source_target_pairs={{0,1},{1,2},{2,3},{3,4},{4,5},{5,6},{6,7},{7,8},{8,9},{9,10},{10,1... | collective-permute-start | bytes 1572872 | tf_op jit(solution)/shard_map/ppermute | solution.py:25

commit v4 on v3

--- a/solution.py
+++ b/solution.py
@@ -15,6 +15,9 @@
 SPAN = 128
 PAIR = 2
 
+APART = (0, 12, 8, 13, 9, 14, 15, 7, 10, 6, 11, 5, 4, 3, 2, 1)
+AHEAD = (12, 8, 13, 9, 14)
+
 epsilon = 1e-06
 MIB = 1 << 20
 
@@ -41,108 +44,118 @@
     return slice(head * HD, (head + 1) * HD)
 
 
-def mixer_kernel(first, heads, has_state, *refs):
+def mixer_kernel(has_state, *refs):
     if has_state:
         state_ref, *refs = refs
-    tokens_ref, w_ref, gain_ref, out_ref, weights, arrived = refs
-    rows, width = tokens_ref.shape
-    spans = rows // SPAN
+    tokens_ref, residual_ref, wq_ref, wk_ref, wv_ref, gain_ref, out_ref = refs
+    tokens = tokens_ref[...]
+    rows = tokens.shape[0]
+    block = 2 * SPAN
+    query = dot(tokens, wq_ref[...]).astype(jnp.bfloat16)
+    key = dot(tokens, wk_ref[...]).astype(jnp.bfloat16)
+    value = dot(tokens, wv_ref[...]).astype(jnp.bfloat16)
+    units = [(head, start) for head in range(PAIR) for start in range(0, rows, block)]
+
+    def scores_of(unit):
+        head, start = unit
+        lanes = head_lanes(head)
+        return dot_nt(query[start : start + block, lanes], key[: start + block, lanes])
+
+    scores = scores_of(units[0])
+    for index, (head, start) in enumerate(units):
+        upcoming = scores_of(units[index + 1]) if index + 1 < len(units) else None
+        lanes = head_lanes(head)
+        here = slice(start, start + block)
+        causal = lax.broadcasted_iota(jnp.int32, scores.shape, 1) <= start + (
+            lax.broadcasted_iota(jnp.int32, scores.shape, 0)
+        )
+        local = jnp.where(causal, scores, 0.0).astype(jnp.bfloat16)
+        out = dot(local, value[: start + block, lanes])
+        if has_state:
+            out += dot(query[here, lanes], state_ref[head].astype(jnp.bfloat16))
+        mean_square = jnp.mean(out * out, axis=-1, keepdims=True)
+        gain = gain_ref[:, lanes].astype(jnp.float32)
+        normed = out * lax.rsqrt(mean_square + epsilon) * gain
+        residual = residual_ref[here, lanes].astype(jnp.float32)
+        out_ref[here, lanes] = (residual + normed).astype(jnp.bfloat16)
+        scores = upcoming
+
+
+def lead_kernel(has_state, *refs):
+    *refs, hidden_ref = refs
+    tiles = refs[-len(AHEAD) :]
+    mixer_kernel(has_state, *refs[: -len(AHEAD)], hidden_ref)
+    size = hidden_ref.shape[0] // SB
+    place = lax.rem(lax.axis_index("tm"), SB)
+    for apart, tile in zip(AHEAD, tiles):
+        start = pl.multiple_of((place ^ apart) * size, size)
+        tile[...] = hidden_ref[pl.ds(start, size), :]
+
+
+def rest_kernel(has_state, lead_ref, *refs):
+    *refs, scratch = refs
+    tiles = refs[-len(APART) :]
+    step = pl.program_id(0)
+    mixer_kernel(has_state, *refs[: -len(APART)], scratch.at[step])
+    size = scratch.shape[1] // SB
+    place = lax.rem(lax.axis_index("tm"), SB)
+
+    @pl.when(step == pl.num_programs(0) - 1)
+    def _():
+        for apart, tile in zip(APART, tiles):
+            rows = pl.ds(pl.multiple_of((place ^ apart) * size, size), size)
+            parts = [scratch[j, rows, :] for j in range(scratch.shape[0])]
+            if apart not in AHEAD:
+                parts.insert(0, lead_ref[rows, :])
+            tile[...] = jnp.concatenate(parts, axis=1)
+
+
+def mixer(first, tokens, w_lin, gain_lin, state, lead=None):
+    rows, width = tokens.shape
     columns = PAIR * HD
-    pairs = heads // PAIR
-    copies = []
-    for pair in range(pairs):
-        for part in range(3):
-            start = part * width + first * HD + pair * columns
-            copies.append(
-                pltpu.make_async_copy(
-                    w_ref.at[:, start : start + columns],
-                    weights.at[pair, part],
-                    arrived.at[pair, part],
-                )
-            )
-    for copy in copies:
-        copy.start()
-    tokens = tokens_ref[...]
-    gains = gain_ref[...].astype(jnp.float32).reshape(1, width)
-    causal = lax.broadcasted_iota(jnp.int32, (SPAN, SPAN), 0) >= lax.broadcasted_iota(
-        jnp.int32, (SPAN, SPAN), 1
-    )
-
-    def project(pair):
-        packed = []
-        for part in range(3):
-            copies[3 * pair + part].wait()
-            packed.append(dot(tokens, weights[pair, part]).astype(jnp.bfloat16))
-        return packed
-
-    def attend(pair, query, key, value):
-        units = []
-        for head in range(PAIR):
-            for span in range(spans):
-                here = slice(span * SPAN, (span + 1) * SPAN)
-                units.append((head, span, here, head_lanes(head)))
-        local, before, mixed = {}, {}, {}
-        for head, span, here, lanes in units:
-            scores = dot_nt(query[here, lanes], key[here, lanes])
-            local[head, span] = jnp.where(causal, scores, 0.0).astype(jnp.bfloat16)
-        for head, span, here, lanes in units:
-            if span == 0:
-                state = state_ref[pair * PAIR + head] if has_state else None
-            before[head, span] = state
-            if span + 1 < spans:
-                update = dot_tn(key[here, lanes], value[here, lanes])
-                state = update if state is None else state + update
-        for head, span, here, lanes in units:
-            if before[head, span] is None:
-                mixed[head, span] = dot(local[head, span], value[here, lanes])
-            else:
-                mixed[head, span] = dot(
-                    jnp.concatenate([query[here, lanes], local[head, span]], axis=1),
-                    jnp.concatenate(
-                        [before[head, span].astype(jnp.bfloat16), value[here, lanes]], axis=0
-                    ),
-                )
-        for head, span, here, lanes in units:
-            out = mixed[head, span]
-            own = pair * PAIR + head
-            mean_square = jnp.mean(out * out, axis=-1, keepdims=True)
-            gain = gains[:, head_lanes(first + own)]
-            normed = out * lax.rsqrt(mean_square + epsilon) * gain
-            residual = tokens_ref[here, head_lanes(first + own)].astype(jnp.float32)
-            out_ref[here, head_lanes(own)] = (residual + normed).astype(jnp.bfloat16)
-
-    packed = project(0)
-    for pair in range(pairs):
-        upcoming = project(pair + 1) if pair + 1 < pairs else None
-        attend(pair, *packed)
-        packed = upcoming
-
-
-def mixer(first, heads, tokens, w_lin, gain_lin, state):
-    rows, width = tokens.shape
-    columns = heads * HD
-    operands = [tokens, w_lin, gain_lin]
+    steps = HEADS // PAIR
+    skip = first // PAIR
+    half = width // 2
+    size = rows // SB
     in_specs = [
-        pl.BlockSpec(memory_space=pltpu.VMEM),
-        pl.BlockSpec(memory_space=pl.ANY),
-        pl.BlockSpec(memory_space=pltpu.VMEM),
+        pl.BlockSpec((rows, width), lambda c: (0, 0)),
+        pl.BlockSpec((rows, columns), lambda c: (0, skip + c)),
+        pl.BlockSpec((width, columns), lambda c: (0, skip + c)),
+        pl.BlockSpec((width, columns), lambda c: (0, steps + skip + c)),
+        pl.BlockSpec((width, columns), lambda c: (0, 2 * steps + skip + c)),
+        pl.BlockSpec((1, columns), lambda c: (0, skip + c)),
     ]
+    operands = [tokens, tokens, w_lin, w_lin, w_lin, gain_lin]
     if state is not None:
-        operands.insert(0, state[first : first + heads])
-        in_specs.insert(0, pl.BlockSpec(memory_space=pltpu.VMEM))
+        operands.insert(0, state)
+        in_specs.insert(0, pl.BlockSpec((PAIR, HD, HD), lambda c: (skip + c, 0, 0)))
+    if lead is None:
+        kernel = lead_kernel
+        out_specs = [pl.BlockSpec((size, columns), lambda c: (0, c)) for _ in AHEAD]
+        out_specs.append(pl.BlockSpec((rows, columns), lambda c: (0, c)))
+        out_shape = [jax.ShapeDtypeStruct((size, half), jnp.bfloat16) for _ in AHEAD]
+        out_shape.append(jax.ShapeDtypeStruct((rows, half), jnp.bfloat16))
+        scratch = []
+    else:
+        kernel = rest_kernel
+        operands.insert(0, lead)
+        in_specs.insert(0, pl.BlockSpec((rows, half), lambda c: (0, 0)))
+        widths = [half if apart in AHEAD else width for apart in APART]
+        out_specs = [pl.BlockSpec((size, wide), lambda c: (0, 0)) for wide in widths]
+        out_shape = [jax.ShapeDtypeStruct((size, wide), jnp.bfloat16) for wide in widths]
+        scratch = [pltpu.VMEM((steps // 2, rows, columns), jnp.bfloat16)]
     return pl.pallas_call(
-        functools.partial(mixer_kernel, first, heads, state is not None),
+        functools.partial(kernel, state is not None),
+        grid=(steps // 2,),
         in_specs=in_specs,
-        out_shape=jax.ShapeDtypeStruct((rows, columns), jnp.bfloat16),
-        scratch_shapes=[
-            pltpu.VMEM((heads // PAIR, 3, width, PAIR * HD), jnp.bfloat16),
-            pltpu.SemaphoreType.DMA((heads // PAIR, 3)),
-        ],
+        out_specs=out_specs,
+        out_shape=out_shape,
+        scratch_shapes=scratch,
         compiler_params=pltpu.CompilerParams(vmem_limit_bytes=56 * MIB),
         cost_estimate=pl.CostEstimate(
-            flops=2 * rows * width * 3 * columns + 8 * rows * SPAN * columns,
-            bytes_accessed=2 * (3 * width * columns + rows * width + rows * columns),
-            transcendentals=rows * heads,
+            flops=2 * rows * width * 3 * half + 8 * rows * SPAN * half,
+            bytes_accessed=2 * (3 * width * half + 2 * rows * width),
+            transcendentals=rows * HEADS // 2,
         ),
         name="mixer",
     )(*operands)
@@ -163,8 +176,16 @@
     return lax.fori_loop(0, time_ranges - 1, advance_hop, jnp.zeros_like(block_total))
 
 
-def pairs_kernel(left_ref, right_ref, gain_ref, w_ref, normed_ref, pairs_ref):
-    widened = jnp.concatenate([left_ref[...], right_ref[...]], axis=1).astype(jnp.float32)
+def pairs_kernel(gain_ref, w_ref, *refs):
+    *parts, normed_ref, pairs_ref = refs
+    parts = iter(parts)
+    rows = []
+    for apart in APART:
+        tile = next(parts)[...]
+        if apart in AHEAD:
+            tile = jnp.concatenate([tile, next(parts)[...]], axis=1)
+        rows.append(tile)
+    widened = jnp.concatenate(rows, axis=0).astype(jnp.float32)
     mean_square = jnp.mean(widened * widened, axis=-1, keepdims=True)
     normed = (
         widened * lax.rsqrt(mean_square + epsilon) * gain_ref[...].astype(jnp.float32).reshape(1, -1)
@@ -173,9 +194,9 @@
     pairs_ref[...] = dot(normed, w_ref[...]).astype(jnp.bfloat16)
 
 
-def make_pairs(left, right, gain, w_kv):
-    rows = left.shape[0]
+def make_pairs(parts, gain, w_kv):
     width, wide = w_kv.shape
+    rows = sum(part.shape[0] * part.shape[1] for part in parts) // width
     return pl.pallas_call(
         pairs_kernel,
         out_shape=[
@@ -189,7 +210,7 @@
             transcendentals=rows,
         ),
         name="pairs",
-    )(left, right, gain, w_kv)
+    )(gain, w_kv, *parts)
 
 
 SCORE_SCALE = math.log2(math.e) / math.sqrt(HD)
@@ -255,7 +276,10 @@
     heads = query_ref.shape[1] // HD
     key = key_ref[...]
     value = with_ones(value_ref[...])
-    barred = jnp.where(lax.axis_index("tm") > 0, 0.0, -jnp.inf)
+    index = lax.axis_index("tm")
+    barred = jnp.where(index > 0, 0.0, -jnp.inf)
+    place = lax.rem(index, SB)
+    size = rows // SB
     scores = dot_nt(query_ref[:, head_lanes(0)], key)
     for head in range(heads):
         lanes = head_lanes(head)
@@ -267,9 +291,12 @@
         raised = jnp.exp2(scores * SCORE_SCALE - below).astype(jnp.bfloat16)
         summed = dot(raised, value)
         share = jnp.exp2(own - largest)
-        out_ref[:, lanes] = (
+        mixed = (
             (partial_ref[:, lanes] * share + summed[:, :HD]) / (share + summed[:, HD:])
         ).astype(jnp.bfloat16)
+        for slot, apart in enumerate(APART):
+            start = pl.multiple_of((place ^ apart) * size, size)
+            out_ref[pl.ds(start, size), lanes] = mixed[slot * size : (slot + 1) * size]
         scores = upcoming
 
 
@@ -299,23 +326,26 @@
     )(query, earlier_pairs, earlier_pairs, partial, log_total)
 
 
-def to_frames(part):
-    rows, columns = part.shape
-    teams = [[t * SB + s for s in range(SB)] for t in range(lax.axis_size("tm") // SB)]
-    moved = lax.all_to_all(
-        part.reshape(SB, rows // SB, columns), "tm", 0, 0, axis_index_groups=teams, tiled=True
-    )
-    return moved.reshape(rows, columns)
+def swap(tile, apart):
+    devices = lax.axis_size("tm")
+    route = [(i, i - i % SB + (i % SB ^ apart)) for i in range(devices)]
+    return lax.ppermute(tile, "tm", route)
 
 
 def body(space_time, w_lin, gain_lin, w_query, w_kv, frame_attention_gain):
     tokens = space_time[0]
     time_ranges = lax.axis_size("tm") // SB
     state = incoming_state(tokens, w_lin, time_ranges) if time_ranges > 1 else None
-    half = HEADS // 2
-    left = to_frames(mixer(0, half, tokens, w_lin, gain_lin, state))
-    right = to_frames(mixer(half, half, tokens, w_lin, gain_lin, state))
-    normed, pairs = make_pairs(left, right, frame_attention_gain, w_kv)
+    gain_lin = gain_lin.reshape(1, -1)
+    *ahead, lead = mixer(0, tokens, w_lin, gain_lin, state)
+    ahead = {apart: swap(tile, apart) for apart, tile in zip(AHEAD, ahead)}
+    tiles = mixer(HEADS // 2, tokens, w_lin, gain_lin, state, lead)
+    parts = []
+    for apart, tile in zip(APART, tiles):
+        if apart in ahead:
+            parts.append(ahead[apart])
+        parts.append(swap(tile, apart) if apart else tile)
+    normed, pairs = make_pairs(parts, frame_attention_gain, w_kv)
     earlier_pairs = shifted(pairs, "tm", 1)
     query, partial, log_total = own_frame(normed, w_query, pairs)
     attended = earlier_frame(query, earlier_pairs, partial, log_total)

time: 64.3 us -> 67.1 us (1.044)
  the two profiles are of different devices: /device:TPU:16 before, /device:TPU:1 now
where the time goes in v4:
time: 67.1 us; the launch traced here: 66.3 us
  starting transfers between devices  34.7 us (52%)
  Pallas kernels  24.4 us (36%)
  waiting for transfers between devices  4.8 us (7%)
  local copies, waits for them, and re-layouts  2.14 us (3%)
    ppermute x20, starting transfers between devices, swap(): return lax.ppermute(tile, 'tm', route)  31.5 us
    pallas_call x2, Pallas kernels, mixer(): pl.pallas_call(functools.partial(kernel, state is not None), grid=(steps...  14 us
    pallas_call x1, Pallas kernels, own_frame(): pl.pallas_call(own_kernel, grid=(KVH,), in_specs=[pl.BlockSpec((rows, wid...  4.77 us
    pallas_call x1, Pallas kernels, earlier_frame(): pl.pallas_call(earlier_kernel, grid=(KVH,), in_specs=[pl.BlockSpec((rows,...  4.62 us
    ppermute x20, waiting for transfers between devices, swap(): return lax.ppermute(tile, 'tm', route)  3.49 us
    ppermute x1, starting transfers between devices, shifted(): return lax.ppermute(block, axis, route)  3.22 us
  transfers between devices with their start and end apart: 21, of which 4 were waited for; matrix products, arithmetic and copies ran while one was open for 0% of the time, Pallas kernels for 7%

profile of v4, /device:TPU:1, one launch (start us, length us, event | category | flops | bytes accessed | tf_op | source)
XLA Modules:
  0.0 66.3 jit_solution(11077688185524489950)
XLA Ops:
  0.0 1.3 %reshape.3.refs_5_ = bf16[1,1024]{1,0:T(2,128)(2,1)} reshape(bf16[1024]{0:T(1024)(128)(2,1)} %param.8) | data formatting | bytes 4096 | tf_op jit(solution)/shard_map/reshape | solution.py:339
  1.3 6.7 %mixer.2 = (bf16[32,512]{1,0:T(8,128)(2,1)}, bf16[32,512]{1,0:T(8,128)(2,1)}, bf16[32,512]{1,0:T(8,128)(2,1)}, bf16[32,512]{1,0:T(8,128)(2,1)}, bf16[32,512]{1,0:T(8,128)(2,1)}, /*index=5*/bf16[512,512]{1,0:T(8,128)(2,1)}) custom-call(bf16[512,1024]{1,0:T(8,128)(2,1)} %bitcast.2, bf16[512,1024]{1,0:T(8,128)(2,1)} %bitcast.3, bf16[1024,3072]{1,0:T(8,128)(2,1)} %refs_4_.3, ...), custom_call_target="tpu_custom_call" | custom-call | flops 1879048192 | bytes 5242880 | tf_op jit(solution)/shard_map/mixer/pallas_call | solution.py:147
  8.0 0.0 copy-start
  8.1 0.0 copy-start.2
  8.1 0.0 copy-start.3
  8.1 7.3 %mixer.3 = (bf16[32,1024]{1,0:T(8,128)(2,1)}, bf16[32,512]{1,0:T(8,128)(2,1)}, bf16[32,512]{1,0:T(8,128)(2,1)}, bf16[32,512]{1,0:T(8,128)(2,1)}, bf16[32,512]{1,...) custom-call(bf16[512,512]{1,0:T(8,128)(2,1)} %get-tuple-element.32.l, ...), custom_call_target="tpu_custom_call" | custom-call | flops 1879048192 | bytes 5242880 | tf_op jit(solution)/shard_map/mixer/pallas_call | solution.py:147
  15.4 4.2 %collective-permute-start.1 = (bf16[32,512]{1,0:T(8,128)(2,1)}, bf16[32,512]{1,0:T(8,128)(2,1)S(1)}, u32[]{:S(2)}, u32[]{:S(2)}) collective-permute-start(bf16[32,512]{1,0:T(8,128)(2,1)} %get-tuple-element.35), channel_id=1, source_target_pairs={{0,12},{1,13},{2,14},{3,15},{4,8},{5,9},{6,10},{7,11},{8,4},{9,5},... | collective-permute-start | bytes 98312 | tf_op jit(solution)/shard_map/ppermute | solution.py:332
  19.6 2.5 %collective-permute-start.5 = (bf16[32,512]{1,0:T(8,128)(2,1)}, bf16[32,512]{1,0:T(8,128)(2,1)S(1)}, u32[]{:S(2)}, u32[]{:S(2)}) collective-permute-start(bf16[32,512]{1,0:T(8,128)(2,1)} %get-tuple-element.39), channel_id=1, source_target_pairs={{0,13},{1,12},{2,15},{3,14},{4,9},{5,8},{6,11},{7,10},{8,5},{9,4},... | collective-permute-start | bytes 98312 | tf_op jit(solution)/shard_map/ppermute | solution.py:332
  22.1 1.0 %collective-permute-start.7 = (bf16[32,512]{1,0:T(8,128)(2,1)}, bf16[32,512]{1,0:T(8,128)(2,1)S(1)}, u32[]{:S(2)}, u32[]{:S(2)}) collective-permute-start(bf16[32,512]{1,0:T(8,128)(2,1)} %get-tuple-element.41), channel_id=1, source_target_pairs={{0,9},{1,8},{2,11},{3,10},{4,13},{5,12},{6,15},{7,14},{8,1},{9,0},... | collective-permute-start | bytes 98312 | tf_op jit(solution)/shard_map/ppermute | solution.py:332
  23.1 2.5 %collective-permute-start.9 = (bf16[32,512]{1,0:T(8,128)(2,1)}, bf16[32,512]{1,0:T(8,128)(2,1)S(1)}, u32[]{:S(2)}, u32[]{:S(2)}) collective-permute-start(bf16[32,512]{1,0:T(8,128)(2,1)} %get-tuple-element.43), channel_id=1, source_target_pairs={{0,14},{1,15},{2,12},{3,13},{4,10},{5,11},{6,8},{7,9},{8,6},{9,7},... | collective-permute-start | bytes 98312 | tf_op jit(solution)/shard_map/ppermute | solution.py:332
  25.6 0.0 collective-permute-done.1.refs_2_
  25.6 1.7 %collective-permute-start = (bf16[32,512]{1,0:T(8,128)(2,1)S(1)}, bf16[32,512]{1,0:T(8,128)(2,1)S(1)}, u32[]{:S(2)}, u32[]{:S(2)}) collective-permute-start(bf16[32,512]{1,0:T(8,128)(2,1)S(1)} %copy-done.8), channel_id=1, source_target_pairs={{0,12},{1,13},{2,14},{3,15},{4,8},{5,9},{6,10},{7,11},{8,4},{9,5},... | collective-permute-start | bytes 98312 | tf_op jit(solution)/shard_map/ppermute | solution.py:332
  27.3 0.0 collective-permute-done.3.refs_4_
  27.4 0.0 collective-permute-done.5.refs_6_
  27.4 3.3 %collective-permute-start.4 = (bf16[32,512]{1,0:T(8,128)(2,1)S(1)}, bf16[32,512]{1,0:T(8,128)(2,1)S(1)}, u32[]{:S(2)}, u32[]{:S(2)}) collective-permute-start(bf16[32,512]{1,0:T(8,128)(2,1)S(1)} %copy-done.6), channel_id=1, source_target_pairs={{0,13},{1,12},{2,15},{3,14},{4,9},{5,8},{6,11},{7,10},{8,5},{9,4},... | collective-permute-start | bytes 98312 | tf_op jit(solution)/shard_map/ppermute | solution.py:332
  30.6 0.0 collective-permute-done.7.refs_8_
  30.7 2.6 %collective-permute-start.8 = (bf16[32,512]{1,0:T(8,128)(2,1)S(1)}, bf16[32,512]{1,0:T(8,128)(2,1)S(1)}, u32[]{:S(2)}, u32[]{:S(2)}) collective-permute-start(bf16[32,512]{1,0:T(8,128)(2,1)S(1)} %copy-done.4), channel_id=1, source_target_pairs={{0,14},{1,15},{2,12},{3,13},{4,10},{5,11},{6,8},{7,9},{8,6},{9,7},... | collective-permute-start | bytes 98312 | tf_op jit(solution)/shard_map/ppermute | solution.py:332
  33.3 3.8 %collective-permute-start.10 = (bf16[32,1024]{1,0:T(8,128)(2,1)}, bf16[32,1024]{1,0:T(8,128)(2,1)S(1)}, u32[]{:S(2)}, u32[]{:S(2)}) collective-permute-start(bf16[32,1024]{1,0:T(8,128)(2,1)} %get-tuple-element.44), channel_id=1, source_target_pairs={{0,15},{1,14},{2,13},{3,12},{4,11},{5,10},{6,9},{7,8},{8,7},{9,6},... | collective-permute-start | bytes 196616 | tf_op jit(solution)/shard_map/ppermute | solution.py:332
  37.1 1.9 %collective-permute-start.12 = (bf16[32,1024]{1,0:T(8,128)(2,1)}, bf16[32,1024]{1,0:T(8,128)(2,1)S(1)}, u32[]{:S(2)}, u32[]{:S(2)}) collective-permute-start(bf16[32,1024]{1,0:T(8,128)(2,1)} %get-tuple-element.46), channel_id=1, source_target_pairs={{0,10},{1,11},{2,8},{3,9},{4,14},{5,15},{6,12},{7,13},{8,2},{9,3},... | collective-permute-start | bytes 196616 | tf_op jit(solution)/shard_map/ppermute | solution.py:332
  39.0 4.6 %collective-permute-start.14 = (bf16[32,1024]{1,0:T(8,128)(2,1)}, bf16[32,1024]{1,0:T(8,128)(2,1)S(1)}, u32[]{:S(2)}, u32[]{:S(2)}) collective-permute-start(bf16[32,1024]{1,0:T(8,128)(2,1)} %get-tuple-element.48), channel_id=1, source_target_pairs={{0,11},{1,10},{2,9},{3,8},{4,15},{5,14},{6,13},{7,12},{8,3},{9,2},... | collective-permute-start | bytes 196616 | tf_op jit(solution)/shard_map/ppermute | solution.py:332
  43.5 0.1 collective-permute-start.16
  43.6 2.2 %collective-permute-start.17 = (bf16[32,1024]{1,0:T(8,128)(2,1)}, bf16[32,1024]{1,0:T(8,128)(2,1)S(1)}, u32[]{:S(2)}, u32[]{:S(2)}) collective-permute-start(bf16[32,1024]{1,0:T(8,128)(2,1)} %get-tuple-element.51), channel_id=1, source_target_pairs={{0,3},{1,2},{2,1},{3,0},{4,7},{5,6},{6,5},{7,4},{8,11},{9,10},{10,... | collective-permute-start | bytes 196616 | tf_op jit(solution)/shard_map/ppermute | solution.py:332
  45.8 1.2 %collective-permute-start.18 = (bf16[32,1024]{1,0:T(8,128)(2,1)}, bf16[32,1024]{1,0:T(8,128)(2,1)S(1)}, u32[]{:S(2)}, u32[]{:S(2)}) collective-permute-start(bf16[32,1024]{1,0:T(8,128)(2,1)} %get-tuple-element.52), channel_id=1, source_target_pairs={{0,2},{1,3},{2,0},{3,1},{4,6},{5,7},{6,4},{7,5},{8,10},{9,11},{10,... | collective-permute-start | bytes 196616 | tf_op jit(solution)/shard_map/ppermute | solution.py:332
  47.0 0.5 collective-permute-done.14.refs_15_
  47.5 0.6 collective-permute-done.15.refs_16_
  48.1 2.4 %collective-permute-done.18.refs_19_ = bf16[32,1024]{1,0:T(8,128)(2,1)S(1)} collective-permute-done((bf16[32,1024]{1,0:T(8,128)(2,1)}, bf16[32,1024]{1,0:T(8,128)(2,1)S(1)}, u32[]{:S(2)}, u32[]{:S(2)}) %collective-permute-start.18) | collective-permute-done | bytes 65568 | tf_op jit(solution)/shard_map/ppermute | solution.py:332
  50.5 0.8 %copy-done.1 = bf16[32,1024]{1,0:T(8,128)(2,1)S(1)} copy-done((bf16[32,1024]{1,0:T(8,128)(2,1)S(1)}, bf16[32,1024]{1,0:T(8,128)(2,1)}, u32[]{:S(2)}) %copy-start.1) | copy-done | bytes 65560
  51.3 1.0 %pairs.1 = (bf16[512,1024]{1,0:T(8,128)(2,1)S(1)}, bf16[512,512]{1,0:T(8,128)(2,1)S(1)}) custom-call(bf16[1024]{0:T(1024)(128)(2,1)S(1)} %copy-done.2, bf16[1024,512]{1,0:T(8,128)(2,1)S(1)} %copy-done, bf16[32,1024]{1,0:T(8,128)(2,1)S(1)} %copy-done.1, bf16[32,512]{1,0:T(8,128)(2,1)S(1)} %collective-permute-done.refs_1_, ...), custom_call_target="tpu_custom_call" | custom-call | flops 536870912 | bytes 3670016 | tf_op jit(solution)/shard_map/pairs/pallas_call | solution.py:200
  52.3 3.2 %collective-permute-start.20 = (bf16[512,512]{1,0:T(8,128)(2,1)S(1)}, bf16[512,512]{1,0:T(8,128)(2,1)S(1)}, u32[]{:S(2)}, u32[]{:S(2)}) collective-permute-start(bf16[512,512]{1,0:T(8,128)(2,1)S(1)} %get-tuple-element.55.key_ref.value_ref), channel_id=1, source_target_pairs={{0,1},{1,2},{2,3},{3,4},{4,5},{5,6},{6,7},{7,8},{8,9},{9,10},{10,1... | collective-permute-start | bytes 1572872 | tf_op jit(solution)/shard_map/ppermute | solution.py:28
  55.5 4.8 %own_frame.1 = (bf16[512,1024]{1,0:T(8,128)(2,1)S(1)}, f32[512,1024]{1,0:T(8,128)S(1)}, f32[512,1024]{1,0:T(8,128)S(1)}) custom-call(bf16[512,1024]{1,0:T(8,128)(2,1)S(1)} %get-tuple-element.54.normed_ref, bf16[1024,1024]{1,0:T(8,128)(2,1)S(1)} %copy-done.3, bf16[512,512]{1,0:T(8,128)(2,1)S(1)} %get-tuple-element.55.key_ref.value_ref, ...), custom_call_target="tpu_custom_call" | custom-call | flops 2147483648 | bytes 6291456 | tf_op jit(solution)/shard_map/own_frame/pallas_call | solution.py:245
  60.3 1.3 %collective-permute-done.20.key_ref.value_ref = bf16[512,512]{1,0:T(8,128)(2,1)S(1)} collective-permute-done((bf16[512,512]{1,0:T(8,128)(2,1)S(1)}, bf16[512,512]{1,0:T(8,128)(2,1)S(1)}, u32[]{:S(2)}, u32[]{:S(2)}) %collective-permute-start.20) | collective-permute-done | bytes 524320 | tf_op jit(solution)/shard_map/ppermute | solution.py:28
  61.6 4.6 %earlier_frame.1 = bf16[512,1024]{1,0:T(8,128)(2,1)} custom-call(bf16[512,1024]{1,0:T(8,128)(2,1)S(1)} %get-tuple-element.56.query_ref, bf16[512,512]{1,0:T(8,128)(2,1)S(1)} %collective-permute-done.20.key_ref.value_ref, bf16[512,512]{1,0:T(8,128)(2,1)S(1)} %collective-permute-done.20.key_ref.value_ref, f32[512,1024]{1,0:T(8,128)S(1)} %get-tuple-element.57.partial_ref, ...), custom_call_target="tpu_custom_call" | custom-call | flops 1073741824 | bytes 5242880 | tf_op jit(solution)/shard_map/earlier_frame/pallas_call | solution.py:307
  (34 shorter events, 0.1 us)
Async XLA Ops:
  8.0 17.6 %copy-start.8 = (bf16[32,512]{1,0:T(8,128)(2,1)S(1)}, bf16[32,512]{1,0:T(8,128)(2,1)}, u32[]{:S(2)}) copy-start(bf16[32,512]{1,0:T(8,128)(2,1)} %get-tuple-element.34) | copy-start | bytes 98308
  8.0 19.3 %copy-start.7 = (bf16[32,512]{1,0:T(8,128)(2,1)S(1)}, bf16[32,512]{1,0:T(8,128)(2,1)}, u32[]{:S(2)}) copy-start(bf16[32,512]{1,0:T(8,128)(2,1)} %get-tuple-element.36) | copy-start | bytes 98308
  8.0 19.4 %copy-start.6 = (bf16[32,512]{1,0:T(8,128)(2,1)S(1)}, bf16[32,512]{1,0:T(8,128)(2,1)}, u32[]{:S(2)}) copy-start(bf16[32,512]{1,0:T(8,128)(2,1)} %get-tuple-element.38) | copy-start | bytes 98308
  8.0 22.6 %copy-start.5 = (bf16[32,512]{1,0:T(8,128)(2,1)S(1)}, bf16[32,512]{1,0:T(8,128)(2,1)}, u32[]{:S(2)}) copy-start(bf16[32,512]{1,0:T(8,128)(2,1)} %get-tuple-element.40) | copy-start | bytes 98308
  8.0 22.6 %copy-start.4 = (bf16[32,512]{1,0:T(8,128)(2,1)S(1)}, bf16[32,512]{1,0:T(8,128)(2,1)}, u32[]{:S(2)}) copy-start(bf16[32,512]{1,0:T(8,128)(2,1)} %get-tuple-element.42) | copy-start | bytes 98308
  8.0 42.5 %copy-start = (bf16[1024,512]{1,0:T(8,128)(2,1)S(1)}, bf16[1024,512]{1,0:T(8,128)(2,1)}, u32[]{:S(2)}) copy-start(bf16[1024,512]{1,0:T(8,128)(2,1)} %w_ref.2) | copy-start | bytes 3145732
  8.1 42.4 %copy-start.2 = (bf16[1024]{0:T(1024)(128)(2,1)S(1)}, bf16[1024]{0:T(1024)(128)(2,1)}, u32[]{:S(2)}) copy-start(bf16[1024]{0:T(1024)(128)(2,1)} %gain_ref.1) | copy-start | bytes 6148
  8.1 47.5 %copy-start.3 = (bf16[1024,1024]{1,0:T(8,128)(2,1)S(1)}, bf16[1024,1024]{1,0:T(8,128)(2,1)}, u32[]{:S(2)}) copy-start(bf16[1024,1024]{1,0:T(8,128)(2,1)} %w_ref.3) | copy-start | bytes 6291460
  15.4 10.2 %collective-permute-start.1 = (bf16[32,512]{1,0:T(8,128)(2,1)}, bf16[32,512]{1,0:T(8,128)(2,1)S(1)}, u32[]{:S(2)}, u32[]{:S(2)}) collective-permute-start(bf16[32,512]{1,0:T(8,128)(2,1)} %get-tuple-element.35), channel_id=1, source_target_pairs={{0,12},{1,13},{2,14},{3,15},{4,8},{5,9},{6,10},{7,11},{8,4},{9,5},... | collective-permute-start | bytes 98312 | tf_op jit(solution)/shard_map/ppermute | solution.py:332
  19.6 7.7 %collective-permute-start.3 = (bf16[32,512]{1,0:T(8,128)(2,1)}, bf16[32,512]{1,0:T(8,128)(2,1)S(1)}, u32[]{:S(2)}, u32[]{:S(2)}) collective-permute-start(bf16[32,512]{1,0:T(8,128)(2,1)} %get-tuple-element.37), channel_id=1, source_target_pairs={{0,8},{1,9},{2,10},{3,11},{4,12},{5,13},{6,14},{7,15},{8,0},{9,1},... | collective-permute-start | bytes 98312 | tf_op jit(solution)/shard_map/ppermute | solution.py:332
  19.6 7.7 %collective-permute-start.5 = (bf16[32,512]{1,0:T(8,128)(2,1)}, bf16[32,512]{1,0:T(8,128)(2,1)S(1)}, u32[]{:S(2)}, u32[]{:S(2)}) collective-permute-start(bf16[32,512]{1,0:T(8,128)(2,1)} %get-tuple-element.39), channel_id=1, source_target_pairs={{0,13},{1,12},{2,15},{3,14},{4,9},{5,8},{6,11},{7,10},{8,5},{9,4},... | collective-permute-start | bytes 98312 | tf_op jit(solution)/shard_map/ppermute | solution.py:332
  22.1 8.5 %collective-permute-start.7 = (bf16[32,512]{1,0:T(8,128)(2,1)}, bf16[32,512]{1,0:T(8,128)(2,1)S(1)}, u32[]{:S(2)}, u32[]{:S(2)}) collective-permute-start(bf16[32,512]{1,0:T(8,128)(2,1)} %get-tuple-element.41), channel_id=1, source_target_pairs={{0,9},{1,8},{2,11},{3,10},{4,13},{5,12},{6,15},{7,14},{8,1},{9,0},... | collective-permute-start | bytes 98312 | tf_op jit(solution)/shard_map/ppermute | solution.py:332
  23.1 7.5 %collective-permute-start.9 = (bf16[32,512]{1,0:T(8,128)(2,1)}, bf16[32,512]{1,0:T(8,128)(2,1)S(1)}, u32[]{:S(2)}, u32[]{:S(2)}) collective-permute-start(bf16[32,512]{1,0:T(8,128)(2,1)} %get-tuple-element.43), channel_id=1, source_target_pairs={{0,14},{1,15},{2,12},{3,13},{4,10},{5,11},{6,8},{7,9},{8,6},{9,7},... | collective-permute-start | bytes 98312 | tf_op jit(solution)/shard_map/ppermute | solution.py:332
  25.6 7.6 %collective-permute-start = (bf16[32,512]{1,0:T(8,128)(2,1)S(1)}, bf16[32,512]{1,0:T(8,128)(2,1)S(1)}, u32[]{:S(2)}, u32[]{:S(2)}) collective-permute-start(bf16[32,512]{1,0:T(8,128)(2,1)S(1)} %copy-done.8), channel_id=1, source_target_pairs={{0,12},{1,13},{2,14},{3,15},{4,8},{5,9},{6,10},{7,11},{8,4},{9,5},... | collective-permute-start | bytes 98312 | tf_op jit(solution)/shard_map/ppermute | solution.py:332
  27.4 9.7 %collective-permute-start.2 = (bf16[32,512]{1,0:T(8,128)(2,1)S(1)}, bf16[32,512]{1,0:T(8,128)(2,1)S(1)}, u32[]{:S(2)}, u32[]{:S(2)}) collective-permute-start(bf16[32,512]{1,0:T(8,128)(2,1)S(1)} %copy-done.7), channel_id=1, source_target_pairs={{0,8},{1,9},{2,10},{3,11},{4,12},{5,13},{6,14},{7,15},{8,0},{9,1},... | collective-permute-start | bytes 98312 | tf_op jit(solution)/shard_map/ppermute | solution.py:332
  27.4 9.7 %collective-permute-start.4 = (bf16[32,512]{1,0:T(8,128)(2,1)S(1)}, bf16[32,512]{1,0:T(8,128)(2,1)S(1)}, u32[]{:S(2)}, u32[]{:S(2)}) collective-permute-start(bf16[32,512]{1,0:T(8,128)(2,1)S(1)} %copy-done.6), channel_id=1, source_target_pairs={{0,13},{1,12},{2,15},{3,14},{4,9},{5,8},{6,11},{7,10},{8,5},{9,4},... | collective-permute-start | bytes 98312 | tf_op jit(solution)/shard_map/ppermute | solution.py:332
  30.7 8.3 %collective-permute-start.6 = (bf16[32,512]{1,0:T(8,128)(2,1)S(1)}, bf16[32,512]{1,0:T(8,128)(2,1)S(1)}, u32[]{:S(2)}, u32[]{:S(2)}) collective-permute-start(bf16[32,512]{1,0:T(8,128)(2,1)S(1)} %copy-done.5), channel_id=1, source_target_pairs={{0,9},{1,8},{2,11},{3,10},{4,13},{5,12},{6,15},{7,14},{8,1},{9,0},... | collective-permute-start | bytes 98312 | tf_op jit(solution)/shard_map/ppermute | solution.py:332
  30.7 8.3 %collective-permute-start.8 = (bf16[32,512]{1,0:T(8,128)(2,1)S(1)}, bf16[32,512]{1,0:T(8,128)(2,1)S(1)}, u32[]{:S(2)}, u32[]{:S(2)}) collective-permute-start(bf16[32,512]{1,0:T(8,128)(2,1)S(1)} %copy-done.4), channel_id=1, source_target_pairs={{0,14},{1,15},{2,12},{3,13},{4,10},{5,11},{6,8},{7,9},{8,6},{9,7},... | collective-permute-start | bytes 98312 | tf_op jit(solution)/shard_map/ppermute | solution.py:332
  33.3 10.3 %collective-permute-start.10 = (bf16[32,1024]{1,0:T(8,128)(2,1)}, bf16[32,1024]{1,0:T(8,128)(2,1)S(1)}, u32[]{:S(2)}, u32[]{:S(2)}) collective-permute-start(bf16[32,1024]{1,0:T(8,128)(2,1)} %get-tuple-element.44), channel_id=1, source_target_pairs={{0,15},{1,14},{2,13},{3,12},{4,11},{5,10},{6,9},{7,8},{8,7},{9,6},... | collective-permute-start | bytes 196616 | tf_op jit(solution)/shard_map/ppermute | solution.py:332
  37.1 6.5 %collective-permute-start.11 = (bf16[32,1024]{1,0:T(8,128)(2,1)}, bf16[32,1024]{1,0:T(8,128)(2,1)S(1)}, u32[]{:S(2)}, u32[]{:S(2)}) collective-permute-start(bf16[32,1024]{1,0:T(8,128)(2,1)} %get-tuple-element.45), channel_id=1, source_target_pairs={{0,7},{1,6},{2,5},{3,4},{4,3},{5,2},{6,1},{7,0},{8,15},{9,14},{10,... | collective-permute-start | bytes 196616 | tf_op jit(solution)/shard_map/ppermute | solution.py:332
  37.1 6.6 %collective-permute-start.12 = (bf16[32,1024]{1,0:T(8,128)(2,1)}, bf16[32,1024]{1,0:T(8,128)(2,1)S(1)}, u32[]{:S(2)}, u32[]{:S(2)}) collective-permute-start(bf16[32,1024]{1,0:T(8,128)(2,1)} %get-tuple-element.46), channel_id=1, source_target_pairs={{0,10},{1,11},{2,8},{3,9},{4,14},{5,15},{6,12},{7,13},{8,2},{9,3},... | collective-permute-start | bytes 196616 | tf_op jit(solution)/shard_map/ppermute | solution.py:332
  38.9 6.9 %collective-permute-start.13 = (bf16[32,1024]{1,0:T(8,128)(2,1)}, bf16[32,1024]{1,0:T(8,128)(2,1)S(1)}, u32[]{:S(2)}, u32[]{:S(2)}) collective-permute-start(bf16[32,1024]{1,0:T(8,128)(2,1)} %get-tuple-element.47), channel_id=1, source_target_pairs={{0,6},{1,7},{2,4},{3,5},{4,2},{5,3},{6,0},{7,1},{8,14},{9,15},{10,... | collective-permute-start | bytes 196616 | tf_op jit(solution)/shard_map/ppermute | solution.py:332
  39.0 8.5 %collective-permute-start.14 = (bf16[32,1024]{1,0:T(8,128)(2,1)}, bf16[32,1024]{1,0:T(8,128)(2,1)S(1)}, u32[]{:S(2)}, u32[]{:S(2)}) collective-permute-start(bf16[32,1024]{1,0:T(8,128)(2,1)} %get-tuple-element.48), channel_id=1, source_target_pairs={{0,11},{1,10},{2,9},{3,8},{4,15},{5,14},{6,13},{7,12},{8,3},{9,2},... | collective-permute-start | bytes 196616 | tf_op jit(solution)/shard_map/ppermute | solution.py:332
  43.5 4.6 %collective-permute-start.15 = (bf16[32,1024]{1,0:T(8,128)(2,1)}, bf16[32,1024]{1,0:T(8,128)(2,1)S(1)}, u32[]{:S(2)}, u32[]{:S(2)}) collective-permute-start(bf16[32,1024]{1,0:T(8,128)(2,1)} %get-tuple-element.49), channel_id=1, source_target_pairs={{0,5},{1,4},{2,7},{3,6},{4,1},{5,0},{6,3},{7,2},{8,13},{9,12},{10,... | collective-permute-start | bytes 196616 | tf_op jit(solution)/shard_map/ppermute | solution.py:332
  43.5 4.6 %collective-permute-start.16 = (bf16[32,1024]{1,0:T(8,128)(2,1)}, bf16[32,1024]{1,0:T(8,128)(2,1)S(1)}, u32[]{:S(2)}, u32[]{:S(2)}) collective-permute-start(bf16[32,1024]{1,0:T(8,128)(2,1)} %get-tuple-element.50), channel_id=1, source_target_pairs={{0,4},{1,5},{2,6},{3,7},{4,0},{5,1},{6,2},{7,3},{8,12},{9,13},{10,... | collective-permute-start | bytes 196616 | tf_op jit(solution)/shard_map/ppermute | solution.py:332
  43.6 4.5 %collective-permute-start.17 = (bf16[32,1024]{1,0:T(8,128)(2,1)}, bf16[32,1024]{1,0:T(8,128)(2,1)S(1)}, u32[]{:S(2)}, u32[]{:S(2)}) collective-permute-start(bf16[32,1024]{1,0:T(8,128)(2,1)} %get-tuple-element.51), channel_id=1, source_target_pairs={{0,3},{1,2},{2,1},{3,0},{4,7},{5,6},{6,5},{7,4},{8,11},{9,10},{10,... | collective-permute-start | bytes 196616 | tf_op jit(solution)/shard_map/ppermute | solution.py:332
  45.8 4.7 %collective-permute-start.18 = (bf16[32,1024]{1,0:T(8,128)(2,1)}, bf16[32,1024]{1,0:T(8,128)(2,1)S(1)}, u32[]{:S(2)}, u32[]{:S(2)}) collective-permute-start(bf16[32,1024]{1,0:T(8,128)(2,1)} %get-tuple-element.52), channel_id=1, source_target_pairs={{0,2},{1,3},{2,0},{3,1},{4,6},{5,7},{6,4},{7,5},{8,10},{9,11},{10,... | collective-permute-start | bytes 196616 | tf_op jit(solution)/shard_map/ppermute | solution.py:332
  47.5 3.0 %collective-permute-start.19 = (bf16[32,1024]{1,0:T(8,128)(2,1)}, bf16[32,1024]{1,0:T(8,128)(2,1)S(1)}, u32[]{:S(2)}, u32[]{:S(2)}) collective-permute-start(bf16[32,1024]{1,0:T(8,128)(2,1)} %get-tuple-element.53), channel_id=1, source_target_pairs={{0,1},{1,0},{2,3},{3,2},{4,5},{5,4},{6,7},{7,6},{8,9},{9,8},{10,11... | collective-permute-start | bytes 196616 | tf_op jit(solution)/shard_map/ppermute | solution.py:332
  50.5 0.8 %copy-start.1 = (bf16[32,1024]{1,0:T(8,128)(2,1)S(1)}, bf16[32,1024]{1,0:T(8,128)(2,1)}, u32[]{:S(2)}) copy-start(bf16[32,1024]{1,0:T(8,128)(2,1)} %get-tuple-element.33.refs_0_) | copy-start | bytes 196612
  52.3 9.3 %collective-permute-start.20 = (bf16[512,512]{1,0:T(8,128)(2,1)S(1)}, bf16[512,512]{1,0:T(8,128)(2,1)S(1)}, u32[]{:S(2)}, u32[]{:S(2)}) collective-permute-start(bf16[512,512]{1,0:T(8,128)(2,1)S(1)} %get-tuple-element.55.key_ref.value_ref), channel_id=1, source_target_pairs={{0,1},{1,2},{2,3},{3,4},{4,5},{5,6},{6,7},{7,8},{8,9},{9,10},{10,1... | collective-permute-start | bytes 1572872 | tf_op jit(solution)/shard_map/ppermute | solution.py:28

commit v5 on v4

v5 whole, which is shorter than its diff:
```python
import functools
import math

import jax
import jax.numpy as jnp
from jax import lax
from jax.experimental import pallas as pl
from jax.experimental.pallas import tpu as pltpu
from jax.sharding import PartitionSpec as P

HEADS = 8
HD = 128
KVH = 2
SB = 16
SPAN = 128
PAIR = 2

APART = (0, 15, 14, 13, 6, 12, 5, 11, 4, 10, 3, 9, 2, 8, 1, 7)

epsilon = 1e-06
MIB = 1 << 20


def shifted(block, axis, distance):
    devices = range(lax.axis_size(axis))
    route = [(i - distance, i) for i in devices if i - distance in devices]
    return lax.ppermute(block, axis, route)


def dot(a, b):
    return jnp.dot(a, b, preferred_element_type=jnp.float32)


def dot_nt(a, b):
    return lax.dot_general(a, b, (((1,), (1,)), ((), ())), preferred_element_type=jnp.float32)


def dot_tn(a, b):
    return lax.dot_general(a, b, (((0,), (0,)), ((), ())), preferred_element_type=jnp.float32)


def head_lanes(head):
    return slice(head * HD, (head + 1) * HD)


def causal_mask():
    shape = (SPAN, SPAN)
    return lax.broadcasted_iota(jnp.int32, shape, 0) >= lax.broadcasted_iota(jnp.int32, shape, 1)


def mix_heads(query, key, value, states, turned):
    rows = query.shape[0]
    causal = causal_mask()
    spans = [slice(start, start + SPAN) for start in range(0, rows, SPAN)]
    heads = range(query.shape[1] // HD)
    local, before, mixed = {}, {}, {}
    turns = {}
    for head in heads:
        lanes = head_lanes(head)
        if turned:
            turns[head] = key[:, lanes].T
        for span, here in enumerate(spans):
            if turned:
                scores = dot(query[here, lanes], turns[head][:, here])
            else:
                scores = dot_nt(query[here, lanes], key[here, lanes])
            local[head, span] = jnp.where(causal, scores, 0.0).astype(jnp.bfloat16)
    for head in heads:
        lanes = head_lanes(head)
        state = states[head]
        for span, here in enumerate(spans):
            before[head, span] = state
            if span + 1 < len(spans):
                if turned:
                    update = dot(turns[head][:, here], value[here, lanes])
                else:
                    update = dot_tn(key[here, lanes], value[here, lanes])
                state = update if state is None else state + update
    for head in heads:
        lanes = head_lanes(head)
        for span, here in enumerate(spans):
            if before[head, span] is None:
                mixed[head, span] = dot(local[head, span], value[here, lanes])
            else:
                mixed[head, span] = dot(
                    jnp.concatenate([query[here, lanes], local[head, span]], axis=1),
                    jnp.concatenate(
                        [before[head, span].astype(jnp.bfloat16), value[here, lanes]], axis=0
                    ),
                )
    return [(head, here, mixed[head, span]) for head in heads for span, here in enumerate(spans)]


def mixer_kernel(first, has_state, turned, *refs):
    if has_state:
        state_ref, *refs = refs
    tokens_ref, residual_ref, wq_ref, wk_ref, wv_ref, gain_ref, out_ref = refs
    tokens = tokens_ref[...]
    query = dot(tokens, wq_ref[...]).astype(jnp.bfloat16)
    key = dot(tokens, wk_ref[...]).astype(jnp.bfloat16)
    value = dot(tokens, wv_ref[...]).astype(jnp.bfloat16)
    states = [state_ref[head] if has_state else None for head in range(PAIR)]
    start = pl.multiple_of(first * HD + pl.program_id(0) * PAIR * HD, PAIR * HD)
    gains = gain_ref[pl.ds(start, PAIR * HD)].astype(jnp.float32).reshape(1, PAIR * HD)
    for head, here, out in mix_heads(query, key, value, states, turned):
        lanes = head_lanes(head)
        mean_square = jnp.mean(out * out, axis=-1, keepdims=True)
        normed = out * lax.rsqrt(mean_square + epsilon) * gains[:, lanes]
        residual = residual_ref[here, lanes].astype(jnp.float32)
        out_ref[here, lanes] = (residual + normed).astype(jnp.bfloat16)


def last_kernel(first, has_state, turned, lead_ref, *refs):
    *refs, scratch = refs
    tiles = refs[-len(APART) :]
    step = pl.program_id(0)
    mixer_kernel(first, has_state, turned, *refs[: -len(APART)], scratch.at[step])
    size = scratch.shape[1] // SB
    place = lax.rem(lax.axis_index("tm"), SB)

    @pl.when(step == pl.num_programs(0) - 1)
    def _():
        for apart, tile in zip(APART, tiles):
            rows = pl.ds(pl.multiple_of((place ^ apart) * size, size), size)
            parts = [lead_ref[rows, :]] + [scratch[j, rows, :] for j in range(scratch.shape[0])]
            tile[...] = jnp.concatenate(parts, axis=1)


def mixer(first, tokens, w_lin, gain_lin, state, lead=None):
    rows, width = tokens.shape
    columns = PAIR * HD
    steps = HEADS // PAIR
    skip = first // PAIR
    half = width // 2
    size = rows // SB
    in_specs = [
        pl.BlockSpec((rows, width), lambda c: (0, 0)),
        pl.BlockSpec((rows, columns), lambda c: (0, skip + c)),
        pl.BlockSpec((width, columns), lambda c: (0, skip + c)),
        pl.BlockSpec((width, columns), lambda c: (0, steps + skip + c)),
        pl.BlockSpec((width, columns), lambda c: (0, 2 * steps + skip + c)),
        pl.BlockSpec(memory_space=pltpu.VMEM),
    ]
    operands = [tokens, tokens, w_lin, w_lin, w_lin, gain_lin]
    if state is not None:
        operands.insert(0, state)
        in_specs.insert(0, pl.BlockSpec((PAIR, HD, HD), lambda c: (skip + c, 0, 0)))
    if lead is None:
        kernel = functools.partial(mixer_kernel, first, state is not None, True)
        out_specs = pl.BlockSpec((rows, columns), lambda c: (0, c))
        out_shape = jax.ShapeDtypeStruct((rows, half), jnp.bfloat16)
        scratch = []
    else:
        kernel = functools.partial(last_kernel, first, state is not None, False)
        operands.insert(0, lead)
        in_specs.insert(0, pl.BlockSpec((rows, half), lambda c: (0, 0)))
        out_specs = [pl.BlockSpec((size, width), lambda c: (0, 0)) for _ in APART]
        out_shape = [jax.ShapeDtypeStruct((size, width), jnp.bfloat16) for _ in APART]
        scratch = [pltpu.VMEM((steps // 2, rows, columns), jnp.bfloat16)]
    return pl.pallas_call(
        kernel,
        grid=(steps // 2,),
        in_specs=in_specs,
        out_specs=out_specs,
        out_shape=out_shape,
        scratch_shapes=scratch,
        compiler_params=pltpu.CompilerParams(vmem_limit_bytes=56 * MIB),
        cost_estimate=pl.CostEstimate(
            flops=2 * rows * width * 3 * half + 8 * rows * SPAN * half,
            bytes_accessed=2 * (3 * width * half + 2 * rows * width),
            transcendentals=rows * HEADS // 2,
        ),
        name="mixer",
    )(*operands)


def incoming_state(tokens, w_lin, time_ranges):
    rows, width = tokens.shape
    packed = dot(tokens, w_lin[:, width:]).astype(jnp.bfloat16).reshape(rows, 2, HEADS, HD)
    block_total = jnp.einsum(
        "nhd,nhe->hde", packed[:, 0], packed[:, 1], preferred_element_type=jnp.float32
    )
    within = lax.axis_index("tm") // SB

    def advance_hop(turn_index, running_total):
        moved = shifted(running_total + block_total, "tm", SB)
        return jnp.where(within > 0, moved, 0.0)

    return lax.fori_loop(0, time_ranges - 1, advance_hop, jnp.zeros_like(block_total))


def pairs_kernel(gain_ref, w_ref, kept_ref, *refs):
    *tiles, normed_ref, first_ref, second_ref, kept, arrived = refs
    copy = pltpu.make_async_copy(kept_ref, kept, arrived)
    copy.start()
    gain = gain_ref[...].astype(jnp.float32).reshape(1, -1)
    w_kv = w_ref[...]

    def norm(rows):
        widened = rows.astype(jnp.float32)
        mean_square = jnp.mean(widened * widened, axis=-1, keepdims=True)
        return (widened * lax.rsqrt(mean_square + epsilon) * gain).astype(jnp.bfloat16)

    def give(normed, start, out_ref):
        rows = normed.shape[0]
        pairs = dot(normed, w_kv).astype(jnp.bfloat16)
        normed_ref[start : start + rows] = normed
        out_ref[: KVH * HD] = pairs[:, : KVH * HD].T
        out_ref[KVH * HD :] = pairs[:, KVH * HD :]

    half = len(APART) // 2
    normed = norm(jnp.concatenate([tile[...] for tile in tiles[half - 1 :]], axis=0))
    give(normed, normed.shape[0], second_ref)
    copy.wait()
    normed = norm(jnp.concatenate([kept[...]] + [tile[...] for tile in tiles[: half - 1]], axis=0))
    give(normed, 0, first_ref)


def make_pairs(tiles, gain, w_kv):
    size, width = tiles[0].shape
    wide = w_kv.shape[1]
    rows = size * len(tiles)
    vmem = pl.BlockSpec(memory_space=pltpu.VMEM)
    return pl.pallas_call(
        pairs_kernel,
        in_specs=[vmem, vmem, pl.BlockSpec(memory_space=pltpu.HBM)] + [vmem] * (len(tiles) - 1),
        out_shape=[jax.ShapeDtypeStruct((rows, width), jnp.bfloat16)]
        + [jax.ShapeDtypeStruct((wide, rows // 2), jnp.bfloat16)] * 2,
        scratch_shapes=[pltpu.VMEM((size, width), jnp.bfloat16), pltpu.SemaphoreType.DMA],
        compiler_params=pltpu.CompilerParams(vmem_limit_bytes=40 * MIB),
        cost_estimate=pl.CostEstimate(
            flops=2 * rows * width * wide,
            bytes_accessed=2 * (2 * rows * width + width * wide + rows * wide),
            transcendentals=rows,
        ),
        name="pairs",
    )(gain, w_kv, *tiles)


SCORE_SCALE = math.log2(math.e) / math.sqrt(HD)
GROUP = HEADS // KVH


def keys_and_values(refs):
    both = []
    for head in range(KVH):
        keys = [ref[head_lanes(head)] for ref in refs]
        values = [ref[KVH * HD :, head_lanes(head)] for ref in refs]
        key = keys[0] if len(keys) == 1 else jnp.concatenate(keys, axis=1)
        value = values[0] if len(values) == 1 else jnp.concatenate(values, axis=0)
        both.append((key, jnp.concatenate([value, jnp.ones_like(value)], axis=1)))
    return both


def own_kernel(normed_ref, w_ref, first_ref, second_ref, query_ref, partial_ref, log_ref):
    both = keys_and_values([first_ref, second_ref])
    columns = GROUP * HD

    def project(group):
        lanes = slice(group * columns, (group + 1) * columns)
        query = dot(normed_ref[...], w_ref[:, lanes]).astype(jnp.bfloat16)
        query_ref[:, lanes] = query
        return query

    queries = {0: project(0)}

    def scores_of(head):
        group = head // GROUP
        return dot(queries[group][:, head_lanes(head % GROUP)], both[group][0])

    scores = scores_of(0)
    for head in range(HEADS):
        if head % GROUP == 0 and head + GROUP < HEADS:
            queries[head // GROUP + 1] = project(head // GROUP + 1)
        upcoming = scores_of(head + 1) if head + 1 < HEADS else None
        largest = jnp.max(scores, axis=-1, keepdims=True)
        raised = jnp.exp2((scores - largest) * SCORE_SCALE).astype(jnp.bfloat16)
        summed = dot(raised, both[head // GROUP][1])
        total = summed[:, HD:]
        partial_ref[:, head_lanes(head)] = summed[:, :HD] / total
        log_ref[:, head_lanes(head)] = largest * SCORE_SCALE + jnp.log2(total)
        scores = upcoming


def own_frame(normed, w_query, first, second):
    rows, width = normed.shape
    return pl.pallas_call(
        own_kernel,
        out_shape=[
            jax.ShapeDtypeStruct((rows, width), jnp.bfloat16),
            jax.ShapeDtypeStruct((rows, width), jnp.float32),
            jax.ShapeDtypeStruct((rows, width), jnp.float32),
        ],
        compiler_params=pltpu.CompilerParams(vmem_limit_bytes=32 * MIB),
        cost_estimate=pl.CostEstimate(
            flops=2 * rows * width * width + 4 * rows * rows * width,
            bytes_accessed=2 * width * width + 8 * rows * width,
            transcendentals=rows * rows * HEADS,
        ),
        name="own_frame",
    )(normed, w_query, first, second)


def earlier_kernel(last, query_ref, pairs_ref, partial_ref, log_ref, *outs):
    rows = query_ref.shape[0]
    both = keys_and_values([pairs_ref])
    index = lax.axis_index("tm")
    barred = jnp.where(index > 0, 0.0, -jnp.inf)
    place = lax.rem(index, SB)
    size = rows // SB

    def scores_of(head):
        return dot(query_ref[:, head_lanes(head)], both[head // GROUP][0])

    scores = scores_of(0)
    for head in range(HEADS):
        lanes = head_lanes(head)
        upcoming = scores_of(head + 1) if head + 1 < HEADS else None
        before = log_ref[:, lanes]
        here = jnp.max(scores, axis=-1, keepdims=True) * SCORE_SCALE + barred
        largest = jnp.maximum(jnp.broadcast_to(here, before.shape), before)
        below = jnp.concatenate([largest - barred] * (scores.shape[1] // HD), axis=1)
        raised = jnp.exp2(scores * SCORE_SCALE - below).astype(jnp.bfloat16)
        summed = dot(raised, both[head // GROUP][1])
        share = jnp.exp2(before - largest)
        total = share + summed[:, HD:]
        mixed = (partial_ref[:, lanes] * share + summed[:, :HD]) / total
        if last:
            mixed = mixed.astype(jnp.bfloat16)
            for slot, apart in enumerate(APART):
                start = pl.multiple_of((place ^ apart) * size, size)
                outs[0][pl.ds(start, size), lanes] = mixed[slot * size : (slot + 1) * size]
        else:
            outs[0][:, lanes] = mixed
            outs[1][:, lanes] = largest + jnp.log2(total)
        scores = upcoming


def earlier_frame(last, query, pairs, partial, log_total):
    rows, width = query.shape
    if last:
        out_shape = jax.ShapeDtypeStruct((rows, width), jnp.bfloat16)
    else:
        out_shape = [jax.ShapeDtypeStruct((rows, width), jnp.float32)] * 2
    return pl.pallas_call(
        functools.partial(earlier_kernel, last),
        out_shape=out_shape,
        compiler_params=pltpu.CompilerParams(vmem_limit_bytes=32 * MIB),
        cost_estimate=pl.CostEstimate(
            flops=4 * rows * pairs.shape[1] * width,
            bytes_accessed=10 * rows * width,
            transcendentals=rows * pairs.shape[1] * HEADS,
        ),
        name="earlier_frame",
    )(query, pairs, partial, log_total)


def swap(tile, apart):
    devices = lax.axis_size("tm")
    route = [(i, i - i % SB + (i % SB ^ apart)) for i in range(devices)]
    return lax.ppermute(tile, "tm", route)


def body(space_time, w_lin, gain_lin, w_query, w_kv, frame_attention_gain):
    tokens = space_time[0]
    time_ranges = lax.axis_size("tm") // SB
    state = incoming_state(tokens, w_lin, time_ranges) if time_ranges > 1 else None
    lead = mixer(0, tokens, w_lin, gain_lin, state)
    tiles = mixer(HEADS // 2, tokens, w_lin, gain_lin, state, lead)
    tiles = [swap(tile, apart) if apart else tile for apart, tile in zip(APART, tiles)]
    normed, first, second = make_pairs(tiles, frame_attention_gain, w_kv)
    earlier_first = shifted(first, "tm", 1)
    earlier_second = shifted(second, "tm", 1)
    query, partial, log_total = own_frame(normed, w_query, first, second)
    partial, log_total = earlier_frame(False, query, earlier_first, partial, log_total)
    attended = earlier_frame(True, query, earlier_second, partial, log_total)
    return attended[None]


def solution(mesh):
    placed = (P(("groups", "tm"), None, None), P(), P(), P(), P(), P())
    return jax.shard_map(
        body, mesh=mesh, in_specs=placed, out_specs=P(("groups", "tm"), None, None), check_vma=False
    )
```

time: 67.1 us -> 60.5 us (0.902)
  starting transfers between devices: 34.7 us -> 30 us
  local copies, waits for them, and re-layouts: 2.14 us -> 0.85 us
  Pallas kernels: 24.4 us -> 23.3 us
  waiting for transfers between devices: 4.8 us -> 5.82 us
    ppermute x20 -> x15, starting transfers between devices: 31.5 us -> 25.7 us  [swap(): return lax.ppermute(tile, 'tm', route)]
    ppermute x20 -> x15, waiting for transfers between devices: 3.49 us -> 5.82 us  [swap(): return lax.ppermute(tile, 'tm', route)]
    ppermute x1 -> x2, waiting for transfers between devices: 1.32 us -> 0.01 us  [shifted(): return lax.ppermute(block, axis, route)]
    reshape x1 -> x0, local copies, waits for them, and re-layouts: 1.27 us -> none  [body(): gain_lin = gain_lin.reshape(1, -1)]
    pallas_call x5 -> x6, Pallas kernels: 24.4 us -> 23.3 us  [the longest x2 13.2 us: mixer(): pl.pallas_call(kernel, grid=(steps // 2,), in_specs=in_specs, out_specs=o...]
    ppermute x1 -> x2, starting transfers between devices: 3.22 us -> 4.26 us  [shifted(): return lax.ppermute(block, axis, route)]
  transfers between devices with their start and end apart: 21 -> 17, of which waited for: 4 -> 6; matrix products, arithmetic and copies ran while one was open for 0% -> 0% of each run, Pallas kernels for 7% -> 10%
where the time goes in v5:
time: 60.5 us; the launch traced here: 60 us
  starting transfers between devices  30 us (50%)
  Pallas kernels  23.3 us (39%)
  waiting for transfers between devices  5.82 us (10%)
  local copies, waits for them, and re-layouts  0.85 us (1%)
    ppermute x15, starting transfers between devices, swap(): return lax.ppermute(tile, 'tm', route)  25.7 us
    pallas_call x2, Pallas kernels, mixer(): pl.pallas_call(kernel, grid=(steps // 2,), in_specs=in_specs, out_specs=o...  13.2 us
    ppermute x15, waiting for transfers between devices, swap(): return lax.ppermute(tile, 'tm', route)  5.82 us
    pallas_call x2, Pallas kernels, earlier_frame(): pl.pallas_call(functools.partial(earlier_kernel, last), out_shape=out_sha...  4.98 us
    ppermute x2, starting transfers between devices, shifted(): return lax.ppermute(block, axis, route)  4.26 us
    pallas_call x1, Pallas kernels, own_frame(): pl.pallas_call(own_kernel, out_shape=[jax.ShapeDtypeStruct((rows, width),...  3.76 us
    pallas_call x1, Pallas kernels, make_pairs(): pl.pallas_call(pairs_kernel, in_specs=[vmem, vmem, pl.BlockSpec(memory_sp...  1.36 us
  transfers between devices with their start and end apart: 17, of which 6 were waited for; matrix products, arithmetic and copies ran while one was open for 0% of the time, Pallas kernels for 10%

profile of v5, /device:TPU:1, one launch (start us, length us, event | category | flops | bytes accessed | tf_op | source)
XLA Modules:
  0.0 60.0 jit_solution(935447988402037819)
XLA Ops:
  0.0 6.2 %mixer.2.lead_ref = bf16[512,512]{1,0:T(8,128)(2,1)} custom-call(bf16[512,1024]{1,0:T(8,128)(2,1)} %bitcast.2, bf16[512,1024]{1,0:T(8,128)(2,1)} %bitcast.3, bf16[1024,3072]{1,0:T(8,128)(2,1)} %refs_4_.3, bf16[1024,3072]{1,0:T(8,128)(2,1)} %refs_4_.3, bf16[1024,3072]{1,0:T(8,128)(2,1)} %refs_4_.3, bf16[1024]{0:T(1024)(128)(2,1)} %refs_5_.3), custom_call_target="tpu_custom_call" | custom-call | flops 1879048192 | bytes 5242880 | tf_op jit(solution)/shard_map/mixer/pallas_call | solution.py:160
  6.2 0.0 copy-start.3
  6.2 7.0 %mixer.3 = (bf16[32,1024]{1,0:T(8,128)(2,1)}, bf16[32,1024]{1,0:T(8,128)(2,1)}, bf16[32,1024]{1,0:T(8,128)(2,1)}, bf16[32,1024]{1,0:T(8,128)(2,1)}, bf16[32,1024...) custom-call(bf16[512,512]{1,0:T(8,128)(2,1)} %mixer.2.lead_ref, ...), custom_call_target="tpu_custom_call" | custom-call | flops 1879048192 | bytes 5242880 | tf_op jit(solution)/shard_map/mixer/pallas_call | solution.py:160
  13.2 5.7 %collective-permute-start = (bf16[32,1024]{1,0:T(8,128)(2,1)}, bf16[32,1024]{1,0:T(8,128)(2,1)S(1)}, u32[]{:S(2)}, u32[]{:S(2)}) collective-permute-start(bf16[32,1024]{1,0:T(8,128)(2,1)} %get-tuple-element.30), channel_id=1, source_target_pairs={{0,15},{1,14},{2,13},{3,12},{4,11},{5,10},{6,9},{7,8},{8,7},{9,6},... | collective-permute-start | bytes 196616 | tf_op jit(solution)/shard_map/ppermute | solution.py:361
  18.9 0.0 collective-permute-start.1
  18.9 3.2 %collective-permute-start.2 = (bf16[32,1024]{1,0:T(8,128)(2,1)}, bf16[32,1024]{1,0:T(8,128)(2,1)S(1)}, u32[]{:S(2)}, u32[]{:S(2)}) collective-permute-start(bf16[32,1024]{1,0:T(8,128)(2,1)} %get-tuple-element.32), channel_id=1, source_target_pairs={{0,13},{1,12},{2,15},{3,14},{4,9},{5,8},{6,11},{7,10},{8,5},{9,4},... | collective-permute-start | bytes 196616 | tf_op jit(solution)/shard_map/ppermute | solution.py:361
  22.2 0.4 collective-permute-start.4
  22.6 2.6 %collective-permute-start.5 = (bf16[32,1024]{1,0:T(8,128)(2,1)}, bf16[32,1024]{1,0:T(8,128)(2,1)S(1)}, u32[]{:S(2)}, u32[]{:S(2)}) collective-permute-start(bf16[32,1024]{1,0:T(8,128)(2,1)} %get-tuple-element.35), channel_id=1, source_target_pairs={{0,5},{1,4},{2,7},{3,6},{4,1},{5,0},{6,3},{7,2},{8,13},{9,12},{10,... | collective-permute-start | bytes 196616 | tf_op jit(solution)/shard_map/ppermute | solution.py:361
  25.1 0.6 collective-permute-done.1.refs_1_
  25.7 3.7 %collective-permute-start.6 = (bf16[32,1024]{1,0:T(8,128)(2,1)}, bf16[32,1024]{1,0:T(8,128)(2,1)S(1)}, u32[]{:S(2)}, u32[]{:S(2)}) collective-permute-start(bf16[32,1024]{1,0:T(8,128)(2,1)} %get-tuple-element.36), channel_id=1, source_target_pairs={{0,11},{1,10},{2,9},{3,8},{4,15},{5,14},{6,13},{7,12},{8,3},{9,2},... | collective-permute-start | bytes 196616 | tf_op jit(solution)/shard_map/ppermute | solution.py:361
  29.4 0.0 collective-permute-done.2.refs_2_
  29.4 0.2 collective-permute-start.7
  29.7 0.3 collective-permute-start.8
  30.0 2.4 %collective-permute-start.9 = (bf16[32,1024]{1,0:T(8,128)(2,1)}, bf16[32,1024]{1,0:T(8,128)(2,1)S(1)}, u32[]{:S(2)}, u32[]{:S(2)}) collective-permute-start(bf16[32,1024]{1,0:T(8,128)(2,1)} %get-tuple-element.39), channel_id=1, source_target_pairs={{0,3},{1,2},{2,1},{3,0},{4,7},{5,6},{6,5},{7,4},{8,11},{9,10},{10,... | collective-permute-start | bytes 196616 | tf_op jit(solution)/shard_map/ppermute | solution.py:361
  32.4 0.0 collective-permute-done.5.refs_5_
  32.4 1.2 %collective-permute-start.10 = (bf16[32,1024]{1,0:T(8,128)(2,1)}, bf16[32,1024]{1,0:T(8,128)(2,1)S(1)}, u32[]{:S(2)}, u32[]{:S(2)}) collective-permute-start(bf16[32,1024]{1,0:T(8,128)(2,1)} %get-tuple-element.40), channel_id=1, source_target_pairs={{0,9},{1,8},{2,11},{3,10},{4,13},{5,12},{6,15},{7,14},{8,1},{9,0},... | collective-permute-start | bytes 196616 | tf_op jit(solution)/shard_map/ppermute | solution.py:361
  33.6 0.3 collective-permute-done.6.refs_6_
  33.8 0.9 %collective-permute-start.11 = (bf16[32,1024]{1,0:T(8,128)(2,1)}, bf16[32,1024]{1,0:T(8,128)(2,1)S(1)}, u32[]{:S(2)}, u32[]{:S(2)}) collective-permute-start(bf16[32,1024]{1,0:T(8,128)(2,1)} %get-tuple-element.41), channel_id=1, source_target_pairs={{0,2},{1,3},{2,0},{3,1},{4,6},{5,7},{6,4},{7,5},{8,10},{9,11},{10,... | collective-permute-start | bytes 196616 | tf_op jit(solution)/shard_map/ppermute | solution.py:361
  34.7 0.2 collective-permute-done.7.refs_7_
  34.9 0.9 %collective-permute-start.12 = (bf16[32,1024]{1,0:T(8,128)(2,1)}, bf16[32,1024]{1,0:T(8,128)(2,1)S(1)}, u32[]{:S(2)}, u32[]{:S(2)}) collective-permute-start(bf16[32,1024]{1,0:T(8,128)(2,1)} %get-tuple-element.42), channel_id=1, source_target_pairs={{0,8},{1,9},{2,10},{3,11},{4,12},{5,13},{6,14},{7,15},{8,0},{9,1},... | collective-permute-start | bytes 196616 | tf_op jit(solution)/shard_map/ppermute | solution.py:361
  35.8 0.0 collective-permute-done.8.refs_8_
  35.8 4.1 %collective-permute-start.13 = (bf16[32,1024]{1,0:T(8,128)(2,1)}, bf16[32,1024]{1,0:T(8,128)(2,1)S(1)}, u32[]{:S(2)}, u32[]{:S(2)}) collective-permute-start(bf16[32,1024]{1,0:T(8,128)(2,1)} %get-tuple-element.43), channel_id=1, source_target_pairs={{0,1},{1,0},{2,3},{3,2},{4,5},{5,4},{6,7},{7,6},{8,9},{9,8},{10,11... | collective-permute-start | bytes 196616 | tf_op jit(solution)/shard_map/ppermute | solution.py:361
  39.9 1.2 %collective-permute-done.10.refs_10_ = bf16[32,1024]{1,0:T(8,128)(2,1)S(1)} collective-permute-done((bf16[32,1024]{1,0:T(8,128)(2,1)}, bf16[32,1024]{1,0:T(8,128)(2,1)S(1)}, u32[]{:S(2)}, u32[]{:S(2)}) %collective-permute-start.10) | collective-permute-done | bytes 65568 | tf_op jit(solution)/shard_map/ppermute | solution.py:361
  41.1 0.7 %collective-permute-done.12.refs_12_ = bf16[32,1024]{1,0:T(8,128)(2,1)S(1)} collective-permute-done((bf16[32,1024]{1,0:T(8,128)(2,1)}, bf16[32,1024]{1,0:T(8,128)(2,1)S(1)}, u32[]{:S(2)}, u32[]{:S(2)}) %collective-permute-start.12) | collective-permute-done | bytes 65568 | tf_op jit(solution)/shard_map/ppermute | solution.py:361
  41.8 2.9 %collective-permute-done.14.refs_14_ = bf16[32,1024]{1,0:T(8,128)(2,1)S(1)} collective-permute-done((bf16[32,1024]{1,0:T(8,128)(2,1)}, bf16[32,1024]{1,0:T(8,128)(2,1)S(1)}, u32[]{:S(2)}, u32[]{:S(2)}) %collective-permute-start.14) | collective-permute-done | bytes 65568 | tf_op jit(solution)/shard_map/ppermute | solution.py:361
  44.7 0.8 %copy-done.1 = bf16[32,1024]{1,0:T(8,128)(2,1)S(1)} copy-done((bf16[32,1024]{1,0:T(8,128)(2,1)S(1)}, bf16[32,1024]{1,0:T(8,128)(2,1)}, u32[]{:S(2)}) %copy-start.1) | copy-done | bytes 65560
  45.6 1.4 %pairs.1 = (bf16[512,1024]{1,0:T(8,128)(2,1)S(1)}, bf16[512,256]{1,0:T(8,128)(2,1)S(1)}, bf16[512,256]{1,0:T(8,128)(2,1)S(1)}) custom-call(bf16[1024]{0:T(1024)(128)(2,1)S(1)} %copy-done.2, bf16[1024,512]{1,0:T(8,128)(2,1)S(1)} %copy-done, bf16[32,1024]{1,0:T(8,128)(2,1)S(1)} %copy-done.1, bf16[32,1024]{1,0:T(8,128)(2,1)S(1)} %collective-permute-done.refs_0_, ...), custom_call_target="tpu_custom_call" | custom-call | flops 536870912 | bytes 3670016 | tf_op jit(solution)/shard_map/pairs/pallas_call | solution.py:224
  47.0 1.9 %collective-permute-start.16 = (bf16[512,256]{1,0:T(8,128)(2,1)S(1)}, bf16[512,256]{1,0:T(8,128)(2,1)S(1)}, u32[]{:S(2)}, u32[]{:S(2)}) collective-permute-start(bf16[512,256]{1,0:T(8,128)(2,1)S(1)} %get-tuple-element.46.first_ref), channel_id=1, source_target_pairs={{0,1},{1,2},{2,3},{3,4},{4,5},{5,6},{6,7},{7,8},{8,9},{9,10},{10,1... | collective-permute-start | bytes 786440 | tf_op jit(solution)/shard_map/ppermute | solution.py:27
  48.9 2.3 %collective-permute-start.15 = (bf16[512,256]{1,0:T(8,128)(2,1)S(1)}, bf16[512,256]{1,0:T(8,128)(2,1)S(1)}, u32[]{:S(2)}, u32[]{:S(2)}) collective-permute-start(bf16[512,256]{1,0:T(8,128)(2,1)S(1)} %get-tuple-element.47.second_ref), channel_id=1, source_target_pairs={{0,1},{1,2},{2,3},{3,4},{4,5},{5,6},{6,7},{7,8},{8,9},{9,10},{10,1... | collective-permute-start | bytes 786440 | tf_op jit(solution)/shard_map/ppermute | solution.py:27
  51.2 3.8 %own_frame.1 = (bf16[512,1024]{1,0:T(8,128)(2,1)S(1)}, f32[512,1024]{1,0:T(8,128)S(1)}, f32[512,1024]{1,0:T(8,128)S(1)}) custom-call(bf16[512,1024]{1,0:T(8,128)(2,1)S(1)} %get-tuple-element.45.normed_ref, bf16[1024,1024]{1,0:T(8,128)(2,1)S(1)} %copy-done.3, bf16[512,256]{1,0:T(8,128)(2,1)S(1)} %get-tuple-element.46.first_ref, ...), custom_call_target="tpu_custom_call" | custom-call | flops 2147483648 | bytes 6291456 | tf_op jit(solution)/shard_map/own_frame/pallas_call | solution.py:287
  55.0 2.0 %earlier_frame.2 = (f32[512,1024]{1,0:T(8,128)S(1)}, f32[512,1024]{1,0:T(8,128)S(1)}) custom-call(bf16[512,1024]{1,0:T(8,128)(2,1)S(1)} %get-tuple-element.48.query_ref, bf16[512,256]{1,0:T(8,128)(2,1)S(1)} %collective-permute-done.16.pairs_ref, f32[512,1024]{1,0:T(8,128)S(1)} %get-tuple-element.49.partial_ref, f32[512,1024]{1,0:T(8,128)S(1)} %get-tuple-element.50.log_ref), custom_call_target="tpu_custom_call" | custom-call | flops 536870912 | bytes 5242880 | tf_op jit(solution)/shard_map/earlier_frame/pallas_call | solution.py:345
  57.1 3.0 %earlier_frame.3 = bf16[512,1024]{1,0:T(8,128)(2,1)} custom-call(bf16[512,1024]{1,0:T(8,128)(2,1)S(1)} %get-tuple-element.48.query_ref, bf16[512,256]{1,0:T(8,128)(2,1)S(1)} %collective-permute-done.15.pairs_ref, f32[512,1024]{1,0:T(8,128)S(1)} %get-tuple-element.51.partial_ref, f32[512,1024]{1,0:T(8,128)S(1)} %get-tuple-element.52.log_ref), custom_call_target="tpu_custom_call" | custom-call | flops 536870912 | bytes 5242880 | tf_op jit(solution)/shard_map/earlier_frame/pallas_call | solution.py:345
  (16 shorter events, 0.0 us)
Async XLA Ops:
  6.2 38.5 %copy-start = (bf16[1024,512]{1,0:T(8,128)(2,1)S(1)}, bf16[1024,512]{1,0:T(8,128)(2,1)}, u32[]{:S(2)}) copy-start(bf16[1024,512]{1,0:T(8,128)(2,1)} %w_ref.2) | copy-start | bytes 3145732
  6.2 38.5 %copy-start.2 = (bf16[1024]{0:T(1024)(128)(2,1)S(1)}, bf16[1024]{0:T(1024)(128)(2,1)}, u32[]{:S(2)}) copy-start(bf16[1024]{0:T(1024)(128)(2,1)} %gain_ref.1) | copy-start | bytes 6148
  6.2 45.0 %copy-start.3 = (bf16[1024,1024]{1,0:T(8,128)(2,1)S(1)}, bf16[1024,1024]{1,0:T(8,128)(2,1)}, u32[]{:S(2)}) copy-start(bf16[1024,1024]{1,0:T(8,128)(2,1)} %w_ref.3) | copy-start | bytes 6291460
  13.2 9.4 %collective-permute-start = (bf16[32,1024]{1,0:T(8,128)(2,1)}, bf16[32,1024]{1,0:T(8,128)(2,1)S(1)}, u32[]{:S(2)}, u32[]{:S(2)}) collective-permute-start(bf16[32,1024]{1,0:T(8,128)(2,1)} %get-tuple-element.30), channel_id=1, source_target_pairs={{0,15},{1,14},{2,13},{3,12},{4,11},{5,10},{6,9},{7,8},{8,7},{9,6},... | collective-permute-start | bytes 196616 | tf_op jit(solution)/shard_map/ppermute | solution.py:361
  18.9 6.8 %collective-permute-start.1 = (bf16[32,1024]{1,0:T(8,128)(2,1)}, bf16[32,1024]{1,0:T(8,128)(2,1)S(1)}, u32[]{:S(2)}, u32[]{:S(2)}) collective-permute-start(bf16[32,1024]{1,0:T(8,128)(2,1)} %get-tuple-element.31), channel_id=1, source_target_pairs={{0,14},{1,15},{2,12},{3,13},{4,10},{5,11},{6,8},{7,9},{8,6},{9,7},... | collective-permute-start | bytes 196616 | tf_op jit(solution)/shard_map/ppermute | solution.py:361
  18.9 10.5 %collective-permute-start.2 = (bf16[32,1024]{1,0:T(8,128)(2,1)}, bf16[32,1024]{1,0:T(8,128)(2,1)S(1)}, u32[]{:S(2)}, u32[]{:S(2)}) collective-permute-start(bf16[32,1024]{1,0:T(8,128)(2,1)} %get-tuple-element.32), channel_id=1, source_target_pairs={{0,13},{1,12},{2,15},{3,14},{4,9},{5,8},{6,11},{7,10},{8,5},{9,4},... | collective-permute-start | bytes 196616 | tf_op jit(solution)/shard_map/ppermute | solution.py:361
  22.2 7.5 %collective-permute-start.3 = (bf16[32,1024]{1,0:T(8,128)(2,1)}, bf16[32,1024]{1,0:T(8,128)(2,1)S(1)}, u32[]{:S(2)}, u32[]{:S(2)}) collective-permute-start(bf16[32,1024]{1,0:T(8,128)(2,1)} %get-tuple-element.33), channel_id=1, source_target_pairs={{0,6},{1,7},{2,4},{3,5},{4,2},{5,3},{6,0},{7,1},{8,14},{9,15},{10,... | collective-permute-start | bytes 196616 | tf_op jit(solution)/shard_map/ppermute | solution.py:361
  22.2 7.8 %collective-permute-start.4 = (bf16[32,1024]{1,0:T(8,128)(2,1)}, bf16[32,1024]{1,0:T(8,128)(2,1)S(1)}, u32[]{:S(2)}, u32[]{:S(2)}) collective-permute-start(bf16[32,1024]{1,0:T(8,128)(2,1)} %get-tuple-element.34), channel_id=1, source_target_pairs={{0,12},{1,13},{2,14},{3,15},{4,8},{5,9},{6,10},{7,11},{8,4},{9,5},... | collective-permute-start | bytes 196616 | tf_op jit(solution)/shard_map/ppermute | solution.py:361
  22.6 9.8 %collective-permute-start.5 = (bf16[32,1024]{1,0:T(8,128)(2,1)}, bf16[32,1024]{1,0:T(8,128)(2,1)S(1)}, u32[]{:S(2)}, u32[]{:S(2)}) collective-permute-start(bf16[32,1024]{1,0:T(8,128)(2,1)} %get-tuple-element.35), channel_id=1, source_target_pairs={{0,5},{1,4},{2,7},{3,6},{4,1},{5,0},{6,3},{7,2},{8,13},{9,12},{10,... | collective-permute-start | bytes 196616 | tf_op jit(solution)/shard_map/ppermute | solution.py:361
  25.7 8.1 %collective-permute-start.6 = (bf16[32,1024]{1,0:T(8,128)(2,1)}, bf16[32,1024]{1,0:T(8,128)(2,1)S(1)}, u32[]{:S(2)}, u32[]{:S(2)}) collective-permute-start(bf16[32,1024]{1,0:T(8,128)(2,1)} %get-tuple-element.36), channel_id=1, source_target_pairs={{0,11},{1,10},{2,9},{3,8},{4,15},{5,14},{6,13},{7,12},{8,3},{9,2},... | collective-permute-start | bytes 196616 | tf_op jit(solution)/shard_map/ppermute | solution.py:361
  29.4 5.4 %collective-permute-start.7 = (bf16[32,1024]{1,0:T(8,128)(2,1)}, bf16[32,1024]{1,0:T(8,128)(2,1)S(1)}, u32[]{:S(2)}, u32[]{:S(2)}) collective-permute-start(bf16[32,1024]{1,0:T(8,128)(2,1)} %get-tuple-element.37), channel_id=1, source_target_pairs={{0,4},{1,5},{2,6},{3,7},{4,0},{5,1},{6,2},{7,3},{8,12},{9,13},{10,... | collective-permute-start | bytes 196616 | tf_op jit(solution)/shard_map/ppermute | solution.py:361
  29.7 6.1 %collective-permute-start.8 = (bf16[32,1024]{1,0:T(8,128)(2,1)}, bf16[32,1024]{1,0:T(8,128)(2,1)S(1)}, u32[]{:S(2)}, u32[]{:S(2)}) collective-permute-start(bf16[32,1024]{1,0:T(8,128)(2,1)} %get-tuple-element.38), channel_id=1, source_target_pairs={{0,10},{1,11},{2,8},{3,9},{4,14},{5,15},{6,12},{7,13},{8,2},{9,3},... | collective-permute-start | bytes 196616 | tf_op jit(solution)/shard_map/ppermute | solution.py:361
  30.0 9.9 %collective-permute-start.9 = (bf16[32,1024]{1,0:T(8,128)(2,1)}, bf16[32,1024]{1,0:T(8,128)(2,1)S(1)}, u32[]{:S(2)}, u32[]{:S(2)}) collective-permute-start(bf16[32,1024]{1,0:T(8,128)(2,1)} %get-tuple-element.39), channel_id=1, source_target_pairs={{0,3},{1,2},{2,1},{3,0},{4,7},{5,6},{6,5},{7,4},{8,11},{9,10},{10,... | collective-permute-start | bytes 196616 | tf_op jit(solution)/shard_map/ppermute | solution.py:361
  32.4 8.7 %collective-permute-start.10 = (bf16[32,1024]{1,0:T(8,128)(2,1)}, bf16[32,1024]{1,0:T(8,128)(2,1)S(1)}, u32[]{:S(2)}, u32[]{:S(2)}) collective-permute-start(bf16[32,1024]{1,0:T(8,128)(2,1)} %get-tuple-element.40), channel_id=1, source_target_pairs={{0,9},{1,8},{2,11},{3,10},{4,13},{5,12},{6,15},{7,14},{8,1},{9,0},... | collective-permute-start | bytes 196616 | tf_op jit(solution)/shard_map/ppermute | solution.py:361
  33.8 7.3 %collective-permute-start.11 = (bf16[32,1024]{1,0:T(8,128)(2,1)}, bf16[32,1024]{1,0:T(8,128)(2,1)S(1)}, u32[]{:S(2)}, u32[]{:S(2)}) collective-permute-start(bf16[32,1024]{1,0:T(8,128)(2,1)} %get-tuple-element.41), channel_id=1, source_target_pairs={{0,2},{1,3},{2,0},{3,1},{4,6},{5,7},{6,4},{7,5},{8,10},{9,11},{10,... | collective-permute-start | bytes 196616 | tf_op jit(solution)/shard_map/ppermute | solution.py:361
  34.9 6.9 %collective-permute-start.12 = (bf16[32,1024]{1,0:T(8,128)(2,1)}, bf16[32,1024]{1,0:T(8,128)(2,1)S(1)}, u32[]{:S(2)}, u32[]{:S(2)}) collective-permute-start(bf16[32,1024]{1,0:T(8,128)(2,1)} %get-tuple-element.42), channel_id=1, source_target_pairs={{0,8},{1,9},{2,10},{3,11},{4,12},{5,13},{6,14},{7,15},{8,0},{9,1},... | collective-permute-start | bytes 196616 | tf_op jit(solution)/shard_map/ppermute | solution.py:361
  35.8 6.0 %collective-permute-start.13 = (bf16[32,1024]{1,0:T(8,128)(2,1)}, bf16[32,1024]{1,0:T(8,128)(2,1)S(1)}, u32[]{:S(2)}, u32[]{:S(2)}) collective-permute-start(bf16[32,1024]{1,0:T(8,128)(2,1)} %get-tuple-element.43), channel_id=1, source_target_pairs={{0,1},{1,0},{2,3},{3,2},{4,5},{5,4},{6,7},{7,6},{8,9},{9,8},{10,11... | collective-permute-start | bytes 196616 | tf_op jit(solution)/shard_map/ppermute | solution.py:361
  39.9 4.8 %collective-permute-start.14 = (bf16[32,1024]{1,0:T(8,128)(2,1)}, bf16[32,1024]{1,0:T(8,128)(2,1)S(1)}, u32[]{:S(2)}, u32[]{:S(2)}) collective-permute-start(bf16[32,1024]{1,0:T(8,128)(2,1)} %get-tuple-element.44), channel_id=1, source_target_pairs={{0,7},{1,6},{2,5},{3,4},{4,3},{5,2},{6,1},{7,0},{8,15},{9,14},{10,... | collective-permute-start | bytes 196616 | tf_op jit(solution)/shard_map/ppermute | solution.py:361
  44.7 0.8 %copy-start.1 = (bf16[32,1024]{1,0:T(8,128)(2,1)S(1)}, bf16[32,1024]{1,0:T(8,128)(2,1)}, u32[]{:S(2)}) copy-start(bf16[32,1024]{1,0:T(8,128)(2,1)} %get-tuple-element.29.kept_ref) | copy-start | bytes 196612
  47.0 8.1 %collective-permute-start.16 = (bf16[512,256]{1,0:T(8,128)(2,1)S(1)}, bf16[512,256]{1,0:T(8,128)(2,1)S(1)}, u32[]{:S(2)}, u32[]{:S(2)}) collective-permute-start(bf16[512,256]{1,0:T(8,128)(2,1)S(1)} %get-tuple-element.46.first_ref), channel_id=1, source_target_pairs={{0,1},{1,2},{2,3},{3,4},{4,5},{5,6},{6,7},{7,8},{8,9},{9,10},{10,1... | collective-permute-start | bytes 786440 | tf_op jit(solution)/shard_map/ppermute | solution.py:27
  48.9 8.1 %collective-permute-start.15 = (bf16[512,256]{1,0:T(8,128)(2,1)S(1)}, bf16[512,256]{1,0:T(8,128)(2,1)S(1)}, u32[]{:S(2)}, u32[]{:S(2)}) collective-permute-start(bf16[512,256]{1,0:T(8,128)(2,1)S(1)} %get-tuple-element.47.second_ref), channel_id=1, source_target_pairs={{0,1},{1,2},{2,3},{3,4},{4,5},{5,6},{6,7},{7,8},{8,9},{9,10},{10,1... | collective-permute-start | bytes 786440 | tf_op jit(solution)/shard_map/ppermute | solution.py:27

commit v6 on v5

--- a/solution.py
+++ b/solution.py
@@ -15,7 +15,8 @@
 SPAN = 128
 PAIR = 2
 
-APART = (0, 15, 14, 13, 6, 12, 5, 11, 4, 10, 3, 9, 2, 8, 1, 7)
+APART = (0, 12, 8, 13, 9, 14, 15, 7, 10, 6, 11, 5, 4, 3, 2, 1)
+AHEAD = (12, 8, 13, 9, 14)
 
 epsilon = 1e-06
 MIB = 1 << 20
@@ -48,85 +49,95 @@
     return lax.broadcasted_iota(jnp.int32, shape, 0) >= lax.broadcasted_iota(jnp.int32, shape, 1)
 
 
-def mix_heads(query, key, value, states, turned):
+def mix_heads(query, key, value, states):
     rows = query.shape[0]
     causal = causal_mask()
     spans = [slice(start, start + SPAN) for start in range(0, rows, SPAN)]
     heads = range(query.shape[1] // HD)
-    local, before, mixed = {}, {}, {}
-    turns = {}
-    for head in heads:
-        lanes = head_lanes(head)
-        if turned:
-            turns[head] = key[:, lanes].T
-        for span, here in enumerate(spans):
-            if turned:
-                scores = dot(query[here, lanes], turns[head][:, here])
-            else:
-                scores = dot_nt(query[here, lanes], key[here, lanes])
-            local[head, span] = jnp.where(causal, scores, 0.0).astype(jnp.bfloat16)
+    units = [(head, span) for head in heads for span in range(len(spans))]
+    local, before, after, mixed = {}, {}, [], []
+    for head, span in units:
+        lanes, here = head_lanes(head), spans[span]
+        scores = dot_nt(query[here, lanes], key[here, lanes])
+        local[head, span] = jnp.where(causal, scores, 0.0).astype(jnp.bfloat16)
     for head in heads:
         lanes = head_lanes(head)
         state = states[head]
         for span, here in enumerate(spans):
             before[head, span] = state
-            if span + 1 < len(spans):
-                if turned:
-                    update = dot(turns[head][:, here], value[here, lanes])
-                else:
-                    update = dot_tn(key[here, lanes], value[here, lanes])
-                state = update if state is None else state + update
-    for head in heads:
-        lanes = head_lanes(head)
-        for span, here in enumerate(spans):
-            if before[head, span] is None:
-                mixed[head, span] = dot(local[head, span], value[here, lanes])
-            else:
-                mixed[head, span] = dot(
-                    jnp.concatenate([query[here, lanes], local[head, span]], axis=1),
-                    jnp.concatenate(
-                        [before[head, span].astype(jnp.bfloat16), value[here, lanes]], axis=0
-                    ),
-                )
-    return [(head, here, mixed[head, span]) for head in heads for span, here in enumerate(spans)]
-
-
-def mixer_kernel(first, has_state, turned, *refs):
+            update = dot_tn(key[here, lanes], value[here, lanes])
+            state = update if state is None else state + update
+        after.append(state)
+    for head, span in units:
+        lanes, here = head_lanes(head), spans[span]
+        if before[head, span] is None:
+            out = dot(local[head, span], value[here, lanes])
+        else:
+            out = dot(
+                jnp.concatenate([query[here, lanes], local[head, span]], axis=1),
+                jnp.concatenate(
+                    [before[head, span].astype(jnp.bfloat16), value[here, lanes]], axis=0
+                ),
+            )
+        mixed.append((head, here, out))
+    return mixed, after
+
+
+def mixer_kernel(first, has_state, *refs):
     if has_state:
         state_ref, *refs = refs
     tokens_ref, residual_ref, wq_ref, wk_ref, wv_ref, gain_ref, out_ref = refs
-    tokens = tokens_ref[...]
-    query = dot(tokens, wq_ref[...]).astype(jnp.bfloat16)
-    key = dot(tokens, wk_ref[...]).astype(jnp.bfloat16)
-    value = dot(tokens, wv_ref[...]).astype(jnp.bfloat16)
+    rows = tokens_ref.shape[0]
+    columns = PAIR * HD
     states = [state_ref[head] if has_state else None for head in range(PAIR)]
-    start = pl.multiple_of(first * HD + pl.program_id(0) * PAIR * HD, PAIR * HD)
-    gains = gain_ref[pl.ds(start, PAIR * HD)].astype(jnp.float32).reshape(1, PAIR * HD)
-    for head, here, out in mix_heads(query, key, value, states, turned):
-        lanes = head_lanes(head)
-        mean_square = jnp.mean(out * out, axis=-1, keepdims=True)
-        normed = out * lax.rsqrt(mean_square + epsilon) * gains[:, lanes]
-        residual = residual_ref[here, lanes].astype(jnp.float32)
-        out_ref[here, lanes] = (residual + normed).astype(jnp.bfloat16)
-
-
-def last_kernel(first, has_state, turned, lead_ref, *refs):
-    *refs, scratch = refs
-    tiles = refs[-len(APART) :]
-    step = pl.program_id(0)
-    mixer_kernel(first, has_state, turned, *refs[: -len(APART)], scratch.at[step])
-    size = scratch.shape[1] // SB
+    step = pl.program_id(0) * columns
+    start = pl.multiple_of(first * HD + step, columns)
+    gains = gain_ref[pl.ds(start, columns)].astype(jnp.float32).reshape(1, columns)
+
+    def store(offset, mixed):
+        for head, here, out in mixed:
+            lanes = head_lanes(head)
+            here = slice(offset + here.start, offset + here.stop)
+            mean_square = jnp.mean(out * out, axis=-1, keepdims=True)
+            normed = out * lax.rsqrt(mean_square + epsilon) * gains[:, lanes]
+            residual = residual_ref[here, lanes].astype(jnp.float32)
+            out_ref[here, pl.ds(pl.multiple_of(step + head * HD, HD), HD)] = (
+                residual + normed
+            ).astype(jnp.bfloat16)
+
+    if first == 0:
+        weights = jnp.concatenate([wq_ref[...], wk_ref[...], wv_ref[...]], axis=1)
+        packed = dot(tokens_ref[...], weights).astype(jnp.bfloat16)
+        parts = [packed[:, part * columns : (part + 1) * columns] for part in range(3)]
+        store(0, mix_heads(*parts, states)[0])
+    else:
+        block = rows // 2
+
+        def project(offset):
+            tokens = tokens_ref[offset : offset + block]
+            return [dot(tokens, w[...]).astype(jnp.bfloat16) for w in (wq_ref, wk_ref, wv_ref)]
+
+        parts = project(0)
+        upcoming = project(block)
+        mixed, states = mix_heads(*parts, states)
+        store(0, mixed)
+        mixed, states = mix_heads(*upcoming, states)
+        store(block, mixed)
+
+
+def ahead_kernel(first, has_state, *refs):
+    *refs, out_ref = refs
+    tiles = refs[-len(AHEAD) :]
+    mixer_kernel(first, has_state, *refs[: -len(AHEAD)], out_ref)
+    size = out_ref.shape[0] // SB
     place = lax.rem(lax.axis_index("tm"), SB)
-
-    @pl.when(step == pl.num_programs(0) - 1)
-    def _():
-        for apart, tile in zip(APART, tiles):
-            rows = pl.ds(pl.multiple_of((place ^ apart) * size, size), size)
-            parts = [lead_ref[rows, :]] + [scratch[j, rows, :] for j in range(scratch.shape[0])]
-            tile[...] = jnp.concatenate(parts, axis=1)
-
-
-def mixer(first, tokens, w_lin, gain_lin, state, lead=None):
+    step = pl.multiple_of(pl.program_id(0) * PAIR * HD, PAIR * HD)
+    for apart, tile in zip(AHEAD, tiles):
+        rows = pl.ds(pl.multiple_of((place ^ apart) * size, size), size)
+        tile[...] = out_ref[rows, pl.ds(step, tile.shape[1])]
+
+
+def mixer(first, tokens, w_lin, gain_lin, state):
     rows, width = tokens.shape
     columns = PAIR * HD
     steps = HEADS // PAIR
@@ -145,26 +156,18 @@
     if state is not None:
         operands.insert(0, state)
         in_specs.insert(0, pl.BlockSpec((PAIR, HD, HD), lambda c: (skip + c, 0, 0)))
-    if lead is None:
-        kernel = functools.partial(mixer_kernel, first, state is not None, True)
-        out_specs = pl.BlockSpec((rows, columns), lambda c: (0, c))
-        out_shape = jax.ShapeDtypeStruct((rows, half), jnp.bfloat16)
-        scratch = []
-    else:
-        kernel = functools.partial(last_kernel, first, state is not None, False)
-        operands.insert(0, lead)
-        in_specs.insert(0, pl.BlockSpec((rows, half), lambda c: (0, 0)))
-        out_specs = [pl.BlockSpec((size, width), lambda c: (0, 0)) for _ in APART]
-        out_shape = [jax.ShapeDtypeStruct((size, width), jnp.bfloat16) for _ in APART]
-        scratch = [pltpu.VMEM((steps // 2, rows, columns), jnp.bfloat16)]
+    tiles = len(AHEAD) if first == 0 else 0
+    out_specs = [pl.BlockSpec((size, columns), lambda c: (0, c))] * tiles
+    out_specs.append(pl.BlockSpec(memory_space=pltpu.VMEM))
+    out_shape = [jax.ShapeDtypeStruct((size, half), jnp.bfloat16)] * tiles
+    out_shape.append(jax.ShapeDtypeStruct((rows, half), jnp.bfloat16))
     return pl.pallas_call(
-        kernel,
+        functools.partial(ahead_kernel if tiles else mixer_kernel, first, state is not None),
         grid=(steps // 2,),
         in_specs=in_specs,
         out_specs=out_specs,
         out_shape=out_shape,
-        scratch_shapes=scratch,
-        compiler_params=pltpu.CompilerParams(vmem_limit_bytes=56 * MIB),
+        compiler_params=pltpu.CompilerParams(vmem_limit_bytes=(56 if tiles else 24) * MIB),
         cost_estimate=pl.CostEstimate(
             flops=2 * rows * width * 3 * half + 8 * rows * SPAN * half,
             bytes_accessed=2 * (3 * width * half + 2 * rows * width),
@@ -174,6 +177,33 @@
     )(*operands)
 
 
+def cut_kernel(left_ref, right_ref, *refs):
+    tiles = refs[len(AHEAD) :]
+    size = left_ref.shape[0] // SB
+    place = lax.rem(lax.axis_index("tm"), SB)
+    for apart, tile in zip(APART, tiles):
+        rows = pl.ds(pl.multiple_of((place ^ apart) * size, size), size)
+        if apart in AHEAD:
+            tile[...] = right_ref[rows, :]
+        else:
+            tile[...] = jnp.concatenate([left_ref[rows, :], right_ref[rows, :]], axis=1)
+
+
+def cut_tiles(left, right, arrived):
+    rows, half = left.shape
+    size = rows // SB
+    vmem = pl.BlockSpec(memory_space=pltpu.VMEM)
+    widths = [half if apart in AHEAD else 2 * half for apart in APART]
+    return pl.pallas_call(
+        cut_kernel,
+        in_specs=[vmem, vmem] + [pl.BlockSpec(memory_space=pl.ANY)] * len(arrived),
+        out_shape=[jax.ShapeDtypeStruct((size, wide), jnp.bfloat16) for wide in widths],
+        compiler_params=pltpu.CompilerParams(vmem_limit_bytes=16 * MIB),
+        cost_estimate=pl.CostEstimate(flops=0, bytes_accessed=8 * rows * half, transcendentals=0),
+        name="cut",
+    )(left, right, *arrived)
+
+
 def incoming_state(tokens, w_lin, time_ranges):
     rows, width = tokens.shape
     packed = dot(tokens, w_lin[:, width:]).astype(jnp.bfloat16).reshape(rows, 2, HEADS, HD)
@@ -189,52 +219,45 @@
     return lax.fori_loop(0, time_ranges - 1, advance_hop, jnp.zeros_like(block_total))
 
 
-def pairs_kernel(gain_ref, w_ref, kept_ref, *refs):
-    *tiles, normed_ref, first_ref, second_ref, kept, arrived = refs
-    copy = pltpu.make_async_copy(kept_ref, kept, arrived)
-    copy.start()
+def pairs_kernel(gain_ref, w_ref, *refs):
+    *parts, normed_ref, first_ref, second_ref = refs
     gain = gain_ref[...].astype(jnp.float32).reshape(1, -1)
     w_kv = w_ref[...]
-
-    def norm(rows):
-        widened = rows.astype(jnp.float32)
+    parts = iter(parts)
+    tiles = []
+    for apart in APART:
+        tile = next(parts)[...]
+        if apart in AHEAD:
+            tile = jnp.concatenate([tile, next(parts)[...]], axis=1)
+        tiles.append(tile)
+    half = len(APART) // 2
+    for index, out_ref in enumerate((first_ref, second_ref)):
+        widened = jnp.concatenate(tiles[index * half : (index + 1) * half], axis=0)
+        widened = widened.astype(jnp.float32)
         mean_square = jnp.mean(widened * widened, axis=-1, keepdims=True)
-        return (widened * lax.rsqrt(mean_square + epsilon) * gain).astype(jnp.bfloat16)
-
-    def give(normed, start, out_ref):
+        normed = (widened * lax.rsqrt(mean_square + epsilon) * gain).astype(jnp.bfloat16)
         rows = normed.shape[0]
+        normed_ref[index * rows : (index + 1) * rows] = normed
         pairs = dot(normed, w_kv).astype(jnp.bfloat16)
-        normed_ref[start : start + rows] = normed
         out_ref[: KVH * HD] = pairs[:, : KVH * HD].T
         out_ref[KVH * HD :] = pairs[:, KVH * HD :]
 
-    half = len(APART) // 2
-    normed = norm(jnp.concatenate([tile[...] for tile in tiles[half - 1 :]], axis=0))
-    give(normed, normed.shape[0], second_ref)
-    copy.wait()
-    normed = norm(jnp.concatenate([kept[...]] + [tile[...] for tile in tiles[: half - 1]], axis=0))
-    give(normed, 0, first_ref)
-
-
-def make_pairs(tiles, gain, w_kv):
-    size, width = tiles[0].shape
-    wide = w_kv.shape[1]
-    rows = size * len(tiles)
-    vmem = pl.BlockSpec(memory_space=pltpu.VMEM)
+
+def make_pairs(parts, gain, w_kv):
+    width, wide = w_kv.shape
+    rows = sum(part.size for part in parts) // width
     return pl.pallas_call(
         pairs_kernel,
-        in_specs=[vmem, vmem, pl.BlockSpec(memory_space=pltpu.HBM)] + [vmem] * (len(tiles) - 1),
         out_shape=[jax.ShapeDtypeStruct((rows, width), jnp.bfloat16)]
         + [jax.ShapeDtypeStruct((wide, rows // 2), jnp.bfloat16)] * 2,
-        scratch_shapes=[pltpu.VMEM((size, width), jnp.bfloat16), pltpu.SemaphoreType.DMA],
-        compiler_params=pltpu.CompilerParams(vmem_limit_bytes=40 * MIB),
+        compiler_params=pltpu.CompilerParams(vmem_limit_bytes=16 * MIB),
         cost_estimate=pl.CostEstimate(
             flops=2 * rows * width * wide,
             bytes_accessed=2 * (2 * rows * width + width * wide + rows * wide),
             transcendentals=rows,
         ),
         name="pairs",
-    )(gain, w_kv, *tiles)
+    )(gain, w_kv, *parts)
 
 
 SCORE_SCALE = math.log2(math.e) / math.sqrt(HD)
@@ -365,10 +388,15 @@
     tokens = space_time[0]
     time_ranges = lax.axis_size("tm") // SB
     state = incoming_state(tokens, w_lin, time_ranges) if time_ranges > 1 else None
-    lead = mixer(0, tokens, w_lin, gain_lin, state)
-    tiles = mixer(HEADS // 2, tokens, w_lin, gain_lin, state, lead)
-    tiles = [swap(tile, apart) if apart else tile for apart, tile in zip(APART, tiles)]
-    normed, first, second = make_pairs(tiles, frame_attention_gain, w_kv)
+    *ahead, left = mixer(0, tokens, w_lin, gain_lin, state)
+    ahead = {apart: swap(tile, apart) for apart, tile in zip(AHEAD, ahead)}
+    (right,) = mixer(HEADS // 2, tokens, w_lin, gain_lin, state)
+    parts = []
+    for apart, tile in zip(APART, cut_tiles(left, right, list(ahead.values()))):
+        if apart in ahead:
+            parts.append(ahead[apart])
+        parts.append(swap(tile, apart) if apart else tile)
+    normed, first, second = make_pairs(parts, frame_attention_gain, w_kv)
     earlier_first = shifted(first, "tm", 1)
     earlier_second = shifted(second, "tm", 1)
     query, partial, log_total = own_frame(normed, w_query, first, second)

time: 60.5 us -> 62.1 us (1.026)
  starting transfers between devices: 30 us -> 39.6 us
  waiting for transfers between devices: 5.82 us -> 1.72 us
  Pallas kernels: 23.3 us -> 20 us
  local copies, waits for them, and re-layouts: 0.85 us -> 0.03 us
    ppermute x15 -> x20, starting transfers between devices: 25.7 us -> 32.6 us  [swap(): return lax.ppermute(tile, 'tm', route)]
    ppermute x15 -> x20, waiting for transfers between devices: 5.82 us -> 1.71 us  [swap(): return lax.ppermute(tile, 'tm', route)]
    pallas_call x3 -> x4, Pallas kernels: 14.5 us -> 11.2 us  [the longest x2 10.3 us: mixer(): pl.pallas_call(functools.partial(ahead_kernel if tiles else mixer_kernel,...]
    ppermute x2, starting transfers between devices: 4.26 us -> 6.99 us  [shifted(): return lax.ppermute(block, axis, route)]
    unnamed x8 -> x16, local copies, waits for them, and re-layouts: 0.85 us -> 0.03 us
  transfers between devices with their start and end apart: 17 -> 22, of which waited for: 6 -> 5; matrix products, arithmetic and copies ran while one was open for 0% -> 0% of each run, Pallas kernels for 10% -> 15%
where the time goes in v6:
time: 62.1 us; the launch traced here: 61.5 us
  starting transfers between devices  39.6 us (64%)
  Pallas kernels  20 us (32%)
  waiting for transfers between devices  1.72 us (3%)
    ppermute x20, starting transfers between devices, swap(): return lax.ppermute(tile, 'tm', route)  32.6 us
    pallas_call x2, Pallas kernels, mixer(): pl.pallas_call(functools.partial(ahead_kernel if tiles else mixer_kernel,...  10.3 us
    ppermute x2, starting transfers between devices, shifted(): return lax.ppermute(block, axis, route)  6.99 us
    pallas_call x2, Pallas kernels, earlier_frame(): pl.pallas_call(functools.partial(earlier_kernel, last), out_shape=out_sha...  4.98 us
    pallas_call x1, Pallas kernels, own_frame(): pl.pallas_call(own_kernel, out_shape=[jax.ShapeDtypeStruct((rows, width),...  3.74 us
    ppermute x20, waiting for transfers between devices, swap(): return lax.ppermute(tile, 'tm', route)  1.71 us
  transfers between devices with their start and end apart: 22, of which 5 were waited for; matrix products, arithmetic and copies ran while one was open for 0% of the time, Pallas kernels for 15%

profile of v6, /device:TPU:1, one launch (start us, length us, event | category | flops | bytes accessed | tf_op | source)
XLA Modules:
  0.0 61.5 jit_solution(4590193466353138466)
XLA Ops:
  0.0 6.5 %mixer.2 = (bf16[32,512]{1,0:T(8,128)(2,1)}, bf16[32,512]{1,0:T(8,128)(2,1)}, bf16[32,512]{1,0:T(8,128)(2,1)}, bf16[32,512]{1,0:T(8,128)(2,1)}, bf16[32,512]{1,0:T(8,128)(2,1)}, /*index=5*/bf16[512,512]{1,0:T(8,128)(2,1)}) custom-call(bf16[512,1024]{1,0:T(8,128)(2,1)} %bitcast.4, bf16[512,1024]{1,0:T(8,128)(2,1)} %bitcast.5, bf16[1024,3072]{1,0:T(8,128)(2,1)} %refs_4_.3, ...), custom_call_target="tpu_custom_call" | custom-call | flops 1879048192 | bytes 5242880 | tf_op jit(solution)/shard_map/mixer/pallas_call | solution.py:164
  6.6 4.2 %collective-permute-start = (bf16[32,512]{1,0:T(8,128)(2,1)}, bf16[32,512]{1,0:T(8,128)(2,1)S(1)}, u32[]{:S(2)}, u32[]{:S(2)}) collective-permute-start(bf16[32,512]{1,0:T(8,128)(2,1)} %get-tuple-element.36), channel_id=1, source_target_pairs={{0,12},{1,13},{2,14},{3,15},{4,8},{5,9},{6,10},{7,11},{8,4},{9,5},... | collective-permute-start | bytes 98312 | tf_op jit(solution)/shard_map/ppermute | solution.py:384
  10.8 2.5 %collective-permute-start.2 = (bf16[32,512]{1,0:T(8,128)(2,1)}, bf16[32,512]{1,0:T(8,128)(2,1)S(1)}, u32[]{:S(2)}, u32[]{:S(2)}) collective-permute-start(bf16[32,512]{1,0:T(8,128)(2,1)} %get-tuple-element.38), channel_id=1, source_target_pairs={{0,13},{1,12},{2,15},{3,14},{4,9},{5,8},{6,11},{7,10},{8,5},{9,4},... | collective-permute-start | bytes 98312 | tf_op jit(solution)/shard_map/ppermute | solution.py:384
  13.2 1.0 %collective-permute-start.3 = (bf16[32,512]{1,0:T(8,128)(2,1)}, bf16[32,512]{1,0:T(8,128)(2,1)S(1)}, u32[]{:S(2)}, u32[]{:S(2)}) collective-permute-start(bf16[32,512]{1,0:T(8,128)(2,1)} %get-tuple-element.39), channel_id=1, source_target_pairs={{0,9},{1,8},{2,11},{3,10},{4,13},{5,12},{6,15},{7,14},{8,1},{9,0},... | collective-permute-start | bytes 98312 | tf_op jit(solution)/shard_map/ppermute | solution.py:384
  14.3 2.5 %collective-permute-start.4 = (bf16[32,512]{1,0:T(8,128)(2,1)}, bf16[32,512]{1,0:T(8,128)(2,1)S(1)}, u32[]{:S(2)}, u32[]{:S(2)}) collective-permute-start(bf16[32,512]{1,0:T(8,128)(2,1)} %get-tuple-element.40), channel_id=1, source_target_pairs={{0,14},{1,15},{2,12},{3,13},{4,10},{5,11},{6,8},{7,9},{8,6},{9,7},... | collective-permute-start | bytes 98312 | tf_op jit(solution)/shard_map/ppermute | solution.py:384
  16.8 3.7 %mixer.3.right_ref = bf16[512,512]{1,0:T(8,128)(2,1)S(1)} custom-call(bf16[512,1024]{1,0:T(8,128)(2,1)S(1)} %bitcast.6, bf16[512,1024]{1,0:T(8,128)(2,1)S(1)} %bitcast.7, bf16[1024,3072]{1,0:T(8,128)(2,1)S(1)} %bitcast.3, bf16[1024,3072]{1,0:T(8,128)(2,1)S(1)} %bitcast.3, bf16[1024,3072]{1,0:T(8,128)(2,1)S(1)} %bitcast.3, bf16[1024]{0:T(1024)(128)(2,1)S(1)} %copy-done.3), custom_call_target="tpu_custom_call" | custom-call | flops 1879048192 | bytes 5242880 | tf_op jit(solution)/shard_map/mixer/pallas_call | solution.py:164
  20.5 0.0 copy-start.5
  20.6 0.1 collective-permute-done.4.refs_4_.refs_9_
  20.6 0.1 cut.1
  20.7 1.8 %collective-permute-start.5 = (bf16[32,512]{1,0:T(8,128)(2,1)S(1)}, bf16[32,512]{1,0:T(8,128)(2,1)S(1)}, u32[]{:S(2)}, u32[]{:S(2)}) collective-permute-start(bf16[32,512]{1,0:T(8,128)(2,1)S(1)} %get-tuple-element.42), channel_id=1, source_target_pairs={{0,12},{1,13},{2,14},{3,15},{4,8},{5,9},{6,10},{7,11},{8,4},{9,5},... | collective-permute-start | bytes 98312 | tf_op jit(solution)/shard_map/ppermute | solution.py:384
  22.5 3.2 %collective-permute-start.7 = (bf16[32,512]{1,0:T(8,128)(2,1)S(1)}, bf16[32,512]{1,0:T(8,128)(2,1)S(1)}, u32[]{:S(2)}, u32[]{:S(2)}) collective-permute-start(bf16[32,512]{1,0:T(8,128)(2,1)S(1)} %get-tuple-element.44), channel_id=1, source_target_pairs={{0,13},{1,12},{2,15},{3,14},{4,9},{5,8},{6,11},{7,10},{8,5},{9,4},... | collective-permute-start | bytes 98312 | tf_op jit(solution)/shard_map/ppermute | solution.py:384
  25.7 1.1 %collective-permute-start.8 = (bf16[32,512]{1,0:T(8,128)(2,1)S(1)}, bf16[32,512]{1,0:T(8,128)(2,1)S(1)}, u32[]{:S(2)}, u32[]{:S(2)}) collective-permute-start(bf16[32,512]{1,0:T(8,128)(2,1)S(1)} %get-tuple-element.45), channel_id=1, source_target_pairs={{0,9},{1,8},{2,11},{3,10},{4,13},{5,12},{6,15},{7,14},{8,1},{9,0},... | collective-permute-start | bytes 98312 | tf_op jit(solution)/shard_map/ppermute | solution.py:384
  26.8 1.6 %collective-permute-start.9 = (bf16[32,512]{1,0:T(8,128)(2,1)S(1)}, bf16[32,512]{1,0:T(8,128)(2,1)S(1)}, u32[]{:S(2)}, u32[]{:S(2)}) collective-permute-start(bf16[32,512]{1,0:T(8,128)(2,1)S(1)} %get-tuple-element.46), channel_id=1, source_target_pairs={{0,14},{1,15},{2,12},{3,13},{4,10},{5,11},{6,8},{7,9},{8,6},{9,7},... | collective-permute-start | bytes 98312 | tf_op jit(solution)/shard_map/ppermute | solution.py:384
  28.4 3.8 %collective-permute-start.10 = (bf16[32,1024]{1,0:T(8,128)(2,1)S(1)}, bf16[32,1024]{1,0:T(8,128)(2,1)S(1)}, u32[]{:S(2)}, u32[]{:S(2)}) collective-permute-start(bf16[32,1024]{1,0:T(8,128)(2,1)S(1)} %get-tuple-element.47), channel_id=1, source_target_pairs={{0,15},{1,14},{2,13},{3,12},{4,11},{5,10},{6,9},{7,8},{8,7},{9,6},... | collective-permute-start | bytes 196616 | tf_op jit(solution)/shard_map/ppermute | solution.py:384
  32.2 1.8 %collective-permute-start.12 = (bf16[32,1024]{1,0:T(8,128)(2,1)S(1)}, bf16[32,1024]{1,0:T(8,128)(2,1)S(1)}, u32[]{:S(2)}, u32[]{:S(2)}) collective-permute-start(bf16[32,1024]{1,0:T(8,128)(2,1)S(1)} %get-tuple-element.49), channel_id=1, source_target_pairs={{0,10},{1,11},{2,8},{3,9},{4,14},{5,15},{6,12},{7,13},{8,2},{9,3},... | collective-permute-start | bytes 196616 | tf_op jit(solution)/shard_map/ppermute | solution.py:384
  34.0 1.2 %collective-permute-start.13 = (bf16[32,1024]{1,0:T(8,128)(2,1)S(1)}, bf16[32,1024]{1,0:T(8,128)(2,1)S(1)}, u32[]{:S(2)}, u32[]{:S(2)}) collective-permute-start(bf16[32,1024]{1,0:T(8,128)(2,1)S(1)} %get-tuple-element.50), channel_id=1, source_target_pairs={{0,6},{1,7},{2,4},{3,5},{4,2},{5,3},{6,0},{7,1},{8,14},{9,15},{10,... | collective-permute-start | bytes 196616 | tf_op jit(solution)/shard_map/ppermute | solution.py:384
  35.2 3.5 %collective-permute-start.14 = (bf16[32,1024]{1,0:T(8,128)(2,1)S(1)}, bf16[32,1024]{1,0:T(8,128)(2,1)S(1)}, u32[]{:S(2)}, u32[]{:S(2)}) collective-permute-start(bf16[32,1024]{1,0:T(8,128)(2,1)S(1)} %get-tuple-element.51), channel_id=1, source_target_pairs={{0,11},{1,10},{2,9},{3,8},{4,15},{5,14},{6,13},{7,12},{8,3},{9,2},... | collective-permute-start | bytes 196616 | tf_op jit(solution)/shard_map/ppermute | solution.py:384
  38.6 0.6 collective-permute-done.11.refs_12_
  39.2 1.7 %collective-permute-start.17 = (bf16[32,1024]{1,0:T(8,128)(2,1)S(1)}, bf16[32,1024]{1,0:T(8,128)(2,1)S(1)}, u32[]{:S(2)}, u32[]{:S(2)}) collective-permute-start(bf16[32,1024]{1,0:T(8,128)(2,1)S(1)} %get-tuple-element.54), channel_id=1, source_target_pairs={{0,3},{1,2},{2,1},{3,0},{4,7},{5,6},{6,5},{7,4},{8,11},{9,10},{10,... | collective-permute-start | bytes 196616 | tf_op jit(solution)/shard_map/ppermute | solution.py:384
  40.9 1.2 %collective-permute-start.18 = (bf16[32,1024]{1,0:T(8,128)(2,1)S(1)}, bf16[32,1024]{1,0:T(8,128)(2,1)S(1)}, u32[]{:S(2)}, u32[]{:S(2)}) collective-permute-start(bf16[32,1024]{1,0:T(8,128)(2,1)S(1)} %get-tuple-element.55), channel_id=1, source_target_pairs={{0,2},{1,3},{2,0},{3,1},{4,6},{5,7},{6,4},{7,5},{8,10},{9,11},{10,... | collective-permute-start | bytes 196616 | tf_op jit(solution)/shard_map/ppermute | solution.py:384
  42.1 0.2 collective-permute-done.14.refs_15_
  42.3 1.6 %collective-permute-start.19 = (bf16[32,1024]{1,0:T(8,128)(2,1)S(1)}, bf16[32,1024]{1,0:T(8,128)(2,1)S(1)}, u32[]{:S(2)}, u32[]{:S(2)}) collective-permute-start(bf16[32,1024]{1,0:T(8,128)(2,1)S(1)} %get-tuple-element.56), channel_id=1, source_target_pairs={{0,1},{1,0},{2,3},{3,2},{4,5},{5,4},{6,7},{7,6},{8,9},{9,8},{10,11... | collective-permute-start | bytes 196616 | tf_op jit(solution)/shard_map/ppermute | solution.py:384
  43.9 0.2 collective-permute-done.15.refs_16_
  44.1 0.0 collective-permute-done.16.refs_17_
  44.1 0.7 %collective-permute-done.18.refs_19_ = bf16[32,1024]{1,0:T(8,128)(2,1)S(1)} collective-permute-done((bf16[32,1024]{1,0:T(8,128)(2,1)S(1)}, bf16[32,1024]{1,0:T(8,128)(2,1)S(1)}, u32[]{:S(2)}, u32[]{:S(2)}) %collective-permute-start.18) | collective-permute-done | bytes 65568 | tf_op jit(solution)/shard_map/ppermute | solution.py:384
  44.8 0.0 collective-permute-done.19.refs_20_
  44.8 0.9 %pairs.1 = (bf16[512,1024]{1,0:T(8,128)(2,1)S(1)}, bf16[512,256]{1,0:T(8,128)(2,1)S(1)}, bf16[512,256]{1,0:T(8,128)(2,1)S(1)}) custom-call(bf16[1024]{0:T(1024)(128)(2,1)S(1)} %copy-done.4, bf16[1024,512]{1,0:T(8,128)(2,1)S(1)} %copy-done.1, bf16[32,1024]{1,0:T(8,128)(2,1)S(1)} %get-tuple-element.41.refs_0_, ...), custom_call_target="tpu_custom_call" | custom-call | flops 536870912 | bytes 3670016 | tf_op jit(solution)/shard_map/pairs/pallas_call | solution.py:249
  45.8 4.9 %collective-permute-start.21 = (bf16[512,256]{1,0:T(8,128)(2,1)S(1)}, bf16[512,256]{1,0:T(8,128)(2,1)S(1)}, u32[]{:S(2)}, u32[]{:S(2)}) collective-permute-start(bf16[512,256]{1,0:T(8,128)(2,1)S(1)} %get-tuple-element.58.first_ref), channel_id=1, source_target_pairs={{0,1},{1,2},{2,3},{3,4},{4,5},{5,6},{6,7},{7,8},{8,9},{9,10},{10,1... | collective-permute-start | bytes 786440 | tf_op jit(solution)/shard_map/ppermute | solution.py:28
  50.6 2.1 %collective-permute-start.20 = (bf16[512,256]{1,0:T(8,128)(2,1)S(1)}, bf16[512,256]{1,0:T(8,128)(2,1)S(1)}, u32[]{:S(2)}, u32[]{:S(2)}) collective-permute-start(bf16[512,256]{1,0:T(8,128)(2,1)S(1)} %get-tuple-element.59.second_ref), channel_id=1, source_target_pairs={{0,1},{1,2},{2,3},{3,4},{4,5},{5,6},{6,7},{7,8},{8,9},{9,10},{10,1... | collective-permute-start | bytes 786440 | tf_op jit(solution)/shard_map/ppermute | solution.py:28
  52.8 3.7 %own_frame.1 = (bf16[512,1024]{1,0:T(8,128)(2,1)S(1)}, f32[512,1024]{1,0:T(8,128)S(1)}, f32[512,1024]{1,0:T(8,128)S(1)}) custom-call(bf16[512,1024]{1,0:T(8,128)(2,1)S(1)} %get-tuple-element.57.normed_ref, bf16[1024,1024]{1,0:T(8,128)(2,1)S(1)} %copy-done.5, bf16[512,256]{1,0:T(8,128)(2,1)S(1)} %get-tuple-element.58.first_ref, ...), custom_call_target="tpu_custom_call" | custom-call | flops 2147483648 | bytes 6291456 | tf_op jit(solution)/shard_map/own_frame/pallas_call | solution.py:310
  56.5 2.0 %earlier_frame.2 = (f32[512,1024]{1,0:T(8,128)S(1)}, f32[512,1024]{1,0:T(8,128)S(1)}) custom-call(bf16[512,1024]{1,0:T(8,128)(2,1)S(1)} %get-tuple-element.60.query_ref, bf16[512,256]{1,0:T(8,128)(2,1)S(1)} %collective-permute-done.21.pairs_ref, f32[512,1024]{1,0:T(8,128)S(1)} %get-tuple-element.61.partial_ref, f32[512,1024]{1,0:T(8,128)S(1)} %get-tuple-element.62.log_ref), custom_call_target="tpu_custom_call" | custom-call | flops 536870912 | bytes 5242880 | tf_op jit(solution)/shard_map/earlier_frame/pallas_call | solution.py:368
  58.6 3.0 %earlier_frame.3 = bf16[512,1024]{1,0:T(8,128)(2,1)} custom-call(bf16[512,1024]{1,0:T(8,128)(2,1)S(1)} %get-tuple-element.60.query_ref, bf16[512,256]{1,0:T(8,128)(2,1)S(1)} %collective-permute-done.20.pairs_ref, f32[512,1024]{1,0:T(8,128)S(1)} %get-tuple-element.63.partial_ref, f32[512,1024]{1,0:T(8,128)S(1)} %get-tuple-element.64.log_ref), custom_call_target="tpu_custom_call" | custom-call | flops 536870912 | bytes 5242880 | tf_op jit(solution)/shard_map/earlier_frame/pallas_call | solution.py:368
  (36 shorter events, 0.1 us)
Async XLA Ops:
  0.0 16.7 %slice-start = ((s8[6291456]{0:T(1024)(128)(4,1)}), s8[4194304]{0:T(1024)(128)(4,1)S(1)}, s32[]{:S(2)}) async-start(s8[6291456]{0:T(1024)(128)(4,1)} %bitcast.2), calls=%async_computation | async-start | bytes 8388608
  0.0 16.7 %slice-start.1 = ((s8[6291456]{0:T(1024)(128)(4,1)}), s8[2097152]{0:T(1024)(128)(4,1)S(1)}, s32[]{:S(2)}) async-start(s8[6291456]{0:T(1024)(128)(4,1)} %bitcast.2), calls=%async_computation.1 | async-start | bytes 4194304
  0.0 16.7 %copy-start = (bf16[1,512,1024]{2,1,0:T(8,128)(2,1)S(1)}, bf16[1,512,1024]{2,1,0:T(8,128)(2,1)}, u32[]{:S(2)}) copy-start(bf16[1,512,1024]{2,1,0:T(8,128)(2,1)} %param.6) | copy-start | bytes 3145732
  0.0 16.7 %copy-start.3 = (bf16[1024]{0:T(1024)(128)(2,1)S(1)}, bf16[1024]{0:T(1024)(128)(2,1)}, u32[]{:S(2)}) copy-start(bf16[1024]{0:T(1024)(128)(2,1)} %refs_5_.3) | copy-start | bytes 6148
  6.6 14.0 %collective-permute-start = (bf16[32,512]{1,0:T(8,128)(2,1)}, bf16[32,512]{1,0:T(8,128)(2,1)S(1)}, u32[]{:S(2)}, u32[]{:S(2)}) collective-permute-start(bf16[32,512]{1,0:T(8,128)(2,1)} %get-tuple-element.36), channel_id=1, source_target_pairs={{0,12},{1,13},{2,14},{3,15},{4,8},{5,9},{6,10},{7,11},{8,4},{9,5},... | collective-permute-start | bytes 98312 | tf_op jit(solution)/shard_map/ppermute | solution.py:384
  10.8 9.8 %collective-permute-start.1 = (bf16[32,512]{1,0:T(8,128)(2,1)}, bf16[32,512]{1,0:T(8,128)(2,1)S(1)}, u32[]{:S(2)}, u32[]{:S(2)}) collective-permute-start(bf16[32,512]{1,0:T(8,128)(2,1)} %get-tuple-element.37), channel_id=1, source_target_pairs={{0,8},{1,9},{2,10},{3,11},{4,12},{5,13},{6,14},{7,15},{8,0},{9,1},... | collective-permute-start | bytes 98312 | tf_op jit(solution)/shard_map/ppermute | solution.py:384
  10.8 9.8 %collective-permute-start.2 = (bf16[32,512]{1,0:T(8,128)(2,1)}, bf16[32,512]{1,0:T(8,128)(2,1)S(1)}, u32[]{:S(2)}, u32[]{:S(2)}) collective-permute-start(bf16[32,512]{1,0:T(8,128)(2,1)} %get-tuple-element.38), channel_id=1, source_target_pairs={{0,13},{1,12},{2,15},{3,14},{4,9},{5,8},{6,11},{7,10},{8,5},{9,4},... | collective-permute-start | bytes 98312 | tf_op jit(solution)/shard_map/ppermute | solution.py:384
  13.2 7.3 %collective-permute-start.3 = (bf16[32,512]{1,0:T(8,128)(2,1)}, bf16[32,512]{1,0:T(8,128)(2,1)S(1)}, u32[]{:S(2)}, u32[]{:S(2)}) collective-permute-start(bf16[32,512]{1,0:T(8,128)(2,1)} %get-tuple-element.39), channel_id=1, source_target_pairs={{0,9},{1,8},{2,11},{3,10},{4,13},{5,12},{6,15},{7,14},{8,1},{9,0},... | collective-permute-start | bytes 98312 | tf_op jit(solution)/shard_map/ppermute | solution.py:384
  14.3 6.4 %copy-start.2 = (bf16[512,512]{1,0:T(8,128)(2,1)S(1)}, bf16[512,512]{1,0:T(8,128)(2,1)}, u32[]{:S(2)}) copy-start(bf16[512,512]{1,0:T(8,128)(2,1)} %get-tuple-element.35.left_ref) | copy-start | bytes 1572868
  14.3 30.5 %copy-start.1 = (bf16[1024,512]{1,0:T(8,128)(2,1)S(1)}, bf16[1024,512]{1,0:T(8,128)(2,1)}, u32[]{:S(2)}) copy-start(bf16[1024,512]{1,0:T(8,128)(2,1)} %w_ref.2) | copy-start | bytes 3145732
  14.3 30.5 %copy-start.4 = (bf16[1024]{0:T(1024)(128)(2,1)S(1)}, bf16[1024]{0:T(1024)(128)(2,1)}, u32[]{:S(2)}) copy-start(bf16[1024]{0:T(1024)(128)(2,1)} %gain_ref.1) | copy-start | bytes 6148
  14.3 6.4 %collective-permute-start.4 = (bf16[32,512]{1,0:T(8,128)(2,1)}, bf16[32,512]{1,0:T(8,128)(2,1)S(1)}, u32[]{:S(2)}, u32[]{:S(2)}) collective-permute-start(bf16[32,512]{1,0:T(8,128)(2,1)} %get-tuple-element.40), channel_id=1, source_target_pairs={{0,14},{1,15},{2,12},{3,13},{4,10},{5,11},{6,8},{7,9},{8,6},{9,7},... | collective-permute-start | bytes 98312 | tf_op jit(solution)/shard_map/ppermute | solution.py:384
  20.5 32.2 %copy-start.5 = (bf16[1024,1024]{1,0:T(8,128)(2,1)S(1)}, bf16[1024,1024]{1,0:T(8,128)(2,1)}, u32[]{:S(2)}) copy-start(bf16[1024,1024]{1,0:T(8,128)(2,1)} %w_ref.3) | copy-start | bytes 6291460
  20.7 7.7 %collective-permute-start.5 = (bf16[32,512]{1,0:T(8,128)(2,1)S(1)}, bf16[32,512]{1,0:T(8,128)(2,1)S(1)}, u32[]{:S(2)}, u32[]{:S(2)}) collective-permute-start(bf16[32,512]{1,0:T(8,128)(2,1)S(1)} %get-tuple-element.42), channel_id=1, source_target_pairs={{0,12},{1,13},{2,14},{3,15},{4,8},{5,9},{6,10},{7,11},{8,4},{9,5},... | collective-permute-start | bytes 98312 | tf_op jit(solution)/shard_map/ppermute | solution.py:384
  22.5 9.7 %collective-permute-start.6 = (bf16[32,512]{1,0:T(8,128)(2,1)S(1)}, bf16[32,512]{1,0:T(8,128)(2,1)S(1)}, u32[]{:S(2)}, u32[]{:S(2)}) collective-permute-start(bf16[32,512]{1,0:T(8,128)(2,1)S(1)} %get-tuple-element.43), channel_id=1, source_target_pairs={{0,8},{1,9},{2,10},{3,11},{4,12},{5,13},{6,14},{7,15},{8,0},{9,1},... | collective-permute-start | bytes 98312 | tf_op jit(solution)/shard_map/ppermute | solution.py:384
  22.5 9.7 %collective-permute-start.7 = (bf16[32,512]{1,0:T(8,128)(2,1)S(1)}, bf16[32,512]{1,0:T(8,128)(2,1)S(1)}, u32[]{:S(2)}, u32[]{:S(2)}) collective-permute-start(bf16[32,512]{1,0:T(8,128)(2,1)S(1)} %get-tuple-element.44), channel_id=1, source_target_pairs={{0,13},{1,12},{2,15},{3,14},{4,9},{5,8},{6,11},{7,10},{8,5},{9,4},... | collective-permute-start | bytes 98312 | tf_op jit(solution)/shard_map/ppermute | solution.py:384
  25.7 8.3 %collective-permute-start.8 = (bf16[32,512]{1,0:T(8,128)(2,1)S(1)}, bf16[32,512]{1,0:T(8,128)(2,1)S(1)}, u32[]{:S(2)}, u32[]{:S(2)}) collective-permute-start(bf16[32,512]{1,0:T(8,128)(2,1)S(1)} %get-tuple-element.45), channel_id=1, source_target_pairs={{0,9},{1,8},{2,11},{3,10},{4,13},{5,12},{6,15},{7,14},{8,1},{9,0},... | collective-permute-start | bytes 98312 | tf_op jit(solution)/shard_map/ppermute | solution.py:384
  26.8 8.4 %collective-permute-start.9 = (bf16[32,512]{1,0:T(8,128)(2,1)S(1)}, bf16[32,512]{1,0:T(8,128)(2,1)S(1)}, u32[]{:S(2)}, u32[]{:S(2)}) collective-permute-start(bf16[32,512]{1,0:T(8,128)(2,1)S(1)} %get-tuple-element.46), channel_id=1, source_target_pairs={{0,14},{1,15},{2,12},{3,13},{4,10},{5,11},{6,8},{7,9},{8,6},{9,7},... | collective-permute-start | bytes 98312 | tf_op jit(solution)/shard_map/ppermute | solution.py:384
  28.4 10.3 %collective-permute-start.10 = (bf16[32,1024]{1,0:T(8,128)(2,1)S(1)}, bf16[32,1024]{1,0:T(8,128)(2,1)S(1)}, u32[]{:S(2)}, u32[]{:S(2)}) collective-permute-start(bf16[32,1024]{1,0:T(8,128)(2,1)S(1)} %get-tuple-element.47), channel_id=1, source_target_pairs={{0,15},{1,14},{2,13},{3,12},{4,11},{5,10},{6,9},{7,8},{8,7},{9,6},... | collective-permute-start | bytes 196616 | tf_op jit(solution)/shard_map/ppermute | solution.py:384
  32.2 7.0 %collective-permute-start.11 = (bf16[32,1024]{1,0:T(8,128)(2,1)S(1)}, bf16[32,1024]{1,0:T(8,128)(2,1)S(1)}, u32[]{:S(2)}, u32[]{:S(2)}) collective-permute-start(bf16[32,1024]{1,0:T(8,128)(2,1)S(1)} %get-tuple-element.48), channel_id=1, source_target_pairs={{0,7},{1,6},{2,5},{3,4},{4,3},{5,2},{6,1},{7,0},{8,15},{9,14},{10,... | collective-permute-start | bytes 196616 | tf_op jit(solution)/shard_map/ppermute | solution.py:384
  32.2 7.0 %collective-permute-start.12 = (bf16[32,1024]{1,0:T(8,128)(2,1)S(1)}, bf16[32,1024]{1,0:T(8,128)(2,1)S(1)}, u32[]{:S(2)}, u32[]{:S(2)}) collective-permute-start(bf16[32,1024]{1,0:T(8,128)(2,1)S(1)} %get-tuple-element.49), channel_id=1, source_target_pairs={{0,10},{1,11},{2,8},{3,9},{4,14},{5,15},{6,12},{7,13},{8,2},{9,3},... | collective-permute-start | bytes 196616 | tf_op jit(solution)/shard_map/ppermute | solution.py:384
  34.0 6.9 %collective-permute-start.13 = (bf16[32,1024]{1,0:T(8,128)(2,1)S(1)}, bf16[32,1024]{1,0:T(8,128)(2,1)S(1)}, u32[]{:S(2)}, u32[]{:S(2)}) collective-permute-start(bf16[32,1024]{1,0:T(8,128)(2,1)S(1)} %get-tuple-element.50), channel_id=1, source_target_pairs={{0,6},{1,7},{2,4},{3,5},{4,2},{5,3},{6,0},{7,1},{8,14},{9,15},{10,... | collective-permute-start | bytes 196616 | tf_op jit(solution)/shard_map/ppermute | solution.py:384
  35.2 7.2 %collective-permute-start.14 = (bf16[32,1024]{1,0:T(8,128)(2,1)S(1)}, bf16[32,1024]{1,0:T(8,128)(2,1)S(1)}, u32[]{:S(2)}, u32[]{:S(2)}) collective-permute-start(bf16[32,1024]{1,0:T(8,128)(2,1)S(1)} %get-tuple-element.51), channel_id=1, source_target_pairs={{0,11},{1,10},{2,9},{3,8},{4,15},{5,14},{6,13},{7,12},{8,3},{9,2},... | collective-permute-start | bytes 196616 | tf_op jit(solution)/shard_map/ppermute | solution.py:384
  38.6 5.4 %collective-permute-start.15 = (bf16[32,1024]{1,0:T(8,128)(2,1)S(1)}, bf16[32,1024]{1,0:T(8,128)(2,1)S(1)}, u32[]{:S(2)}, u32[]{:S(2)}) collective-permute-start(bf16[32,1024]{1,0:T(8,128)(2,1)S(1)} %get-tuple-element.52), channel_id=1, source_target_pairs={{0,5},{1,4},{2,7},{3,6},{4,1},{5,0},{6,3},{7,2},{8,13},{9,12},{10,... | collective-permute-start | bytes 196616 | tf_op jit(solution)/shard_map/ppermute | solution.py:384
  39.2 4.9 %collective-permute-start.16 = (bf16[32,1024]{1,0:T(8,128)(2,1)S(1)}, bf16[32,1024]{1,0:T(8,128)(2,1)S(1)}, u32[]{:S(2)}, u32[]{:S(2)}) collective-permute-start(bf16[32,1024]{1,0:T(8,128)(2,1)S(1)} %get-tuple-element.53), channel_id=1, source_target_pairs={{0,4},{1,5},{2,6},{3,7},{4,0},{5,1},{6,2},{7,3},{8,12},{9,13},{10,... | collective-permute-start | bytes 196616 | tf_op jit(solution)/shard_map/ppermute | solution.py:384
  39.2 4.9 %collective-permute-start.17 = (bf16[32,1024]{1,0:T(8,128)(2,1)S(1)}, bf16[32,1024]{1,0:T(8,128)(2,1)S(1)}, u32[]{:S(2)}, u32[]{:S(2)}) collective-permute-start(bf16[32,1024]{1,0:T(8,128)(2,1)S(1)} %get-tuple-element.54), channel_id=1, source_target_pairs={{0,3},{1,2},{2,1},{3,0},{4,7},{5,6},{6,5},{7,4},{8,11},{9,10},{10,... | collective-permute-start | bytes 196616 | tf_op jit(solution)/shard_map/ppermute | solution.py:384
  40.9 3.9 %collective-permute-start.18 = (bf16[32,1024]{1,0:T(8,128)(2,1)S(1)}, bf16[32,1024]{1,0:T(8,128)(2,1)S(1)}, u32[]{:S(2)}, u32[]{:S(2)}) collective-permute-start(bf16[32,1024]{1,0:T(8,128)(2,1)S(1)} %get-tuple-element.55), channel_id=1, source_target_pairs={{0,2},{1,3},{2,0},{3,1},{4,6},{5,7},{6,4},{7,5},{8,10},{9,11},{10,... | collective-permute-start | bytes 196616 | tf_op jit(solution)/shard_map/ppermute | solution.py:384
  42.3 2.5 %collective-permute-start.19 = (bf16[32,1024]{1,0:T(8,128)(2,1)S(1)}, bf16[32,1024]{1,0:T(8,128)(2,1)S(1)}, u32[]{:S(2)}, u32[]{:S(2)}) collective-permute-start(bf16[32,1024]{1,0:T(8,128)(2,1)S(1)} %get-tuple-element.56), channel_id=1, source_target_pairs={{0,1},{1,0},{2,3},{3,2},{4,5},{5,4},{6,7},{7,6},{8,9},{9,8},{10,11... | collective-permute-start | bytes 196616 | tf_op jit(solution)/shard_map/ppermute | solution.py:384
  45.8 10.8 %collective-permute-start.21 = (bf16[512,256]{1,0:T(8,128)(2,1)S(1)}, bf16[512,256]{1,0:T(8,128)(2,1)S(1)}, u32[]{:S(2)}, u32[]{:S(2)}) collective-permute-start(bf16[512,256]{1,0:T(8,128)(2,1)S(1)} %get-tuple-element.58.first_ref), channel_id=1, source_target_pairs={{0,1},{1,2},{2,3},{3,4},{4,5},{5,6},{6,7},{7,8},{8,9},{9,10},{10,1... | collective-permute-start | bytes 786440 | tf_op jit(solution)/shard_map/ppermute | solution.py:28
  50.6 7.9 %collective-permute-start.20 = (bf16[512,256]{1,0:T(8,128)(2,1)S(1)}, bf16[512,256]{1,0:T(8,128)(2,1)S(1)}, u32[]{:S(2)}, u32[]{:S(2)}) collective-permute-start(bf16[512,256]{1,0:T(8,128)(2,1)S(1)} %get-tuple-element.59.second_ref), channel_id=1, source_target_pairs={{0,1},{1,2},{2,3},{3,4},{4,5},{5,6},{6,7},{7,8},{8,9},{9,10},{10,1... | collective-permute-start | bytes 786440 | tf_op jit(solution)/shard_map/ppermute | solution.py:28

commit v7 on v6

v7 whole, which is shorter than its diff:
```python
import functools
import math

import jax
import jax.numpy as jnp
from jax import lax
from jax.experimental import pallas as pl
from jax.experimental.pallas import tpu as pltpu
from jax.sharding import PartitionSpec as P

HEADS = 8
HD = 128
KVH = 2
SB = 16
SPAN = 128
PAIR = 2

epsilon = 1e-06
MIB = 1 << 20


def shifted(block, axis, distance):
    devices = range(lax.axis_size(axis))
    route = [(i - distance, i) for i in devices if i - distance in devices]
    return lax.ppermute(block, axis, route)


def dot(a, b):
    return jnp.dot(a, b, preferred_element_type=jnp.float32)


def dot_nt(a, b):
    return lax.dot_general(a, b, (((1,), (1,)), ((), ())), preferred_element_type=jnp.float32)


def dot_tn(a, b):
    return lax.dot_general(a, b, (((0,), (0,)), ((), ())), preferred_element_type=jnp.float32)


def head_lanes(head):
    return slice(head * HD, (head + 1) * HD)


def causal_mask():
    shape = (SPAN, SPAN)
    return lax.broadcasted_iota(jnp.int32, shape, 0) >= lax.broadcasted_iota(jnp.int32, shape, 1)


def mix_heads(query, key, value, states):
    rows = query.shape[0]
    causal = causal_mask()
    spans = [slice(start, start + SPAN) for start in range(0, rows, SPAN)]
    heads = range(query.shape[1] // HD)
    units = [(head, span) for head in heads for span in range(len(spans))]
    local, before, after, mixed = {}, {}, [], []
    for head, span in units:
        lanes, here = head_lanes(head), spans[span]
        scores = dot_nt(query[here, lanes], key[here, lanes])
        local[head, span] = jnp.where(causal, scores, 0.0).astype(jnp.bfloat16)
    for head in heads:
        lanes = head_lanes(head)
        state = states[head]
        for span, here in enumerate(spans):
            before[head, span] = state
            update = dot_tn(key[here, lanes], value[here, lanes])
            state = update if state is None else state + update
        after.append(state)
    for head, span in units:
        lanes, here = head_lanes(head), spans[span]
        if before[head, span] is None:
            out = dot(local[head, span], value[here, lanes])
        else:
            out = dot(
                jnp.concatenate([query[here, lanes], local[head, span]], axis=1),
                jnp.concatenate(
                    [before[head, span].astype(jnp.bfloat16), value[here, lanes]], axis=0
                ),
            )
        mixed.append((head, here, out))
    return mixed, after


def mixer_kernel(has_state, *refs):
    if has_state:
        state_ref, *refs = refs
    tokens_hbm, w_hbm, gain_ref, out_ref, tokens_ref, weights, tokens_in, weights_in = refs
    rows, width = tokens_ref.shape
    block = rows // 2
    columns = PAIR * HD
    step = pl.program_id(0)
    slot = lax.rem(step, 2)

    def token_copy(index):
        here = slice(index * block, (index + 1) * block)
        return pltpu.make_async_copy(
            tokens_hbm.at[here], tokens_ref.at[here], tokens_in.at[index]
        )

    def weight_copy(pair, to, part):
        start = pl.multiple_of(part * width + pair * columns, columns)
        return pltpu.make_async_copy(
            w_hbm.at[:, pl.ds(start, columns)], weights.at[to, part], weights_in.at[to, part]
        )

    @pl.when(step == 0)
    def _():
        token_copy(0).start()
        weight_copy(0, 0, 0).start()
        weight_copy(0, 0, 1).start()
        token_copy(1).start()
        weight_copy(0, 0, 2).start()

    @pl.when(step + 1 < pl.num_programs(0))
    def _():
        for part in range(3):
            weight_copy(step + 1, 1 - slot, part).start()

    @pl.when(step == 0)
    def _():
        token_copy(0).wait()
        token_copy(1).wait()

    for part in range(3):
        weight_copy(step, slot, part).wait()

    states = [state_ref[head] if has_state else None for head in range(PAIR)]
    start = pl.multiple_of(step * columns, columns)
    gains = gain_ref[pl.ds(start, columns)].astype(jnp.float32).reshape(1, columns)

    def project(offset):
        tokens = tokens_ref[offset : offset + block]
        return [dot(tokens, weights[slot, part]).astype(jnp.bfloat16) for part in range(3)]

    def store(offset, mixed):
        for head, here, out in mixed:
            lanes = head_lanes(head)
            here = slice(offset + here.start, offset + here.stop)
            mean_square = jnp.mean(out * out, axis=-1, keepdims=True)
            normed = out * lax.rsqrt(mean_square + epsilon) * gains[:, lanes]
            there = pl.ds(pl.multiple_of(start + head * HD, HD), HD)
            residual = tokens_ref[here, there].astype(jnp.float32)
            out_ref[here, lanes] = (residual + normed).astype(jnp.bfloat16)

    parts = project(0)
    upcoming = project(block)
    mixed, states = mix_heads(*parts, states)
    store(0, mixed)
    mixed, states = mix_heads(*upcoming, states)
    store(block, mixed)


def mixer(tokens, w_lin, gain_lin, state):
    rows, width = tokens.shape
    columns = PAIR * HD
    in_specs = [
        pl.BlockSpec(memory_space=pl.ANY),
        pl.BlockSpec(memory_space=pl.ANY),
        pl.BlockSpec(memory_space=pltpu.VMEM),
    ]
    operands = [tokens, w_lin, gain_lin]
    if state is not None:
        operands.insert(0, state)
        in_specs.insert(0, pl.BlockSpec((PAIR, HD, HD), lambda c: (c, 0, 0)))
    return pl.pallas_call(
        functools.partial(mixer_kernel, state is not None),
        grid=(HEADS // PAIR,),
        in_specs=in_specs,
        out_specs=pl.BlockSpec((rows, columns), lambda c: (0, c)),
        out_shape=jax.ShapeDtypeStruct((rows, width), jnp.bfloat16),
        scratch_shapes=[
            pltpu.VMEM((rows, width), jnp.bfloat16),
            pltpu.VMEM((2, 3, width, columns), jnp.bfloat16),
            pltpu.SemaphoreType.DMA((2,)),
            pltpu.SemaphoreType.DMA((2, 3)),
        ],
        compiler_params=pltpu.CompilerParams(vmem_limit_bytes=56 * MIB),
        cost_estimate=pl.CostEstimate(
            flops=2 * rows * width * 3 * width + 8 * rows * SPAN * width,
            bytes_accessed=2 * (3 * width * width + 2 * rows * width),
            transcendentals=rows * HEADS,
        ),
        name="mixer",
    )(*operands)


def incoming_state(tokens, w_lin, time_ranges):
    rows, width = tokens.shape
    packed = dot(tokens, w_lin[:, width:]).astype(jnp.bfloat16).reshape(rows, 2, HEADS, HD)
    block_total = jnp.einsum(
        "nhd,nhe->hde", packed[:, 0], packed[:, 1], preferred_element_type=jnp.float32
    )
    within = lax.axis_index("tm") // SB

    def advance_hop(turn_index, running_total):
        moved = shifted(running_total + block_total, "tm", SB)
        return jnp.where(within > 0, moved, 0.0)

    return lax.fori_loop(0, time_ranges - 1, advance_hop, jnp.zeros_like(block_total))


def pairs_kernel(hidden_ref, gain_ref, w_ref, normed_ref, *outs):
    gain = gain_ref[...].astype(jnp.float32).reshape(1, -1)
    widened = hidden_ref[...].astype(jnp.float32)
    mean_square = jnp.mean(widened * widened, axis=-1, keepdims=True)
    normed = (widened * lax.rsqrt(mean_square + epsilon) * gain).astype(jnp.bfloat16)
    normed_ref[...] = normed
    pairs = dot(normed, w_ref[...]).astype(jnp.bfloat16)
    offset = 0
    for out_ref in outs:
        for start in range(0, out_ref.shape[0], HD):
            here = slice(offset + start, offset + start + HD)
            for head in range(KVH):
                out_ref[start : start + HD, head_lanes(head)] = pairs[here, head_lanes(head)].T
        rows = out_ref.shape[0]
        out_ref[:, KVH * HD :] = pairs[offset : offset + rows, KVH * HD :]
        offset += rows


def make_pairs(hidden, gain, w_kv):
    rows, width = hidden.shape
    wide = w_kv.shape[1]
    return pl.pallas_call(
        pairs_kernel,
        out_shape=[
            jax.ShapeDtypeStruct((rows, width), jnp.bfloat16),
            jax.ShapeDtypeStruct((rows - LATE, wide), jnp.bfloat16),
            jax.ShapeDtypeStruct((LATE, wide), jnp.bfloat16),
        ],
        compiler_params=pltpu.CompilerParams(vmem_limit_bytes=16 * MIB),
        cost_estimate=pl.CostEstimate(
            flops=2 * rows * width * wide,
            bytes_accessed=2 * (2 * rows * width + width * wide + rows * wide),
            transcendentals=rows,
        ),
        name="pairs",
    )(hidden, gain, w_kv)


SCORE_SCALE = math.log2(math.e) / math.sqrt(HD)
GROUP = HEADS // KVH
LATE = 128


def keys_and_values(refs):
    both = []
    for head in range(KVH):
        keys, values = [], []
        for ref in refs:
            for start in range(0, ref.shape[0], HD):
                keys.append(ref[start : start + HD, head_lanes(head)])
            values.append(ref[:, head_lanes(KVH + head)])
        key = jnp.concatenate(keys, axis=1)
        value = jnp.concatenate(values, axis=0)
        both.append((key, jnp.concatenate([value, jnp.ones_like(value)], axis=1)))
    return both


def own_kernel(normed_ref, w_ref, first_ref, second_ref, query_ref, partial_ref, log_ref):
    both = keys_and_values([first_ref, second_ref])
    columns = GROUP * HD

    def project(group):
        lanes = slice(group * columns, (group + 1) * columns)
        query = dot(normed_ref[...], w_ref[:, lanes]).astype(jnp.bfloat16)
        query_ref[:, lanes] = query
        return query

    queries = {0: project(0)}

    def scores_of(head):
        group = head // GROUP
        return dot(queries[group][:, head_lanes(head % GROUP)], both[group][0])

    scores = scores_of(0)
    for head in range(HEADS):
        if head % GROUP == 0 and head + GROUP < HEADS:
            queries[head // GROUP + 1] = project(head // GROUP + 1)
        upcoming = scores_of(head + 1) if head + 1 < HEADS else None
        largest = jnp.max(scores, axis=-1, keepdims=True)
        raised = jnp.exp2((scores - largest) * SCORE_SCALE).astype(jnp.bfloat16)
        summed = dot(raised, both[head // GROUP][1])
        total = summed[:, HD:]
        partial_ref[:, head_lanes(head)] = summed[:, :HD] / total
        log_ref[:, head_lanes(head)] = largest * SCORE_SCALE + jnp.log2(total)
        scores = upcoming


def own_frame(normed, w_query, first, second):
    rows, width = normed.shape
    return pl.pallas_call(
        own_kernel,
        out_shape=[
            jax.ShapeDtypeStruct((rows, width), jnp.bfloat16),
            jax.ShapeDtypeStruct((rows, width), jnp.float32),
            jax.ShapeDtypeStruct((rows, width), jnp.float32),
        ],
        compiler_params=pltpu.CompilerParams(vmem_limit_bytes=32 * MIB),
        cost_estimate=pl.CostEstimate(
            flops=2 * rows * width * width + 4 * rows * rows * width,
            bytes_accessed=2 * width * width + 8 * rows * width,
            transcendentals=rows * rows * HEADS,
        ),
        name="own_frame",
    )(normed, w_query, first, second)


def earlier_kernel(last, query_ref, pairs_ref, partial_ref, log_ref, *outs):
    both = keys_and_values([pairs_ref])
    barred = jnp.where(lax.axis_index("tm") > 0, 0.0, -jnp.inf)

    def scores_of(head):
        return dot(query_ref[:, head_lanes(head)], both[head // GROUP][0])

    scores = scores_of(0)
    for head in range(HEADS):
        lanes = head_lanes(head)
        upcoming = scores_of(head + 1) if head + 1 < HEADS else None
        before = log_ref[:, lanes]
        here = jnp.max(scores, axis=-1, keepdims=True) * SCORE_SCALE + barred
        largest = jnp.maximum(jnp.broadcast_to(here, before.shape), before)
        below = jnp.concatenate([largest - barred] * (scores.shape[1] // HD), axis=1)
        raised = jnp.exp2(scores * SCORE_SCALE - below).astype(jnp.bfloat16)
        summed = dot(raised, both[head // GROUP][1])
        share = jnp.exp2(before - largest)
        total = share + summed[:, HD:]
        mixed = (partial_ref[:, lanes] * share + summed[:, :HD]) / total
        if last:
            outs[0][:, lanes] = mixed.astype(jnp.bfloat16)
        else:
            outs[0][:, lanes] = mixed
            outs[1][:, lanes] = largest + jnp.log2(total)
        scores = upcoming


def earlier_frame(last, query, pairs, partial, log_total):
    rows, width = query.shape
    if last:
        out_shape = jax.ShapeDtypeStruct((rows, width), jnp.bfloat16)
    else:
        out_shape = [jax.ShapeDtypeStruct((rows, width), jnp.float32)] * 2
    return pl.pallas_call(
        functools.partial(earlier_kernel, last),
        out_shape=out_shape,
        compiler_params=pltpu.CompilerParams(vmem_limit_bytes=32 * MIB),
        cost_estimate=pl.CostEstimate(
            flops=4 * rows * pairs.shape[0] * width,
            bytes_accessed=10 * rows * width,
            transcendentals=rows * pairs.shape[0] * HEADS,
        ),
        name="earlier_frame",
    )(query, pairs, partial, log_total)


def to_frames(hidden):
    rows, columns = hidden.shape
    teams = [[t * SB + s for s in range(SB)] for t in range(lax.axis_size("tm") // SB)]
    moved = lax.all_to_all(
        hidden.reshape(SB, rows // SB, columns), "tm", 0, 0, axis_index_groups=teams, tiled=True
    )
    return moved.reshape(rows, columns)


def body(space_time, w_lin, gain_lin, w_query, w_kv, frame_attention_gain):
    tokens = space_time[0]
    time_ranges = lax.axis_size("tm") // SB
    state = incoming_state(tokens, w_lin, time_ranges) if time_ranges > 1 else None
    frame_rows = to_frames(mixer(tokens, w_lin, gain_lin, state))
    normed, first, second = make_pairs(frame_rows, frame_attention_gain, w_kv)
    earlier_first = shifted(first, "tm", 1)
    earlier_second = shifted(second, "tm", 1)
    query, partial, log_total = own_frame(normed, w_query, first, second)
    partial, log_total = earlier_frame(False, query, earlier_first, partial, log_total)
    attended = earlier_frame(True, query, earlier_second, partial, log_total)
    return attended[None]


def solution(mesh):
    placed = (P(("groups", "tm"), None, None), P(), P(), P(), P(), P())
    return jax.shard_map(
        body, mesh=mesh, in_specs=placed, out_specs=P(("groups", "tm"), None, None), check_vma=False
    )
```

time: 62.1 us -> 58.3 us (0.939)
  starting transfers between devices: 39.6 us -> 5.2 us
  blocking collectives: 0 us -> 32.8 us
  waiting for transfers between devices: 1.72 us -> 0.01 us
    all_to_all x0 -> x1, blocking collectives: none -> 32.8 us  [to_frames(): lax.all_to_all(hidden.reshape(SB, rows // SB, columns), 'tm', 0, 0, axis_...]
    ppermute x20 -> x0, starting transfers between devices: 32.6 us -> none  [swap(): return lax.ppermute(tile, 'tm', route)]
    ppermute x2, starting transfers between devices: 6.99 us -> 5.2 us  [shifted(): return lax.ppermute(block, axis, route)]
    ppermute x20 -> x0, waiting for transfers between devices: 1.71 us -> none  [swap(): return lax.ppermute(tile, 'tm', route)]
    pallas_call x3 -> x1, Pallas kernels: 10.3 us -> 9.95 us  [mixer(): pl.pallas_call(functools.partial(mixer_kernel, state is not None), grid=(...]
  transfers between devices with their start and end apart: 22 -> 2, of which waited for: 5 -> 0; matrix products, arithmetic and copies ran while one was open for 0% -> 0% of each run, Pallas kernels for 15% -> 11%
where the time goes in v7:
time: 58.3 us; the launch traced here: 58.1 us
  blocking collectives  32.8 us (56%)
  Pallas kernels  20 us (34%)
  starting transfers between devices  5.2 us (9%)
    all_to_all x1, blocking collectives, to_frames(): lax.all_to_all(hidden.reshape(SB, rows // SB, columns), 'tm', 0, 0, axis_...  32.8 us
    pallas_call x1, Pallas kernels, mixer(): pl.pallas_call(functools.partial(mixer_kernel, state is not None), grid=(...  9.95 us
    pallas_call x2, Pallas kernels, earlier_frame(): pl.pallas_call(functools.partial(earlier_kernel, last), out_shape=out_sha...  5.29 us
    ppermute x2, starting transfers between devices, shifted(): return lax.ppermute(block, axis, route)  5.2 us
    pallas_call x1, Pallas kernels, own_frame(): pl.pallas_call(own_kernel, out_shape=[jax.ShapeDtypeStruct((rows, width),...  3.74 us
  transfers between devices with their start and end apart: 2, of which 0 were waited for; matrix products, arithmetic and copies ran while one was open for 0% of the time, Pallas kernels for 11%

profile of v7, /device:TPU:1, one launch (start us, length us, event | category | flops | bytes accessed | tf_op | source)
XLA Modules:
  0.0 58.1 jit_solution(9585715736658716212)
XLA Ops:
  0.0 10.0 %mixer.1 = bf16[512,1024]{1,0:T(8,128)(2,1)} custom-call(bf16[512,1024]{1,0:T(8,128)(2,1)} %bitcast.6, bf16[1024,3072]{1,0:T(8,128)(2,1)} %refs_1_.1, bf16[1024]{0:T(1024)(128)(2,1)} %refs_2_.1), custom_call_target="tpu_custom_call" | custom-call | flops 3758096384 | bytes 8388608 | tf_op jit(solution)/shard_map/mixer/pallas_call | solution.py:164
  10.0 0.0 copy-start
  10.0 0.0 copy-start.1
  10.0 0.0 copy-start.2
  10.0 32.8 %all_to_all.5 = bf16[16,32,1024]{2,1,0:T(8,128)(2,1)S(1)} all-to-all(bf16[16,32,1024]{2,1,0:T(8,128)(2,1)} %bitcast.5), channel_id=1, replica_groups={{0,1,2,3,4,5,6,7,8,9,10,11,12,13,14,15},{16,17,18,19,20,21,22,23,24,25,..., dimensions={0} | all-to-all | bytes 2097152 | tf_op jit(solution)/shard_map/all_to_all | solution.py:357
  42.8 0.0 copy-done
  42.8 0.0 copy-done.1
  42.8 1.0 %pairs.1 = (bf16[512,1024]{1,0:T(8,128)(2,1)S(1)}, bf16[384,512]{1,0:T(8,128)(2,1)S(1)}, bf16[128,512]{1,0:T(8,128)(2,1)S(1)}) custom-call(bf16[512,1024]{1,0:T(8,128)(2,1)S(1)} %bitcast.4, bf16[1024]{0:T(1024)(128)(2,1)S(1)} %copy-done.1, bf16[1024,512]{1,0:T(8,128)(2,1)S(1)} %copy-done), custom_call_target="tpu_custom_call" | custom-call | flops 536870912 | bytes 3670016 | tf_op jit(solution)/shard_map/pairs/pallas_call | solution.py:222
  43.8 2.5 %collective-permute-start.1 = (bf16[384,512]{1,0:T(8,128)(2,1)S(1)}, bf16[384,512]{1,0:T(8,128)(2,1)S(1)}, u32[]{:S(2)}, u32[]{:S(2)}) collective-permute-start(bf16[384,512]{1,0:T(8,128)(2,1)S(1)} %get-tuple-element.14.first_ref), channel_id=1, source_target_pairs={{0,1},{1,2},{2,3},{3,4},{4,5},{5,6},{6,7},{7,8},{8,9},{9,10},{10,1... | collective-permute-start | bytes 1179656 | tf_op jit(solution)/shard_map/ppermute | solution.py:25
  46.3 2.7 %collective-permute-start = (bf16[128,512]{1,0:T(8,128)(2,1)S(1)}, bf16[128,512]{1,0:T(8,128)(2,1)S(1)}, u32[]{:S(2)}, u32[]{:S(2)}) collective-permute-start(bf16[128,512]{1,0:T(8,128)(2,1)S(1)} %get-tuple-element.15.second_ref), channel_id=1, source_target_pairs={{0,1},{1,2},{2,3},{3,4},{4,5},{5,6},{6,7},{7,8},{8,9},{9,10},{10,1... | collective-permute-start | bytes 393224 | tf_op jit(solution)/shard_map/ppermute | solution.py:25
  49.0 0.0 copy-done.2
  49.0 3.7 %own_frame.1 = (bf16[512,1024]{1,0:T(8,128)(2,1)S(1)}, f32[512,1024]{1,0:T(8,128)S(1)}, f32[512,1024]{1,0:T(8,128)S(1)}) custom-call(bf16[512,1024]{1,0:T(8,128)(2,1)S(1)} %get-tuple-element.13.normed_ref, bf16[1024,1024]{1,0:T(8,128)(2,1)S(1)} %copy-done.2, bf16[384,512]{1,0:T(8,128)(2,1)S(1)} %get-tuple-element.14.first_ref, ...), custom_call_target="tpu_custom_call" | custom-call | flops 2147483648 | bytes 6291456 | tf_op jit(solution)/shard_map/own_frame/pallas_call | solution.py:290
  52.8 0.0 collective-permute-done.1.pairs_ref
  52.8 2.7 %earlier_frame.2 = (f32[512,1024]{1,0:T(8,128)S(1)}, f32[512,1024]{1,0:T(8,128)S(1)}) custom-call(bf16[512,1024]{1,0:T(8,128)(2,1)S(1)} %get-tuple-element.16.query_ref, bf16[384,512]{1,0:T(8,128)(2,1)S(1)} %collective-permute-done.1.pairs_ref, f32[512,1024]{1,0:T(8,128)S(1)} %get-tuple-element.17.partial_ref, f32[512,1024]{1,0:T(8,128)S(1)} %get-tuple-element.18.log_ref), custom_call_target="tpu_custom_call" | custom-call | flops 805306368 | bytes 5242880 | tf_op jit(solution)/shard_map/earlier_frame/pallas_call | solution.py:341
  55.5 0.0 collective-permute-done.pairs_ref
  55.5 2.5 %earlier_frame.3 = bf16[512,1024]{1,0:T(8,128)(2,1)} custom-call(bf16[512,1024]{1,0:T(8,128)(2,1)S(1)} %get-tuple-element.16.query_ref, bf16[128,512]{1,0:T(8,128)(2,1)S(1)} %collective-permute-done.pairs_ref, f32[512,1024]{1,0:T(8,128)S(1)} %get-tuple-element.19.partial_ref, f32[512,1024]{1,0:T(8,128)S(1)} %get-tuple-element.20.log_ref), custom_call_target="tpu_custom_call" | custom-call | flops 268435456 | bytes 5242880 | tf_op jit(solution)/shard_map/earlier_frame/pallas_call | solution.py:341
Async XLA Ops:
  10.0 32.9 %copy-start = (bf16[1024,512]{1,0:T(8,128)(2,1)S(1)}, bf16[1024,512]{1,0:T(8,128)(2,1)}, u32[]{:S(2)}) copy-start(bf16[1024,512]{1,0:T(8,128)(2,1)} %w_ref.2) | copy-start | bytes 3145732
  10.0 32.9 %copy-start.1 = (bf16[1024]{0:T(1024)(128)(2,1)S(1)}, bf16[1024]{0:T(1024)(128)(2,1)}, u32[]{:S(2)}) copy-start(bf16[1024]{0:T(1024)(128)(2,1)} %gain_ref.1) | copy-start | bytes 6148
  10.0 39.0 %copy-start.2 = (bf16[1024,1024]{1,0:T(8,128)(2,1)S(1)}, bf16[1024,1024]{1,0:T(8,128)(2,1)}, u32[]{:S(2)}) copy-start(bf16[1024,1024]{1,0:T(8,128)(2,1)} %w_ref.3) | copy-start | bytes 6291460
  43.8 9.0 %collective-permute-start.1 = (bf16[384,512]{1,0:T(8,128)(2,1)S(1)}, bf16[384,512]{1,0:T(8,128)(2,1)S(1)}, u32[]{:S(2)}, u32[]{:S(2)}) collective-permute-start(bf16[384,512]{1,0:T(8,128)(2,1)S(1)} %get-tuple-element.14.first_ref), channel_id=1, source_target_pairs={{0,1},{1,2},{2,3},{3,4},{4,5},{5,6},{6,7},{7,8},{8,9},{9,10},{10,1... | collective-permute-start | bytes 1179656 | tf_op jit(solution)/shard_map/ppermute | solution.py:25
  46.3 9.2 %collective-permute-start = (bf16[128,512]{1,0:T(8,128)(2,1)S(1)}, bf16[128,512]{1,0:T(8,128)(2,1)S(1)}, u32[]{:S(2)}, u32[]{:S(2)}) collective-permute-start(bf16[128,512]{1,0:T(8,128)(2,1)S(1)} %get-tuple-element.15.second_ref), channel_id=1, source_target_pairs={{0,1},{1,2},{2,3},{3,4},{4,5},{5,6},{6,7},{7,8},{8,9},{9,10},{10,1... | collective-permute-start | bytes 393224 | tf_op jit(solution)/shard_map/ppermute | solution.py:25

commit v8 on v7

--- a/solution.py
+++ b/solution.py
@@ -13,7 +13,7 @@
 KVH = 2
 SB = 16
 SPAN = 128
-PAIR = 2
+PAIR = 4
 
 epsilon = 1e-06
 MIB = 1 << 20
@@ -199,10 +199,9 @@
 
 
 def pairs_kernel(hidden_ref, gain_ref, w_ref, normed_ref, *outs):
-    gain = gain_ref[...].astype(jnp.float32).reshape(1, -1)
     widened = hidden_ref[...].astype(jnp.float32)
     mean_square = jnp.mean(widened * widened, axis=-1, keepdims=True)
-    normed = (widened * lax.rsqrt(mean_square + epsilon) * gain).astype(jnp.bfloat16)
+    normed = (widened * lax.rsqrt(mean_square + epsilon) * gain_ref[...]).astype(jnp.bfloat16)
     normed_ref[...] = normed
     pairs = dot(normed, w_ref[...]).astype(jnp.bfloat16)
     offset = 0
@@ -255,8 +254,8 @@
     return both
 
 
-def own_kernel(normed_ref, w_ref, first_ref, second_ref, query_ref, partial_ref, log_ref):
-    both = keys_and_values([first_ref, second_ref])
+def own_kernel(normed_ref, w_ref, first_ref, last_ref, query_ref, sum_ref, total_ref, top_ref):
+    both = keys_and_values([first_ref, last_ref])
     columns = GROUP * HD
 
     def project(group):
@@ -276,24 +275,22 @@
         if head % GROUP == 0 and head + GROUP < HEADS:
             queries[head // GROUP + 1] = project(head // GROUP + 1)
         upcoming = scores_of(head + 1) if head + 1 < HEADS else None
+        lanes = head_lanes(head)
         largest = jnp.max(scores, axis=-1, keepdims=True)
         raised = jnp.exp2((scores - largest) * SCORE_SCALE).astype(jnp.bfloat16)
         summed = dot(raised, both[head // GROUP][1])
-        total = summed[:, HD:]
-        partial_ref[:, head_lanes(head)] = summed[:, :HD] / total
-        log_ref[:, head_lanes(head)] = largest * SCORE_SCALE + jnp.log2(total)
+        sum_ref[:, lanes] = summed[:, :HD]
+        total_ref[:, lanes] = summed[:, HD:]
+        top_ref[:, lanes] = jnp.broadcast_to(largest * SCORE_SCALE, (scores.shape[0], HD))
         scores = upcoming
 
 
-def own_frame(normed, w_query, first, second):
+def own_frame(normed, w_query, first, last):
     rows, width = normed.shape
     return pl.pallas_call(
         own_kernel,
-        out_shape=[
-            jax.ShapeDtypeStruct((rows, width), jnp.bfloat16),
-            jax.ShapeDtypeStruct((rows, width), jnp.float32),
-            jax.ShapeDtypeStruct((rows, width), jnp.float32),
-        ],
+        out_shape=[jax.ShapeDtypeStruct((rows, width), jnp.bfloat16)]
+        + [jax.ShapeDtypeStruct((rows, width), jnp.float32)] * 3,
         compiler_params=pltpu.CompilerParams(vmem_limit_bytes=32 * MIB),
         cost_estimate=pl.CostEstimate(
             flops=2 * rows * width * width + 4 * rows * rows * width,
@@ -301,46 +298,65 @@
             transcendentals=rows * rows * HEADS,
         ),
         name="own_frame",
-    )(normed, w_query, first, second)
-
-
-def earlier_kernel(last, query_ref, pairs_ref, partial_ref, log_ref, *outs):
+    )(normed, w_query, first, last)
+
+
+def earlier_kernel(last, query_ref, pairs_ref, sum_ref, total_ref, top_ref, *refs):
     both = keys_and_values([pairs_ref])
     barred = jnp.where(lax.axis_index("tm") > 0, 0.0, -jnp.inf)
 
     def scores_of(head):
         return dot(query_ref[:, head_lanes(head)], both[head // GROUP][0])
 
+    copies = []
     scores = scores_of(0)
     for head in range(HEADS):
         lanes = head_lanes(head)
         upcoming = scores_of(head + 1) if head + 1 < HEADS else None
-        before = log_ref[:, lanes]
+        before = top_ref[:, lanes]
         here = jnp.max(scores, axis=-1, keepdims=True) * SCORE_SCALE + barred
         largest = jnp.maximum(jnp.broadcast_to(here, before.shape), before)
         below = jnp.concatenate([largest - barred] * (scores.shape[1] // HD), axis=1)
         raised = jnp.exp2(scores * SCORE_SCALE - below).astype(jnp.bfloat16)
         summed = dot(raised, both[head // GROUP][1])
         share = jnp.exp2(before - largest)
-        total = share + summed[:, HD:]
-        mixed = (partial_ref[:, lanes] * share + summed[:, :HD]) / total
+        mixed = sum_ref[:, lanes] * share + summed[:, :HD]
+        total = total_ref[:, lanes] * share + summed[:, HD:]
         if last:
-            outs[0][:, lanes] = mixed.astype(jnp.bfloat16)
+            out_hbm, out_ref, sent = refs
+            out_ref[:, lanes] = (mixed / total).astype(jnp.bfloat16)
+            if head % 2:
+                columns = slice((head - 1) * HD, (head + 1) * HD)
+                copies.append(
+                    pltpu.make_async_copy(
+                        out_ref.at[:, columns], out_hbm.at[:, columns], sent.at[head // 2]
+                    )
+                )
+                copies[-1].start()
         else:
-            outs[0][:, lanes] = mixed
-            outs[1][:, lanes] = largest + jnp.log2(total)
+            refs[0][:, lanes] = mixed
+            refs[1][:, lanes] = total
+            refs[2][:, lanes] = largest
         scores = upcoming
-
-
-def earlier_frame(last, query, pairs, partial, log_total):
+    for copy in copies:
+        copy.wait()
+
+
+def earlier_frame(last, query, pairs, *so_far):
     rows, width = query.shape
     if last:
-        out_shape = jax.ShapeDtypeStruct((rows, width), jnp.bfloat16)
+        extra = dict(
+            out_shape=jax.ShapeDtypeStruct((rows, width), jnp.bfloat16),
+            out_specs=pl.BlockSpec(memory_space=pl.ANY),
+            scratch_shapes=[
+                pltpu.VMEM((rows, width), jnp.bfloat16),
+                pltpu.SemaphoreType.DMA((HEADS // 2,)),
+            ],
+        )
     else:
-        out_shape = [jax.ShapeDtypeStruct((rows, width), jnp.float32)] * 2
+        extra = dict(out_shape=[jax.ShapeDtypeStruct((rows, width), jnp.float32)] * 3)
     return pl.pallas_call(
         functools.partial(earlier_kernel, last),
-        out_shape=out_shape,
         compiler_params=pltpu.CompilerParams(vmem_limit_bytes=32 * MIB),
         cost_estimate=pl.CostEstimate(
             flops=4 * rows * pairs.shape[0] * width,
@@ -348,7 +364,8 @@
             transcendentals=rows * pairs.shape[0] * HEADS,
         ),
         name="earlier_frame",
-    )(query, pairs, partial, log_total)
+        **extra,
+    )(query, pairs, *so_far)
 
 
 def to_frames(hidden):
@@ -364,13 +381,16 @@
     tokens = space_time[0]
     time_ranges = lax.axis_size("tm") // SB
     state = incoming_state(tokens, w_lin, time_ranges) if time_ranges > 1 else None
-    frame_rows = to_frames(mixer(tokens, w_lin, gain_lin, state))
-    normed, first, second = make_pairs(frame_rows, frame_attention_gain, w_kv)
+    hidden = mixer(tokens, w_lin, gain_lin, state)
+    hidden, gain = lax.optimization_barrier((hidden, frame_attention_gain))
+    frame_rows = to_frames(hidden)
+    gain = gain.astype(jnp.float32).reshape(1, -1)
+    normed, first, last = make_pairs(frame_rows, gain, w_kv)
     earlier_first = shifted(first, "tm", 1)
-    earlier_second = shifted(second, "tm", 1)
-    query, partial, log_total = own_frame(normed, w_query, first, second)
-    partial, log_total = earlier_frame(False, query, earlier_first, partial, log_total)
-    attended = earlier_frame(True, query, earlier_second, partial, log_total)
+    earlier_last = shifted(last, "tm", 1)
+    query, *so_far = own_frame(normed, w_query, first, last)
+    so_far = earlier_frame(False, query, earlier_first, *so_far)
+    attended = earlier_frame(True, query, earlier_last, *so_far)
     return attended[None]
 
 

time: 58.3 us -> 58.1 us (level)
  the two profiles are of different devices: /device:TPU:1 before, /device:TPU:16 now
where the time goes in v8:
time: 58.1 us; the launch traced here: 57.9 us
  waiting for transfers between devices  27.6 us (48%)
  Pallas kernels  20 us (34%)
  starting transfers between devices  10.2 us (18%)
    all_to_all x1, waiting for transfers between devices, to_frames(): lax.all_to_all(hidden.reshape(SB, rows // SB, columns), 'tm', 0, 0, axis_...  25.2 us
    pallas_call x1, Pallas kernels, mixer(): pl.pallas_call(functools.partial(mixer_kernel, state is not None), grid=(...  9.83 us
    all_to_all x1, starting transfers between devices, to_frames(): lax.all_to_all(hidden.reshape(SB, rows // SB, columns), 'tm', 0, 0, axis_...  6.33 us
    pallas_call x2, Pallas kernels, earlier_frame(): pl.pallas_call(functools.partial(earlier_kernel, last), compiler_params=p...  5.5 us
    ppermute x2, starting transfers between devices, shifted(): return lax.ppermute(block, axis, route)  3.84 us
    pallas_call x1, Pallas kernels, own_frame(): pl.pallas_call(own_kernel, out_shape=[jax.ShapeDtypeStruct((rows, width),...  3.7 us
    ppermute x2, waiting for transfers between devices, shifted(): return lax.ppermute(block, axis, route)  2.43 us
  transfers between devices with their start and end apart: 3, of which 2 were waited for; matrix products, arithmetic and copies ran while one was open for 0% of the time, Pallas kernels for 12%

profile of v8, /device:TPU:16, one launch (start us, length us, event | category | flops | bytes accessed | tf_op | source)
XLA Modules:
  0.0 57.9 jit_solution(15597217182316609424)
XLA Ops:
  0.0 9.8 %mixer.1 = bf16[512,1024]{1,0:T(8,128)(2,1)} custom-call(bf16[512,1024]{1,0:T(8,128)(2,1)} %bitcast.8, bf16[1024,3072]{1,0:T(8,128)(2,1)} %refs_1_.1, bf16[1024]{0:T(1024)(128)(2,1)} %refs_2_.1), custom_call_target="tpu_custom_call" | custom-call | flops 3758096384 | bytes 8388608 | tf_op jit(solution)/shard_map/mixer/pallas_call | solution.py:164
  9.8 0.0 copy-start.2
  9.9 0.0 copy-start
  9.9 6.3 %all-to-all-start = ((bf16[16,32,1024]{2,1,0:T(8,128)(2,1)}), bf16[16,32,1024]{2,1,0:T(8,128)(2,1)S(1)}, u32[]{:S(2)}, u32[]{:S(2)}) async-start(bf16[16,32,1024]{2,1,0:T(8,128)(2,1)} %bitcast.7), calls=%async_computation | async-start | bytes 2097152 | tf_op jit(solution)/shard_map/all_to_all | solution.py:374
  16.2 0.0 copy-done.2
  16.2 25.2 %all-to-all-done = bf16[16,32,1024]{2,1,0:T(8,128)(2,1)S(1)} async-done(((bf16[16,32,1024]{2,1,0:T(8,128)(2,1)}), bf16[16,32,1024]{2,1,0:T(8,128)(2,1)S(1)}, u32[]{:S(2)}, u32[]{:S(2)}) %all-to-all-start) | async-done | bytes 1048608 | tf_op jit(solution)/shard_map/all_to_all | solution.py:374
  41.4 0.0 copy-start.1
  41.4 0.0 copy-done
  41.4 1.0 %pairs.1 = (bf16[512,1024]{1,0:T(8,128)(2,1)S(1)}, bf16[384,512]{1,0:T(8,128)(2,1)S(1)}, bf16[128,512]{1,0:T(8,128)(2,1)S(1)}) custom-call(bf16[512,1024]{1,0:T(8,128)(2,1)S(1)} %bitcast.5, f32[1,1024]{1,0:T(1,128)S(1)} %bitcast.6, bf16[1024,512]{1,0:T(8,128)(2,1)S(1)} %copy-done), custom_call_target="tpu_custom_call" | custom-call | flops 536870912 | bytes 3670016 | tf_op jit(solution)/shard_map/pairs/pallas_call | solution.py:221
  42.3 1.9 %collective-permute-start.1 = (bf16[384,512]{1,0:T(8,128)(2,1)S(1)}, bf16[384,512]{1,0:T(8,128)(2,1)S(1)}, u32[]{:S(2)}, u32[]{:S(2)}) collective-permute-start(bf16[384,512]{1,0:T(8,128)(2,1)S(1)} %get-tuple-element.20.first_ref), channel_id=1, source_target_pairs={{0,1},{1,2},{2,3},{3,4},{4,5},{5,6},{6,7},{7,8},{8,9},{9,10},{10,1... | collective-permute-start | bytes 1179656 | tf_op jit(solution)/shard_map/ppermute | solution.py:25
  44.3 1.9 %collective-permute-start = (bf16[128,512]{1,0:T(8,128)(2,1)S(1)}, bf16[128,512]{1,0:T(8,128)(2,1)S(1)}, u32[]{:S(2)}, u32[]{:S(2)}) collective-permute-start(bf16[128,512]{1,0:T(8,128)(2,1)S(1)} %get-tuple-element.21.last_ref), channel_id=1, source_target_pairs={{0,1},{1,2},{2,3},{3,4},{4,5},{5,6},{6,7},{7,8},{8,9},{9,10},{10,1... | collective-permute-start | bytes 393224 | tf_op jit(solution)/shard_map/ppermute | solution.py:25
  46.2 0.0 copy-done.1
  46.2 3.7 %own_frame.1 = (bf16[512,1024]{1,0:T(8,128)(2,1)S(1)}, f32[512,1024]{1,0:T(8,128)S(1)}, f32[512,1024]{1,0:T(8,128)S(1)}, f32[512,1024]{1,0:T(8,128)S(1)}) custom-call(bf16[512,1024]{1,0:T(8,128)(2,1)S(1)} %get-tuple-element.19.normed_ref, bf16[1024,1024]{1,0:T(8,128)(2,1)S(1)} %copy-done.1, bf16[384,512]{1,0:T(8,128)(2,1)S(1)} %get-tuple-element.20.first_ref, ...), custom_call_target="tpu_custom_call" | custom-call | flops 2147483648 | bytes 6291456 | tf_op jit(solution)/shard_map/own_frame/pallas_call | solution.py:290
  49.9 2.4 %collective-permute-done.1.pairs_ref = bf16[384,512]{1,0:T(8,128)(2,1)S(1)} collective-permute-done((bf16[384,512]{1,0:T(8,128)(2,1)S(1)}, bf16[384,512]{1,0:T(8,128)(2,1)S(1)}, u32[]{:S(2)}, u32[]{:S(2)}) %collective-permute-start.1) | collective-permute-done | bytes 393248 | tf_op jit(solution)/shard_map/ppermute | solution.py:25
  52.3 3.1 %earlier_frame.2 = (f32[512,1024]{1,0:T(8,128)S(1)}, f32[512,1024]{1,0:T(8,128)S(1)}, f32[512,1024]{1,0:T(8,128)S(1)}) custom-call(bf16[512,1024]{1,0:T(8,128)(2,1)S(1)} %get-tuple-element.22.query_ref, bf16[384,512]{1,0:T(8,128)(2,1)S(1)} %collective-permute-done.1.pairs_ref, f32[512,1024]{1,0:T(8,128)S(1)} %get-tuple-element.23.sum_ref, ...), custom_call_target="tpu_custom_call" | custom-call | flops 805306368 | bytes 5242880 | tf_op jit(solution)/shard_map/earlier_frame/pallas_call | solution.py:358
  55.4 0.0 collective-permute-done.pairs_ref
  55.4 2.4 %earlier_frame.3 = bf16[512,1024]{1,0:T(8,128)(2,1)} custom-call(bf16[512,1024]{1,0:T(8,128)(2,1)S(1)} %get-tuple-element.22.query_ref, bf16[128,512]{1,0:T(8,128)(2,1)S(1)} %collective-permute-done.pairs_ref, f32[512,1024]{1,0:T(8,128)S(1)} %get-tuple-element.26.sum_ref, f32[512,1024]{1,0:T(8,128)S(1)} %get-tuple-element.27.total_ref, ...), custom_call_target="tpu_custom_call" | custom-call | flops 268435456 | bytes 5242880 | tf_op jit(solution)/shard_map/earlier_frame/pallas_call | solution.py:358
  (1 shorter events, 0.0 us)
Async XLA Ops:
  9.8 6.4 %copy-start.2 = (bf16[1024]{0:T(1024)(128)(2,1)S(1)}, bf16[1024]{0:T(1024)(128)(2,1)}, u32[]{:S(2)}) copy-start(bf16[1024]{0:T(1024)(128)(2,1)} %param.11) | copy-start | bytes 6148
  9.9 31.5 %copy-start = (bf16[1024,512]{1,0:T(8,128)(2,1)S(1)}, bf16[1024,512]{1,0:T(8,128)(2,1)}, u32[]{:S(2)}) copy-start(bf16[1024,512]{1,0:T(8,128)(2,1)} %w_ref.2) | copy-start | bytes 3145732
  9.9 31.5 %all-to-all-start = ((bf16[16,32,1024]{2,1,0:T(8,128)(2,1)}), bf16[16,32,1024]{2,1,0:T(8,128)(2,1)S(1)}, u32[]{:S(2)}, u32[]{:S(2)}) async-start(bf16[16,32,1024]{2,1,0:T(8,128)(2,1)} %bitcast.7), calls=%async_computation | async-start | bytes 2097152 | tf_op jit(solution)/shard_map/all_to_all | solution.py:374
  41.4 4.8 %copy-start.1 = (bf16[1024,1024]{1,0:T(8,128)(2,1)S(1)}, bf16[1024,1024]{1,0:T(8,128)(2,1)}, u32[]{:S(2)}) copy-start(bf16[1024,1024]{1,0:T(8,128)(2,1)} %w_ref.3) | copy-start | bytes 6291460
  42.3 10.0 %collective-permute-start.1 = (bf16[384,512]{1,0:T(8,128)(2,1)S(1)}, bf16[384,512]{1,0:T(8,128)(2,1)S(1)}, u32[]{:S(2)}, u32[]{:S(2)}) collective-permute-start(bf16[384,512]{1,0:T(8,128)(2,1)S(1)} %get-tuple-element.20.first_ref), channel_id=1, source_target_pairs={{0,1},{1,2},{2,3},{3,4},{4,5},{5,6},{6,7},{7,8},{8,9},{9,10},{10,1... | collective-permute-start | bytes 1179656 | tf_op jit(solution)/shard_map/ppermute | solution.py:25
  44.3 11.2 %collective-permute-start = (bf16[128,512]{1,0:T(8,128)(2,1)S(1)}, bf16[128,512]{1,0:T(8,128)(2,1)S(1)}, u32[]{:S(2)}, u32[]{:S(2)}) collective-permute-start(bf16[128,512]{1,0:T(8,128)(2,1)S(1)} %get-tuple-element.21.last_ref), channel_id=1, source_target_pairs={{0,1},{1,2},{2,3},{3,4},{4,5},{5,6},{6,7},{7,8},{8,9},{9,10},{10,1... | collective-permute-start | bytes 393224 | tf_op jit(solution)/shard_map/ppermute | solution.py:25

commit v9 on v8

--- a/solution.py
+++ b/solution.py
@@ -104,10 +104,10 @@
 
     @pl.when(step == 0)
     def _():
+        weight_copy(0, 0, 0).start()
         token_copy(0).start()
-        weight_copy(0, 0, 0).start()
+        token_copy(1).start()
         weight_copy(0, 0, 1).start()
-        token_copy(1).start()
         weight_copy(0, 0, 2).start()
 
     @pl.when(step + 1 < pl.num_programs(0))
@@ -120,16 +120,16 @@
         token_copy(0).wait()
         token_copy(1).wait()
 
-    for part in range(3):
-        weight_copy(step, slot, part).wait()
-
     states = [state_ref[head] if has_state else None for head in range(PAIR)]
     start = pl.multiple_of(step * columns, columns)
     gains = gain_ref[pl.ds(start, columns)].astype(jnp.float32).reshape(1, columns)
 
-    def project(offset):
-        tokens = tokens_ref[offset : offset + block]
-        return [dot(tokens, weights[slot, part]).astype(jnp.bfloat16) for part in range(3)]
+    packed = [[], []]
+    for part in range(3):
+        weight_copy(step, slot, part).wait()
+        for index in range(2):
+            tokens = tokens_ref[index * block : (index + 1) * block]
+            packed[index].append(dot(tokens, weights[slot, part]).astype(jnp.bfloat16))
 
     def store(offset, mixed):
         for head, here, out in mixed:
@@ -141,12 +141,9 @@
             residual = tokens_ref[here, there].astype(jnp.float32)
             out_ref[here, lanes] = (residual + normed).astype(jnp.bfloat16)
 
-    parts = project(0)
-    upcoming = project(block)
-    mixed, states = mix_heads(*parts, states)
-    store(0, mixed)
-    mixed, states = mix_heads(*upcoming, states)
-    store(block, mixed)
+    for index in range(2):
+        mixed, states = mix_heads(*packed[index], states)
+        store(index * block, mixed)
 
 
 def mixer(tokens, w_lin, gain_lin, state):
@@ -237,7 +234,7 @@
 
 SCORE_SCALE = math.log2(math.e) / math.sqrt(HD)
 GROUP = HEADS // KVH
-LATE = 128
+LATE = 256
 
 
 def keys_and_values(refs):

time: 58.1 us -> 57.5 us (0.990)
  the two profiles are of different devices: /device:TPU:16 before, /device:TPU:1 now
where the time goes in v9:
time: 57.5 us; the launch traced here: 56.6 us
  waiting for transfers between devices  23.1 us (40%)
  Pallas kernels  20 us (35%)
  starting transfers between devices  13.4 us (23%)
    all_to_all x1, waiting for transfers between devices, to_frames(): lax.all_to_all(hidden.reshape(SB, rows // SB, columns), 'tm', 0, 0, axis_...  23.1 us
    pallas_call x1, Pallas kernels, mixer(): pl.pallas_call(functools.partial(mixer_kernel, state is not None), grid=(...  10.5 us
    all_to_all x1, starting transfers between devices, to_frames(): lax.all_to_all(hidden.reshape(SB, rows // SB, columns), 'tm', 0, 0, axis_...  7.49 us
    ppermute x2, starting transfers between devices, shifted(): return lax.ppermute(block, axis, route)  5.9 us
    pallas_call x2, Pallas kernels, earlier_frame(): pl.pallas_call(functools.partial(earlier_kernel, last), compiler_params=p...  4.83 us
    pallas_call x1, Pallas kernels, own_frame(): pl.pallas_call(own_kernel, out_shape=[jax.ShapeDtypeStruct((rows, width),...  3.7 us
  transfers between devices with their start and end apart: 3, of which 1 were waited for; matrix products, arithmetic and copies ran while one was open for 0% of the time, Pallas kernels for 10%

profile of v9, /device:TPU:1, one launch (start us, length us, event | category | flops | bytes accessed | tf_op | source)
XLA Modules:
  0.0 56.6 jit_solution(7711039245193103637)
XLA Ops:
  0.0 10.5 %mixer.1 = bf16[512,1024]{1,0:T(8,128)(2,1)} custom-call(bf16[512,1024]{1,0:T(8,128)(2,1)} %bitcast.8, bf16[1024,3072]{1,0:T(8,128)(2,1)} %refs_1_.1, bf16[1024]{0:T(1024)(128)(2,1)} %refs_2_.1), custom_call_target="tpu_custom_call" | custom-call | flops 3758096384 | bytes 8388608 | tf_op jit(solution)/shard_map/mixer/pallas_call | solution.py:161
  10.5 0.0 copy-start.2
  10.5 0.0 copy-start
  10.5 7.5 %all-to-all-start = ((bf16[16,32,1024]{2,1,0:T(8,128)(2,1)}), bf16[16,32,1024]{2,1,0:T(8,128)(2,1)S(1)}, u32[]{:S(2)}, u32[]{:S(2)}) async-start(bf16[16,32,1024]{2,1,0:T(8,128)(2,1)} %bitcast.7), calls=%async_computation | async-start | bytes 2097152 | tf_op jit(solution)/shard_map/all_to_all | solution.py:371
  18.0 0.0 copy-done.2
  18.0 23.1 %all-to-all-done = bf16[16,32,1024]{2,1,0:T(8,128)(2,1)S(1)} async-done(((bf16[16,32,1024]{2,1,0:T(8,128)(2,1)}), bf16[16,32,1024]{2,1,0:T(8,128)(2,1)S(1)}, u32[]{:S(2)}, u32[]{:S(2)}) %all-to-all-start) | async-done | bytes 1048608 | tf_op jit(solution)/shard_map/all_to_all | solution.py:371
  41.1 0.0 copy-start.1
  41.1 0.0 copy-done
  41.2 0.9 %pairs.1 = (bf16[512,1024]{1,0:T(8,128)(2,1)S(1)}, bf16[256,512]{1,0:T(8,128)(2,1)S(1)}, bf16[256,512]{1,0:T(8,128)(2,1)S(1)}) custom-call(bf16[512,1024]{1,0:T(8,128)(2,1)S(1)} %bitcast.5, f32[1,1024]{1,0:T(1,128)S(1)} %bitcast.6, bf16[1024,512]{1,0:T(8,128)(2,1)S(1)} %copy-done), custom_call_target="tpu_custom_call" | custom-call | flops 536870912 | bytes 3670016 | tf_op jit(solution)/shard_map/pairs/pallas_call | solution.py:218
  42.1 3.2 %collective-permute-start.1 = (bf16[256,512]{1,0:T(8,128)(2,1)S(1)}, bf16[256,512]{1,0:T(8,128)(2,1)S(1)}, u32[]{:S(2)}, u32[]{:S(2)}) collective-permute-start(bf16[256,512]{1,0:T(8,128)(2,1)S(1)} %get-tuple-element.20.first_ref), channel_id=1, source_target_pairs={{0,1},{1,2},{2,3},{3,4},{4,5},{5,6},{6,7},{7,8},{8,9},{9,10},{10,1... | collective-permute-start | bytes 786440 | tf_op jit(solution)/shard_map/ppermute | solution.py:25
  45.3 2.7 %collective-permute-start = (bf16[256,512]{1,0:T(8,128)(2,1)S(1)}, bf16[256,512]{1,0:T(8,128)(2,1)S(1)}, u32[]{:S(2)}, u32[]{:S(2)}) collective-permute-start(bf16[256,512]{1,0:T(8,128)(2,1)S(1)} %get-tuple-element.21.last_ref), channel_id=1, source_target_pairs={{0,1},{1,2},{2,3},{3,4},{4,5},{5,6},{6,7},{7,8},{8,9},{9,10},{10,1... | collective-permute-start | bytes 786440 | tf_op jit(solution)/shard_map/ppermute | solution.py:25
  48.0 0.0 copy-done.1
  48.0 3.7 %own_frame.1 = (bf16[512,1024]{1,0:T(8,128)(2,1)S(1)}, f32[512,1024]{1,0:T(8,128)S(1)}, f32[512,1024]{1,0:T(8,128)S(1)}, f32[512,1024]{1,0:T(8,128)S(1)}) custom-call(bf16[512,1024]{1,0:T(8,128)(2,1)S(1)} %get-tuple-element.19.normed_ref, bf16[1024,1024]{1,0:T(8,128)(2,1)S(1)} %copy-done.1, bf16[256,512]{1,0:T(8,128)(2,1)S(1)} %get-tuple-element.20.first_ref, ...), custom_call_target="tpu_custom_call" | custom-call | flops 2147483648 | bytes 6291456 | tf_op jit(solution)/shard_map/own_frame/pallas_call | solution.py:287
  51.7 0.0 collective-permute-done.1.pairs_ref
  51.8 2.0 %earlier_frame.2 = (f32[512,1024]{1,0:T(8,128)S(1)}, f32[512,1024]{1,0:T(8,128)S(1)}, f32[512,1024]{1,0:T(8,128)S(1)}) custom-call(bf16[512,1024]{1,0:T(8,128)(2,1)S(1)} %get-tuple-element.22.query_ref, bf16[256,512]{1,0:T(8,128)(2,1)S(1)} %collective-permute-done.1.pairs_ref, f32[512,1024]{1,0:T(8,128)S(1)} %get-tuple-element.23.sum_ref, ...), custom_call_target="tpu_custom_call" | custom-call | flops 536870912 | bytes 5242880 | tf_op jit(solution)/shard_map/earlier_frame/pallas_call | solution.py:355
  53.8 0.0 collective-permute-done.pairs_ref
  53.8 2.8 %earlier_frame.3 = bf16[512,1024]{1,0:T(8,128)(2,1)} custom-call(bf16[512,1024]{1,0:T(8,128)(2,1)S(1)} %get-tuple-element.22.query_ref, bf16[256,512]{1,0:T(8,128)(2,1)S(1)} %collective-permute-done.pairs_ref, f32[512,1024]{1,0:T(8,128)S(1)} %get-tuple-element.26.sum_ref, f32[512,1024]{1,0:T(8,128)S(1)} %get-tuple-element.27.total_ref, ...), custom_call_target="tpu_custom_call" | custom-call | flops 536870912 | bytes 5242880 | tf_op jit(solution)/shard_map/earlier_frame/pallas_call | solution.py:355
  (1 shorter events, 0.0 us)
Async XLA Ops:
  10.5 7.5 %copy-start.2 = (bf16[1024]{0:T(1024)(128)(2,1)S(1)}, bf16[1024]{0:T(1024)(128)(2,1)}, u32[]{:S(2)}) copy-start(bf16[1024]{0:T(1024)(128)(2,1)} %param.11) | copy-start | bytes 6148
  10.5 30.6 %copy-start = (bf16[1024,512]{1,0:T(8,128)(2,1)S(1)}, bf16[1024,512]{1,0:T(8,128)(2,1)}, u32[]{:S(2)}) copy-start(bf16[1024,512]{1,0:T(8,128)(2,1)} %w_ref.2) | copy-start | bytes 3145732
  10.5 30.6 %all-to-all-start = ((bf16[16,32,1024]{2,1,0:T(8,128)(2,1)}), bf16[16,32,1024]{2,1,0:T(8,128)(2,1)S(1)}, u32[]{:S(2)}, u32[]{:S(2)}) async-start(bf16[16,32,1024]{2,1,0:T(8,128)(2,1)} %bitcast.7), calls=%async_computation | async-start | bytes 2097152 | tf_op jit(solution)/shard_map/all_to_all | solution.py:371
  41.1 6.9 %copy-start.1 = (bf16[1024,1024]{1,0:T(8,128)(2,1)S(1)}, bf16[1024,1024]{1,0:T(8,128)(2,1)}, u32[]{:S(2)}) copy-start(bf16[1024,1024]{1,0:T(8,128)(2,1)} %w_ref.3) | copy-start | bytes 6291460
  42.1 9.6 %collective-permute-start.1 = (bf16[256,512]{1,0:T(8,128)(2,1)S(1)}, bf16[256,512]{1,0:T(8,128)(2,1)S(1)}, u32[]{:S(2)}, u32[]{:S(2)}) collective-permute-start(bf16[256,512]{1,0:T(8,128)(2,1)S(1)} %get-tuple-element.20.first_ref), channel_id=1, source_target_pairs={{0,1},{1,2},{2,3},{3,4},{4,5},{5,6},{6,7},{7,8},{8,9},{9,10},{10,1... | collective-permute-start | bytes 786440 | tf_op jit(solution)/shard_map/ppermute | solution.py:25
  45.3 8.5 %collective-permute-start = (bf16[256,512]{1,0:T(8,128)(2,1)S(1)}, bf16[256,512]{1,0:T(8,128)(2,1)S(1)}, u32[]{:S(2)}, u32[]{:S(2)}) collective-permute-start(bf16[256,512]{1,0:T(8,128)(2,1)S(1)} %get-tuple-element.21.last_ref), channel_id=1, source_target_pairs={{0,1},{1,2},{2,3},{3,4},{4,5},{5,6},{6,7},{7,8},{8,9},{9,10},{10,1... | collective-permute-start | bytes 786440 | tf_op jit(solution)/shard_map/ppermute | solution.py:25

commit v10 on v9

--- a/solution.py
+++ b/solution.py
@@ -52,7 +52,7 @@
     spans = [slice(start, start + SPAN) for start in range(0, rows, SPAN)]
     heads = range(query.shape[1] // HD)
     units = [(head, span) for head in heads for span in range(len(spans))]
-    local, before, after, mixed = {}, {}, [], []
+    local, before, mixed = {}, {}, []
     for head, span in units:
         lanes, here = head_lanes(head), spans[span]
         scores = dot_nt(query[here, lanes], key[here, lanes])
@@ -62,9 +62,9 @@
         state = states[head]
         for span, here in enumerate(spans):
             before[head, span] = state
-            update = dot_tn(key[here, lanes], value[here, lanes])
-            state = update if state is None else state + update
-        after.append(state)
+            if span + 1 < len(spans):
+                update = dot_tn(key[here, lanes], value[here, lanes])
+                state = update if state is None else state + update
     for head, span in units:
         lanes, here = head_lanes(head), spans[span]
         if before[head, span] is None:
@@ -77,98 +77,91 @@
                 ),
             )
         mixed.append((head, here, out))
-    return mixed, after
+    return mixed
 
 
 def mixer_kernel(has_state, *refs):
     if has_state:
         state_ref, *refs = refs
-    tokens_hbm, w_hbm, gain_ref, out_ref, tokens_ref, weights, tokens_in, weights_in = refs
+    tokens_hbm, w_hbm, gain_ref, out_hbm, tokens_ref, weights, out_ref, *arrived = refs
+    tokens_in, weights_in, sent = arrived
     rows, width = tokens_ref.shape
-    block = rows // 2
     columns = PAIR * HD
-    step = pl.program_id(0)
-    slot = lax.rem(step, 2)
-
-    def token_copy(index):
-        here = slice(index * block, (index + 1) * block)
-        return pltpu.make_async_copy(
-            tokens_hbm.at[here], tokens_ref.at[here], tokens_in.at[index]
-        )
-
-    def weight_copy(pair, to, part):
-        start = pl.multiple_of(part * width + pair * columns, columns)
-        return pltpu.make_async_copy(
-            w_hbm.at[:, pl.ds(start, columns)], weights.at[to, part], weights_in.at[to, part]
-        )
-
-    @pl.when(step == 0)
-    def _():
-        weight_copy(0, 0, 0).start()
-        token_copy(0).start()
-        token_copy(1).start()
-        weight_copy(0, 0, 1).start()
-        weight_copy(0, 0, 2).start()
-
-    @pl.when(step + 1 < pl.num_programs(0))
-    def _():
+    groups = HEADS // PAIR
+
+    copies = [[pltpu.make_async_copy(tokens_hbm, tokens_ref, tokens_in)]]
+    for group in range(groups):
+        here = []
         for part in range(3):
-            weight_copy(step + 1, 1 - slot, part).start()
-
-    @pl.when(step == 0)
-    def _():
-        token_copy(0).wait()
-        token_copy(1).wait()
-
-    states = [state_ref[head] if has_state else None for head in range(PAIR)]
-    start = pl.multiple_of(step * columns, columns)
-    gains = gain_ref[pl.ds(start, columns)].astype(jnp.float32).reshape(1, columns)
-
-    packed = [[], []]
-    for part in range(3):
-        weight_copy(step, slot, part).wait()
-        for index in range(2):
-            tokens = tokens_ref[index * block : (index + 1) * block]
-            packed[index].append(dot(tokens, weights[slot, part]).astype(jnp.bfloat16))
-
-    def store(offset, mixed):
-        for head, here, out in mixed:
-            lanes = head_lanes(head)
-            here = slice(offset + here.start, offset + here.stop)
+            start = part * width + group * columns
+            here.append(
+                pltpu.make_async_copy(
+                    w_hbm.at[:, start : start + columns],
+                    weights.at[group, part],
+                    weights_in.at[group, part],
+                )
+            )
+        copies.append(here)
+    for copy in sum(copies, []):
+        copy.start()
+    gains = gain_ref[...].astype(jnp.float32).reshape(1, width)
+
+    def project(group):
+        tokens = tokens_ref[...]
+        return [dot(tokens, weights[group, part]).astype(jnp.bfloat16) for part in range(3)]
+
+    def mix(group, parts):
+        start = group * columns
+        heads = range(group * PAIR, (group + 1) * PAIR)
+        states = [state_ref[head] if has_state else None for head in heads]
+        for head, here, out in mix_heads(*parts, states):
+            lanes = head_lanes(group * PAIR + head)
             mean_square = jnp.mean(out * out, axis=-1, keepdims=True)
             normed = out * lax.rsqrt(mean_square + epsilon) * gains[:, lanes]
-            there = pl.ds(pl.multiple_of(start + head * HD, HD), HD)
-            residual = tokens_ref[here, there].astype(jnp.float32)
+            residual = tokens_ref[here, lanes].astype(jnp.float32)
             out_ref[here, lanes] = (residual + normed).astype(jnp.bfloat16)
-
-    for index in range(2):
-        mixed, states = mix_heads(*packed[index], states)
-        store(index * block, mixed)
+        there = slice(start, start + columns)
+        copy = pltpu.make_async_copy(out_ref.at[:, there], out_hbm.at[:, there], sent.at[group])
+        copy.start()
+        return copy
+
+    for copy in copies[0] + copies[1]:
+        copy.wait()
+    parts = project(0)
+    for copy in sum(copies[2:], []):
+        copy.wait()
+    leaving = []
+    for group in range(groups):
+        upcoming = project(group + 1) if group + 1 < groups else None
+        leaving.append(mix(group, parts))
+        parts = upcoming
+    for copy in leaving:
+        copy.wait()
 
 
 def mixer(tokens, w_lin, gain_lin, state):
     rows, width = tokens.shape
     columns = PAIR * HD
-    in_specs = [
-        pl.BlockSpec(memory_space=pl.ANY),
-        pl.BlockSpec(memory_space=pl.ANY),
-        pl.BlockSpec(memory_space=pltpu.VMEM),
-    ]
+    groups = HEADS // PAIR
+    hbm = pl.BlockSpec(memory_space=pl.ANY)
+    vmem = pl.BlockSpec(memory_space=pltpu.VMEM)
+    in_specs = [hbm, hbm, vmem]
     operands = [tokens, w_lin, gain_lin]
     if state is not None:
         operands.insert(0, state)
-        in_specs.insert(0, pl.BlockSpec((PAIR, HD, HD), lambda c: (c, 0, 0)))
+        in_specs.insert(0, vmem)
     return pl.pallas_call(
         functools.partial(mixer_kernel, state is not None),
-        grid=(HEADS // PAIR,),
         in_specs=in_specs,
-        out_specs=pl.BlockSpec((rows, columns), lambda c: (0, c)),
+        out_specs=hbm,
         out_shape=jax.ShapeDtypeStruct((rows, width), jnp.bfloat16),
         scratch_shapes=[
             pltpu.VMEM((rows, width), jnp.bfloat16),
-            pltpu.VMEM((2, 3, width, columns), jnp.bfloat16),
-            pltpu.SemaphoreType.DMA((2,)),
-            pltpu.SemaphoreType.DMA((2, 3)),
+            pltpu.VMEM((groups, 3, width, columns), jnp.bfloat16),
+            pltpu.VMEM((rows, width), jnp.bfloat16),
+            pltpu.SemaphoreType.DMA,
+            pltpu.SemaphoreType.DMA((groups, 3)),
+            pltpu.SemaphoreType.DMA((groups,)),
         ],
         compiler_params=pltpu.CompilerParams(vmem_limit_bytes=56 * MIB),
         cost_estimate=pl.CostEstimate(

time: 57.5 us -> 56.9 us (0.990)
  Pallas kernels: 20 us -> 19.1 us
    pallas_call x1, Pallas kernels: 10.5 us -> 9.61 us  [mixer(): pl.pallas_call(functools.partial(mixer_kernel, state is not None), in_spe...]
where the time goes in v10:
time: 56.9 us; the launch traced here: 56.1 us
  waiting for transfers between devices  23.1 us (41%)
  Pallas kernels  19.1 us (34%)
  starting transfers between devices  13.6 us (24%)
    all_to_all x1, waiting for transfers between devices, to_frames(): lax.all_to_all(hidden.reshape(SB, rows // SB, columns), 'tm', 0, 0, axis_...  23.1 us
    pallas_call x1, Pallas kernels, mixer(): pl.pallas_call(functools.partial(mixer_kernel, state is not None), in_spe...  9.61 us
    all_to_all x1, starting transfers between devices, to_frames(): lax.all_to_all(hidden.reshape(SB, rows // SB, columns), 'tm', 0, 0, axis_...  7.5 us
    ppermute x2, starting transfers between devices, shifted(): return lax.ppermute(block, axis, route)  6.08 us
    pallas_call x2, Pallas kernels, earlier_frame(): pl.pallas_call(functools.partial(earlier_kernel, last), compiler_params=p...  4.82 us
    pallas_call x1, Pallas kernels, own_frame(): pl.pallas_call(own_kernel, out_shape=[jax.ShapeDtypeStruct((rows, width),...  3.7 us
  transfers between devices with their start and end apart: 3, of which 1 were waited for; matrix products, arithmetic and copies ran while one was open for 0% of the time, Pallas kernels for 10%

profile of v10, /device:TPU:1, one launch (start us, length us, event | category | flops | bytes accessed | tf_op | source)
XLA Modules:
  0.0 56.1 jit_solution(8765983143456730980)
XLA Ops:
  0.0 9.6 %mixer.1 = bf16[512,1024]{1,0:T(8,128)(2,1)} custom-call(bf16[512,1024]{1,0:T(8,128)(2,1)} %bitcast.8, bf16[1024,3072]{1,0:T(8,128)(2,1)} %refs_1_.1, bf16[1024]{0:T(1024)(128)(2,1)} %refs_2_.1), custom_call_target="tpu_custom_call" | custom-call | flops 3758096384 | bytes 8388608 | tf_op jit(solution)/shard_map/mixer/pallas_call | solution.py:153
  9.6 0.0 copy-start.2
  9.6 0.0 copy-start
  9.6 7.5 %all-to-all-start = ((bf16[16,32,1024]{2,1,0:T(8,128)(2,1)}), bf16[16,32,1024]{2,1,0:T(8,128)(2,1)S(1)}, u32[]{:S(2)}, u32[]{:S(2)}) async-start(bf16[16,32,1024]{2,1,0:T(8,128)(2,1)} %bitcast.7), calls=%async_computation | async-start | bytes 2097152 | tf_op jit(solution)/shard_map/all_to_all | solution.py:364
  17.1 0.0 copy-done.2
  17.2 23.1 %all-to-all-done = bf16[16,32,1024]{2,1,0:T(8,128)(2,1)S(1)} async-done(((bf16[16,32,1024]{2,1,0:T(8,128)(2,1)}), bf16[16,32,1024]{2,1,0:T(8,128)(2,1)S(1)}, u32[]{:S(2)}, u32[]{:S(2)}) %all-to-all-start) | async-done | bytes 1048608 | tf_op jit(solution)/shard_map/all_to_all | solution.py:364
  40.3 0.0 copy-start.1
  40.3 0.0 copy-done
  40.3 1.0 %pairs.1 = (bf16[512,1024]{1,0:T(8,128)(2,1)S(1)}, bf16[256,512]{1,0:T(8,128)(2,1)S(1)}, bf16[256,512]{1,0:T(8,128)(2,1)S(1)}) custom-call(bf16[512,1024]{1,0:T(8,128)(2,1)S(1)} %bitcast.5, f32[1,1024]{1,0:T(1,128)S(1)} %bitcast.6, bf16[1024,512]{1,0:T(8,128)(2,1)S(1)} %copy-done), custom_call_target="tpu_custom_call" | custom-call | flops 536870912 | bytes 3670016 | tf_op jit(solution)/shard_map/pairs/pallas_call | solution.py:211
  41.2 3.2 %collective-permute-start.1 = (bf16[256,512]{1,0:T(8,128)(2,1)S(1)}, bf16[256,512]{1,0:T(8,128)(2,1)S(1)}, u32[]{:S(2)}, u32[]{:S(2)}) collective-permute-start(bf16[256,512]{1,0:T(8,128)(2,1)S(1)} %get-tuple-element.20.first_ref), channel_id=1, source_target_pairs={{0,1},{1,2},{2,3},{3,4},{4,5},{5,6},{6,7},{7,8},{8,9},{9,10},{10,1... | collective-permute-start | bytes 786440 | tf_op jit(solution)/shard_map/ppermute | solution.py:25
  44.5 2.9 %collective-permute-start = (bf16[256,512]{1,0:T(8,128)(2,1)S(1)}, bf16[256,512]{1,0:T(8,128)(2,1)S(1)}, u32[]{:S(2)}, u32[]{:S(2)}) collective-permute-start(bf16[256,512]{1,0:T(8,128)(2,1)S(1)} %get-tuple-element.21.last_ref), channel_id=1, source_target_pairs={{0,1},{1,2},{2,3},{3,4},{4,5},{5,6},{6,7},{7,8},{8,9},{9,10},{10,1... | collective-permute-start | bytes 786440 | tf_op jit(solution)/shard_map/ppermute | solution.py:25
  47.3 0.0 copy-done.1
  47.4 3.7 %own_frame.1 = (bf16[512,1024]{1,0:T(8,128)(2,1)S(1)}, f32[512,1024]{1,0:T(8,128)S(1)}, f32[512,1024]{1,0:T(8,128)S(1)}, f32[512,1024]{1,0:T(8,128)S(1)}) custom-call(bf16[512,1024]{1,0:T(8,128)(2,1)S(1)} %get-tuple-element.19.normed_ref, bf16[1024,1024]{1,0:T(8,128)(2,1)S(1)} %copy-done.1, bf16[256,512]{1,0:T(8,128)(2,1)S(1)} %get-tuple-element.20.first_ref, ...), custom_call_target="tpu_custom_call" | custom-call | flops 2147483648 | bytes 6291456 | tf_op jit(solution)/shard_map/own_frame/pallas_call | solution.py:280
  51.1 0.0 collective-permute-done.1.pairs_ref
  51.1 2.0 %earlier_frame.2 = (f32[512,1024]{1,0:T(8,128)S(1)}, f32[512,1024]{1,0:T(8,128)S(1)}, f32[512,1024]{1,0:T(8,128)S(1)}) custom-call(bf16[512,1024]{1,0:T(8,128)(2,1)S(1)} %get-tuple-element.22.query_ref, bf16[256,512]{1,0:T(8,128)(2,1)S(1)} %collective-permute-done.1.pairs_ref, f32[512,1024]{1,0:T(8,128)S(1)} %get-tuple-element.23.sum_ref, ...), custom_call_target="tpu_custom_call" | custom-call | flops 536870912 | bytes 5242880 | tf_op jit(solution)/shard_map/earlier_frame/pallas_call | solution.py:348
  53.1 0.0 collective-permute-done.pairs_ref
  53.1 2.8 %earlier_frame.3 = bf16[512,1024]{1,0:T(8,128)(2,1)} custom-call(bf16[512,1024]{1,0:T(8,128)(2,1)S(1)} %get-tuple-element.22.query_ref, bf16[256,512]{1,0:T(8,128)(2,1)S(1)} %collective-permute-done.pairs_ref, f32[512,1024]{1,0:T(8,128)S(1)} %get-tuple-element.26.sum_ref, f32[512,1024]{1,0:T(8,128)S(1)} %get-tuple-element.27.total_ref, ...), custom_call_target="tpu_custom_call" | custom-call | flops 536870912 | bytes 5242880 | tf_op jit(solution)/shard_map/earlier_frame/pallas_call | solution.py:348
  (1 shorter events, 0.0 us)
Async XLA Ops:
  9.6 7.5 %copy-start.2 = (bf16[1024]{0:T(1024)(128)(2,1)S(1)}, bf16[1024]{0:T(1024)(128)(2,1)}, u32[]{:S(2)}) copy-start(bf16[1024]{0:T(1024)(128)(2,1)} %param.11) | copy-start | bytes 6148
  9.6 30.7 %copy-start = (bf16[1024,512]{1,0:T(8,128)(2,1)S(1)}, bf16[1024,512]{1,0:T(8,128)(2,1)}, u32[]{:S(2)}) copy-start(bf16[1024,512]{1,0:T(8,128)(2,1)} %w_ref.2) | copy-start | bytes 3145732
  9.6 30.6 %all-to-all-start = ((bf16[16,32,1024]{2,1,0:T(8,128)(2,1)}), bf16[16,32,1024]{2,1,0:T(8,128)(2,1)S(1)}, u32[]{:S(2)}, u32[]{:S(2)}) async-start(bf16[16,32,1024]{2,1,0:T(8,128)(2,1)} %bitcast.7), calls=%async_computation | async-start | bytes 2097152 | tf_op jit(solution)/shard_map/all_to_all | solution.py:364
  40.3 7.1 %copy-start.1 = (bf16[1024,1024]{1,0:T(8,128)(2,1)S(1)}, bf16[1024,1024]{1,0:T(8,128)(2,1)}, u32[]{:S(2)}) copy-start(bf16[1024,1024]{1,0:T(8,128)(2,1)} %w_ref.3) | copy-start | bytes 6291460
  41.2 9.8 %collective-permute-start.1 = (bf16[256,512]{1,0:T(8,128)(2,1)S(1)}, bf16[256,512]{1,0:T(8,128)(2,1)S(1)}, u32[]{:S(2)}, u32[]{:S(2)}) collective-permute-start(bf16[256,512]{1,0:T(8,128)(2,1)S(1)} %get-tuple-element.20.first_ref), channel_id=1, source_target_pairs={{0,1},{1,2},{2,3},{3,4},{4,5},{5,6},{6,7},{7,8},{8,9},{9,10},{10,1... | collective-permute-start | bytes 786440 | tf_op jit(solution)/shard_map/ppermute | solution.py:25
  44.5 8.6 %collective-permute-start = (bf16[256,512]{1,0:T(8,128)(2,1)S(1)}, bf16[256,512]{1,0:T(8,128)(2,1)S(1)}, u32[]{:S(2)}, u32[]{:S(2)}) collective-permute-start(bf16[256,512]{1,0:T(8,128)(2,1)S(1)} %get-tuple-element.21.last_ref), channel_id=1, source_target_pairs={{0,1},{1,2},{2,3},{3,4},{4,5},{5,6},{6,7},{7,8},{8,9},{9,10},{10,1... | collective-permute-start | bytes 786440 | tf_op jit(solution)/shard_map/ppermute | solution.py:25

commit v11 on v10

--- a/solution.py
+++ b/solution.py
@@ -13,7 +13,7 @@
 KVH = 2
 SB = 16
 SPAN = 128
-PAIR = 4
+GROUPS = ((0, 2), (2, 6), (6, 8))
 
 epsilon = 1e-06
 MIB = 1 << 20
@@ -83,57 +83,52 @@
 def mixer_kernel(has_state, *refs):
     if has_state:
         state_ref, *refs = refs
-    tokens_hbm, w_hbm, gain_ref, out_hbm, tokens_ref, weights, out_ref, *arrived = refs
-    tokens_in, weights_in, sent = arrived
+    tokens_hbm, w_hbm, gain_ref, out_hbm, tokens_ref, out_ref, *refs = refs
+    *weights, tokens_in, weights_in, sent = refs
     rows, width = tokens_ref.shape
-    columns = PAIR * HD
-    groups = HEADS // PAIR
-
-    copies = [[pltpu.make_async_copy(tokens_hbm, tokens_ref, tokens_in)]]
-    for group in range(groups):
+
+    first = [pltpu.make_async_copy(tokens_hbm, tokens_ref, tokens_in)]
+    copies = []
+    for index, (low, high) in enumerate(GROUPS):
         here = []
         for part in range(3):
-            start = part * width + group * columns
+            columns = slice(part * width + low * HD, part * width + high * HD)
             here.append(
                 pltpu.make_async_copy(
-                    w_hbm.at[:, start : start + columns],
-                    weights.at[group, part],
-                    weights_in.at[group, part],
+                    w_hbm.at[:, columns], weights[index].at[part], weights_in.at[index, part]
                 )
             )
         copies.append(here)
-    for copy in sum(copies, []):
+    for copy in first + sum(copies, []):
         copy.start()
     gains = gain_ref[...].astype(jnp.float32).reshape(1, width)
 
-    def project(group):
+    def project(index):
+        for copy in copies[index]:
+            copy.wait()
         tokens = tokens_ref[...]
-        return [dot(tokens, weights[group, part]).astype(jnp.bfloat16) for part in range(3)]
-
-    def mix(group, parts):
-        start = group * columns
-        heads = range(group * PAIR, (group + 1) * PAIR)
-        states = [state_ref[head] if has_state else None for head in heads]
+        return [dot(tokens, weights[index][part]).astype(jnp.bfloat16) for part in range(3)]
+
+    def mix(index, parts):
+        low, high = GROUPS[index]
+        states = [state_ref[head] if has_state else None for head in range(low, high)]
         for head, here, out in mix_heads(*parts, states):
-            lanes = head_lanes(group * PAIR + head)
+            lanes = head_lanes(low + head)
             mean_square = jnp.mean(out * out, axis=-1, keepdims=True)
             normed = out * lax.rsqrt(mean_square + epsilon) * gains[:, lanes]
             residual = tokens_ref[here, lanes].astype(jnp.float32)
             out_ref[here, lanes] = (residual + normed).astype(jnp.bfloat16)
-        there = slice(start, start + columns)
-        copy = pltpu.make_async_copy(out_ref.at[:, there], out_hbm.at[:, there], sent.at[group])
+        there = slice(low * HD, high * HD)
+        copy = pltpu.make_async_copy(out_ref.at[:, there], out_hbm.at[:, there], sent.at[index])
         copy.start()
         return copy
 
-    for copy in copies[0] + copies[1]:
-        copy.wait()
+    first[0].wait()
     parts = project(0)
-    for copy in sum(copies[2:], []):
-        copy.wait()
     leaving = []
-    for group in range(groups):
-        upcoming = project(group + 1) if group + 1 < groups else None
-        leaving.append(mix(group, parts))
+    for index in range(len(GROUPS)):
+        upcoming = project(index + 1) if index + 1 < len(GROUPS) else None
+        leaving.append(mix(index, parts))
         parts = upcoming
     for copy in leaving:
         copy.wait()
@@ -141,8 +136,6 @@
 
 def mixer(tokens, w_lin, gain_lin, state):
     rows, width = tokens.shape
-    columns = PAIR * HD
-    groups = HEADS // PAIR
     hbm = pl.BlockSpec(memory_space=pl.ANY)
     vmem = pl.BlockSpec(memory_space=pltpu.VMEM)
     in_specs = [hbm, hbm, vmem]
@@ -155,13 +148,12 @@
         in_specs=in_specs,
         out_specs=hbm,
         out_shape=jax.ShapeDtypeStruct((rows, width), jnp.bfloat16),
-        scratch_shapes=[
-            pltpu.VMEM((rows, width), jnp.bfloat16),
-            pltpu.VMEM((groups, 3, width, columns), jnp.bfloat16),
-            pltpu.VMEM((rows, width), jnp.bfloat16),
+        scratch_shapes=[pltpu.VMEM((rows, width), jnp.bfloat16)] * 2
+        + [pltpu.VMEM((3, width, (high - low) * HD), jnp.bfloat16) for low, high in GROUPS]
+        + [
             pltpu.SemaphoreType.DMA,
-            pltpu.SemaphoreType.DMA((groups, 3)),
-            pltpu.SemaphoreType.DMA((groups,)),
+            pltpu.SemaphoreType.DMA((len(GROUPS), 3)),
+            pltpu.SemaphoreType.DMA((len(GROUPS),)),
         ],
         compiler_params=pltpu.CompilerParams(vmem_limit_bytes=56 * MIB),
         cost_estimate=pl.CostEstimate(
@@ -194,15 +186,11 @@
     normed = (widened * lax.rsqrt(mean_square + epsilon) * gain_ref[...]).astype(jnp.bfloat16)
     normed_ref[...] = normed
     pairs = dot(normed, w_ref[...]).astype(jnp.bfloat16)
-    offset = 0
-    for out_ref in outs:
-        for start in range(0, out_ref.shape[0], HD):
-            here = slice(offset + start, offset + start + HD)
-            for head in range(KVH):
-                out_ref[start : start + HD, head_lanes(head)] = pairs[here, head_lanes(head)].T
-        rows = out_ref.shape[0]
-        out_ref[:, KVH * HD :] = pairs[offset : offset + rows, KVH * HD :]
-        offset += rows
+    for head, out_ref in enumerate(outs):
+        for start in range(0, pairs.shape[0], HD):
+            here = slice(start, start + HD)
+            out_ref[here, :HD] = pairs[here, head_lanes(head)].T
+        out_ref[:, HD:] = pairs[:, head_lanes(KVH + head)]
 
 
 def make_pairs(hidden, gain, w_kv):
@@ -210,11 +198,8 @@
     wide = w_kv.shape[1]
     return pl.pallas_call(
         pairs_kernel,
-        out_shape=[
-            jax.ShapeDtypeStruct((rows, width), jnp.bfloat16),
-            jax.ShapeDtypeStruct((rows - LATE, wide), jnp.bfloat16),
-            jax.ShapeDtypeStruct((LATE, wide), jnp.bfloat16),
-        ],
+        out_shape=[jax.ShapeDtypeStruct((rows, width), jnp.bfloat16)]
+        + [jax.ShapeDtypeStruct((rows, wide // KVH), jnp.bfloat16)] * KVH,
         compiler_params=pltpu.CompilerParams(vmem_limit_bytes=16 * MIB),
         cost_estimate=pl.CostEstimate(
             flops=2 * rows * width * wide,
@@ -227,25 +212,19 @@
 
 SCORE_SCALE = math.log2(math.e) / math.sqrt(HD)
 GROUP = HEADS // KVH
-LATE = 256
-
-
-def keys_and_values(refs):
-    both = []
-    for head in range(KVH):
-        keys, values = [], []
-        for ref in refs:
-            for start in range(0, ref.shape[0], HD):
-                keys.append(ref[start : start + HD, head_lanes(head)])
-            values.append(ref[:, head_lanes(KVH + head)])
-        key = jnp.concatenate(keys, axis=1)
-        value = jnp.concatenate(values, axis=0)
-        both.append((key, jnp.concatenate([value, jnp.ones_like(value)], axis=1)))
-    return both
-
-
-def own_kernel(normed_ref, w_ref, first_ref, last_ref, query_ref, sum_ref, total_ref, top_ref):
-    both = keys_and_values([first_ref, last_ref])
+
+
+def key_and_value(ref):
+    key = jnp.concatenate(
+        [ref[start : start + HD, :HD] for start in range(0, ref.shape[0], HD)], axis=1
+    )
+    value = ref[:, HD:]
+    return key, jnp.concatenate([value, jnp.ones_like(value)], axis=1)
+
+
+def own_kernel(normed_ref, w_ref, *refs):
+    both = [key_and_value(ref) for ref in refs[:KVH]]
+    query_ref, sum_ref, total_ref, top_ref = refs[KVH:]
     columns = GROUP * HD
 
     def project(group):
@@ -275,7 +254,7 @@
         scores = upcoming
 
 
-def own_frame(normed, w_query, first, last):
+def own_frame(normed, w_query, pairs):
     rows, width = normed.shape
     return pl.pallas_call(
         own_kernel,
@@ -288,74 +267,79 @@
             transcendentals=rows * rows * HEADS,
         ),
         name="own_frame",
-    )(normed, w_query, first, last)
-
-
-def earlier_kernel(last, query_ref, pairs_ref, sum_ref, total_ref, top_ref, *refs):
-    both = keys_and_values([pairs_ref])
+    )(normed, w_query, *pairs)
+
+
+def earlier_kernel(group, query_ref, pairs_ref, sum_ref, total_ref, top_ref, *refs):
+    key, value = key_and_value(pairs_ref)
     barred = jnp.where(lax.axis_index("tm") > 0, 0.0, -jnp.inf)
+    columns = GROUP * HD
+    last = group == KVH - 1
+    copies = []
+    if last:
+        *done_refs, out_hbm, out_ref, sent = refs
+
+        def leave(source, start):
+            there = out_hbm.at[:, start : start + source.shape[1]]
+            copies.append(pltpu.make_async_copy(source, there, sent.at[len(copies)]))
+            copies[-1].start()
+
+        for index, ref in enumerate(done_refs):
+            leave(ref, index * columns)
+    else:
+        (out_ref,) = refs
 
     def scores_of(head):
-        return dot(query_ref[:, head_lanes(head)], both[head // GROUP][0])
-
-    copies = []
+        return dot(query_ref[:, head_lanes(group * GROUP + head)], key)
+
     scores = scores_of(0)
-    for head in range(HEADS):
-        lanes = head_lanes(head)
-        upcoming = scores_of(head + 1) if head + 1 < HEADS else None
+    for head in range(GROUP):
+        lanes = head_lanes(group * GROUP + head)
+        upcoming = scores_of(head + 1) if head + 1 < GROUP else None
         before = top_ref[:, lanes]
         here = jnp.max(scores, axis=-1, keepdims=True) * SCORE_SCALE + barred
         largest = jnp.maximum(jnp.broadcast_to(here, before.shape), before)
         below = jnp.concatenate([largest - barred] * (scores.shape[1] // HD), axis=1)
         raised = jnp.exp2(scores * SCORE_SCALE - below).astype(jnp.bfloat16)
-        summed = dot(raised, both[head // GROUP][1])
+        summed = dot(raised, value)
         share = jnp.exp2(before - largest)
         mixed = sum_ref[:, lanes] * share + summed[:, :HD]
         total = total_ref[:, lanes] * share + summed[:, HD:]
-        if last:
-            out_hbm, out_ref, sent = refs
-            out_ref[:, lanes] = (mixed / total).astype(jnp.bfloat16)
-            if head % 2:
-                columns = slice((head - 1) * HD, (head + 1) * HD)
-                copies.append(
-                    pltpu.make_async_copy(
-                        out_ref.at[:, columns], out_hbm.at[:, columns], sent.at[head // 2]
-                    )
-                )
-                copies[-1].start()
-        else:
-            refs[0][:, lanes] = mixed
-            refs[1][:, lanes] = total
-            refs[2][:, lanes] = largest
+        out_ref[:, head_lanes(head)] = (mixed / total).astype(jnp.bfloat16)
+        if last and head % 2:
+            start = (head - 1) * HD
+            leave(out_ref.at[:, start : start + 2 * HD], group * columns + start)
         scores = upcoming
     for copy in copies:
         copy.wait()
 
 
-def earlier_frame(last, query, pairs, *so_far):
+def earlier_frame(group, query, pairs, so_far, done):
     rows, width = query.shape
+    columns = GROUP * HD
+    last = group == KVH - 1
+    extra = dict(out_shape=jax.ShapeDtypeStruct((rows, columns), jnp.bfloat16))
     if last:
         extra = dict(
             out_shape=jax.ShapeDtypeStruct((rows, width), jnp.bfloat16),
             out_specs=pl.BlockSpec(memory_space=pl.ANY),
             scratch_shapes=[
-                pltpu.VMEM((rows, width), jnp.bfloat16),
-                pltpu.SemaphoreType.DMA((HEADS // 2,)),
+                pltpu.VMEM((rows, columns), jnp.bfloat16),
+                pltpu.SemaphoreType.DMA((KVH - 1 + GROUP // 2,)),
             ],
         )
-    else:
-        extra = dict(out_shape=[jax.ShapeDtypeStruct((rows, width), jnp.float32)] * 3)
+    operands = [query, pairs, *so_far] + (done if last else [])
     return pl.pallas_call(
-        functools.partial(earlier_kernel, last),
+        functools.partial(earlier_kernel, group),
         compiler_params=pltpu.CompilerParams(vmem_limit_bytes=32 * MIB),
         cost_estimate=pl.CostEstimate(
-            flops=4 * rows * pairs.shape[0] * width,
-            bytes_accessed=10 * rows * width,
-            transcendentals=rows * pairs.shape[0] * HEADS,
+            flops=4 * rows * rows * columns,
+            bytes_accessed=20 * rows * columns,
+            transcendentals=rows * rows * GROUP,
         ),
         name="earlier_frame",
         **extra,
-    )(query, pairs, *so_far)
+    )(*operands)
 
 
 def to_frames(hidden):
@@ -375,13 +359,13 @@
     hidden, gain = lax.optimization_barrier((hidden, frame_attention_gain))
     frame_rows = to_frames(hidden)
     gain = gain.astype(jnp.float32).reshape(1, -1)
-    normed, first, last = make_pairs(frame_rows, gain, w_kv)
-    earlier_first = shifted(first, "tm", 1)
-    earlier_last = shifted(last, "tm", 1)
-    query, *so_far = own_frame(normed, w_query, first, last)
-    so_far = earlier_frame(False, query, earlier_first, *so_far)
-    attended = earlier_frame(True, query, earlier_last, *so_far)
-    return attended[None]
+    normed, *pairs = make_pairs(frame_rows, gain, w_kv)
+    earlier_pairs = [shifted(part, "tm", 1) for part in pairs]
+    query, *so_far = own_frame(normed, w_query, pairs)
+    done = []
+    for group, part in enumerate(earlier_pairs):
+        done.append(earlier_frame(group, query, part, so_far, done))
+    return done[-1][None]
 
 
 def solution(mesh):

time: 56.9 us -> 57.3 us (level)
    pallas_call x1, Pallas kernels: 9.61 us -> 10.5 us  [mixer(): pl.pallas_call(functools.partial(mixer_kernel, state is not None), in_spe...]
    pallas_call x2, Pallas kernels: 4.82 us -> 4.17 us  [earlier_frame(): pl.pallas_call(functools.partial(earlier_kernel, group), compiler_params=...]
where the time goes in v11:
time: 57.3 us; the launch traced here: 56.3 us
  waiting for transfers between devices  23.1 us (40%)
  Pallas kernels  19.3 us (34%)
  starting transfers between devices  13.6 us (24%)
    all_to_all x1, waiting for transfers between devices, to_frames(): lax.all_to_all(hidden.reshape(SB, rows // SB, columns), 'tm', 0, 0, axis_...  23.1 us
    pallas_call x1, Pallas kernels, mixer(): pl.pallas_call(functools.partial(mixer_kernel, state is not None), in_spe...  10.5 us
    all_to_all x1, starting transfers between devices, to_frames(): lax.all_to_all(hidden.reshape(SB, rows // SB, columns), 'tm', 0, 0, axis_...  7.49 us
    ppermute x2, starting transfers between devices, shifted(): return lax.ppermute(block, axis, route)  6.08 us
    pallas_call x2, Pallas kernels, earlier_frame(): pl.pallas_call(functools.partial(earlier_kernel, group), compiler_params=...  4.17 us
    pallas_call x1, Pallas kernels, own_frame(): pl.pallas_call(own_kernel, out_shape=[jax.ShapeDtypeStruct((rows, width),...  3.7 us
  transfers between devices with their start and end apart: 3, of which 1 were waited for; matrix products, arithmetic and copies ran while one was open for 0% of the time, Pallas kernels for 10%

profile of v11, /device:TPU:1, one launch (start us, length us, event | category | flops | bytes accessed | tf_op | source)
XLA Modules:
  0.0 56.3 jit_solution(8738824887705680003)
XLA Ops:
  0.0 10.5 %mixer.1 = bf16[512,1024]{1,0:T(8,128)(2,1)} custom-call(bf16[512,1024]{1,0:T(8,128)(2,1)} %bitcast.8, bf16[1024,3072]{1,0:T(8,128)(2,1)} %refs_1_.1, bf16[1024]{0:T(1024)(128)(2,1)} %refs_2_.1), custom_call_target="tpu_custom_call" | custom-call | flops 3758096384 | bytes 8388608 | tf_op jit(solution)/shard_map/mixer/pallas_call | solution.py:146
  10.5 0.0 copy-start.2
  10.5 0.0 copy-start
  10.5 7.5 %all-to-all-start = ((bf16[16,32,1024]{2,1,0:T(8,128)(2,1)}), bf16[16,32,1024]{2,1,0:T(8,128)(2,1)S(1)}, u32[]{:S(2)}, u32[]{:S(2)}) async-start(bf16[16,32,1024]{2,1,0:T(8,128)(2,1)} %bitcast.7), calls=%async_computation | async-start | bytes 2097152 | tf_op jit(solution)/shard_map/all_to_all | solution.py:348
  18.0 0.0 copy-done.2
  18.0 23.1 %all-to-all-done = bf16[16,32,1024]{2,1,0:T(8,128)(2,1)S(1)} async-done(((bf16[16,32,1024]{2,1,0:T(8,128)(2,1)}), bf16[16,32,1024]{2,1,0:T(8,128)(2,1)S(1)}, u32[]{:S(2)}, u32[]{:S(2)}) %all-to-all-start) | async-done | bytes 1048608 | tf_op jit(solution)/shard_map/all_to_all | solution.py:348
  41.1 0.0 copy-start.1
  41.2 0.0 copy-done
  41.2 1.0 %pairs.1 = (bf16[512,1024]{1,0:T(8,128)(2,1)S(1)}, bf16[512,256]{1,0:T(8,128)(2,1)S(1)}, bf16[512,256]{1,0:T(8,128)(2,1)S(1)}) custom-call(bf16[512,1024]{1,0:T(8,128)(2,1)S(1)} %bitcast.5, f32[1,1024]{1,0:T(1,128)S(1)} %bitcast.6, bf16[1024,512]{1,0:T(8,128)(2,1)S(1)} %copy-done), custom_call_target="tpu_custom_call" | custom-call | flops 536870912 | bytes 3670016 | tf_op jit(solution)/shard_map/pairs/pallas_call | solution.py:199
  42.1 3.2 %collective-permute-start.1 = (bf16[512,256]{1,0:T(8,128)(2,1)S(1)}, bf16[512,256]{1,0:T(8,128)(2,1)S(1)}, u32[]{:S(2)}, u32[]{:S(2)}) collective-permute-start(bf16[512,256]{1,0:T(8,128)(2,1)S(1)} %get-tuple-element.17.refs_0_), channel_id=1, source_target_pairs={{0,1},{1,2},{2,3},{3,4},{4,5},{5,6},{6,7},{7,8},{8,9},{9,10},{10,1... | collective-permute-start | bytes 786440 | tf_op jit(solution)/shard_map/ppermute | solution.py:25
  45.4 2.9 %collective-permute-start = (bf16[512,256]{1,0:T(8,128)(2,1)S(1)}, bf16[512,256]{1,0:T(8,128)(2,1)S(1)}, u32[]{:S(2)}, u32[]{:S(2)}) collective-permute-start(bf16[512,256]{1,0:T(8,128)(2,1)S(1)} %get-tuple-element.18.refs_1_), channel_id=1, source_target_pairs={{0,1},{1,2},{2,3},{3,4},{4,5},{5,6},{6,7},{7,8},{8,9},{9,10},{10,1... | collective-permute-start | bytes 786440 | tf_op jit(solution)/shard_map/ppermute | solution.py:25
  48.2 0.0 copy-done.1
  48.2 3.7 %own_frame.1 = (bf16[512,1024]{1,0:T(8,128)(2,1)S(1)}, f32[512,1024]{1,0:T(8,128)S(1)}, f32[512,1024]{1,0:T(8,128)S(1)}, f32[512,1024]{1,0:T(8,128)S(1)}) custom-call(bf16[512,1024]{1,0:T(8,128)(2,1)S(1)} %get-tuple-element.16.normed_ref, bf16[1024,1024]{1,0:T(8,128)(2,1)S(1)} %copy-done.1, bf16[512,256]{1,0:T(8,128)(2,1)S(1)} %get-tuple-element.17.refs_0_, ...), custom_call_target="tpu_custom_call" | custom-call | flops 2147483648 | bytes 6291456 | tf_op jit(solution)/shard_map/own_frame/pallas_call | solution.py:259
  51.9 0.0 collective-permute-done.1.pairs_ref
  51.9 1.7 %earlier_frame.2.refs_0_ = bf16[512,512]{1,0:T(8,128)(2,1)S(1)} custom-call(bf16[512,1024]{1,0:T(8,128)(2,1)S(1)} %get-tuple-element.19.query_ref, bf16[512,256]{1,0:T(8,128)(2,1)S(1)} %collective-permute-done.1.pairs_ref, f32[512,1024]{1,0:T(8,128)S(1)} %get-tuple-element.20.sum_ref, f32[512,1024]{1,0:T(8,128)S(1)} %get-tuple-element.21.total_ref, ...), custom_call_target="tpu_custom_call" | custom-call | flops 536870912 | bytes 5242880 | tf_op jit(solution)/shard_map/earlier_frame/pallas_call | solution.py:332
  53.7 0.0 collective-permute-done.pairs_ref
  53.7 2.5 %earlier_frame.3 = bf16[512,1024]{1,0:T(8,128)(2,1)} custom-call(bf16[512,1024]{1,0:T(8,128)(2,1)S(1)} %get-tuple-element.19.query_ref, bf16[512,256]{1,0:T(8,128)(2,1)S(1)} %collective-permute-done.pairs_ref, f32[512,1024]{1,0:T(8,128)S(1)} %get-tuple-element.20.sum_ref, f32[512,1024]{1,0:T(8,128)S(1)} %get-tuple-element.21.total_ref, ...), custom_call_target="tpu_custom_call" | custom-call | flops 536870912 | bytes 5242880 | tf_op jit(solution)/shard_map/earlier_frame/pallas_call | solution.py:332
  (1 shorter events, 0.0 us)
Async XLA Ops:
  10.5 7.5 %copy-start.2 = (bf16[1024]{0:T(1024)(128)(2,1)S(1)}, bf16[1024]{0:T(1024)(128)(2,1)}, u32[]{:S(2)}) copy-start(bf16[1024]{0:T(1024)(128)(2,1)} %param.11) | copy-start | bytes 6148
  10.5 30.6 %copy-start = (bf16[1024,512]{1,0:T(8,128)(2,1)S(1)}, bf16[1024,512]{1,0:T(8,128)(2,1)}, u32[]{:S(2)}) copy-start(bf16[1024,512]{1,0:T(8,128)(2,1)} %w_ref.2) | copy-start | bytes 3145732
  10.5 30.6 %all-to-all-start = ((bf16[16,32,1024]{2,1,0:T(8,128)(2,1)}), bf16[16,32,1024]{2,1,0:T(8,128)(2,1)S(1)}, u32[]{:S(2)}, u32[]{:S(2)}) async-start(bf16[16,32,1024]{2,1,0:T(8,128)(2,1)} %bitcast.7), calls=%async_computation | async-start | bytes 2097152 | tf_op jit(solution)/shard_map/all_to_all | solution.py:348
  41.1 7.1 %copy-start.1 = (bf16[1024,1024]{1,0:T(8,128)(2,1)S(1)}, bf16[1024,1024]{1,0:T(8,128)(2,1)}, u32[]{:S(2)}) copy-start(bf16[1024,1024]{1,0:T(8,128)(2,1)} %w_ref.3) | copy-start | bytes 6291460
  42.1 9.8 %collective-permute-start.1 = (bf16[512,256]{1,0:T(8,128)(2,1)S(1)}, bf16[512,256]{1,0:T(8,128)(2,1)S(1)}, u32[]{:S(2)}, u32[]{:S(2)}) collective-permute-start(bf16[512,256]{1,0:T(8,128)(2,1)S(1)} %get-tuple-element.17.refs_0_), channel_id=1, source_target_pairs={{0,1},{1,2},{2,3},{3,4},{4,5},{5,6},{6,7},{7,8},{8,9},{9,10},{10,1... | collective-permute-start | bytes 786440 | tf_op jit(solution)/shard_map/ppermute | solution.py:25
  45.4 8.3 %collective-permute-start = (bf16[512,256]{1,0:T(8,128)(2,1)S(1)}, bf16[512,256]{1,0:T(8,128)(2,1)S(1)}, u32[]{:S(2)}, u32[]{:S(2)}) collective-permute-start(bf16[512,256]{1,0:T(8,128)(2,1)S(1)} %get-tuple-element.18.refs_1_), channel_id=1, source_target_pairs={{0,1},{1,2},{2,3},{3,4},{4,5},{5,6},{6,7},{7,8},{8,9},{9,10},{10,1... | collective-permute-start | bytes 786440 | tf_op jit(solution)/shard_map/ppermute | solution.py:25

commit v12 on v11

--- a/solution.py
+++ b/solution.py
@@ -13,7 +13,7 @@
 KVH = 2
 SB = 16
 SPAN = 128
-GROUPS = ((0, 2), (2, 6), (6, 8))
+GROUPS = ((0, 4), (4, 8))
 
 epsilon = 1e-06
 MIB = 1 << 20
@@ -33,10 +33,6 @@
     return lax.dot_general(a, b, (((1,), (1,)), ((), ())), preferred_element_type=jnp.float32)
 
 
-def dot_tn(a, b):
-    return lax.dot_general(a, b, (((0,), (0,)), ((), ())), preferred_element_type=jnp.float32)
-
-
 def head_lanes(head):
     return slice(head * HD, (head + 1) * HD)
 
@@ -44,6 +40,20 @@
 def causal_mask():
     shape = (SPAN, SPAN)
     return lax.broadcasted_iota(jnp.int32, shape, 0) >= lax.broadcasted_iota(jnp.int32, shape, 1)
+
+
+def unit_matrix():
+    shape = (HD, HD)
+    same = lax.broadcasted_iota(jnp.int32, shape, 0) == lax.broadcasted_iota(jnp.int32, shape, 1)
+    return jnp.where(same, 1.0, 0.0).astype(jnp.bfloat16)
+
+
+def mean_of_squares(out):
+    squares = out * out
+    high = squares.astype(jnp.bfloat16)
+    low = (squares - high.astype(jnp.float32)).astype(jnp.bfloat16)
+    ones = jnp.ones((2 * HD, HD), jnp.bfloat16)
+    return dot(jnp.concatenate([high, low], axis=1), ones) * (1.0 / HD)
 
 
 def mix_heads(query, key, value, states):
@@ -57,13 +67,15 @@
         lanes, here = head_lanes(head), spans[span]
         scores = dot_nt(query[here, lanes], key[here, lanes])
         local[head, span] = jnp.where(causal, scores, 0.0).astype(jnp.bfloat16)
+    identity = unit_matrix()
     for head in heads:
         lanes = head_lanes(head)
         state = states[head]
+        turned = dot_nt(identity, key[: rows - SPAN, lanes]).astype(jnp.bfloat16)
         for span, here in enumerate(spans):
             before[head, span] = state
             if span + 1 < len(spans):
-                update = dot_tn(key[here, lanes], value[here, lanes])
+                update = dot(turned[:, here], value[here, lanes])
                 state = update if state is None else state + update
     for head, span in units:
         lanes, here = head_lanes(head), spans[span]
@@ -114,8 +126,7 @@
         states = [state_ref[head] if has_state else None for head in range(low, high)]
         for head, here, out in mix_heads(*parts, states):
             lanes = head_lanes(low + head)
-            mean_square = jnp.mean(out * out, axis=-1, keepdims=True)
-            normed = out * lax.rsqrt(mean_square + epsilon) * gains[:, lanes]
+            normed = out * lax.rsqrt(mean_of_squares(out) + epsilon) * gains[:, lanes]
             residual = tokens_ref[here, lanes].astype(jnp.float32)
             out_ref[here, lanes] = (residual + normed).astype(jnp.bfloat16)
         there = slice(low * HD, high * HD)

time: 57.3 us -> 57.9 us (1.010)
  Pallas kernels: 19.3 us -> 19.9 us
    pallas_call x1, Pallas kernels: 10.5 us -> 11.1 us  [mixer(): pl.pallas_call(functools.partial(mixer_kernel, state is not None), in_spe...]
where the time goes in v12:
time: 57.9 us; the launch traced here: 56.9 us
  waiting for transfers between devices  23.1 us (40%)
  Pallas kernels  19.9 us (34%)
  starting transfers between devices  13.6 us (23%)
    all_to_all x1, waiting for transfers between devices, to_frames(): lax.all_to_all(hidden.reshape(SB, rows // SB, columns), 'tm', 0, 0, axis_...  23.1 us
    pallas_call x1, Pallas kernels, mixer(): pl.pallas_call(functools.partial(mixer_kernel, state is not None), in_spe...  11.1 us
    all_to_all x1, starting transfers between devices, to_frames(): lax.all_to_all(hidden.reshape(SB, rows // SB, columns), 'tm', 0, 0, axis_...  7.5 us
    ppermute x2, starting transfers between devices, shifted(): return lax.ppermute(block, axis, route)  6.08 us
    pallas_call x2, Pallas kernels, earlier_frame(): pl.pallas_call(functools.partial(earlier_kernel, group), compiler_params=...  4.17 us
    pallas_call x1, Pallas kernels, own_frame(): pl.pallas_call(own_kernel, out_shape=[jax.ShapeDtypeStruct((rows, width),...  3.7 us
  transfers between devices with their start and end apart: 3, of which 1 were waited for; matrix products, arithmetic and copies ran while one was open for 0% of the time, Pallas kernels for 10%

profile of v12, /device:TPU:1, one launch (start us, length us, event | category | flops | bytes accessed | tf_op | source)
XLA Modules:
  0.0 56.9 jit_solution(9121138808525126374)
XLA Ops:
  0.0 11.1 %mixer.1 = bf16[512,1024]{1,0:T(8,128)(2,1)} custom-call(bf16[512,1024]{1,0:T(8,128)(2,1)} %bitcast.8, bf16[1024,3072]{1,0:T(8,128)(2,1)} %refs_1_.1, bf16[1024]{0:T(1024)(128)(2,1)} %refs_2_.1), custom_call_target="tpu_custom_call" | custom-call | flops 3758096384 | bytes 8388608 | tf_op jit(solution)/shard_map/mixer/pallas_call | solution.py:157
  11.1 0.0 copy-start.2
  11.1 0.0 copy-start
  11.1 7.5 %all-to-all-start = ((bf16[16,32,1024]{2,1,0:T(8,128)(2,1)}), bf16[16,32,1024]{2,1,0:T(8,128)(2,1)S(1)}, u32[]{:S(2)}, u32[]{:S(2)}) async-start(bf16[16,32,1024]{2,1,0:T(8,128)(2,1)} %bitcast.7), calls=%async_computation | async-start | bytes 2097152 | tf_op jit(solution)/shard_map/all_to_all | solution.py:359
  18.6 0.0 copy-done.2
  18.7 23.1 %all-to-all-done = bf16[16,32,1024]{2,1,0:T(8,128)(2,1)S(1)} async-done(((bf16[16,32,1024]{2,1,0:T(8,128)(2,1)}), bf16[16,32,1024]{2,1,0:T(8,128)(2,1)S(1)}, u32[]{:S(2)}, u32[]{:S(2)}) %all-to-all-start) | async-done | bytes 1048608 | tf_op jit(solution)/shard_map/all_to_all | solution.py:359
  41.8 0.0 copy-start.1
  41.8 0.0 copy-done
  41.8 1.0 %pairs.1 = (bf16[512,1024]{1,0:T(8,128)(2,1)S(1)}, bf16[512,256]{1,0:T(8,128)(2,1)S(1)}, bf16[512,256]{1,0:T(8,128)(2,1)S(1)}) custom-call(bf16[512,1024]{1,0:T(8,128)(2,1)S(1)} %bitcast.5, f32[1,1024]{1,0:T(1,128)S(1)} %bitcast.6, bf16[1024,512]{1,0:T(8,128)(2,1)S(1)} %copy-done), custom_call_target="tpu_custom_call" | custom-call | flops 536870912 | bytes 3670016 | tf_op jit(solution)/shard_map/pairs/pallas_call | solution.py:210
  42.8 3.2 %collective-permute-start.1 = (bf16[512,256]{1,0:T(8,128)(2,1)S(1)}, bf16[512,256]{1,0:T(8,128)(2,1)S(1)}, u32[]{:S(2)}, u32[]{:S(2)}) collective-permute-start(bf16[512,256]{1,0:T(8,128)(2,1)S(1)} %get-tuple-element.17.refs_0_), channel_id=1, source_target_pairs={{0,1},{1,2},{2,3},{3,4},{4,5},{5,6},{6,7},{7,8},{8,9},{9,10},{10,1... | collective-permute-start | bytes 786440 | tf_op jit(solution)/shard_map/ppermute | solution.py:25
  46.0 2.9 %collective-permute-start = (bf16[512,256]{1,0:T(8,128)(2,1)S(1)}, bf16[512,256]{1,0:T(8,128)(2,1)S(1)}, u32[]{:S(2)}, u32[]{:S(2)}) collective-permute-start(bf16[512,256]{1,0:T(8,128)(2,1)S(1)} %get-tuple-element.18.refs_1_), channel_id=1, source_target_pairs={{0,1},{1,2},{2,3},{3,4},{4,5},{5,6},{6,7},{7,8},{8,9},{9,10},{10,1... | collective-permute-start | bytes 786440 | tf_op jit(solution)/shard_map/ppermute | solution.py:25
  48.8 0.0 copy-done.1
  48.9 3.7 %own_frame.1 = (bf16[512,1024]{1,0:T(8,128)(2,1)S(1)}, f32[512,1024]{1,0:T(8,128)S(1)}, f32[512,1024]{1,0:T(8,128)S(1)}, f32[512,1024]{1,0:T(8,128)S(1)}) custom-call(bf16[512,1024]{1,0:T(8,128)(2,1)S(1)} %get-tuple-element.16.normed_ref, bf16[1024,1024]{1,0:T(8,128)(2,1)S(1)} %copy-done.1, bf16[512,256]{1,0:T(8,128)(2,1)S(1)} %get-tuple-element.17.refs_0_, ...), custom_call_target="tpu_custom_call" | custom-call | flops 2147483648 | bytes 6291456 | tf_op jit(solution)/shard_map/own_frame/pallas_call | solution.py:270
  52.6 0.0 collective-permute-done.1.pairs_ref
  52.6 1.7 %earlier_frame.2.refs_0_ = bf16[512,512]{1,0:T(8,128)(2,1)S(1)} custom-call(bf16[512,1024]{1,0:T(8,128)(2,1)S(1)} %get-tuple-element.19.query_ref, bf16[512,256]{1,0:T(8,128)(2,1)S(1)} %collective-permute-done.1.pairs_ref, f32[512,1024]{1,0:T(8,128)S(1)} %get-tuple-element.20.sum_ref, f32[512,1024]{1,0:T(8,128)S(1)} %get-tuple-element.21.total_ref, ...), custom_call_target="tpu_custom_call" | custom-call | flops 536870912 | bytes 5242880 | tf_op jit(solution)/shard_map/earlier_frame/pallas_call | solution.py:343
  54.3 0.0 collective-permute-done.pairs_ref
  54.3 2.5 %earlier_frame.3 = bf16[512,1024]{1,0:T(8,128)(2,1)} custom-call(bf16[512,1024]{1,0:T(8,128)(2,1)S(1)} %get-tuple-element.19.query_ref, bf16[512,256]{1,0:T(8,128)(2,1)S(1)} %collective-permute-done.pairs_ref, f32[512,1024]{1,0:T(8,128)S(1)} %get-tuple-element.20.sum_ref, f32[512,1024]{1,0:T(8,128)S(1)} %get-tuple-element.21.total_ref, ...), custom_call_target="tpu_custom_call" | custom-call | flops 536870912 | bytes 5242880 | tf_op jit(solution)/shard_map/earlier_frame/pallas_call | solution.py:343
  (1 shorter events, 0.0 us)
Async XLA Ops:
  11.1 7.5 %copy-start.2 = (bf16[1024]{0:T(1024)(128)(2,1)S(1)}, bf16[1024]{0:T(1024)(128)(2,1)}, u32[]{:S(2)}) copy-start(bf16[1024]{0:T(1024)(128)(2,1)} %param.11) | copy-start | bytes 6148
  11.1 30.7 %copy-start = (bf16[1024,512]{1,0:T(8,128)(2,1)S(1)}, bf16[1024,512]{1,0:T(8,128)(2,1)}, u32[]{:S(2)}) copy-start(bf16[1024,512]{1,0:T(8,128)(2,1)} %w_ref.2) | copy-start | bytes 3145732
  11.1 30.6 %all-to-all-start = ((bf16[16,32,1024]{2,1,0:T(8,128)(2,1)}), bf16[16,32,1024]{2,1,0:T(8,128)(2,1)S(1)}, u32[]{:S(2)}, u32[]{:S(2)}) async-start(bf16[16,32,1024]{2,1,0:T(8,128)(2,1)} %bitcast.7), calls=%async_computation | async-start | bytes 2097152 | tf_op jit(solution)/shard_map/all_to_all | solution.py:359
  41.8 7.1 %copy-start.1 = (bf16[1024,1024]{1,0:T(8,128)(2,1)S(1)}, bf16[1024,1024]{1,0:T(8,128)(2,1)}, u32[]{:S(2)}) copy-start(bf16[1024,1024]{1,0:T(8,128)(2,1)} %w_ref.3) | copy-start | bytes 6291460
  42.8 9.8 %collective-permute-start.1 = (bf16[512,256]{1,0:T(8,128)(2,1)S(1)}, bf16[512,256]{1,0:T(8,128)(2,1)S(1)}, u32[]{:S(2)}, u32[]{:S(2)}) collective-permute-start(bf16[512,256]{1,0:T(8,128)(2,1)S(1)} %get-tuple-element.17.refs_0_), channel_id=1, source_target_pairs={{0,1},{1,2},{2,3},{3,4},{4,5},{5,6},{6,7},{7,8},{8,9},{9,10},{10,1... | collective-permute-start | bytes 786440 | tf_op jit(solution)/shard_map/ppermute | solution.py:25
  46.0 8.3 %collective-permute-start = (bf16[512,256]{1,0:T(8,128)(2,1)S(1)}, bf16[512,256]{1,0:T(8,128)(2,1)S(1)}, u32[]{:S(2)}, u32[]{:S(2)}) collective-permute-start(bf16[512,256]{1,0:T(8,128)(2,1)S(1)} %get-tuple-element.18.refs_1_), channel_id=1, source_target_pairs={{0,1},{1,2},{2,3},{3,4},{4,5},{5,6},{6,7},{7,8},{8,9},{9,10},{10,1... | collective-permute-start | bytes 786440 | tf_op jit(solution)/shard_map/ppermute | solution.py:25

commit v13 on v11

--- a/solution.py
+++ b/solution.py
@@ -13,7 +13,8 @@
 KVH = 2
 SB = 16
 SPAN = 128
-GROUPS = ((0, 2), (2, 6), (6, 8))
+GROUPS = ((0, 4), (4, 8))
+APART = (0, 10, 11, 9, 2, 12, 6, 13, 3, 7, 1, 14, 4, 15, 8, 5)
 
 epsilon = 1e-06
 MIB = 1 << 20
@@ -83,9 +84,11 @@
 def mixer_kernel(has_state, *refs):
     if has_state:
         state_ref, *refs = refs
-    tokens_hbm, w_hbm, gain_ref, out_hbm, tokens_ref, out_ref, *refs = refs
-    *weights, tokens_in, weights_in, sent = refs
+    tokens_hbm, w_hbm, gain_ref, *refs = refs
+    tiles, (tokens_ref, out_ref, *weights, tokens_in, weights_in, sent) = refs[:SB], refs[SB:]
     rows, width = tokens_ref.shape
+    size = rows // SB
+    place = lax.rem(lax.axis_index("tm"), SB)
 
     first = [pltpu.make_async_copy(tokens_hbm, tokens_ref, tokens_in)]
     copies = []
@@ -103,6 +106,8 @@
         copy.start()
     gains = gain_ref[...].astype(jnp.float32).reshape(1, width)
 
+    leaving = []
+
     def project(index):
         for copy in copies[index]:
             copy.wait()
@@ -118,17 +123,20 @@
             normed = out * lax.rsqrt(mean_square + epsilon) * gains[:, lanes]
             residual = tokens_ref[here, lanes].astype(jnp.float32)
             out_ref[here, lanes] = (residual + normed).astype(jnp.bfloat16)
-        there = slice(low * HD, high * HD)
-        copy = pltpu.make_async_copy(out_ref.at[:, there], out_hbm.at[:, there], sent.at[index])
-        copy.start()
-        return copy
+        lanes = slice(low * HD, high * HD)
+        for slot, (apart, tile) in enumerate(zip(APART, tiles)):
+            here = pl.ds(pl.multiple_of((place ^ apart) * size, size), size)
+            copy = pltpu.make_async_copy(
+                out_ref.at[here, lanes], tile.at[:, lanes], sent.at[index, slot]
+            )
+            copy.start()
+            leaving.append(copy)
 
     first[0].wait()
     parts = project(0)
-    leaving = []
     for index in range(len(GROUPS)):
         upcoming = project(index + 1) if index + 1 < len(GROUPS) else None
-        leaving.append(mix(index, parts))
+        mix(index, parts)
         parts = upcoming
     for copy in leaving:
         copy.wait()
@@ -146,14 +154,14 @@
     return pl.pallas_call(
         functools.partial(mixer_kernel, state is not None),
         in_specs=in_specs,
-        out_specs=hbm,
-        out_shape=jax.ShapeDtypeStruct((rows, width), jnp.bfloat16),
+        out_specs=[hbm] * SB,
+        out_shape=[jax.ShapeDtypeStruct((rows // SB, width), jnp.bfloat16)] * SB,
         scratch_shapes=[pltpu.VMEM((rows, width), jnp.bfloat16)] * 2
         + [pltpu.VMEM((3, width, (high - low) * HD), jnp.bfloat16) for low, high in GROUPS]
         + [
             pltpu.SemaphoreType.DMA,
             pltpu.SemaphoreType.DMA((len(GROUPS), 3)),
-            pltpu.SemaphoreType.DMA((len(GROUPS),)),
+            pltpu.SemaphoreType.DMA((len(GROUPS), SB)),
         ],
         compiler_params=pltpu.CompilerParams(vmem_limit_bytes=56 * MIB),
         cost_estimate=pl.CostEstimate(
@@ -180,10 +188,12 @@
     return lax.fori_loop(0, time_ranges - 1, advance_hop, jnp.zeros_like(block_total))
 
 
-def pairs_kernel(hidden_ref, gain_ref, w_ref, normed_ref, *outs):
-    widened = hidden_ref[...].astype(jnp.float32)
+def pairs_kernel(gain_ref, w_ref, *refs):
+    tiles, normed_ref, outs = refs[:SB], refs[SB], refs[SB + 1 :]
+    gain = gain_ref[...].astype(jnp.float32).reshape(1, -1)
+    widened = jnp.concatenate([tile[...] for tile in tiles], axis=0).astype(jnp.float32)
     mean_square = jnp.mean(widened * widened, axis=-1, keepdims=True)
-    normed = (widened * lax.rsqrt(mean_square + epsilon) * gain_ref[...]).astype(jnp.bfloat16)
+    normed = (widened * lax.rsqrt(mean_square + epsilon) * gain).astype(jnp.bfloat16)
     normed_ref[...] = normed
     pairs = dot(normed, w_ref[...]).astype(jnp.bfloat16)
     for head, out_ref in enumerate(outs):
@@ -193,9 +203,9 @@
         out_ref[:, HD:] = pairs[:, head_lanes(KVH + head)]
 
 
-def make_pairs(hidden, gain, w_kv):
-    rows, width = hidden.shape
-    wide = w_kv.shape[1]
+def make_pairs(tiles, gain, w_kv):
+    width, wide = w_kv.shape
+    rows = sum(tile.shape[0] for tile in tiles)
     return pl.pallas_call(
         pairs_kernel,
         out_shape=[jax.ShapeDtypeStruct((rows, width), jnp.bfloat16)]
@@ -207,7 +217,7 @@
             transcendentals=rows,
         ),
         name="pairs",
-    )(hidden, gain, w_kv)
+    )(gain, w_kv, *tiles)
 
 
 SCORE_SCALE = math.log2(math.e) / math.sqrt(HD)
@@ -272,7 +282,10 @@
 
 def earlier_kernel(group, query_ref, pairs_ref, sum_ref, total_ref, top_ref, *refs):
     key, value = key_and_value(pairs_ref)
-    barred = jnp.where(lax.axis_index("tm") > 0, 0.0, -jnp.inf)
+    index = lax.axis_index("tm")
+    barred = jnp.where(index > 0, 0.0, -jnp.inf)
+    place = lax.rem(index, SB)
+    size = query_ref.shape[0] // SB
     columns = GROUP * HD
     last = group == KVH - 1
     copies = []
@@ -284,8 +297,8 @@
             copies.append(pltpu.make_async_copy(source, there, sent.at[len(copies)]))
             copies[-1].start()
 
-        for index, ref in enumerate(done_refs):
-            leave(ref, index * columns)
+        for part, ref in enumerate(done_refs):
+            leave(ref, part * columns)
     else:
         (out_ref,) = refs
 
@@ -305,7 +318,10 @@
         share = jnp.exp2(before - largest)
         mixed = sum_ref[:, lanes] * share + summed[:, :HD]
         total = total_ref[:, lanes] * share + summed[:, HD:]
-        out_ref[:, head_lanes(head)] = (mixed / total).astype(jnp.bfloat16)
+        mixed = (mixed / total).astype(jnp.bfloat16)
+        for slot, apart in enumerate(APART):
+            there = pl.ds(pl.multiple_of((place ^ apart) * size, size), size)
+            out_ref[there, head_lanes(head)] = mixed[slot * size : (slot + 1) * size]
         if last and head % 2:
             start = (head - 1) * HD
             leave(out_ref.at[:, start : start + 2 * HD], group * columns + start)
@@ -342,24 +358,22 @@
     )(*operands)
 
 
-def to_frames(hidden):
-    rows, columns = hidden.shape
-    teams = [[t * SB + s for s in range(SB)] for t in range(lax.axis_size("tm") // SB)]
-    moved = lax.all_to_all(
-        hidden.reshape(SB, rows // SB, columns), "tm", 0, 0, axis_index_groups=teams, tiled=True
-    )
-    return moved.reshape(rows, columns)
+def swap(tile, apart):
+    devices = lax.axis_size("tm")
+    route = [(i, i - i % SB + (i % SB ^ apart)) for i in range(devices)]
+    return lax.ppermute(tile, "tm", route)
 
 
 def body(space_time, w_lin, gain_lin, w_query, w_kv, frame_attention_gain):
     tokens = space_time[0]
     time_ranges = lax.axis_size("tm") // SB
     state = incoming_state(tokens, w_lin, time_ranges) if time_ranges > 1 else None
-    hidden = mixer(tokens, w_lin, gain_lin, state)
-    hidden, gain = lax.optimization_barrier((hidden, frame_attention_gain))
-    frame_rows = to_frames(hidden)
-    gain = gain.astype(jnp.float32).reshape(1, -1)
-    normed, *pairs = make_pairs(frame_rows, gain, w_kv)
+    tiles = list(mixer(tokens, w_lin, gain_lin, state))
+    tiles[0], w_query, w_kv, frame_attention_gain = lax.optimization_barrier(
+        (tiles[0], w_query, w_kv, frame_attention_gain)
+    )
+    tiles = [swap(tile, apart) if apart else tile for apart, tile in zip(APART, tiles)]
+    normed, *pairs = make_pairs(tiles, frame_attention_gain, w_kv)
     earlier_pairs = [shifted(part, "tm", 1) for part in pairs]
     query, *so_far = own_frame(normed, w_query, pairs)
     done = []

time: 57.3 us -> 57.7 us (level)
  waiting for transfers between devices: 23.1 us -> 4.75 us
  starting transfers between devices: 13.6 us -> 31.9 us
  local copies, waits for them, and re-layouts: 0.02 us -> 0.85 us
    ppermute x0 -> x15, starting transfers between devices: none -> 26.5 us  [swap(): return lax.ppermute(tile, 'tm', route)]
    all_to_all x1 -> x0, waiting for transfers between devices: 23.1 us -> none  [to_frames(): lax.all_to_all(hidden.reshape(SB, rows // SB, columns), 'tm', 0, 0, axis_...]
    all_to_all x1 -> x0, starting transfers between devices: 7.49 us -> none  [to_frames(): lax.all_to_all(hidden.reshape(SB, rows // SB, columns), 'tm', 0, 0, axis_...]
    ppermute x0 -> x15, waiting for transfers between devices: none -> 4.75 us  [swap(): return lax.ppermute(tile, 'tm', route)]
    unnamed x6 -> x8, local copies, waits for them, and re-layouts: 0.02 us -> 0.85 us
    ppermute x2, starting transfers between devices: 6.08 us -> 5.38 us  [shifted(): return lax.ppermute(block, axis, route)]
  transfers between devices with their start and end apart: 3 -> 17, of which waited for: 1 -> 3; matrix products, arithmetic and copies ran while one was open for 0% -> 0% of each run, Pallas kernels for 10% -> 10%
where the time goes in v13:
time: 57.7 us; the launch traced here: 57.2 us
  starting transfers between devices  31.9 us (55%)
  Pallas kernels  19.4 us (34%)
  waiting for transfers between devices  4.75 us (8%)
  local copies, waits for them, and re-layouts  0.85 us (1%)
    ppermute x15, starting transfers between devices, swap(): return lax.ppermute(tile, 'tm', route)  26.5 us
    pallas_call x1, Pallas kernels, mixer(): pl.pallas_call(functools.partial(mixer_kernel, state is not None), in_spe...  10.4 us
    ppermute x2, starting transfers between devices, shifted(): return lax.ppermute(block, axis, route)  5.38 us
    ppermute x15, waiting for transfers between devices, swap(): return lax.ppermute(tile, 'tm', route)  4.75 us
    pallas_call x2, Pallas kernels, earlier_frame(): pl.pallas_call(functools.partial(earlier_kernel, group), compiler_params=...  4.19 us
    pallas_call x1, Pallas kernels, own_frame(): pl.pallas_call(own_kernel, out_shape=[jax.ShapeDtypeStruct((rows, width),...  3.72 us
  transfers between devices with their start and end apart: 17, of which 3 were waited for; matrix products, arithmetic and copies ran while one was open for 0% of the time, Pallas kernels for 10%

profile of v13, /device:TPU:1, one launch (start us, length us, event | category | flops | bytes accessed | tf_op | source)
XLA Modules:
  0.0 57.2 jit_solution(16431735999652598806)
XLA Ops:
  0.0 10.4 %mixer.1 = (bf16[32,1024]{1,0:T(8,128)(2,1)}, bf16[32,1024]{1,0:T(8,128)(2,1)}, bf16[32,1024]{1,0:T(8,128)(2,1)}, bf16[32,1024]{1,0:T(8,128)(2,1)}, bf16[32,1024...) custom-call(bf16[512,1024]{1,0:T(8,128)(2,1)} %bitcast.2, ...), custom_call_target="tpu_custom_call" | custom-call | flops 3758096384 | bytes 8388608 | tf_op jit(solution)/shard_map/mixer/pallas_call | solution.py:154
  10.5 4.2 %collective-permute-start = (bf16[32,1024]{1,0:T(8,128)(2,1)}, bf16[32,1024]{1,0:T(8,128)(2,1)S(1)}, u32[]{:S(2)}, u32[]{:S(2)}) collective-permute-start(bf16[32,1024]{1,0:T(8,128)(2,1)} %get-tuple-element.36), channel_id=1, source_target_pairs={{0,10},{1,11},{2,8},{3,9},{4,14},{5,15},{6,12},{7,13},{8,2},{9,3},... | collective-permute-start | bytes 196616 | tf_op jit(solution)/shard_map/ppermute | solution.py:364
  14.6 0.6 %collective-permute-start.1 = (bf16[32,1024]{1,0:T(8,128)(2,1)}, bf16[32,1024]{1,0:T(8,128)(2,1)S(1)}, u32[]{:S(2)}, u32[]{:S(2)}) collective-permute-start(bf16[32,1024]{1,0:T(8,128)(2,1)} %get-tuple-element.37), channel_id=1, source_target_pairs={{0,11},{1,10},{2,9},{3,8},{4,15},{5,14},{6,13},{7,12},{8,3},{9,2},... | collective-permute-start | bytes 196616 | tf_op jit(solution)/shard_map/ppermute | solution.py:364
  15.3 4.5 %collective-permute-start.10 = (bf16[32,1024]{1,0:T(8,128)(2,1)}, bf16[32,1024]{1,0:T(8,128)(2,1)S(1)}, u32[]{:S(2)}, u32[]{:S(2)}) collective-permute-start(bf16[32,1024]{1,0:T(8,128)(2,1)} %get-tuple-element.46), channel_id=1, source_target_pairs={{0,14},{1,15},{2,12},{3,13},{4,10},{5,11},{6,8},{7,9},{8,6},{9,7},... | collective-permute-start | bytes 196616 | tf_op jit(solution)/shard_map/ppermute | solution.py:364
  19.7 0.0 collective-permute-start.11
  19.7 0.9 %collective-permute-start.12 = (bf16[32,1024]{1,0:T(8,128)(2,1)}, bf16[32,1024]{1,0:T(8,128)(2,1)S(1)}, u32[]{:S(2)}, u32[]{:S(2)}) collective-permute-start(bf16[32,1024]{1,0:T(8,128)(2,1)} %get-tuple-element.48), channel_id=1, source_target_pairs={{0,15},{1,14},{2,13},{3,12},{4,11},{5,10},{6,9},{7,8},{8,7},{9,6},... | collective-permute-start | bytes 196616 | tf_op jit(solution)/shard_map/ppermute | solution.py:364
  20.6 1.7 %collective-permute-start.13 = (bf16[32,1024]{1,0:T(8,128)(2,1)}, bf16[32,1024]{1,0:T(8,128)(2,1)S(1)}, u32[]{:S(2)}, u32[]{:S(2)}) collective-permute-start(bf16[32,1024]{1,0:T(8,128)(2,1)} %get-tuple-element.49), channel_id=1, source_target_pairs={{0,8},{1,9},{2,10},{3,11},{4,12},{5,13},{6,14},{7,15},{8,0},{9,1},... | collective-permute-start | bytes 196616 | tf_op jit(solution)/shard_map/ppermute | solution.py:364
  22.3 1.3 %collective-permute-done.1.refs_2_ = bf16[32,1024]{1,0:T(8,128)(2,1)S(1)} collective-permute-done((bf16[32,1024]{1,0:T(8,128)(2,1)}, bf16[32,1024]{1,0:T(8,128)(2,1)S(1)}, u32[]{:S(2)}, u32[]{:S(2)}) %collective-permute-start.1) | collective-permute-done | bytes 65568 | tf_op jit(solution)/shard_map/ppermute | solution.py:364
  23.7 1.2 %collective-permute-start.14 = (bf16[32,1024]{1,0:T(8,128)(2,1)}, bf16[32,1024]{1,0:T(8,128)(2,1)S(1)}, u32[]{:S(2)}, u32[]{:S(2)}) collective-permute-start(bf16[32,1024]{1,0:T(8,128)(2,1)} %get-tuple-element.50), channel_id=1, source_target_pairs={{0,5},{1,4},{2,7},{3,6},{4,1},{5,0},{6,3},{7,2},{8,13},{9,12},{10,... | collective-permute-start | bytes 196616 | tf_op jit(solution)/shard_map/ppermute | solution.py:364
  24.9 0.0 collective-permute-done.10.refs_11_
  24.9 5.5 %collective-permute-start.2 = (bf16[32,1024]{1,0:T(8,128)(2,1)}, bf16[32,1024]{1,0:T(8,128)(2,1)S(1)}, u32[]{:S(2)}, u32[]{:S(2)}) collective-permute-start(bf16[32,1024]{1,0:T(8,128)(2,1)} %get-tuple-element.38), channel_id=1, source_target_pairs={{0,9},{1,8},{2,11},{3,10},{4,13},{5,12},{6,15},{7,14},{8,1},{9,0},... | collective-permute-start | bytes 196616 | tf_op jit(solution)/shard_map/ppermute | solution.py:364
  30.4 0.9 %collective-permute-start.3 = (bf16[32,1024]{1,0:T(8,128)(2,1)}, bf16[32,1024]{1,0:T(8,128)(2,1)S(1)}, u32[]{:S(2)}, u32[]{:S(2)}) collective-permute-start(bf16[32,1024]{1,0:T(8,128)(2,1)} %get-tuple-element.39), channel_id=1, source_target_pairs={{0,2},{1,3},{2,0},{3,1},{4,6},{5,7},{6,4},{7,5},{8,10},{9,11},{10,... | collective-permute-start | bytes 196616 | tf_op jit(solution)/shard_map/ppermute | solution.py:364
  31.3 0.2 collective-permute-start.4
  31.5 0.7 %collective-permute-start.5 = (bf16[32,1024]{1,0:T(8,128)(2,1)}, bf16[32,1024]{1,0:T(8,128)(2,1)S(1)}, u32[]{:S(2)}, u32[]{:S(2)}) collective-permute-start(bf16[32,1024]{1,0:T(8,128)(2,1)} %get-tuple-element.41), channel_id=1, source_target_pairs={{0,6},{1,7},{2,4},{3,5},{4,2},{5,3},{6,0},{7,1},{8,14},{9,15},{10,... | collective-permute-start | bytes 196616 | tf_op jit(solution)/shard_map/ppermute | solution.py:364
  32.2 2.8 %collective-permute-start.6 = (bf16[32,1024]{1,0:T(8,128)(2,1)}, bf16[32,1024]{1,0:T(8,128)(2,1)S(1)}, u32[]{:S(2)}, u32[]{:S(2)}) collective-permute-start(bf16[32,1024]{1,0:T(8,128)(2,1)} %get-tuple-element.42), channel_id=1, source_target_pairs={{0,13},{1,12},{2,15},{3,14},{4,9},{5,8},{6,11},{7,10},{8,5},{9,4},... | collective-permute-start | bytes 196616 | tf_op jit(solution)/shard_map/ppermute | solution.py:364
  35.0 0.5 collective-permute-start.7
  35.5 1.3 %collective-permute-start.8 = (bf16[32,1024]{1,0:T(8,128)(2,1)}, bf16[32,1024]{1,0:T(8,128)(2,1)S(1)}, u32[]{:S(2)}, u32[]{:S(2)}) collective-permute-start(bf16[32,1024]{1,0:T(8,128)(2,1)} %get-tuple-element.44), channel_id=1, source_target_pairs={{0,7},{1,6},{2,5},{3,4},{4,3},{5,2},{6,1},{7,0},{8,15},{9,14},{10,... | collective-permute-start | bytes 196616 | tf_op jit(solution)/shard_map/ppermute | solution.py:364
  36.7 0.0 collective-permute-done.4.refs_5_
  36.8 1.6 %collective-permute-start.9 = (bf16[32,1024]{1,0:T(8,128)(2,1)}, bf16[32,1024]{1,0:T(8,128)(2,1)S(1)}, u32[]{:S(2)}, u32[]{:S(2)}) collective-permute-start(bf16[32,1024]{1,0:T(8,128)(2,1)} %get-tuple-element.45), channel_id=1, source_target_pairs={{0,1},{1,0},{2,3},{3,2},{4,5},{5,4},{6,7},{7,6},{8,9},{9,8},{10,11... | collective-permute-start | bytes 196616 | tf_op jit(solution)/shard_map/ppermute | solution.py:364
  38.4 1.9 %collective-permute-done.6.refs_7_ = bf16[32,1024]{1,0:T(8,128)(2,1)S(1)} collective-permute-done((bf16[32,1024]{1,0:T(8,128)(2,1)}, bf16[32,1024]{1,0:T(8,128)(2,1)S(1)}, u32[]{:S(2)}, u32[]{:S(2)}) %collective-permute-start.6) | collective-permute-done | bytes 65568 | tf_op jit(solution)/shard_map/ppermute | solution.py:364
  40.3 1.5 %collective-permute-done.8.refs_9_ = bf16[32,1024]{1,0:T(8,128)(2,1)S(1)} collective-permute-done((bf16[32,1024]{1,0:T(8,128)(2,1)}, bf16[32,1024]{1,0:T(8,128)(2,1)S(1)}, u32[]{:S(2)}, u32[]{:S(2)}) %collective-permute-start.8) | collective-permute-done | bytes 65568 | tf_op jit(solution)/shard_map/ppermute | solution.py:364
  41.8 0.0 collective-permute-done.9.refs_10_
  41.8 0.0 copy-start.1
  41.8 0.8 %copy-done.1 = bf16[32,1024]{1,0:T(8,128)(2,1)S(1)} copy-done((bf16[32,1024]{1,0:T(8,128)(2,1)S(1)}, bf16[32,1024]{1,0:T(8,128)(2,1)}, u32[]{:S(2)}) %copy-start.1) | copy-done | bytes 65560
  42.6 1.0 %pairs.1 = (bf16[512,1024]{1,0:T(8,128)(2,1)S(1)}, bf16[512,256]{1,0:T(8,128)(2,1)S(1)}, bf16[512,256]{1,0:T(8,128)(2,1)S(1)}) custom-call(bf16[1024]{0:T(1024)(128)(2,1)S(1)} %copy-done.2, bf16[1024,512]{1,0:T(8,128)(2,1)S(1)} %copy-done, bf16[32,1024]{1,0:T(8,128)(2,1)S(1)} %copy-done.1, bf16[32,1024]{1,0:T(8,128)(2,1)S(1)} %collective-permute-done.refs_1_, ...), custom_call_target="tpu_custom_call" | custom-call | flops 536870912 | bytes 3670016 | tf_op jit(solution)/shard_map/pairs/pallas_call | solution.py:209
  43.7 3.2 %collective-permute-start.16 = (bf16[512,256]{1,0:T(8,128)(2,1)S(1)}, bf16[512,256]{1,0:T(8,128)(2,1)S(1)}, u32[]{:S(2)}, u32[]{:S(2)}) collective-permute-start(bf16[512,256]{1,0:T(8,128)(2,1)S(1)} %get-tuple-element.53.refs_0_), channel_id=1, source_target_pairs={{0,1},{1,2},{2,3},{3,4},{4,5},{5,6},{6,7},{7,8},{8,9},{9,10},{10,1... | collective-permute-start | bytes 786440 | tf_op jit(solution)/shard_map/ppermute | solution.py:26
  46.8 2.2 %collective-permute-start.15 = (bf16[512,256]{1,0:T(8,128)(2,1)S(1)}, bf16[512,256]{1,0:T(8,128)(2,1)S(1)}, u32[]{:S(2)}, u32[]{:S(2)}) collective-permute-start(bf16[512,256]{1,0:T(8,128)(2,1)S(1)} %get-tuple-element.54.refs_1_), channel_id=1, source_target_pairs={{0,1},{1,2},{2,3},{3,4},{4,5},{5,6},{6,7},{7,8},{8,9},{9,10},{10,1... | collective-permute-start | bytes 786440 | tf_op jit(solution)/shard_map/ppermute | solution.py:26
  49.1 3.7 %own_frame.1 = (bf16[512,1024]{1,0:T(8,128)(2,1)S(1)}, f32[512,1024]{1,0:T(8,128)S(1)}, f32[512,1024]{1,0:T(8,128)S(1)}, f32[512,1024]{1,0:T(8,128)S(1)}) custom-call(bf16[512,1024]{1,0:T(8,128)(2,1)S(1)} %get-tuple-element.51.normed_ref, bf16[1024,1024]{1,0:T(8,128)(2,1)S(1)} %copy-done.3, bf16[512,256]{1,0:T(8,128)(2,1)S(1)} %get-tuple-element.53.refs_0_, ...), custom_call_target="tpu_custom_call" | custom-call | flops 2147483648 | bytes 6291456 | tf_op jit(solution)/shard_map/own_frame/pallas_call | solution.py:269
  52.8 0.0 collective-permute-done.16.pairs_ref
  52.8 1.7 %earlier_frame.2.refs_0_ = bf16[512,512]{1,0:T(8,128)(2,1)S(1)} custom-call(bf16[512,1024]{1,0:T(8,128)(2,1)S(1)} %get-tuple-element.55.query_ref, bf16[512,256]{1,0:T(8,128)(2,1)S(1)} %collective-permute-done.16.pairs_ref, f32[512,1024]{1,0:T(8,128)S(1)} %get-tuple-element.56.sum_ref, f32[512,1024]{1,0:T(8,128)S(1)} %get-tuple-element.57.total_ref, ...), custom_call_target="tpu_custom_call" | custom-call | flops 536870912 | bytes 5242880 | tf_op jit(solution)/shard_map/earlier_frame/pallas_call | solution.py:348
  54.5 0.0 collective-permute-done.15.pairs_ref
  54.5 2.5 %earlier_frame.3 = bf16[512,1024]{1,0:T(8,128)(2,1)} custom-call(bf16[512,1024]{1,0:T(8,128)(2,1)S(1)} %get-tuple-element.55.query_ref, bf16[512,256]{1,0:T(8,128)(2,1)S(1)} %collective-permute-done.15.pairs_ref, f32[512,1024]{1,0:T(8,128)S(1)} %get-tuple-element.56.sum_ref, f32[512,1024]{1,0:T(8,128)S(1)} %get-tuple-element.57.total_ref, ...), custom_call_target="tpu_custom_call" | custom-call | flops 536870912 | bytes 5242880 | tf_op jit(solution)/shard_map/earlier_frame/pallas_call | solution.py:348
  (15 shorter events, 0.0 us)
Async XLA Ops:
  0.0 41.8 %copy-start = (bf16[1024,512]{1,0:T(8,128)(2,1)S(1)}, bf16[1024,512]{1,0:T(8,128)(2,1)}, u32[]{:S(2)}) copy-start(bf16[1024,512]{1,0:T(8,128)(2,1)} %w_ref) | copy-start | bytes 3145732
  0.0 41.8 %copy-start.2 = (bf16[1024]{0:T(1024)(128)(2,1)S(1)}, bf16[1024]{0:T(1024)(128)(2,1)}, u32[]{:S(2)}) copy-start(bf16[1024]{0:T(1024)(128)(2,1)} %gain_ref) | copy-start | bytes 6148
  0.0 49.0 %copy-start.3 = (bf16[1024,1024]{1,0:T(8,128)(2,1)S(1)}, bf16[1024,1024]{1,0:T(8,128)(2,1)}, u32[]{:S(2)}) copy-start(bf16[1024,1024]{1,0:T(8,128)(2,1)} %w_ref.1) | copy-start | bytes 6291460
  10.5 10.2 %collective-permute-start = (bf16[32,1024]{1,0:T(8,128)(2,1)}, bf16[32,1024]{1,0:T(8,128)(2,1)S(1)}, u32[]{:S(2)}, u32[]{:S(2)}) collective-permute-start(bf16[32,1024]{1,0:T(8,128)(2,1)} %get-tuple-element.36), channel_id=1, source_target_pairs={{0,10},{1,11},{2,8},{3,9},{4,14},{5,15},{6,12},{7,13},{8,2},{9,3},... | collective-permute-start | bytes 196616 | tf_op jit(solution)/shard_map/ppermute | solution.py:364
  14.6 9.0 %collective-permute-start.1 = (bf16[32,1024]{1,0:T(8,128)(2,1)}, bf16[32,1024]{1,0:T(8,128)(2,1)S(1)}, u32[]{:S(2)}, u32[]{:S(2)}) collective-permute-start(bf16[32,1024]{1,0:T(8,128)(2,1)} %get-tuple-element.37), channel_id=1, source_target_pairs={{0,11},{1,10},{2,9},{3,8},{4,15},{5,14},{6,13},{7,12},{8,3},{9,2},... | collective-permute-start | bytes 196616 | tf_op jit(solution)/shard_map/ppermute | solution.py:364
  15.3 9.6 %collective-permute-start.10 = (bf16[32,1024]{1,0:T(8,128)(2,1)}, bf16[32,1024]{1,0:T(8,128)(2,1)S(1)}, u32[]{:S(2)}, u32[]{:S(2)}) collective-permute-start(bf16[32,1024]{1,0:T(8,128)(2,1)} %get-tuple-element.46), channel_id=1, source_target_pairs={{0,14},{1,15},{2,12},{3,13},{4,10},{5,11},{6,8},{7,9},{8,6},{9,7},... | collective-permute-start | bytes 196616 | tf_op jit(solution)/shard_map/ppermute | solution.py:364
  19.7 10.6 %collective-permute-start.11 = (bf16[32,1024]{1,0:T(8,128)(2,1)}, bf16[32,1024]{1,0:T(8,128)(2,1)S(1)}, u32[]{:S(2)}, u32[]{:S(2)}) collective-permute-start(bf16[32,1024]{1,0:T(8,128)(2,1)} %get-tuple-element.47), channel_id=1, source_target_pairs={{0,4},{1,5},{2,6},{3,7},{4,0},{5,1},{6,2},{7,3},{8,12},{9,13},{10,... | collective-permute-start | bytes 196616 | tf_op jit(solution)/shard_map/ppermute | solution.py:364
  19.7 11.5 %collective-permute-start.12 = (bf16[32,1024]{1,0:T(8,128)(2,1)}, bf16[32,1024]{1,0:T(8,128)(2,1)S(1)}, u32[]{:S(2)}, u32[]{:S(2)}) collective-permute-start(bf16[32,1024]{1,0:T(8,128)(2,1)} %get-tuple-element.48), channel_id=1, source_target_pairs={{0,15},{1,14},{2,13},{3,12},{4,11},{5,10},{6,9},{7,8},{8,7},{9,6},... | collective-permute-start | bytes 196616 | tf_op jit(solution)/shard_map/ppermute | solution.py:364
  20.6 10.9 %collective-permute-start.13 = (bf16[32,1024]{1,0:T(8,128)(2,1)}, bf16[32,1024]{1,0:T(8,128)(2,1)S(1)}, u32[]{:S(2)}, u32[]{:S(2)}) collective-permute-start(bf16[32,1024]{1,0:T(8,128)(2,1)} %get-tuple-element.49), channel_id=1, source_target_pairs={{0,8},{1,9},{2,10},{3,11},{4,12},{5,13},{6,14},{7,15},{8,0},{9,1},... | collective-permute-start | bytes 196616 | tf_op jit(solution)/shard_map/ppermute | solution.py:364
  23.7 8.6 %collective-permute-start.14 = (bf16[32,1024]{1,0:T(8,128)(2,1)}, bf16[32,1024]{1,0:T(8,128)(2,1)S(1)}, u32[]{:S(2)}, u32[]{:S(2)}) collective-permute-start(bf16[32,1024]{1,0:T(8,128)(2,1)} %get-tuple-element.50), channel_id=1, source_target_pairs={{0,5},{1,4},{2,7},{3,6},{4,1},{5,0},{6,3},{7,2},{8,13},{9,12},{10,... | collective-permute-start | bytes 196616 | tf_op jit(solution)/shard_map/ppermute | solution.py:364
  24.9 10.1 %collective-permute-start.2 = (bf16[32,1024]{1,0:T(8,128)(2,1)}, bf16[32,1024]{1,0:T(8,128)(2,1)S(1)}, u32[]{:S(2)}, u32[]{:S(2)}) collective-permute-start(bf16[32,1024]{1,0:T(8,128)(2,1)} %get-tuple-element.38), channel_id=1, source_target_pairs={{0,9},{1,8},{2,11},{3,10},{4,13},{5,12},{6,15},{7,14},{8,1},{9,0},... | collective-permute-start | bytes 196616 | tf_op jit(solution)/shard_map/ppermute | solution.py:364
  30.4 5.1 %collective-permute-start.3 = (bf16[32,1024]{1,0:T(8,128)(2,1)}, bf16[32,1024]{1,0:T(8,128)(2,1)S(1)}, u32[]{:S(2)}, u32[]{:S(2)}) collective-permute-start(bf16[32,1024]{1,0:T(8,128)(2,1)} %get-tuple-element.39), channel_id=1, source_target_pairs={{0,2},{1,3},{2,0},{3,1},{4,6},{5,7},{6,4},{7,5},{8,10},{9,11},{10,... | collective-permute-start | bytes 196616 | tf_op jit(solution)/shard_map/ppermute | solution.py:364
  31.3 5.5 %collective-permute-start.4 = (bf16[32,1024]{1,0:T(8,128)(2,1)}, bf16[32,1024]{1,0:T(8,128)(2,1)S(1)}, u32[]{:S(2)}, u32[]{:S(2)}) collective-permute-start(bf16[32,1024]{1,0:T(8,128)(2,1)} %get-tuple-element.40), channel_id=1, source_target_pairs={{0,12},{1,13},{2,14},{3,15},{4,8},{5,9},{6,10},{7,11},{8,4},{9,5},... | collective-permute-start | bytes 196616 | tf_op jit(solution)/shard_map/ppermute | solution.py:364
  31.5 6.9 %collective-permute-start.5 = (bf16[32,1024]{1,0:T(8,128)(2,1)}, bf16[32,1024]{1,0:T(8,128)(2,1)S(1)}, u32[]{:S(2)}, u32[]{:S(2)}) collective-permute-start(bf16[32,1024]{1,0:T(8,128)(2,1)} %get-tuple-element.41), channel_id=1, source_target_pairs={{0,6},{1,7},{2,4},{3,5},{4,2},{5,3},{6,0},{7,1},{8,14},{9,15},{10,... | collective-permute-start | bytes 196616 | tf_op jit(solution)/shard_map/ppermute | solution.py:364
  32.2 8.1 %collective-permute-start.6 = (bf16[32,1024]{1,0:T(8,128)(2,1)}, bf16[32,1024]{1,0:T(8,128)(2,1)S(1)}, u32[]{:S(2)}, u32[]{:S(2)}) collective-permute-start(bf16[32,1024]{1,0:T(8,128)(2,1)} %get-tuple-element.42), channel_id=1, source_target_pairs={{0,13},{1,12},{2,15},{3,14},{4,9},{5,8},{6,11},{7,10},{8,5},{9,4},... | collective-permute-start | bytes 196616 | tf_op jit(solution)/shard_map/ppermute | solution.py:364
  35.0 5.3 %collective-permute-start.7 = (bf16[32,1024]{1,0:T(8,128)(2,1)}, bf16[32,1024]{1,0:T(8,128)(2,1)S(1)}, u32[]{:S(2)}, u32[]{:S(2)}) collective-permute-start(bf16[32,1024]{1,0:T(8,128)(2,1)} %get-tuple-element.43), channel_id=1, source_target_pairs={{0,3},{1,2},{2,1},{3,0},{4,7},{5,6},{6,5},{7,4},{8,11},{9,10},{10,... | collective-permute-start | bytes 196616 | tf_op jit(solution)/shard_map/ppermute | solution.py:364
  35.5 6.3 %collective-permute-start.8 = (bf16[32,1024]{1,0:T(8,128)(2,1)}, bf16[32,1024]{1,0:T(8,128)(2,1)S(1)}, u32[]{:S(2)}, u32[]{:S(2)}) collective-permute-start(bf16[32,1024]{1,0:T(8,128)(2,1)} %get-tuple-element.44), channel_id=1, source_target_pairs={{0,7},{1,6},{2,5},{3,4},{4,3},{5,2},{6,1},{7,0},{8,15},{9,14},{10,... | collective-permute-start | bytes 196616 | tf_op jit(solution)/shard_map/ppermute | solution.py:364
  36.8 5.0 %collective-permute-start.9 = (bf16[32,1024]{1,0:T(8,128)(2,1)}, bf16[32,1024]{1,0:T(8,128)(2,1)S(1)}, u32[]{:S(2)}, u32[]{:S(2)}) collective-permute-start(bf16[32,1024]{1,0:T(8,128)(2,1)} %get-tuple-element.45), channel_id=1, source_target_pairs={{0,1},{1,0},{2,3},{3,2},{4,5},{5,4},{6,7},{7,6},{8,9},{9,8},{10,11... | collective-permute-start | bytes 196616 | tf_op jit(solution)/shard_map/ppermute | solution.py:364
  41.8 0.8 %copy-start.1 = (bf16[32,1024]{1,0:T(8,128)(2,1)S(1)}, bf16[32,1024]{1,0:T(8,128)(2,1)}, u32[]{:S(2)}) copy-start(bf16[32,1024]{1,0:T(8,128)(2,1)} %get-tuple-element.35.refs_0_) | copy-start | bytes 196612
  43.7 9.1 %collective-permute-start.16 = (bf16[512,256]{1,0:T(8,128)(2,1)S(1)}, bf16[512,256]{1,0:T(8,128)(2,1)S(1)}, u32[]{:S(2)}, u32[]{:S(2)}) collective-permute-start(bf16[512,256]{1,0:T(8,128)(2,1)S(1)} %get-tuple-element.53.refs_0_), channel_id=1, source_target_pairs={{0,1},{1,2},{2,3},{3,4},{4,5},{5,6},{6,7},{7,8},{8,9},{9,10},{10,1... | collective-permute-start | bytes 786440 | tf_op jit(solution)/shard_map/ppermute | solution.py:26
  46.8 7.7 %collective-permute-start.15 = (bf16[512,256]{1,0:T(8,128)(2,1)S(1)}, bf16[512,256]{1,0:T(8,128)(2,1)S(1)}, u32[]{:S(2)}, u32[]{:S(2)}) collective-permute-start(bf16[512,256]{1,0:T(8,128)(2,1)S(1)} %get-tuple-element.54.refs_1_), channel_id=1, source_target_pairs={{0,1},{1,2},{2,3},{3,4},{4,5},{5,6},{6,7},{7,8},{8,9},{9,10},{10,1... | collective-permute-start | bytes 786440 | tf_op jit(solution)/shard_map/ppermute | solution.py:26

commit v14 on v13

--- a/solution.py
+++ b/solution.py
@@ -14,7 +14,23 @@
 SB = 16
 SPAN = 128
 GROUPS = ((0, 4), (4, 8))
-APART = (0, 10, 11, 9, 2, 12, 6, 13, 3, 7, 1, 14, 4, 15, 8, 5)
+PLANE = 4
+HOPS = (
+    (0, 0), (1, 0), (2, 0), (1, 2),
+    (2, 2), (0, 2), (3, 0), (3, 3),
+    (0, 3), (3, 1), (3, 2), (1, 3),
+    (2, 3), (0, 1), (1, 1), (2, 1),
+)
+
+
+def place_after(place, hop, back=False):
+    planes = SB // PLANE
+    turn = planes - hop[0] if back else hop[0]
+    if isinstance(place, int):
+        return (place // PLANE + turn) % planes * PLANE + (place % PLANE ^ hop[1])
+    plane = lax.rem(lax.div(place, PLANE) + turn, planes)
+    return plane * PLANE + (lax.rem(place, PLANE) ^ hop[1])
+
 
 epsilon = 1e-06
 MIB = 1 << 20
@@ -106,8 +122,6 @@
         copy.start()
     gains = gain_ref[...].astype(jnp.float32).reshape(1, width)
 
-    leaving = []
-
     def project(index):
         for copy in copies[index]:
             copy.wait()
@@ -123,14 +137,6 @@
             normed = out * lax.rsqrt(mean_square + epsilon) * gains[:, lanes]
             residual = tokens_ref[here, lanes].astype(jnp.float32)
             out_ref[here, lanes] = (residual + normed).astype(jnp.bfloat16)
-        lanes = slice(low * HD, high * HD)
-        for slot, (apart, tile) in enumerate(zip(APART, tiles)):
-            here = pl.ds(pl.multiple_of((place ^ apart) * size, size), size)
-            copy = pltpu.make_async_copy(
-                out_ref.at[here, lanes], tile.at[:, lanes], sent.at[index, slot]
-            )
-            copy.start()
-            leaving.append(copy)
 
     first[0].wait()
     parts = project(0)
@@ -138,6 +144,11 @@
         upcoming = project(index + 1) if index + 1 < len(GROUPS) else None
         mix(index, parts)
         parts = upcoming
+    leaving = []
+    for slot, (hop, tile) in enumerate(zip(HOPS, tiles)):
+        here = pl.ds(pl.multiple_of(place_after(place, hop) * size, size), size)
+        leaving.append(pltpu.make_async_copy(out_ref.at[here], tile, sent.at[slot]))
+        leaving[-1].start()
     for copy in leaving:
         copy.wait()
 
@@ -161,7 +172,7 @@
         + [
             pltpu.SemaphoreType.DMA,
             pltpu.SemaphoreType.DMA((len(GROUPS), 3)),
-            pltpu.SemaphoreType.DMA((len(GROUPS), SB)),
+            pltpu.SemaphoreType.DMA((SB,)),
         ],
         compiler_params=pltpu.CompilerParams(vmem_limit_bytes=56 * MIB),
         cost_estimate=pl.CostEstimate(
@@ -286,6 +297,7 @@
     barred = jnp.where(index > 0, 0.0, -jnp.inf)
     place = lax.rem(index, SB)
     size = query_ref.shape[0] // SB
+    starts = [pl.multiple_of(place_after(place, hop, True) * size, size) for hop in HOPS]
     columns = GROUP * HD
     last = group == KVH - 1
     copies = []
@@ -319,8 +331,8 @@
         mixed = sum_ref[:, lanes] * share + summed[:, :HD]
         total = total_ref[:, lanes] * share + summed[:, HD:]
         mixed = (mixed / total).astype(jnp.bfloat16)
-        for slot, apart in enumerate(APART):
-            there = pl.ds(pl.multiple_of((place ^ apart) * size, size), size)
+        for slot, start in enumerate(starts):
+            there = pl.ds(start, size)
             out_ref[there, head_lanes(head)] = mixed[slot * size : (slot + 1) * size]
         if last and head % 2:
             start = (head - 1) * HD
@@ -358,9 +370,9 @@
     )(*operands)
 
 
-def swap(tile, apart):
+def send(tile, hop):
     devices = lax.axis_size("tm")
-    route = [(i, i - i % SB + (i % SB ^ apart)) for i in range(devices)]
+    route = [(i, i - i % SB + place_after(i % SB, hop)) for i in range(devices)]
     return lax.ppermute(tile, "tm", route)
 
 
@@ -372,7 +384,7 @@
     tiles[0], w_query, w_kv, frame_attention_gain = lax.optimization_barrier(
         (tiles[0], w_query, w_kv, frame_attention_gain)
     )
-    tiles = [swap(tile, apart) if apart else tile for apart, tile in zip(APART, tiles)]
+    tiles = [send(tile, hop) if any(hop) else tile for hop, tile in zip(HOPS, tiles)]
     normed, *pairs = make_pairs(tiles, frame_attention_gain, w_kv)
     earlier_pairs = [shifted(part, "tm", 1) for part in pairs]
     query, *so_far = own_frame(normed, w_query, pairs)

time: 57.7 us -> 57.6 us (level)
  starting transfers between devices: 31.9 us -> 27.3 us
  waiting for transfers between devices: 4.75 us -> 9.31 us
    ppermute x15, starting transfers between devices: 26.5 us -> 21.9 us  [send(): return lax.ppermute(tile, 'tm', route)]
    ppermute x15, waiting for transfers between devices: 4.75 us -> 9.3 us  [send(): return lax.ppermute(tile, 'tm', route)]
  transfers between devices with their start and end apart: 17 -> 17, of which waited for: 3 -> 7; matrix products, arithmetic and copies ran while one was open for 0% -> 0% of each run, Pallas kernels for 10% -> 10%
where the time goes in v14:
time: 57.6 us; the launch traced here: 57.1 us
  starting transfers between devices  27.3 us (47%)
  Pallas kernels  19.4 us (34%)
  waiting for transfers between devices  9.31 us (16%)
  local copies, waits for them, and re-layouts  0.85 us (1%)
    ppermute x15, starting transfers between devices, send(): return lax.ppermute(tile, 'tm', route)  21.9 us
    pallas_call x1, Pallas kernels, mixer(): pl.pallas_call(functools.partial(mixer_kernel, state is not None), in_spe...  10.5 us
    ppermute x15, waiting for transfers between devices, send(): return lax.ppermute(tile, 'tm', route)  9.3 us
    ppermute x2, starting transfers between devices, shifted(): return lax.ppermute(block, axis, route)  5.42 us
    pallas_call x2, Pallas kernels, earlier_frame(): pl.pallas_call(functools.partial(earlier_kernel, group), compiler_params=...  4.19 us
    pallas_call x1, Pallas kernels, own_frame(): pl.pallas_call(own_kernel, out_shape=[jax.ShapeDtypeStruct((rows, width),...  3.72 us
  transfers between devices with their start and end apart: 17, of which 7 were waited for; matrix products, arithmetic and copies ran while one was open for 0% of the time, Pallas kernels for 10%

profile of v14, /device:TPU:1, one launch (start us, length us, event | category | flops | bytes accessed | tf_op | source)
XLA Modules:
  0.0 57.1 jit_solution(12567422326132754592)
XLA Ops:
  0.0 10.5 %mixer.1 = (bf16[32,1024]{1,0:T(8,128)(2,1)}, bf16[32,1024]{1,0:T(8,128)(2,1)}, bf16[32,1024]{1,0:T(8,128)(2,1)}, bf16[32,1024]{1,0:T(8,128)(2,1)}, bf16[32,1024...) custom-call(bf16[512,1024]{1,0:T(8,128)(2,1)} %bitcast.2, ...), custom_call_target="tpu_custom_call" | custom-call | flops 3758096384 | bytes 8388608 | tf_op jit(solution)/shard_map/mixer/pallas_call | solution.py:165
  10.5 2.2 %collective-permute-start = (bf16[32,1024]{1,0:T(8,128)(2,1)}, bf16[32,1024]{1,0:T(8,128)(2,1)S(1)}, u32[]{:S(2)}, u32[]{:S(2)}) collective-permute-start(bf16[32,1024]{1,0:T(8,128)(2,1)} %get-tuple-element.36), channel_id=1, source_target_pairs={{0,4},{1,5},{2,6},{3,7},{4,8},{5,9},{6,10},{7,11},{8,12},{9,13},{1... | collective-permute-start | bytes 196616 | tf_op jit(solution)/shard_map/ppermute | solution.py:376
  12.7 2.3 %collective-permute-start.1 = (bf16[32,1024]{1,0:T(8,128)(2,1)}, bf16[32,1024]{1,0:T(8,128)(2,1)S(1)}, u32[]{:S(2)}, u32[]{:S(2)}) collective-permute-start(bf16[32,1024]{1,0:T(8,128)(2,1)} %get-tuple-element.37), channel_id=1, source_target_pairs={{0,8},{1,9},{2,10},{3,11},{4,12},{5,13},{6,14},{7,15},{8,0},{9,1},... | collective-permute-start | bytes 196616 | tf_op jit(solution)/shard_map/ppermute | solution.py:376
  15.0 2.0 %collective-permute-start.10 = (bf16[32,1024]{1,0:T(8,128)(2,1)}, bf16[32,1024]{1,0:T(8,128)(2,1)S(1)}, u32[]{:S(2)}, u32[]{:S(2)}) collective-permute-start(bf16[32,1024]{1,0:T(8,128)(2,1)} %get-tuple-element.46), channel_id=1, source_target_pairs={{0,7},{1,6},{2,5},{3,4},{4,11},{5,10},{6,9},{7,8},{8,15},{9,14},{1... | collective-permute-start | bytes 196616 | tf_op jit(solution)/shard_map/ppermute | solution.py:376
  17.0 0.5 collective-permute-start.11
  17.5 1.2 %collective-permute-start.12 = (bf16[32,1024]{1,0:T(8,128)(2,1)}, bf16[32,1024]{1,0:T(8,128)(2,1)S(1)}, u32[]{:S(2)}, u32[]{:S(2)}) collective-permute-start(bf16[32,1024]{1,0:T(8,128)(2,1)} %get-tuple-element.48), channel_id=1, source_target_pairs={{0,1},{1,0},{2,3},{3,2},{4,5},{5,4},{6,7},{7,6},{8,9},{9,8},{10,11... | collective-permute-start | bytes 196616 | tf_op jit(solution)/shard_map/ppermute | solution.py:376
  18.7 0.0 collective-permute-done.refs_1_
  18.7 2.1 %collective-permute-start.13 = (bf16[32,1024]{1,0:T(8,128)(2,1)}, bf16[32,1024]{1,0:T(8,128)(2,1)S(1)}, u32[]{:S(2)}, u32[]{:S(2)}) collective-permute-start(bf16[32,1024]{1,0:T(8,128)(2,1)} %get-tuple-element.49), channel_id=1, source_target_pairs={{0,5},{1,4},{2,7},{3,6},{4,9},{5,8},{6,11},{7,10},{8,13},{9,12},{1... | collective-permute-start | bytes 196616 | tf_op jit(solution)/shard_map/ppermute | solution.py:376
  20.8 0.0 collective-permute-done.1.refs_2_
  20.8 0.5 collective-permute-start.14
  21.3 0.7 %collective-permute-done.10.refs_11_ = bf16[32,1024]{1,0:T(8,128)(2,1)S(1)} collective-permute-done((bf16[32,1024]{1,0:T(8,128)(2,1)}, bf16[32,1024]{1,0:T(8,128)(2,1)S(1)}, u32[]{:S(2)}, u32[]{:S(2)}) %collective-permute-start.10) | collective-permute-done | bytes 65568 | tf_op jit(solution)/shard_map/ppermute | solution.py:376
  22.1 3.1 %collective-permute-start.2 = (bf16[32,1024]{1,0:T(8,128)(2,1)}, bf16[32,1024]{1,0:T(8,128)(2,1)S(1)}, u32[]{:S(2)}, u32[]{:S(2)}) collective-permute-start(bf16[32,1024]{1,0:T(8,128)(2,1)} %get-tuple-element.38), channel_id=1, source_target_pairs={{0,6},{1,7},{2,4},{3,5},{4,10},{5,11},{6,8},{7,9},{8,14},{9,15},{1... | collective-permute-start | bytes 196616 | tf_op jit(solution)/shard_map/ppermute | solution.py:376
  25.2 3.6 %collective-permute-done.11.refs_12_ = bf16[32,1024]{1,0:T(8,128)(2,1)S(1)} collective-permute-done((bf16[32,1024]{1,0:T(8,128)(2,1)}, bf16[32,1024]{1,0:T(8,128)(2,1)S(1)}, u32[]{:S(2)}, u32[]{:S(2)}) %collective-permute-start.11) | collective-permute-done | bytes 65568 | tf_op jit(solution)/shard_map/ppermute | solution.py:376
  28.8 0.4 collective-permute-start.3
  29.2 0.6 %collective-permute-start.4 = (bf16[32,1024]{1,0:T(8,128)(2,1)}, bf16[32,1024]{1,0:T(8,128)(2,1)S(1)}, u32[]{:S(2)}, u32[]{:S(2)}) collective-permute-start(bf16[32,1024]{1,0:T(8,128)(2,1)} %get-tuple-element.40), channel_id=1, source_target_pairs={{0,2},{1,3},{2,0},{3,1},{4,6},{5,7},{6,4},{7,5},{8,10},{9,11},{10,... | collective-permute-start | bytes 196616 | tf_op jit(solution)/shard_map/ppermute | solution.py:376
  29.8 2.9 %collective-permute-start.5 = (bf16[32,1024]{1,0:T(8,128)(2,1)}, bf16[32,1024]{1,0:T(8,128)(2,1)S(1)}, u32[]{:S(2)}, u32[]{:S(2)}) collective-permute-start(bf16[32,1024]{1,0:T(8,128)(2,1)} %get-tuple-element.41), channel_id=1, source_target_pairs={{0,12},{1,13},{2,14},{3,15},{4,0},{5,1},{6,2},{7,3},{8,4},{9,5},{1... | collective-permute-start | bytes 196616 | tf_op jit(solution)/shard_map/ppermute | solution.py:376
  32.7 1.7 %collective-permute-start.6 = (bf16[32,1024]{1,0:T(8,128)(2,1)}, bf16[32,1024]{1,0:T(8,128)(2,1)S(1)}, u32[]{:S(2)}, u32[]{:S(2)}) collective-permute-start(bf16[32,1024]{1,0:T(8,128)(2,1)} %get-tuple-element.42), channel_id=1, source_target_pairs={{0,15},{1,14},{2,13},{3,12},{4,3},{5,2},{6,1},{7,0},{8,7},{9,6},{1... | collective-permute-start | bytes 196616 | tf_op jit(solution)/shard_map/ppermute | solution.py:376
  34.3 0.7 %collective-permute-start.7 = (bf16[32,1024]{1,0:T(8,128)(2,1)}, bf16[32,1024]{1,0:T(8,128)(2,1)S(1)}, u32[]{:S(2)}, u32[]{:S(2)}) collective-permute-start(bf16[32,1024]{1,0:T(8,128)(2,1)} %get-tuple-element.43), channel_id=1, source_target_pairs={{0,3},{1,2},{2,1},{3,0},{4,7},{5,6},{6,5},{7,4},{8,11},{9,10},{10,... | collective-permute-start | bytes 196616 | tf_op jit(solution)/shard_map/ppermute | solution.py:376
  35.0 0.2 collective-permute-done.3.refs_4_
  35.2 1.4 %collective-permute-start.8 = (bf16[32,1024]{1,0:T(8,128)(2,1)}, bf16[32,1024]{1,0:T(8,128)(2,1)S(1)}, u32[]{:S(2)}, u32[]{:S(2)}) collective-permute-start(bf16[32,1024]{1,0:T(8,128)(2,1)} %get-tuple-element.44), channel_id=1, source_target_pairs={{0,13},{1,12},{2,15},{3,14},{4,1},{5,0},{6,3},{7,2},{8,5},{9,4},{1... | collective-permute-start | bytes 196616 | tf_op jit(solution)/shard_map/ppermute | solution.py:376
  36.6 0.3 collective-permute-start.9
  36.9 0.6 %collective-permute-done.6.refs_7_ = bf16[32,1024]{1,0:T(8,128)(2,1)S(1)} collective-permute-done((bf16[32,1024]{1,0:T(8,128)(2,1)}, bf16[32,1024]{1,0:T(8,128)(2,1)S(1)}, u32[]{:S(2)}, u32[]{:S(2)}) %collective-permute-start.6) | collective-permute-done | bytes 65568 | tf_op jit(solution)/shard_map/ppermute | solution.py:376
  37.5 1.6 %collective-permute-done.7.refs_8_ = bf16[32,1024]{1,0:T(8,128)(2,1)S(1)} collective-permute-done((bf16[32,1024]{1,0:T(8,128)(2,1)}, bf16[32,1024]{1,0:T(8,128)(2,1)S(1)}, u32[]{:S(2)}, u32[]{:S(2)}) %collective-permute-start.7) | collective-permute-done | bytes 65568 | tf_op jit(solution)/shard_map/ppermute | solution.py:376
  39.1 0.5 collective-permute-done.8.refs_9_
  39.6 2.0 %collective-permute-done.9.refs_10_ = bf16[32,1024]{1,0:T(8,128)(2,1)S(1)} collective-permute-done((bf16[32,1024]{1,0:T(8,128)(2,1)}, bf16[32,1024]{1,0:T(8,128)(2,1)S(1)}, u32[]{:S(2)}, u32[]{:S(2)}) %collective-permute-start.9) | collective-permute-done | bytes 65568 | tf_op jit(solution)/shard_map/ppermute | solution.py:376
  41.7 0.8 %copy-done.1 = bf16[32,1024]{1,0:T(8,128)(2,1)S(1)} copy-done((bf16[32,1024]{1,0:T(8,128)(2,1)S(1)}, bf16[32,1024]{1,0:T(8,128)(2,1)}, u32[]{:S(2)}) %copy-start.1) | copy-done | bytes 65560
  42.5 1.0 %pairs.1 = (bf16[512,1024]{1,0:T(8,128)(2,1)S(1)}, bf16[512,256]{1,0:T(8,128)(2,1)S(1)}, bf16[512,256]{1,0:T(8,128)(2,1)S(1)}) custom-call(bf16[1024]{0:T(1024)(128)(2,1)S(1)} %copy-done.2, bf16[1024,512]{1,0:T(8,128)(2,1)S(1)} %copy-done, bf16[32,1024]{1,0:T(8,128)(2,1)S(1)} %copy-done.1, bf16[32,1024]{1,0:T(8,128)(2,1)S(1)} %collective-permute-done.refs_1_, ...), custom_call_target="tpu_custom_call" | custom-call | flops 536870912 | bytes 3670016 | tf_op jit(solution)/shard_map/pairs/pallas_call | solution.py:220
  43.5 3.2 %collective-permute-start.16 = (bf16[512,256]{1,0:T(8,128)(2,1)S(1)}, bf16[512,256]{1,0:T(8,128)(2,1)S(1)}, u32[]{:S(2)}, u32[]{:S(2)}) collective-permute-start(bf16[512,256]{1,0:T(8,128)(2,1)S(1)} %get-tuple-element.53.refs_0_), channel_id=1, source_target_pairs={{0,1},{1,2},{2,3},{3,4},{4,5},{5,6},{6,7},{7,8},{8,9},{9,10},{10,1... | collective-permute-start | bytes 786440 | tf_op jit(solution)/shard_map/ppermute | solution.py:42
  46.8 2.2 %collective-permute-start.15 = (bf16[512,256]{1,0:T(8,128)(2,1)S(1)}, bf16[512,256]{1,0:T(8,128)(2,1)S(1)}, u32[]{:S(2)}, u32[]{:S(2)}) collective-permute-start(bf16[512,256]{1,0:T(8,128)(2,1)S(1)} %get-tuple-element.54.refs_1_), channel_id=1, source_target_pairs={{0,1},{1,2},{2,3},{3,4},{4,5},{5,6},{6,7},{7,8},{8,9},{9,10},{10,1... | collective-permute-start | bytes 786440 | tf_op jit(solution)/shard_map/ppermute | solution.py:42
  49.0 3.7 %own_frame.1 = (bf16[512,1024]{1,0:T(8,128)(2,1)S(1)}, f32[512,1024]{1,0:T(8,128)S(1)}, f32[512,1024]{1,0:T(8,128)S(1)}, f32[512,1024]{1,0:T(8,128)S(1)}) custom-call(bf16[512,1024]{1,0:T(8,128)(2,1)S(1)} %get-tuple-element.51.normed_ref, bf16[1024,1024]{1,0:T(8,128)(2,1)S(1)} %copy-done.3, bf16[512,256]{1,0:T(8,128)(2,1)S(1)} %get-tuple-element.53.refs_0_, ...), custom_call_target="tpu_custom_call" | custom-call | flops 2147483648 | bytes 6291456 | tf_op jit(solution)/shard_map/own_frame/pallas_call | solution.py:280
  52.7 1.7 %earlier_frame.2.refs_0_ = bf16[512,512]{1,0:T(8,128)(2,1)S(1)} custom-call(bf16[512,1024]{1,0:T(8,128)(2,1)S(1)} %get-tuple-element.55.query_ref, bf16[512,256]{1,0:T(8,128)(2,1)S(1)} %collective-permute-done.16.pairs_ref, f32[512,1024]{1,0:T(8,128)S(1)} %get-tuple-element.56.sum_ref, f32[512,1024]{1,0:T(8,128)S(1)} %get-tuple-element.57.total_ref, ...), custom_call_target="tpu_custom_call" | custom-call | flops 536870912 | bytes 5242880 | tf_op jit(solution)/shard_map/earlier_frame/pallas_call | solution.py:360
  54.5 2.5 %earlier_frame.3 = bf16[512,1024]{1,0:T(8,128)(2,1)} custom-call(bf16[512,1024]{1,0:T(8,128)(2,1)S(1)} %get-tuple-element.55.query_ref, bf16[512,256]{1,0:T(8,128)(2,1)S(1)} %collective-permute-done.15.pairs_ref, f32[512,1024]{1,0:T(8,128)S(1)} %get-tuple-element.56.sum_ref, f32[512,1024]{1,0:T(8,128)S(1)} %get-tuple-element.57.total_ref, ...), custom_call_target="tpu_custom_call" | custom-call | flops 536870912 | bytes 5242880 | tf_op jit(solution)/shard_map/earlier_frame/pallas_call | solution.py:360
  (15 shorter events, 0.0 us)
Async XLA Ops:
  0.0 41.7 %copy-start = (bf16[1024,512]{1,0:T(8,128)(2,1)S(1)}, bf16[1024,512]{1,0:T(8,128)(2,1)}, u32[]{:S(2)}) copy-start(bf16[1024,512]{1,0:T(8,128)(2,1)} %w_ref) | copy-start | bytes 3145732
  0.0 41.7 %copy-start.2 = (bf16[1024]{0:T(1024)(128)(2,1)S(1)}, bf16[1024]{0:T(1024)(128)(2,1)}, u32[]{:S(2)}) copy-start(bf16[1024]{0:T(1024)(128)(2,1)} %gain_ref) | copy-start | bytes 6148
  0.0 49.0 %copy-start.3 = (bf16[1024,1024]{1,0:T(8,128)(2,1)S(1)}, bf16[1024,1024]{1,0:T(8,128)(2,1)}, u32[]{:S(2)}) copy-start(bf16[1024,1024]{1,0:T(8,128)(2,1)} %w_ref.1) | copy-start | bytes 6291460
  10.5 8.3 %collective-permute-start = (bf16[32,1024]{1,0:T(8,128)(2,1)}, bf16[32,1024]{1,0:T(8,128)(2,1)S(1)}, u32[]{:S(2)}, u32[]{:S(2)}) collective-permute-start(bf16[32,1024]{1,0:T(8,128)(2,1)} %get-tuple-element.36), channel_id=1, source_target_pairs={{0,4},{1,5},{2,6},{3,7},{4,8},{5,9},{6,10},{7,11},{8,12},{9,13},{1... | collective-permute-start | bytes 196616 | tf_op jit(solution)/shard_map/ppermute | solution.py:376
  12.7 8.2 %collective-permute-start.1 = (bf16[32,1024]{1,0:T(8,128)(2,1)}, bf16[32,1024]{1,0:T(8,128)(2,1)S(1)}, u32[]{:S(2)}, u32[]{:S(2)}) collective-permute-start(bf16[32,1024]{1,0:T(8,128)(2,1)} %get-tuple-element.37), channel_id=1, source_target_pairs={{0,8},{1,9},{2,10},{3,11},{4,12},{5,13},{6,14},{7,15},{8,0},{9,1},... | collective-permute-start | bytes 196616 | tf_op jit(solution)/shard_map/ppermute | solution.py:376
  15.0 7.1 %collective-permute-start.10 = (bf16[32,1024]{1,0:T(8,128)(2,1)}, bf16[32,1024]{1,0:T(8,128)(2,1)S(1)}, u32[]{:S(2)}, u32[]{:S(2)}) collective-permute-start(bf16[32,1024]{1,0:T(8,128)(2,1)} %get-tuple-element.46), channel_id=1, source_target_pairs={{0,7},{1,6},{2,5},{3,4},{4,11},{5,10},{6,9},{7,8},{8,15},{9,14},{1... | collective-permute-start | bytes 196616 | tf_op jit(solution)/shard_map/ppermute | solution.py:376
  17.0 11.8 %collective-permute-start.11 = (bf16[32,1024]{1,0:T(8,128)(2,1)}, bf16[32,1024]{1,0:T(8,128)(2,1)S(1)}, u32[]{:S(2)}, u32[]{:S(2)}) collective-permute-start(bf16[32,1024]{1,0:T(8,128)(2,1)} %get-tuple-element.47), channel_id=1, source_target_pairs={{0,11},{1,10},{2,9},{3,8},{4,15},{5,14},{6,13},{7,12},{8,3},{9,2},... | collective-permute-start | bytes 196616 | tf_op jit(solution)/shard_map/ppermute | solution.py:376
  17.5 11.7 %collective-permute-start.12 = (bf16[32,1024]{1,0:T(8,128)(2,1)}, bf16[32,1024]{1,0:T(8,128)(2,1)S(1)}, u32[]{:S(2)}, u32[]{:S(2)}) collective-permute-start(bf16[32,1024]{1,0:T(8,128)(2,1)} %get-tuple-element.48), channel_id=1, source_target_pairs={{0,1},{1,0},{2,3},{3,2},{4,5},{5,4},{6,7},{7,6},{8,9},{9,8},{10,11... | collective-permute-start | bytes 196616 | tf_op jit(solution)/shard_map/ppermute | solution.py:376
  18.7 11.1 %collective-permute-start.13 = (bf16[32,1024]{1,0:T(8,128)(2,1)}, bf16[32,1024]{1,0:T(8,128)(2,1)S(1)}, u32[]{:S(2)}, u32[]{:S(2)}) collective-permute-start(bf16[32,1024]{1,0:T(8,128)(2,1)} %get-tuple-element.49), channel_id=1, source_target_pairs={{0,5},{1,4},{2,7},{3,6},{4,9},{5,8},{6,11},{7,10},{8,13},{9,12},{1... | collective-permute-start | bytes 196616 | tf_op jit(solution)/shard_map/ppermute | solution.py:376
  20.8 11.9 %collective-permute-start.14 = (bf16[32,1024]{1,0:T(8,128)(2,1)}, bf16[32,1024]{1,0:T(8,128)(2,1)S(1)}, u32[]{:S(2)}, u32[]{:S(2)}) collective-permute-start(bf16[32,1024]{1,0:T(8,128)(2,1)} %get-tuple-element.50), channel_id=1, source_target_pairs={{0,9},{1,8},{2,11},{3,10},{4,13},{5,12},{6,15},{7,14},{8,1},{9,0},... | collective-permute-start | bytes 196616 | tf_op jit(solution)/shard_map/ppermute | solution.py:376
  22.1 12.3 %collective-permute-start.2 = (bf16[32,1024]{1,0:T(8,128)(2,1)}, bf16[32,1024]{1,0:T(8,128)(2,1)S(1)}, u32[]{:S(2)}, u32[]{:S(2)}) collective-permute-start(bf16[32,1024]{1,0:T(8,128)(2,1)} %get-tuple-element.38), channel_id=1, source_target_pairs={{0,6},{1,7},{2,4},{3,5},{4,10},{5,11},{6,8},{7,9},{8,14},{9,15},{1... | collective-permute-start | bytes 196616 | tf_op jit(solution)/shard_map/ppermute | solution.py:376
  28.8 6.4 %collective-permute-start.3 = (bf16[32,1024]{1,0:T(8,128)(2,1)}, bf16[32,1024]{1,0:T(8,128)(2,1)S(1)}, u32[]{:S(2)}, u32[]{:S(2)}) collective-permute-start(bf16[32,1024]{1,0:T(8,128)(2,1)} %get-tuple-element.39), channel_id=1, source_target_pairs={{0,10},{1,11},{2,8},{3,9},{4,14},{5,15},{6,12},{7,13},{8,2},{9,3},... | collective-permute-start | bytes 196616 | tf_op jit(solution)/shard_map/ppermute | solution.py:376
  29.2 7.4 %collective-permute-start.4 = (bf16[32,1024]{1,0:T(8,128)(2,1)}, bf16[32,1024]{1,0:T(8,128)(2,1)S(1)}, u32[]{:S(2)}, u32[]{:S(2)}) collective-permute-start(bf16[32,1024]{1,0:T(8,128)(2,1)} %get-tuple-element.40), channel_id=1, source_target_pairs={{0,2},{1,3},{2,0},{3,1},{4,6},{5,7},{6,4},{7,5},{8,10},{9,11},{10,... | collective-permute-start | bytes 196616 | tf_op jit(solution)/shard_map/ppermute | solution.py:376
  29.8 7.1 %collective-permute-start.5 = (bf16[32,1024]{1,0:T(8,128)(2,1)}, bf16[32,1024]{1,0:T(8,128)(2,1)S(1)}, u32[]{:S(2)}, u32[]{:S(2)}) collective-permute-start(bf16[32,1024]{1,0:T(8,128)(2,1)} %get-tuple-element.41), channel_id=1, source_target_pairs={{0,12},{1,13},{2,14},{3,15},{4,0},{5,1},{6,2},{7,3},{8,4},{9,5},{1... | collective-permute-start | bytes 196616 | tf_op jit(solution)/shard_map/ppermute | solution.py:376
  32.7 4.8 %collective-permute-start.6 = (bf16[32,1024]{1,0:T(8,128)(2,1)}, bf16[32,1024]{1,0:T(8,128)(2,1)S(1)}, u32[]{:S(2)}, u32[]{:S(2)}) collective-permute-start(bf16[32,1024]{1,0:T(8,128)(2,1)} %get-tuple-element.42), channel_id=1, source_target_pairs={{0,15},{1,14},{2,13},{3,12},{4,3},{5,2},{6,1},{7,0},{8,7},{9,6},{1... | collective-permute-start | bytes 196616 | tf_op jit(solution)/shard_map/ppermute | solution.py:376
  34.3 4.8 %collective-permute-start.7 = (bf16[32,1024]{1,0:T(8,128)(2,1)}, bf16[32,1024]{1,0:T(8,128)(2,1)S(1)}, u32[]{:S(2)}, u32[]{:S(2)}) collective-permute-start(bf16[32,1024]{1,0:T(8,128)(2,1)} %get-tuple-element.43), channel_id=1, source_target_pairs={{0,3},{1,2},{2,1},{3,0},{4,7},{5,6},{6,5},{7,4},{8,11},{9,10},{10,... | collective-permute-start | bytes 196616 | tf_op jit(solution)/shard_map/ppermute | solution.py:376
  35.2 4.4 %collective-permute-start.8 = (bf16[32,1024]{1,0:T(8,128)(2,1)}, bf16[32,1024]{1,0:T(8,128)(2,1)S(1)}, u32[]{:S(2)}, u32[]{:S(2)}) collective-permute-start(bf16[32,1024]{1,0:T(8,128)(2,1)} %get-tuple-element.44), channel_id=1, source_target_pairs={{0,13},{1,12},{2,15},{3,14},{4,1},{5,0},{6,3},{7,2},{8,5},{9,4},{1... | collective-permute-start | bytes 196616 | tf_op jit(solution)/shard_map/ppermute | solution.py:376
  36.6 5.1 %collective-permute-start.9 = (bf16[32,1024]{1,0:T(8,128)(2,1)}, bf16[32,1024]{1,0:T(8,128)(2,1)S(1)}, u32[]{:S(2)}, u32[]{:S(2)}) collective-permute-start(bf16[32,1024]{1,0:T(8,128)(2,1)} %get-tuple-element.45), channel_id=1, source_target_pairs={{0,14},{1,15},{2,12},{3,13},{4,2},{5,3},{6,0},{7,1},{8,6},{9,7},{1... | collective-permute-start | bytes 196616 | tf_op jit(solution)/shard_map/ppermute | solution.py:376
  41.7 0.8 %copy-start.1 = (bf16[32,1024]{1,0:T(8,128)(2,1)S(1)}, bf16[32,1024]{1,0:T(8,128)(2,1)}, u32[]{:S(2)}) copy-start(bf16[32,1024]{1,0:T(8,128)(2,1)} %get-tuple-element.35.refs_0_) | copy-start | bytes 196612
  43.5 9.2 %collective-permute-start.16 = (bf16[512,256]{1,0:T(8,128)(2,1)S(1)}, bf16[512,256]{1,0:T(8,128)(2,1)S(1)}, u32[]{:S(2)}, u32[]{:S(2)}) collective-permute-start(bf16[512,256]{1,0:T(8,128)(2,1)S(1)} %get-tuple-element.53.refs_0_), channel_id=1, source_target_pairs={{0,1},{1,2},{2,3},{3,4},{4,5},{5,6},{6,7},{7,8},{8,9},{9,10},{10,1... | collective-permute-start | bytes 786440 | tf_op jit(solution)/shard_map/ppermute | solution.py:42
  46.8 7.7 %collective-permute-start.15 = (bf16[512,256]{1,0:T(8,128)(2,1)S(1)}, bf16[512,256]{1,0:T(8,128)(2,1)S(1)}, u32[]{:S(2)}, u32[]{:S(2)}) collective-permute-start(bf16[512,256]{1,0:T(8,128)(2,1)S(1)} %get-tuple-element.54.refs_1_), channel_id=1, source_target_pairs={{0,1},{1,2},{2,3},{3,4},{4,5},{5,6},{6,7},{7,8},{8,9},{9,10},{10,1... | collective-permute-start | bytes 786440 | tf_op jit(solution)/shard_map/ppermute | solution.py:42

commit v15 on v13

--- a/solution.py
+++ b/solution.py
@@ -14,7 +14,8 @@
 SB = 16
 SPAN = 128
 GROUPS = ((0, 4), (4, 8))
-APART = (0, 10, 11, 9, 2, 12, 6, 13, 3, 7, 1, 14, 4, 15, 8, 5)
+APART = (0, 10, 11, 14, 4, 15, 8, 5, 9, 2, 12, 6, 13, 3, 7, 1)
+EARLY = SB // 2
 
 epsilon = 1e-06
 MIB = 1 << 20
@@ -163,7 +164,7 @@
             pltpu.SemaphoreType.DMA((len(GROUPS), 3)),
             pltpu.SemaphoreType.DMA((len(GROUPS), SB)),
         ],
-        compiler_params=pltpu.CompilerParams(vmem_limit_bytes=56 * MIB),
+        compiler_params=pltpu.CompilerParams(vmem_limit_bytes=62 * MIB),
         cost_estimate=pl.CostEstimate(
             flops=2 * rows * width * 3 * width + 8 * rows * SPAN * width,
             bytes_accessed=2 * (3 * width * width + 2 * rows * width),
@@ -188,28 +189,66 @@
     return lax.fori_loop(0, time_ranges - 1, advance_hop, jnp.zeros_like(block_total))
 
 
-def pairs_kernel(gain_ref, w_ref, *refs):
-    tiles, normed_ref, outs = refs[:SB], refs[SB], refs[SB + 1 :]
+def norm_rows(gain_ref, tiles):
     gain = gain_ref[...].astype(jnp.float32).reshape(1, -1)
     widened = jnp.concatenate([tile[...] for tile in tiles], axis=0).astype(jnp.float32)
     mean_square = jnp.mean(widened * widened, axis=-1, keepdims=True)
-    normed = (widened * lax.rsqrt(mean_square + epsilon) * gain).astype(jnp.bfloat16)
+    return (widened * lax.rsqrt(mean_square + epsilon) * gain).astype(jnp.bfloat16)
+
+
+def write_pairs(normed, w_ref, offset, outs):
+    pairs = dot(normed, w_ref[...]).astype(jnp.bfloat16)
+    rows = pairs.shape[0]
+    for head, out_ref in enumerate(outs):
+        for start in range(0, rows, HD):
+            there = slice(offset + start, offset + start + HD)
+            out_ref[there, :HD] = pairs[start : start + HD, head_lanes(head)].T
+        out_ref[offset : offset + rows, HD:] = pairs[:, head_lanes(KVH + head)]
+
+
+def early_kernel(gain_ref, w_kv_ref, w_query_ref, *refs):
+    tiles, query_ref, outs = refs[:EARLY], refs[EARLY], refs[EARLY + 1 :]
+    normed = norm_rows(gain_ref, tiles)
+    write_pairs(normed, w_kv_ref, 0, outs)
+    query_ref[...] = dot(normed, w_query_ref[...]).astype(jnp.bfloat16)
+
+
+def pairs_kernel(gain_ref, w_kv_ref, *refs):
+    late = SB - EARLY
+    tiles, done, normed_ref, outs = refs[:late], refs[late:-KVH - 1], refs[-KVH - 1], refs[-KVH:]
+    normed = norm_rows(gain_ref, tiles)
     normed_ref[...] = normed
-    pairs = dot(normed, w_ref[...]).astype(jnp.bfloat16)
-    for head, out_ref in enumerate(outs):
-        for start in range(0, pairs.shape[0], HD):
-            here = slice(start, start + HD)
-            out_ref[here, :HD] = pairs[here, head_lanes(head)].T
-        out_ref[:, HD:] = pairs[:, head_lanes(KVH + head)]
-
-
-def make_pairs(tiles, gain, w_kv):
+    rows = done[0].shape[0]
+    for done_ref, out_ref in zip(done, outs):
+        out_ref[:rows] = done_ref[...]
+    write_pairs(normed, w_kv_ref, rows, outs)
+
+
+def make_early(tiles, gain, w_kv, w_query):
     width, wide = w_kv.shape
     rows = sum(tile.shape[0] for tile in tiles)
     return pl.pallas_call(
+        early_kernel,
+        out_shape=[jax.ShapeDtypeStruct((rows, w_query.shape[1]), jnp.bfloat16)]
+        + [jax.ShapeDtypeStruct((rows, wide // KVH), jnp.bfloat16)] * KVH,
+        compiler_params=pltpu.CompilerParams(vmem_limit_bytes=16 * MIB),
+        cost_estimate=pl.CostEstimate(
+            flops=2 * rows * width * (wide + width),
+            bytes_accessed=2 * (2 * rows * width + width * wide + width * width),
+            transcendentals=rows,
+        ),
+        name="early_rows",
+    )(gain, w_kv, w_query, *tiles)
+
+
+def make_pairs(tiles, gain, w_kv, done):
+    width, wide = w_kv.shape
+    rows = sum(tile.shape[0] for tile in tiles)
+    total = rows + done[0].shape[0]
+    return pl.pallas_call(
         pairs_kernel,
         out_shape=[jax.ShapeDtypeStruct((rows, width), jnp.bfloat16)]
-        + [jax.ShapeDtypeStruct((rows, wide // KVH), jnp.bfloat16)] * KVH,
+        + [jax.ShapeDtypeStruct((total, wide // KVH), jnp.bfloat16)] * KVH,
         compiler_params=pltpu.CompilerParams(vmem_limit_bytes=16 * MIB),
         cost_estimate=pl.CostEstimate(
             flops=2 * rows * width * wide,
@@ -217,7 +256,7 @@
             transcendentals=rows,
         ),
         name="pairs",
-    )(gain, w_kv, *tiles)
+    )(gain, w_kv, *tiles, *done)
 
 
 SCORE_SCALE = math.log2(math.e) / math.sqrt(HD)
@@ -232,14 +271,15 @@
     return key, jnp.concatenate([value, jnp.ones_like(value)], axis=1)
 
 
-def own_kernel(normed_ref, w_ref, *refs):
+def own_kernel(normed_ref, w_ref, early_ref, *refs):
     both = [key_and_value(ref) for ref in refs[:KVH]]
     query_ref, sum_ref, total_ref, top_ref = refs[KVH:]
     columns = GROUP * HD
 
     def project(group):
         lanes = slice(group * columns, (group + 1) * columns)
-        query = dot(normed_ref[...], w_ref[:, lanes]).astype(jnp.bfloat16)
+        late = dot(normed_ref[...], w_ref[:, lanes]).astype(jnp.bfloat16)
+        query = jnp.concatenate([early_ref[:, lanes], late], axis=0)
         query_ref[:, lanes] = query
         return query
 
@@ -264,8 +304,8 @@
         scores = upcoming
 
 
-def own_frame(normed, w_query, pairs):
-    rows, width = normed.shape
+def own_frame(normed, w_query, early, pairs):
+    rows, width = pairs[0].shape[0], normed.shape[1]
     return pl.pallas_call(
         own_kernel,
         out_shape=[jax.ShapeDtypeStruct((rows, width), jnp.bfloat16)]
@@ -277,7 +317,7 @@
             transcendentals=rows * rows * HEADS,
         ),
         name="own_frame",
-    )(normed, w_query, *pairs)
+    )(normed, w_query, early, *pairs)
 
 
 def earlier_kernel(group, query_ref, pairs_ref, sum_ref, total_ref, top_ref, *refs):
@@ -368,14 +408,12 @@
     tokens = space_time[0]
     time_ranges = lax.axis_size("tm") // SB
     state = incoming_state(tokens, w_lin, time_ranges) if time_ranges > 1 else None
-    tiles = list(mixer(tokens, w_lin, gain_lin, state))
-    tiles[0], w_query, w_kv, frame_attention_gain = lax.optimization_barrier(
-        (tiles[0], w_query, w_kv, frame_attention_gain)
-    )
+    tiles = mixer(tokens, w_lin, gain_lin, state)
     tiles = [swap(tile, apart) if apart else tile for apart, tile in zip(APART, tiles)]
-    normed, *pairs = make_pairs(tiles, frame_attention_gain, w_kv)
+    early, *done = make_early(tiles[:EARLY], frame_attention_gain, w_kv, w_query)
+    normed, *pairs = make_pairs(tiles[EARLY:], frame_attention_gain, w_kv, done)
     earlier_pairs = [shifted(part, "tm", 1) for part in pairs]
-    query, *so_far = own_frame(normed, w_query, pairs)
+    query, *so_far = own_frame(normed, w_query, early, pairs)
     done = []
     for group, part in enumerate(earlier_pairs):
         done.append(earlier_frame(group, query, part, so_far, done))

time: 57.7 us -> 55.8 us (0.967)
  starting transfers between devices: 31.9 us -> 27 us
  local copies, waits for them, and re-layouts: 0.85 us -> 2.44 us
  waiting for transfers between devices: 4.75 us -> 6.12 us
    ppermute x15, starting transfers between devices: 26.5 us -> 21.9 us  [swap(): return lax.ppermute(tile, 'tm', route)]
    unnamed x8 -> x10, local copies, waits for them, and re-layouts: 0.85 us -> 2.44 us
    ppermute x15, waiting for transfers between devices: 4.75 us -> 6.11 us  [swap(): return lax.ppermute(tile, 'tm', route)]
    pallas_call x0 -> x1, Pallas kernels: none -> 1.11 us  [make_early(): pl.pallas_call(early_kernel, out_shape=[jax.ShapeDtypeStruct((rows, w_que...]
  transfers between devices with their start and end apart: 17 -> 17, of which waited for: 3 -> 4; matrix products, arithmetic and copies ran while one was open for 0% -> 0% of each run, Pallas kernels for 10% -> 11%
where the time goes in v15:
time: 55.8 us; the launch traced here: 55.2 us
  starting transfers between devices  27 us (48%)
  Pallas kernels  19.4 us (35%)
  waiting for transfers between devices  6.12 us (11%)
  local copies, waits for them, and re-layouts  2.44 us (4%)
    ppermute x15, starting transfers between devices, swap(): return lax.ppermute(tile, 'tm', route)  21.9 us
    pallas_call x1, Pallas kernels, mixer(): pl.pallas_call(functools.partial(mixer_kernel, state is not None), in_spe...  10.3 us
    ppermute x15, waiting for transfers between devices, swap(): return lax.ppermute(tile, 'tm', route)  6.11 us
    ppermute x2, starting transfers between devices, shifted(): return lax.ppermute(block, axis, route)  5.11 us
    pallas_call x2, Pallas kernels, earlier_frame(): pl.pallas_call(functools.partial(earlier_kernel, group), compiler_params=...  4.19 us
    pallas_call x1, Pallas kernels, own_frame(): pl.pallas_call(own_kernel, out_shape=[jax.ShapeDtypeStruct((rows, width),...  3.17 us
    unnamed x10, local copies, waits for them, and re-layouts  2.44 us
  transfers between devices with their start and end apart: 17, of which 4 were waited for; matrix products, arithmetic and copies ran while one was open for 0% of the time, Pallas kernels for 11%

profile of v15, /device:TPU:1, one launch (start us, length us, event | category | flops | bytes accessed | tf_op | source)
XLA Modules:
  0.0 55.2 jit_solution(2854979033761318359)
XLA Ops:
  0.0 10.3 %mixer.1 = (bf16[32,1024]{1,0:T(8,128)(2,1)}, bf16[32,1024]{1,0:T(8,128)(2,1)}, bf16[32,1024]{1,0:T(8,128)(2,1)}, bf16[32,1024]{1,0:T(8,128)(2,1)}, bf16[32,1024...) custom-call(bf16[512,1024]{1,0:T(8,128)(2,1)} %bitcast.2, ...), custom_call_target="tpu_custom_call" | custom-call | flops 3758096384 | bytes 8388608 | tf_op jit(solution)/shard_map/mixer/pallas_call | solution.py:155
  10.3 5.2 %collective-permute-start.10 = (bf16[32,1024]{1,0:T(8,128)(2,1)}, bf16[32,1024]{1,0:T(8,128)(2,1)S(1)}, u32[]{:S(2)}, u32[]{:S(2)}) collective-permute-start(bf16[32,1024]{1,0:T(8,128)(2,1)} %get-tuple-element.42), channel_id=1, source_target_pairs={{0,14},{1,15},{2,12},{3,13},{4,10},{5,11},{6,8},{7,9},{8,6},{9,7},... | collective-permute-start | bytes 196616 | tf_op jit(solution)/shard_map/ppermute | solution.py:404
  15.4 0.0 collective-permute-start.11
  15.4 1.4 %collective-permute-start.12 = (bf16[32,1024]{1,0:T(8,128)(2,1)}, bf16[32,1024]{1,0:T(8,128)(2,1)S(1)}, u32[]{:S(2)}, u32[]{:S(2)}) collective-permute-start(bf16[32,1024]{1,0:T(8,128)(2,1)} %get-tuple-element.44), channel_id=1, source_target_pairs={{0,15},{1,14},{2,13},{3,12},{4,11},{5,10},{6,9},{7,8},{8,7},{9,6},... | collective-permute-start | bytes 196616 | tf_op jit(solution)/shard_map/ppermute | solution.py:404
  16.8 2.3 %collective-permute-start.13 = (bf16[32,1024]{1,0:T(8,128)(2,1)}, bf16[32,1024]{1,0:T(8,128)(2,1)S(1)}, u32[]{:S(2)}, u32[]{:S(2)}) collective-permute-start(bf16[32,1024]{1,0:T(8,128)(2,1)} %get-tuple-element.45), channel_id=1, source_target_pairs={{0,8},{1,9},{2,10},{3,11},{4,12},{5,13},{6,14},{7,15},{8,0},{9,1},... | collective-permute-start | bytes 196616 | tf_op jit(solution)/shard_map/ppermute | solution.py:404
  19.2 0.3 collective-permute-start.14
  19.5 1.2 %collective-permute-start.8 = (bf16[32,1024]{1,0:T(8,128)(2,1)}, bf16[32,1024]{1,0:T(8,128)(2,1)S(1)}, u32[]{:S(2)}, u32[]{:S(2)}) collective-permute-start(bf16[32,1024]{1,0:T(8,128)(2,1)} %get-tuple-element.40), channel_id=1, source_target_pairs={{0,10},{1,11},{2,8},{3,9},{4,14},{5,15},{6,12},{7,13},{8,2},{9,3},... | collective-permute-start | bytes 196616 | tf_op jit(solution)/shard_map/ppermute | solution.py:404
  20.7 2.9 %collective-permute-start.9 = (bf16[32,1024]{1,0:T(8,128)(2,1)}, bf16[32,1024]{1,0:T(8,128)(2,1)S(1)}, u32[]{:S(2)}, u32[]{:S(2)}) collective-permute-start(bf16[32,1024]{1,0:T(8,128)(2,1)} %get-tuple-element.41), channel_id=1, source_target_pairs={{0,11},{1,10},{2,9},{3,8},{4,15},{5,14},{6,13},{7,12},{8,3},{9,2},... | collective-permute-start | bytes 196616 | tf_op jit(solution)/shard_map/ppermute | solution.py:404
  23.6 0.0 collective-permute-done.12.refs_5_
  23.6 1.9 %collective-permute-start = (bf16[32,1024]{1,0:T(8,128)(2,1)}, bf16[32,1024]{1,0:T(8,128)(2,1)S(1)}, u32[]{:S(2)}, u32[]{:S(2)}) collective-permute-start(bf16[32,1024]{1,0:T(8,128)(2,1)} %get-tuple-element.31), channel_id=1, source_target_pairs={{0,9},{1,8},{2,11},{3,10},{4,13},{5,12},{6,15},{7,14},{8,1},{9,0},... | collective-permute-start | bytes 196616 | tf_op jit(solution)/shard_map/ppermute | solution.py:404
  25.5 3.5 %collective-permute-done.13.refs_6_ = bf16[32,1024]{1,0:T(8,128)(2,1)S(1)} collective-permute-done((bf16[32,1024]{1,0:T(8,128)(2,1)}, bf16[32,1024]{1,0:T(8,128)(2,1)S(1)}, u32[]{:S(2)}, u32[]{:S(2)}) %collective-permute-start.13) | collective-permute-done | bytes 65568 | tf_op jit(solution)/shard_map/ppermute | solution.py:404
  29.0 2.6 %collective-permute-start.1 = (bf16[32,1024]{1,0:T(8,128)(2,1)}, bf16[32,1024]{1,0:T(8,128)(2,1)S(1)}, u32[]{:S(2)}, u32[]{:S(2)}) collective-permute-start(bf16[32,1024]{1,0:T(8,128)(2,1)} %get-tuple-element.32), channel_id=1, source_target_pairs={{0,2},{1,3},{2,0},{3,1},{4,6},{5,7},{6,4},{7,5},{8,10},{9,11},{10,... | collective-permute-start | bytes 196616 | tf_op jit(solution)/shard_map/ppermute | solution.py:404
  31.6 0.0 collective-permute-start.2
  31.6 0.9 %collective-permute-done.8.refs_1_ = bf16[32,1024]{1,0:T(8,128)(2,1)S(1)} collective-permute-done((bf16[32,1024]{1,0:T(8,128)(2,1)}, bf16[32,1024]{1,0:T(8,128)(2,1)S(1)}, u32[]{:S(2)}, u32[]{:S(2)}) %collective-permute-start.8) | collective-permute-done | bytes 65568 | tf_op jit(solution)/shard_map/ppermute | solution.py:404
  32.5 0.7 %collective-permute-done.9.refs_2_ = bf16[32,1024]{1,0:T(8,128)(2,1)S(1)} collective-permute-done((bf16[32,1024]{1,0:T(8,128)(2,1)}, bf16[32,1024]{1,0:T(8,128)(2,1)S(1)}, u32[]{:S(2)}, u32[]{:S(2)}) %collective-permute-start.9) | collective-permute-done | bytes 65568 | tf_op jit(solution)/shard_map/ppermute | solution.py:404
  33.2 1.7 %collective-permute-start.4 = (bf16[32,1024]{1,0:T(8,128)(2,1)}, bf16[32,1024]{1,0:T(8,128)(2,1)S(1)}, u32[]{:S(2)}, u32[]{:S(2)}) collective-permute-start(bf16[32,1024]{1,0:T(8,128)(2,1)} %get-tuple-element.35), channel_id=1, source_target_pairs={{0,13},{1,12},{2,15},{3,14},{4,9},{5,8},{6,11},{7,10},{8,5},{9,4},... | collective-permute-start | bytes 196616 | tf_op jit(solution)/shard_map/ppermute | solution.py:404
  34.9 0.0 collective-permute-done.refs_0_
  34.9 2.2 %collective-permute-start.5 = (bf16[32,1024]{1,0:T(8,128)(2,1)}, bf16[32,1024]{1,0:T(8,128)(2,1)S(1)}, u32[]{:S(2)}, u32[]{:S(2)}) collective-permute-start(bf16[32,1024]{1,0:T(8,128)(2,1)} %get-tuple-element.36), channel_id=1, source_target_pairs={{0,3},{1,2},{2,1},{3,0},{4,7},{5,6},{6,5},{7,4},{8,11},{9,10},{10,... | collective-permute-start | bytes 196616 | tf_op jit(solution)/shard_map/ppermute | solution.py:404
  37.0 0.0 collective-permute-start.6
  37.0 0.0 collective-permute-done.2.refs_2_
  37.0 0.2 collective-permute-start.7
  37.2 1.6 %copy-done.1 = bf16[1024,1024]{1,0:T(8,128)(2,1)S(1)} copy-done((bf16[1024,1024]{1,0:T(8,128)(2,1)S(1)}, bf16[1024,1024]{1,0:T(8,128)(2,1)}, u32[]{:S(2)}) %copy-start.1) | copy-done | bytes 2097176
  38.8 0.8 %copy-done.3 = bf16[32,1024]{1,0:T(8,128)(2,1)S(1)} copy-done((bf16[32,1024]{1,0:T(8,128)(2,1)S(1)}, bf16[32,1024]{1,0:T(8,128)(2,1)}, u32[]{:S(2)}) %copy-start.3) | copy-done | bytes 65560
  39.6 1.1 %early_rows.1 = (bf16[256,1024]{1,0:T(8,128)(2,1)S(1)}, bf16[256,256]{1,0:T(8,128)(2,1)S(1)}, bf16[256,256]{1,0:T(8,128)(2,1)S(1)}) custom-call(bf16[1024]{0:T(1024)(128)(2,1)S(1)} %copy-done.4, bf16[1024,512]{1,0:T(8,128)(2,1)S(1)} %copy-done, bf16[1024,1024]{1,0:T(8,128)(2,1)S(1)} %copy-done.1, bf16[32,1024]{1,0:T(8,128)(2,1)S(1)} %copy-done.3, ...), custom_call_target="tpu_custom_call" | custom-call | flops 805306368 | bytes 4194304 | tf_op jit(solution)/shard_map/early_rows/pallas_call | solution.py:230
  40.8 0.0 collective-permute-done.4.refs_4_
  40.8 1.1 %collective-permute-done.6.refs_6_ = bf16[32,1024]{1,0:T(8,128)(2,1)S(1)} collective-permute-done((bf16[32,1024]{1,0:T(8,128)(2,1)}, bf16[32,1024]{1,0:T(8,128)(2,1)S(1)}, u32[]{:S(2)}, u32[]{:S(2)}) %collective-permute-start.6) | collective-permute-done | bytes 65568 | tf_op jit(solution)/shard_map/ppermute | solution.py:404
  41.8 0.7 %pairs.1 = (bf16[256,1024]{1,0:T(8,128)(2,1)S(1)}, bf16[512,256]{1,0:T(8,128)(2,1)S(1)}, bf16[512,256]{1,0:T(8,128)(2,1)S(1)}) custom-call(bf16[1024]{0:T(1024)(128)(2,1)S(1)} %copy-done.4, bf16[1024,512]{1,0:T(8,128)(2,1)S(1)} %copy-done, bf16[32,1024]{1,0:T(8,128)(2,1)S(1)} %collective-permute-done.refs_0_, ...), custom_call_target="tpu_custom_call" | custom-call | flops 268435456 | bytes 2359296 | tf_op jit(solution)/shard_map/pairs/pallas_call | solution.py:248
  42.5 2.9 %collective-permute-start.16 = (bf16[512,256]{1,0:T(8,128)(2,1)S(1)}, bf16[512,256]{1,0:T(8,128)(2,1)S(1)}, u32[]{:S(2)}, u32[]{:S(2)}) collective-permute-start(bf16[512,256]{1,0:T(8,128)(2,1)S(1)} %get-tuple-element.51.refs_0_), channel_id=1, source_target_pairs={{0,1},{1,2},{2,3},{3,4},{4,5},{5,6},{6,7},{7,8},{8,9},{9,10},{10,1... | collective-permute-start | bytes 786440 | tf_op jit(solution)/shard_map/ppermute | solution.py:27
  45.4 2.2 %collective-permute-start.15 = (bf16[512,256]{1,0:T(8,128)(2,1)S(1)}, bf16[512,256]{1,0:T(8,128)(2,1)S(1)}, u32[]{:S(2)}, u32[]{:S(2)}) collective-permute-start(bf16[512,256]{1,0:T(8,128)(2,1)S(1)} %get-tuple-element.52.refs_1_), channel_id=1, source_target_pairs={{0,1},{1,2},{2,3},{3,4},{4,5},{5,6},{6,7},{7,8},{8,9},{9,10},{10,1... | collective-permute-start | bytes 786440 | tf_op jit(solution)/shard_map/ppermute | solution.py:27
  47.7 3.2 %own_frame.1 = (bf16[512,1024]{1,0:T(8,128)(2,1)S(1)}, f32[512,1024]{1,0:T(8,128)S(1)}, f32[512,1024]{1,0:T(8,128)S(1)}, f32[512,1024]{1,0:T(8,128)S(1)}) custom-call(bf16[256,1024]{1,0:T(8,128)(2,1)S(1)} %get-tuple-element.49.normed_ref, bf16[1024,1024]{1,0:T(8,128)(2,1)S(1)} %copy-done.2, bf16[256,1024]{1,0:T(8,128)(2,1)S(1)} %get-tuple-element.50.early_ref, ...), custom_call_target="tpu_custom_call" | custom-call | flops 2147483648 | bytes 6291456 | tf_op jit(solution)/shard_map/own_frame/pallas_call | solution.py:309
  50.8 1.7 %earlier_frame.2.refs_0_ = bf16[512,512]{1,0:T(8,128)(2,1)S(1)} custom-call(bf16[512,1024]{1,0:T(8,128)(2,1)S(1)} %get-tuple-element.53.query_ref, bf16[512,256]{1,0:T(8,128)(2,1)S(1)} %collective-permute-done.16.pairs_ref, f32[512,1024]{1,0:T(8,128)S(1)} %get-tuple-element.54.sum_ref, f32[512,1024]{1,0:T(8,128)S(1)} %get-tuple-element.55.total_ref, ...), custom_call_target="tpu_custom_call" | custom-call | flops 536870912 | bytes 5242880 | tf_op jit(solution)/shard_map/earlier_frame/pallas_call | solution.py:388
  52.6 2.5 %earlier_frame.3 = bf16[512,1024]{1,0:T(8,128)(2,1)} custom-call(bf16[512,1024]{1,0:T(8,128)(2,1)S(1)} %get-tuple-element.53.query_ref, bf16[512,256]{1,0:T(8,128)(2,1)S(1)} %collective-permute-done.15.pairs_ref, f32[512,1024]{1,0:T(8,128)S(1)} %get-tuple-element.54.sum_ref, f32[512,1024]{1,0:T(8,128)S(1)} %get-tuple-element.55.total_ref, ...), custom_call_target="tpu_custom_call" | custom-call | flops 536870912 | bytes 5242880 | tf_op jit(solution)/shard_map/earlier_frame/pallas_call | solution.py:388
  (18 shorter events, 0.0 us)
Async XLA Ops:
  0.0 37.2 %copy-start = (bf16[1024,512]{1,0:T(8,128)(2,1)S(1)}, bf16[1024,512]{1,0:T(8,128)(2,1)}, u32[]{:S(2)}) copy-start(bf16[1024,512]{1,0:T(8,128)(2,1)} %w_kv_ref.3) | copy-start | bytes 3145732
  0.0 37.2 %copy-start.4 = (bf16[1024]{0:T(1024)(128)(2,1)S(1)}, bf16[1024]{0:T(1024)(128)(2,1)}, u32[]{:S(2)}) copy-start(bf16[1024]{0:T(1024)(128)(2,1)} %gain_ref.3) | copy-start | bytes 6148
  10.3 9.2 %collective-permute-start.10 = (bf16[32,1024]{1,0:T(8,128)(2,1)}, bf16[32,1024]{1,0:T(8,128)(2,1)S(1)}, u32[]{:S(2)}, u32[]{:S(2)}) collective-permute-start(bf16[32,1024]{1,0:T(8,128)(2,1)} %get-tuple-element.42), channel_id=1, source_target_pairs={{0,14},{1,15},{2,12},{3,13},{4,10},{5,11},{6,8},{7,9},{8,6},{9,7},... | collective-permute-start | bytes 196616 | tf_op jit(solution)/shard_map/ppermute | solution.py:404
  15.4 5.2 %collective-permute-start.11 = (bf16[32,1024]{1,0:T(8,128)(2,1)}, bf16[32,1024]{1,0:T(8,128)(2,1)S(1)}, u32[]{:S(2)}, u32[]{:S(2)}) collective-permute-start(bf16[32,1024]{1,0:T(8,128)(2,1)} %get-tuple-element.43), channel_id=1, source_target_pairs={{0,4},{1,5},{2,6},{3,7},{4,0},{5,1},{6,2},{7,3},{8,12},{9,13},{10,... | collective-permute-start | bytes 196616 | tf_op jit(solution)/shard_map/ppermute | solution.py:404
  15.4 8.2 %collective-permute-start.12 = (bf16[32,1024]{1,0:T(8,128)(2,1)}, bf16[32,1024]{1,0:T(8,128)(2,1)S(1)}, u32[]{:S(2)}, u32[]{:S(2)}) collective-permute-start(bf16[32,1024]{1,0:T(8,128)(2,1)} %get-tuple-element.44), channel_id=1, source_target_pairs={{0,15},{1,14},{2,13},{3,12},{4,11},{5,10},{6,9},{7,8},{8,7},{9,6},... | collective-permute-start | bytes 196616 | tf_op jit(solution)/shard_map/ppermute | solution.py:404
  16.8 12.1 %collective-permute-start.13 = (bf16[32,1024]{1,0:T(8,128)(2,1)}, bf16[32,1024]{1,0:T(8,128)(2,1)S(1)}, u32[]{:S(2)}, u32[]{:S(2)}) collective-permute-start(bf16[32,1024]{1,0:T(8,128)(2,1)} %get-tuple-element.45), channel_id=1, source_target_pairs={{0,8},{1,9},{2,10},{3,11},{4,12},{5,13},{6,14},{7,15},{8,0},{9,1},... | collective-permute-start | bytes 196616 | tf_op jit(solution)/shard_map/ppermute | solution.py:404
  19.2 12.5 %collective-permute-start.14 = (bf16[32,1024]{1,0:T(8,128)(2,1)}, bf16[32,1024]{1,0:T(8,128)(2,1)S(1)}, u32[]{:S(2)}, u32[]{:S(2)}) collective-permute-start(bf16[32,1024]{1,0:T(8,128)(2,1)} %get-tuple-element.46), channel_id=1, source_target_pairs={{0,5},{1,4},{2,7},{3,6},{4,1},{5,0},{6,3},{7,2},{8,13},{9,12},{10,... | collective-permute-start | bytes 196616 | tf_op jit(solution)/shard_map/ppermute | solution.py:404
  19.5 13.0 %collective-permute-start.8 = (bf16[32,1024]{1,0:T(8,128)(2,1)}, bf16[32,1024]{1,0:T(8,128)(2,1)S(1)}, u32[]{:S(2)}, u32[]{:S(2)}) collective-permute-start(bf16[32,1024]{1,0:T(8,128)(2,1)} %get-tuple-element.40), channel_id=1, source_target_pairs={{0,10},{1,11},{2,8},{3,9},{4,14},{5,15},{6,12},{7,13},{8,2},{9,3},... | collective-permute-start | bytes 196616 | tf_op jit(solution)/shard_map/ppermute | solution.py:404
  20.7 12.5 %collective-permute-start.9 = (bf16[32,1024]{1,0:T(8,128)(2,1)}, bf16[32,1024]{1,0:T(8,128)(2,1)S(1)}, u32[]{:S(2)}, u32[]{:S(2)}) collective-permute-start(bf16[32,1024]{1,0:T(8,128)(2,1)} %get-tuple-element.41), channel_id=1, source_target_pairs={{0,11},{1,10},{2,9},{3,8},{4,15},{5,14},{6,13},{7,12},{8,3},{9,2},... | collective-permute-start | bytes 196616 | tf_op jit(solution)/shard_map/ppermute | solution.py:404
  23.6 11.2 %collective-permute-start = (bf16[32,1024]{1,0:T(8,128)(2,1)}, bf16[32,1024]{1,0:T(8,128)(2,1)S(1)}, u32[]{:S(2)}, u32[]{:S(2)}) collective-permute-start(bf16[32,1024]{1,0:T(8,128)(2,1)} %get-tuple-element.31), channel_id=1, source_target_pairs={{0,9},{1,8},{2,11},{3,10},{4,13},{5,12},{6,15},{7,14},{8,1},{9,0},... | collective-permute-start | bytes 196616 | tf_op jit(solution)/shard_map/ppermute | solution.py:404
  29.0 8.1 %collective-permute-start.1 = (bf16[32,1024]{1,0:T(8,128)(2,1)}, bf16[32,1024]{1,0:T(8,128)(2,1)S(1)}, u32[]{:S(2)}, u32[]{:S(2)}) collective-permute-start(bf16[32,1024]{1,0:T(8,128)(2,1)} %get-tuple-element.32), channel_id=1, source_target_pairs={{0,2},{1,3},{2,0},{3,1},{4,6},{5,7},{6,4},{7,5},{8,10},{9,11},{10,... | collective-permute-start | bytes 196616 | tf_op jit(solution)/shard_map/ppermute | solution.py:404
  31.6 5.4 %collective-permute-start.2 = (bf16[32,1024]{1,0:T(8,128)(2,1)}, bf16[32,1024]{1,0:T(8,128)(2,1)S(1)}, u32[]{:S(2)}, u32[]{:S(2)}) collective-permute-start(bf16[32,1024]{1,0:T(8,128)(2,1)} %get-tuple-element.33), channel_id=1, source_target_pairs={{0,12},{1,13},{2,14},{3,15},{4,8},{5,9},{6,10},{7,11},{8,4},{9,5},... | collective-permute-start | bytes 196616 | tf_op jit(solution)/shard_map/ppermute | solution.py:404
  32.5 8.2 %collective-permute-start.3 = (bf16[32,1024]{1,0:T(8,128)(2,1)}, bf16[32,1024]{1,0:T(8,128)(2,1)S(1)}, u32[]{:S(2)}, u32[]{:S(2)}) collective-permute-start(bf16[32,1024]{1,0:T(8,128)(2,1)} %get-tuple-element.34), channel_id=1, source_target_pairs={{0,6},{1,7},{2,4},{3,5},{4,2},{5,3},{6,0},{7,1},{8,14},{9,15},{10,... | collective-permute-start | bytes 196616 | tf_op jit(solution)/shard_map/ppermute | solution.py:404
  33.2 7.6 %collective-permute-start.4 = (bf16[32,1024]{1,0:T(8,128)(2,1)}, bf16[32,1024]{1,0:T(8,128)(2,1)S(1)}, u32[]{:S(2)}, u32[]{:S(2)}) collective-permute-start(bf16[32,1024]{1,0:T(8,128)(2,1)} %get-tuple-element.35), channel_id=1, source_target_pairs={{0,13},{1,12},{2,15},{3,14},{4,9},{5,8},{6,11},{7,10},{8,5},{9,4},... | collective-permute-start | bytes 196616 | tf_op jit(solution)/shard_map/ppermute | solution.py:404
  34.9 5.9 %collective-permute-start.5 = (bf16[32,1024]{1,0:T(8,128)(2,1)}, bf16[32,1024]{1,0:T(8,128)(2,1)S(1)}, u32[]{:S(2)}, u32[]{:S(2)}) collective-permute-start(bf16[32,1024]{1,0:T(8,128)(2,1)} %get-tuple-element.36), channel_id=1, source_target_pairs={{0,3},{1,2},{2,1},{3,0},{4,7},{5,6},{6,5},{7,4},{8,11},{9,10},{10,... | collective-permute-start | bytes 196616 | tf_op jit(solution)/shard_map/ppermute | solution.py:404
  37.0 4.8 %collective-permute-start.6 = (bf16[32,1024]{1,0:T(8,128)(2,1)}, bf16[32,1024]{1,0:T(8,128)(2,1)S(1)}, u32[]{:S(2)}, u32[]{:S(2)}) collective-permute-start(bf16[32,1024]{1,0:T(8,128)(2,1)} %get-tuple-element.37), channel_id=1, source_target_pairs={{0,7},{1,6},{2,5},{3,4},{4,3},{5,2},{6,1},{7,0},{8,15},{9,14},{10,... | collective-permute-start | bytes 196616 | tf_op jit(solution)/shard_map/ppermute | solution.py:404
  37.0 4.8 %collective-permute-start.7 = (bf16[32,1024]{1,0:T(8,128)(2,1)}, bf16[32,1024]{1,0:T(8,128)(2,1)S(1)}, u32[]{:S(2)}, u32[]{:S(2)}) collective-permute-start(bf16[32,1024]{1,0:T(8,128)(2,1)} %get-tuple-element.38), channel_id=1, source_target_pairs={{0,1},{1,0},{2,3},{3,2},{4,5},{5,4},{6,7},{7,6},{8,9},{9,8},{10,11... | collective-permute-start | bytes 196616 | tf_op jit(solution)/shard_map/ppermute | solution.py:404
  37.2 1.6 %copy-start.1 = (bf16[1024,1024]{1,0:T(8,128)(2,1)S(1)}, bf16[1024,1024]{1,0:T(8,128)(2,1)}, u32[]{:S(2)}) copy-start(bf16[1024,1024]{1,0:T(8,128)(2,1)} %w_ref.1) | copy-start | bytes 6291460
  38.8 0.8 %copy-start.3 = (bf16[32,1024]{1,0:T(8,128)(2,1)S(1)}, bf16[32,1024]{1,0:T(8,128)(2,1)}, u32[]{:S(2)}) copy-start(bf16[32,1024]{1,0:T(8,128)(2,1)} %get-tuple-element.39.refs_0_) | copy-start | bytes 196612
  39.6 8.0 %copy-start.2 = (bf16[1024,1024]{1,0:T(8,128)(2,1)S(1)}, bf16[1024,1024]{1,0:T(8,128)(2,1)}, u32[]{:S(2)}) copy-start(bf16[1024,1024]{1,0:T(8,128)(2,1)} %w_ref.1) | copy-start | bytes 6291460
  42.5 8.3 %collective-permute-start.16 = (bf16[512,256]{1,0:T(8,128)(2,1)S(1)}, bf16[512,256]{1,0:T(8,128)(2,1)S(1)}, u32[]{:S(2)}, u32[]{:S(2)}) collective-permute-start(bf16[512,256]{1,0:T(8,128)(2,1)S(1)} %get-tuple-element.51.refs_0_), channel_id=1, source_target_pairs={{0,1},{1,2},{2,3},{3,4},{4,5},{5,6},{6,7},{7,8},{8,9},{9,10},{10,1... | collective-permute-start | bytes 786440 | tf_op jit(solution)/shard_map/ppermute | solution.py:27
  45.4 7.1 %collective-permute-start.15 = (bf16[512,256]{1,0:T(8,128)(2,1)S(1)}, bf16[512,256]{1,0:T(8,128)(2,1)S(1)}, u32[]{:S(2)}, u32[]{:S(2)}) collective-permute-start(bf16[512,256]{1,0:T(8,128)(2,1)S(1)} %get-tuple-element.52.refs_1_), channel_id=1, source_target_pairs={{0,1},{1,2},{2,3},{3,4},{4,5},{5,6},{6,7},{7,8},{8,9},{9,10},{10,1... | collective-permute-start | bytes 786440 | tf_op jit(solution)/shard_map/ppermute | solution.py:27

commit v16 on v15

--- a/solution.py
+++ b/solution.py
@@ -14,7 +14,7 @@
 SB = 16
 SPAN = 128
 GROUPS = ((0, 4), (4, 8))
-APART = (0, 10, 11, 14, 4, 15, 8, 5, 9, 2, 12, 6, 13, 3, 7, 1)
+APART = (0, 5, 11, 8, 4, 14, 10, 15, 9, 2, 12, 6, 13, 3, 7, 1)
 EARLY = SB // 2
 
 epsilon = 1e-06
@@ -164,7 +164,7 @@
             pltpu.SemaphoreType.DMA((len(GROUPS), 3)),
             pltpu.SemaphoreType.DMA((len(GROUPS), SB)),
         ],
-        compiler_params=pltpu.CompilerParams(vmem_limit_bytes=62 * MIB),
+        compiler_params=pltpu.CompilerParams(vmem_limit_bytes=60 * MIB),
         cost_estimate=pl.CostEstimate(
             flops=2 * rows * width * 3 * width + 8 * rows * SPAN * width,
             bytes_accessed=2 * (3 * width * width + 2 * rows * width),

time: 55.8 us -> 55.1 us (0.987)
  starting transfers between devices: 27 us -> 31.1 us
  waiting for transfers between devices: 6.12 us -> 3.05 us
  local copies, waits for them, and re-layouts: 2.44 us -> 0.85 us
    ppermute x15, starting transfers between devices: 21.9 us -> 25.7 us  [swap(): return lax.ppermute(tile, 'tm', route)]
    ppermute x15, waiting for transfers between devices: 6.11 us -> 3.05 us  [swap(): return lax.ppermute(tile, 'tm', route)]
    unnamed x10 -> x8, local copies, waits for them, and re-layouts: 2.44 us -> 0.85 us
  transfers between devices with their start and end apart: 17 -> 17, of which waited for: 4 -> 3; matrix products, arithmetic and copies ran while one was open for 0% -> 0% of each run, Pallas kernels for 11% -> 11%
where the time goes in v16:
time: 55.1 us; the launch traced here: 54.9 us
  starting transfers between devices  31.1 us (56%)
  Pallas kernels  19.6 us (36%)
  waiting for transfers between devices  3.05 us (6%)
  local copies, waits for them, and re-layouts  0.85 us (2%)
    ppermute x15, starting transfers between devices, swap(): return lax.ppermute(tile, 'tm', route)  25.7 us
    pallas_call x1, Pallas kernels, mixer(): pl.pallas_call(functools.partial(mixer_kernel, state is not None), in_spe...  10.4 us
    ppermute x2, starting transfers between devices, shifted(): return lax.ppermute(block, axis, route)  5.41 us
    pallas_call x2, Pallas kernels, earlier_frame(): pl.pallas_call(functools.partial(earlier_kernel, group), compiler_params=...  4.19 us
    pallas_call x1, Pallas kernels, own_frame(): pl.pallas_call(own_kernel, out_shape=[jax.ShapeDtypeStruct((rows, width),...  3.17 us
    ppermute x15, waiting for transfers between devices, swap(): return lax.ppermute(tile, 'tm', route)  3.05 us
  transfers between devices with their start and end apart: 17, of which 3 were waited for; matrix products, arithmetic and copies ran while one was open for 0% of the time, Pallas kernels for 11%

profile of v16, /device:TPU:1, one launch (start us, length us, event | category | flops | bytes accessed | tf_op | source)
XLA Modules:
  0.0 54.9 jit_solution(15530019465137510990)
XLA Ops:
  0.0 10.4 %mixer.1 = (bf16[32,1024]{1,0:T(8,128)(2,1)}, bf16[32,1024]{1,0:T(8,128)(2,1)}, bf16[32,1024]{1,0:T(8,128)(2,1)}, bf16[32,1024]{1,0:T(8,128)(2,1)}, bf16[32,1024...) custom-call(bf16[512,1024]{1,0:T(8,128)(2,1)} %bitcast.2, ...), custom_call_target="tpu_custom_call" | custom-call | flops 3758096384 | bytes 8388608 | tf_op jit(solution)/shard_map/mixer/pallas_call | solution.py:155
  10.5 3.2 %collective-permute-start.10 = (bf16[32,1024]{1,0:T(8,128)(2,1)}, bf16[32,1024]{1,0:T(8,128)(2,1)S(1)}, u32[]{:S(2)}, u32[]{:S(2)}) collective-permute-start(bf16[32,1024]{1,0:T(8,128)(2,1)} %get-tuple-element.42), channel_id=1, source_target_pairs={{0,8},{1,9},{2,10},{3,11},{4,12},{5,13},{6,14},{7,15},{8,0},{9,1},... | collective-permute-start | bytes 196616 | tf_op jit(solution)/shard_map/ppermute | solution.py:404
  13.7 1.3 %collective-permute-start.11 = (bf16[32,1024]{1,0:T(8,128)(2,1)}, bf16[32,1024]{1,0:T(8,128)(2,1)S(1)}, u32[]{:S(2)}, u32[]{:S(2)}) collective-permute-start(bf16[32,1024]{1,0:T(8,128)(2,1)} %get-tuple-element.43), channel_id=1, source_target_pairs={{0,4},{1,5},{2,6},{3,7},{4,0},{5,1},{6,2},{7,3},{8,12},{9,13},{10,... | collective-permute-start | bytes 196616 | tf_op jit(solution)/shard_map/ppermute | solution.py:404
  15.0 0.9 %collective-permute-start.12 = (bf16[32,1024]{1,0:T(8,128)(2,1)}, bf16[32,1024]{1,0:T(8,128)(2,1)S(1)}, u32[]{:S(2)}, u32[]{:S(2)}) collective-permute-start(bf16[32,1024]{1,0:T(8,128)(2,1)} %get-tuple-element.44), channel_id=1, source_target_pairs={{0,14},{1,15},{2,12},{3,13},{4,10},{5,11},{6,8},{7,9},{8,6},{9,7},... | collective-permute-start | bytes 196616 | tf_op jit(solution)/shard_map/ppermute | solution.py:404
  15.9 1.3 %collective-permute-start.13 = (bf16[32,1024]{1,0:T(8,128)(2,1)}, bf16[32,1024]{1,0:T(8,128)(2,1)S(1)}, u32[]{:S(2)}, u32[]{:S(2)}) collective-permute-start(bf16[32,1024]{1,0:T(8,128)(2,1)} %get-tuple-element.45), channel_id=1, source_target_pairs={{0,10},{1,11},{2,8},{3,9},{4,14},{5,15},{6,12},{7,13},{8,2},{9,3},... | collective-permute-start | bytes 196616 | tf_op jit(solution)/shard_map/ppermute | solution.py:404
  17.2 3.7 %collective-permute-start.14 = (bf16[32,1024]{1,0:T(8,128)(2,1)}, bf16[32,1024]{1,0:T(8,128)(2,1)S(1)}, u32[]{:S(2)}, u32[]{:S(2)}) collective-permute-start(bf16[32,1024]{1,0:T(8,128)(2,1)} %get-tuple-element.46), channel_id=1, source_target_pairs={{0,15},{1,14},{2,13},{3,12},{4,11},{5,10},{6,9},{7,8},{8,7},{9,6},... | collective-permute-start | bytes 196616 | tf_op jit(solution)/shard_map/ppermute | solution.py:404
  20.9 0.2 collective-permute-start.8
  21.1 0.0 collective-permute-done.11.refs_4_
  21.1 2.5 %collective-permute-start.9 = (bf16[32,1024]{1,0:T(8,128)(2,1)}, bf16[32,1024]{1,0:T(8,128)(2,1)S(1)}, u32[]{:S(2)}, u32[]{:S(2)}) collective-permute-start(bf16[32,1024]{1,0:T(8,128)(2,1)} %get-tuple-element.41), channel_id=1, source_target_pairs={{0,11},{1,10},{2,9},{3,8},{4,15},{5,14},{6,13},{7,12},{8,3},{9,2},... | collective-permute-start | bytes 196616 | tf_op jit(solution)/shard_map/ppermute | solution.py:404
  23.6 0.0 collective-permute-done.12.refs_5_
  23.6 4.0 %collective-permute-start = (bf16[32,1024]{1,0:T(8,128)(2,1)}, bf16[32,1024]{1,0:T(8,128)(2,1)S(1)}, u32[]{:S(2)}, u32[]{:S(2)}) collective-permute-start(bf16[32,1024]{1,0:T(8,128)(2,1)} %get-tuple-element.31), channel_id=1, source_target_pairs={{0,9},{1,8},{2,11},{3,10},{4,13},{5,12},{6,15},{7,14},{8,1},{9,0},... | collective-permute-start | bytes 196616 | tf_op jit(solution)/shard_map/ppermute | solution.py:404
  27.6 0.0 collective-permute-done.13.refs_6_
  27.6 0.2 collective-permute-start.1
  27.8 0.0 collective-permute-done.14.refs_7_
  27.8 1.4 %collective-permute-start.2 = (bf16[32,1024]{1,0:T(8,128)(2,1)}, bf16[32,1024]{1,0:T(8,128)(2,1)S(1)}, u32[]{:S(2)}, u32[]{:S(2)}) collective-permute-start(bf16[32,1024]{1,0:T(8,128)(2,1)} %get-tuple-element.33), channel_id=1, source_target_pairs={{0,12},{1,13},{2,14},{3,15},{4,8},{5,9},{6,10},{7,11},{8,4},{9,5},... | collective-permute-start | bytes 196616 | tf_op jit(solution)/shard_map/ppermute | solution.py:404
  29.2 3.2 %collective-permute-start.3 = (bf16[32,1024]{1,0:T(8,128)(2,1)}, bf16[32,1024]{1,0:T(8,128)(2,1)S(1)}, u32[]{:S(2)}, u32[]{:S(2)}) collective-permute-start(bf16[32,1024]{1,0:T(8,128)(2,1)} %get-tuple-element.34), channel_id=1, source_target_pairs={{0,6},{1,7},{2,4},{3,5},{4,2},{5,3},{6,0},{7,1},{8,14},{9,15},{10,... | collective-permute-start | bytes 196616 | tf_op jit(solution)/shard_map/ppermute | solution.py:404
  32.4 0.0 collective-permute-done.9.refs_2_
  32.5 2.1 %collective-permute-start.4 = (bf16[32,1024]{1,0:T(8,128)(2,1)}, bf16[32,1024]{1,0:T(8,128)(2,1)S(1)}, u32[]{:S(2)}, u32[]{:S(2)}) collective-permute-start(bf16[32,1024]{1,0:T(8,128)(2,1)} %get-tuple-element.35), channel_id=1, source_target_pairs={{0,13},{1,12},{2,15},{3,14},{4,9},{5,8},{6,11},{7,10},{8,5},{9,4},... | collective-permute-start | bytes 196616 | tf_op jit(solution)/shard_map/ppermute | solution.py:404
  34.6 1.5 %collective-permute-start.5 = (bf16[32,1024]{1,0:T(8,128)(2,1)}, bf16[32,1024]{1,0:T(8,128)(2,1)S(1)}, u32[]{:S(2)}, u32[]{:S(2)}) collective-permute-start(bf16[32,1024]{1,0:T(8,128)(2,1)} %get-tuple-element.36), channel_id=1, source_target_pairs={{0,3},{1,2},{2,1},{3,0},{4,7},{5,6},{6,5},{7,4},{8,11},{9,10},{10,... | collective-permute-start | bytes 196616 | tf_op jit(solution)/shard_map/ppermute | solution.py:404
  36.2 0.1 collective-permute-start.7
  36.3 0.0 copy-start.2
  36.3 0.8 %copy-done.2 = bf16[32,1024]{1,0:T(8,128)(2,1)S(1)} copy-done((bf16[32,1024]{1,0:T(8,128)(2,1)S(1)}, bf16[32,1024]{1,0:T(8,128)(2,1)}, u32[]{:S(2)}) %copy-start.2) | copy-done | bytes 65560
  37.1 1.1 %early_rows.1 = (bf16[256,1024]{1,0:T(8,128)(2,1)S(1)}, bf16[256,256]{1,0:T(8,128)(2,1)S(1)}, bf16[256,256]{1,0:T(8,128)(2,1)S(1)}) custom-call(bf16[1024]{0:T(1024)(128)(2,1)S(1)} %copy-done.3, bf16[1024,512]{1,0:T(8,128)(2,1)S(1)} %copy-done, bf16[1024,1024]{1,0:T(8,128)(2,1)S(1)} %copy-done.1, bf16[32,1024]{1,0:T(8,128)(2,1)S(1)} %copy-done.2, ...), custom_call_target="tpu_custom_call" | custom-call | flops 805306368 | bytes 4194304 | tf_op jit(solution)/shard_map/early_rows/pallas_call | solution.py:230
  38.2 0.1 collective-permute-done.4.refs_4_
  38.3 0.2 collective-permute-done.5.refs_5_
  38.5 2.7 %collective-permute-done.6.refs_6_ = bf16[32,1024]{1,0:T(8,128)(2,1)S(1)} collective-permute-done((bf16[32,1024]{1,0:T(8,128)(2,1)}, bf16[32,1024]{1,0:T(8,128)(2,1)S(1)}, u32[]{:S(2)}, u32[]{:S(2)}) %collective-permute-start.6) | collective-permute-done | bytes 65568 | tf_op jit(solution)/shard_map/ppermute | solution.py:404
  41.2 0.7 %pairs.1 = (bf16[256,1024]{1,0:T(8,128)(2,1)S(1)}, bf16[512,256]{1,0:T(8,128)(2,1)S(1)}, bf16[512,256]{1,0:T(8,128)(2,1)S(1)}) custom-call(bf16[1024]{0:T(1024)(128)(2,1)S(1)} %copy-done.3, bf16[1024,512]{1,0:T(8,128)(2,1)S(1)} %copy-done, bf16[32,1024]{1,0:T(8,128)(2,1)S(1)} %collective-permute-done.refs_0_, ...), custom_call_target="tpu_custom_call" | custom-call | flops 268435456 | bytes 2359296 | tf_op jit(solution)/shard_map/pairs/pallas_call | solution.py:248
  41.9 2.1 %collective-permute-start.16 = (bf16[512,256]{1,0:T(8,128)(2,1)S(1)}, bf16[512,256]{1,0:T(8,128)(2,1)S(1)}, u32[]{:S(2)}, u32[]{:S(2)}) collective-permute-start(bf16[512,256]{1,0:T(8,128)(2,1)S(1)} %get-tuple-element.51.refs_0_), channel_id=1, source_target_pairs={{0,1},{1,2},{2,3},{3,4},{4,5},{5,6},{6,7},{7,8},{8,9},{9,10},{10,1... | collective-permute-start | bytes 786440 | tf_op jit(solution)/shard_map/ppermute | solution.py:27
  44.0 3.3 %collective-permute-start.15 = (bf16[512,256]{1,0:T(8,128)(2,1)S(1)}, bf16[512,256]{1,0:T(8,128)(2,1)S(1)}, u32[]{:S(2)}, u32[]{:S(2)}) collective-permute-start(bf16[512,256]{1,0:T(8,128)(2,1)S(1)} %get-tuple-element.52.refs_1_), channel_id=1, source_target_pairs={{0,1},{1,2},{2,3},{3,4},{4,5},{5,6},{6,7},{7,8},{8,9},{9,10},{10,1... | collective-permute-start | bytes 786440 | tf_op jit(solution)/shard_map/ppermute | solution.py:27
  47.3 3.2 %own_frame.1 = (bf16[512,1024]{1,0:T(8,128)(2,1)S(1)}, f32[512,1024]{1,0:T(8,128)S(1)}, f32[512,1024]{1,0:T(8,128)S(1)}, f32[512,1024]{1,0:T(8,128)S(1)}) custom-call(bf16[256,1024]{1,0:T(8,128)(2,1)S(1)} %get-tuple-element.49.normed_ref, bf16[1024,1024]{1,0:T(8,128)(2,1)S(1)} %copy-done.1, bf16[256,1024]{1,0:T(8,128)(2,1)S(1)} %get-tuple-element.50.early_ref, ...), custom_call_target="tpu_custom_call" | custom-call | flops 2147483648 | bytes 6291456 | tf_op jit(solution)/shard_map/own_frame/pallas_call | solution.py:309
  50.5 1.7 %earlier_frame.2.refs_0_ = bf16[512,512]{1,0:T(8,128)(2,1)S(1)} custom-call(bf16[512,1024]{1,0:T(8,128)(2,1)S(1)} %get-tuple-element.53.query_ref, bf16[512,256]{1,0:T(8,128)(2,1)S(1)} %collective-permute-done.16.pairs_ref, f32[512,1024]{1,0:T(8,128)S(1)} %get-tuple-element.54.sum_ref, f32[512,1024]{1,0:T(8,128)S(1)} %get-tuple-element.55.total_ref, ...), custom_call_target="tpu_custom_call" | custom-call | flops 536870912 | bytes 5242880 | tf_op jit(solution)/shard_map/earlier_frame/pallas_call | solution.py:388
  52.2 2.5 %earlier_frame.3 = bf16[512,1024]{1,0:T(8,128)(2,1)} custom-call(bf16[512,1024]{1,0:T(8,128)(2,1)S(1)} %get-tuple-element.53.query_ref, bf16[512,256]{1,0:T(8,128)(2,1)S(1)} %collective-permute-done.15.pairs_ref, f32[512,1024]{1,0:T(8,128)S(1)} %get-tuple-element.54.sum_ref, f32[512,1024]{1,0:T(8,128)S(1)} %get-tuple-element.55.total_ref, ...), custom_call_target="tpu_custom_call" | custom-call | flops 536870912 | bytes 5242880 | tf_op jit(solution)/shard_map/earlier_frame/pallas_call | solution.py:388
  (16 shorter events, 0.0 us)
Async XLA Ops:
  0.0 36.2 %copy-start = (bf16[1024,512]{1,0:T(8,128)(2,1)S(1)}, bf16[1024,512]{1,0:T(8,128)(2,1)}, u32[]{:S(2)}) copy-start(bf16[1024,512]{1,0:T(8,128)(2,1)} %w_kv_ref.3) | copy-start | bytes 3145732
  0.0 36.2 %copy-start.1 = (bf16[1024,1024]{1,0:T(8,128)(2,1)S(1)}, bf16[1024,1024]{1,0:T(8,128)(2,1)}, u32[]{:S(2)}) copy-start(bf16[1024,1024]{1,0:T(8,128)(2,1)} %w_ref.1) | copy-start | bytes 6291460
  0.0 36.3 %copy-start.3 = (bf16[1024]{0:T(1024)(128)(2,1)S(1)}, bf16[1024]{0:T(1024)(128)(2,1)}, u32[]{:S(2)}) copy-start(bf16[1024]{0:T(1024)(128)(2,1)} %gain_ref.3) | copy-start | bytes 6148
  10.5 10.5 %collective-permute-start.10 = (bf16[32,1024]{1,0:T(8,128)(2,1)}, bf16[32,1024]{1,0:T(8,128)(2,1)S(1)}, u32[]{:S(2)}, u32[]{:S(2)}) collective-permute-start(bf16[32,1024]{1,0:T(8,128)(2,1)} %get-tuple-element.42), channel_id=1, source_target_pairs={{0,8},{1,9},{2,10},{3,11},{4,12},{5,13},{6,14},{7,15},{8,0},{9,1},... | collective-permute-start | bytes 196616 | tf_op jit(solution)/shard_map/ppermute | solution.py:404
  13.7 7.5 %collective-permute-start.11 = (bf16[32,1024]{1,0:T(8,128)(2,1)}, bf16[32,1024]{1,0:T(8,128)(2,1)S(1)}, u32[]{:S(2)}, u32[]{:S(2)}) collective-permute-start(bf16[32,1024]{1,0:T(8,128)(2,1)} %get-tuple-element.43), channel_id=1, source_target_pairs={{0,4},{1,5},{2,6},{3,7},{4,0},{5,1},{6,2},{7,3},{8,12},{9,13},{10,... | collective-permute-start | bytes 196616 | tf_op jit(solution)/shard_map/ppermute | solution.py:404
  15.0 8.7 %collective-permute-start.12 = (bf16[32,1024]{1,0:T(8,128)(2,1)}, bf16[32,1024]{1,0:T(8,128)(2,1)S(1)}, u32[]{:S(2)}, u32[]{:S(2)}) collective-permute-start(bf16[32,1024]{1,0:T(8,128)(2,1)} %get-tuple-element.44), channel_id=1, source_target_pairs={{0,14},{1,15},{2,12},{3,13},{4,10},{5,11},{6,8},{7,9},{8,6},{9,7},... | collective-permute-start | bytes 196616 | tf_op jit(solution)/shard_map/ppermute | solution.py:404
  15.9 11.7 %collective-permute-start.13 = (bf16[32,1024]{1,0:T(8,128)(2,1)}, bf16[32,1024]{1,0:T(8,128)(2,1)S(1)}, u32[]{:S(2)}, u32[]{:S(2)}) collective-permute-start(bf16[32,1024]{1,0:T(8,128)(2,1)} %get-tuple-element.45), channel_id=1, source_target_pairs={{0,10},{1,11},{2,8},{3,9},{4,14},{5,15},{6,12},{7,13},{8,2},{9,3},... | collective-permute-start | bytes 196616 | tf_op jit(solution)/shard_map/ppermute | solution.py:404
  17.2 10.6 %collective-permute-start.14 = (bf16[32,1024]{1,0:T(8,128)(2,1)}, bf16[32,1024]{1,0:T(8,128)(2,1)S(1)}, u32[]{:S(2)}, u32[]{:S(2)}) collective-permute-start(bf16[32,1024]{1,0:T(8,128)(2,1)} %get-tuple-element.46), channel_id=1, source_target_pairs={{0,15},{1,14},{2,13},{3,12},{4,11},{5,10},{6,9},{7,8},{8,7},{9,6},... | collective-permute-start | bytes 196616 | tf_op jit(solution)/shard_map/ppermute | solution.py:404
  20.9 8.3 %collective-permute-start.8 = (bf16[32,1024]{1,0:T(8,128)(2,1)}, bf16[32,1024]{1,0:T(8,128)(2,1)S(1)}, u32[]{:S(2)}, u32[]{:S(2)}) collective-permute-start(bf16[32,1024]{1,0:T(8,128)(2,1)} %get-tuple-element.40), channel_id=1, source_target_pairs={{0,5},{1,4},{2,7},{3,6},{4,1},{5,0},{6,3},{7,2},{8,13},{9,12},{10,... | collective-permute-start | bytes 196616 | tf_op jit(solution)/shard_map/ppermute | solution.py:404
  21.1 11.4 %collective-permute-start.9 = (bf16[32,1024]{1,0:T(8,128)(2,1)}, bf16[32,1024]{1,0:T(8,128)(2,1)S(1)}, u32[]{:S(2)}, u32[]{:S(2)}) collective-permute-start(bf16[32,1024]{1,0:T(8,128)(2,1)} %get-tuple-element.41), channel_id=1, source_target_pairs={{0,11},{1,10},{2,9},{3,8},{4,15},{5,14},{6,13},{7,12},{8,3},{9,2},... | collective-permute-start | bytes 196616 | tf_op jit(solution)/shard_map/ppermute | solution.py:404
  23.6 11.0 %collective-permute-start = (bf16[32,1024]{1,0:T(8,128)(2,1)}, bf16[32,1024]{1,0:T(8,128)(2,1)S(1)}, u32[]{:S(2)}, u32[]{:S(2)}) collective-permute-start(bf16[32,1024]{1,0:T(8,128)(2,1)} %get-tuple-element.31), channel_id=1, source_target_pairs={{0,9},{1,8},{2,11},{3,10},{4,13},{5,12},{6,15},{7,14},{8,1},{9,0},... | collective-permute-start | bytes 196616 | tf_op jit(solution)/shard_map/ppermute | solution.py:404
  27.6 8.6 %collective-permute-start.1 = (bf16[32,1024]{1,0:T(8,128)(2,1)}, bf16[32,1024]{1,0:T(8,128)(2,1)S(1)}, u32[]{:S(2)}, u32[]{:S(2)}) collective-permute-start(bf16[32,1024]{1,0:T(8,128)(2,1)} %get-tuple-element.32), channel_id=1, source_target_pairs={{0,2},{1,3},{2,0},{3,1},{4,6},{5,7},{6,4},{7,5},{8,10},{9,11},{10,... | collective-permute-start | bytes 196616 | tf_op jit(solution)/shard_map/ppermute | solution.py:404
  27.8 8.3 %collective-permute-start.2 = (bf16[32,1024]{1,0:T(8,128)(2,1)}, bf16[32,1024]{1,0:T(8,128)(2,1)S(1)}, u32[]{:S(2)}, u32[]{:S(2)}) collective-permute-start(bf16[32,1024]{1,0:T(8,128)(2,1)} %get-tuple-element.33), channel_id=1, source_target_pairs={{0,12},{1,13},{2,14},{3,15},{4,8},{5,9},{6,10},{7,11},{8,4},{9,5},... | collective-permute-start | bytes 196616 | tf_op jit(solution)/shard_map/ppermute | solution.py:404
  29.2 9.0 %collective-permute-start.3 = (bf16[32,1024]{1,0:T(8,128)(2,1)}, bf16[32,1024]{1,0:T(8,128)(2,1)S(1)}, u32[]{:S(2)}, u32[]{:S(2)}) collective-permute-start(bf16[32,1024]{1,0:T(8,128)(2,1)} %get-tuple-element.34), channel_id=1, source_target_pairs={{0,6},{1,7},{2,4},{3,5},{4,2},{5,3},{6,0},{7,1},{8,14},{9,15},{10,... | collective-permute-start | bytes 196616 | tf_op jit(solution)/shard_map/ppermute | solution.py:404
  32.5 5.9 %collective-permute-start.4 = (bf16[32,1024]{1,0:T(8,128)(2,1)}, bf16[32,1024]{1,0:T(8,128)(2,1)S(1)}, u32[]{:S(2)}, u32[]{:S(2)}) collective-permute-start(bf16[32,1024]{1,0:T(8,128)(2,1)} %get-tuple-element.35), channel_id=1, source_target_pairs={{0,13},{1,12},{2,15},{3,14},{4,9},{5,8},{6,11},{7,10},{8,5},{9,4},... | collective-permute-start | bytes 196616 | tf_op jit(solution)/shard_map/ppermute | solution.py:404
  34.6 3.9 %collective-permute-start.5 = (bf16[32,1024]{1,0:T(8,128)(2,1)}, bf16[32,1024]{1,0:T(8,128)(2,1)S(1)}, u32[]{:S(2)}, u32[]{:S(2)}) collective-permute-start(bf16[32,1024]{1,0:T(8,128)(2,1)} %get-tuple-element.36), channel_id=1, source_target_pairs={{0,3},{1,2},{2,1},{3,0},{4,7},{5,6},{6,5},{7,4},{8,11},{9,10},{10,... | collective-permute-start | bytes 196616 | tf_op jit(solution)/shard_map/ppermute | solution.py:404
  36.2 5.0 %collective-permute-start.6 = (bf16[32,1024]{1,0:T(8,128)(2,1)}, bf16[32,1024]{1,0:T(8,128)(2,1)S(1)}, u32[]{:S(2)}, u32[]{:S(2)}) collective-permute-start(bf16[32,1024]{1,0:T(8,128)(2,1)} %get-tuple-element.37), channel_id=1, source_target_pairs={{0,7},{1,6},{2,5},{3,4},{4,3},{5,2},{6,1},{7,0},{8,15},{9,14},{10,... | collective-permute-start | bytes 196616 | tf_op jit(solution)/shard_map/ppermute | solution.py:404
  36.2 5.0 %collective-permute-start.7 = (bf16[32,1024]{1,0:T(8,128)(2,1)}, bf16[32,1024]{1,0:T(8,128)(2,1)S(1)}, u32[]{:S(2)}, u32[]{:S(2)}) collective-permute-start(bf16[32,1024]{1,0:T(8,128)(2,1)} %get-tuple-element.38), channel_id=1, source_target_pairs={{0,1},{1,0},{2,3},{3,2},{4,5},{5,4},{6,7},{7,6},{8,9},{9,8},{10,11... | collective-permute-start | bytes 196616 | tf_op jit(solution)/shard_map/ppermute | solution.py:404
  36.3 0.8 %copy-start.2 = (bf16[32,1024]{1,0:T(8,128)(2,1)S(1)}, bf16[32,1024]{1,0:T(8,128)(2,1)}, u32[]{:S(2)}) copy-start(bf16[32,1024]{1,0:T(8,128)(2,1)} %get-tuple-element.39.refs_0_) | copy-start | bytes 196612
  41.9 8.6 %collective-permute-start.16 = (bf16[512,256]{1,0:T(8,128)(2,1)S(1)}, bf16[512,256]{1,0:T(8,128)(2,1)S(1)}, u32[]{:S(2)}, u32[]{:S(2)}) collective-permute-start(bf16[512,256]{1,0:T(8,128)(2,1)S(1)} %get-tuple-element.51.refs_0_), channel_id=1, source_target_pairs={{0,1},{1,2},{2,3},{3,4},{4,5},{5,6},{6,7},{7,8},{8,9},{9,10},{10,1... | collective-permute-start | bytes 786440 | tf_op jit(solution)/shard_map/ppermute | solution.py:27
  44.0 8.3 %collective-permute-start.15 = (bf16[512,256]{1,0:T(8,128)(2,1)S(1)}, bf16[512,256]{1,0:T(8,128)(2,1)S(1)}, u32[]{:S(2)}, u32[]{:S(2)}) collective-permute-start(bf16[512,256]{1,0:T(8,128)(2,1)S(1)} %get-tuple-element.52.refs_1_), channel_id=1, source_target_pairs={{0,1},{1,2},{2,3},{3,4},{4,5},{5,6},{6,7},{7,8},{8,9},{9,10},{10,1... | collective-permute-start | bytes 786440 | tf_op jit(solution)/shard_map/ppermute | solution.py:27

commit v17 on v16

--- a/solution.py
+++ b/solution.py
@@ -14,7 +14,7 @@
 SB = 16
 SPAN = 128
 GROUPS = ((0, 4), (4, 8))
-APART = (0, 5, 11, 8, 4, 14, 10, 15, 9, 2, 12, 6, 13, 3, 7, 1)
+APART = (0, 5, 11, 8, 4, 14, 10, 15, 9, 12, 13, 6, 7, 2, 3, 1)
 EARLY = SB // 2
 
 epsilon = 1e-06

time: 55.1 us -> 55.8 us (1.013)
  waiting for transfers between devices: 3.05 us -> 6.22 us
  starting transfers between devices: 31.1 us -> 28.3 us
    ppermute x15, waiting for transfers between devices: 3.05 us -> 6.21 us  [swap(): return lax.ppermute(tile, 'tm', route)]
    ppermute x15, starting transfers between devices: 25.7 us -> 23.3 us  [swap(): return lax.ppermute(tile, 'tm', route)]
  transfers between devices with their start and end apart: 17 -> 17, of which waited for: 3 -> 4; matrix products, arithmetic and copies ran while one was open for 0% -> 0% of each run, Pallas kernels for 11% -> 11%
where the time goes in v17:
time: 55.8 us; the launch traced here: 55.2 us
  starting transfers between devices  28.3 us (51%)
  Pallas kernels  19.6 us (35%)
  waiting for transfers between devices  6.22 us (11%)
  local copies, waits for them, and re-layouts  0.85 us (2%)
    ppermute x15, starting transfers between devices, swap(): return lax.ppermute(tile, 'tm', route)  23.3 us
    pallas_call x1, Pallas kernels, mixer(): pl.pallas_call(functools.partial(mixer_kernel, state is not None), in_spe...  10.4 us
    ppermute x15, waiting for transfers between devices, swap(): return lax.ppermute(tile, 'tm', route)  6.21 us
    ppermute x2, starting transfers between devices, shifted(): return lax.ppermute(block, axis, route)  5.04 us
    pallas_call x2, Pallas kernels, earlier_frame(): pl.pallas_call(functools.partial(earlier_kernel, group), compiler_params=...  4.19 us
    pallas_call x1, Pallas kernels, own_frame(): pl.pallas_call(own_kernel, out_shape=[jax.ShapeDtypeStruct((rows, width),...  3.17 us
  transfers between devices with their start and end apart: 17, of which 4 were waited for; matrix products, arithmetic and copies ran while one was open for 0% of the time, Pallas kernels for 11%

profile of v17, /device:TPU:1, one launch (start us, length us, event | category | flops | bytes accessed | tf_op | source)
XLA Modules:
  0.0 55.2 jit_solution(9795282588863562139)
XLA Ops:
  0.0 10.4 %mixer.1 = (bf16[32,1024]{1,0:T(8,128)(2,1)}, bf16[32,1024]{1,0:T(8,128)(2,1)}, bf16[32,1024]{1,0:T(8,128)(2,1)}, bf16[32,1024]{1,0:T(8,128)(2,1)}, bf16[32,1024...) custom-call(bf16[512,1024]{1,0:T(8,128)(2,1)} %bitcast.2, ...), custom_call_target="tpu_custom_call" | custom-call | flops 3758096384 | bytes 8388608 | tf_op jit(solution)/shard_map/mixer/pallas_call | solution.py:155
  10.5 3.2 %collective-permute-start.10 = (bf16[32,1024]{1,0:T(8,128)(2,1)}, bf16[32,1024]{1,0:T(8,128)(2,1)S(1)}, u32[]{:S(2)}, u32[]{:S(2)}) collective-permute-start(bf16[32,1024]{1,0:T(8,128)(2,1)} %get-tuple-element.42), channel_id=1, source_target_pairs={{0,8},{1,9},{2,10},{3,11},{4,12},{5,13},{6,14},{7,15},{8,0},{9,1},... | collective-permute-start | bytes 196616 | tf_op jit(solution)/shard_map/ppermute | solution.py:404
  13.7 1.3 %collective-permute-start.11 = (bf16[32,1024]{1,0:T(8,128)(2,1)}, bf16[32,1024]{1,0:T(8,128)(2,1)S(1)}, u32[]{:S(2)}, u32[]{:S(2)}) collective-permute-start(bf16[32,1024]{1,0:T(8,128)(2,1)} %get-tuple-element.43), channel_id=1, source_target_pairs={{0,4},{1,5},{2,6},{3,7},{4,0},{5,1},{6,2},{7,3},{8,12},{9,13},{10,... | collective-permute-start | bytes 196616 | tf_op jit(solution)/shard_map/ppermute | solution.py:404
  15.0 0.9 %collective-permute-start.12 = (bf16[32,1024]{1,0:T(8,128)(2,1)}, bf16[32,1024]{1,0:T(8,128)(2,1)S(1)}, u32[]{:S(2)}, u32[]{:S(2)}) collective-permute-start(bf16[32,1024]{1,0:T(8,128)(2,1)} %get-tuple-element.44), channel_id=1, source_target_pairs={{0,14},{1,15},{2,12},{3,13},{4,10},{5,11},{6,8},{7,9},{8,6},{9,7},... | collective-permute-start | bytes 196616 | tf_op jit(solution)/shard_map/ppermute | solution.py:404
  15.9 1.3 %collective-permute-start.13 = (bf16[32,1024]{1,0:T(8,128)(2,1)}, bf16[32,1024]{1,0:T(8,128)(2,1)S(1)}, u32[]{:S(2)}, u32[]{:S(2)}) collective-permute-start(bf16[32,1024]{1,0:T(8,128)(2,1)} %get-tuple-element.45), channel_id=1, source_target_pairs={{0,10},{1,11},{2,8},{3,9},{4,14},{5,15},{6,12},{7,13},{8,2},{9,3},... | collective-permute-start | bytes 196616 | tf_op jit(solution)/shard_map/ppermute | solution.py:404
  17.2 3.7 %collective-permute-start.14 = (bf16[32,1024]{1,0:T(8,128)(2,1)}, bf16[32,1024]{1,0:T(8,128)(2,1)S(1)}, u32[]{:S(2)}, u32[]{:S(2)}) collective-permute-start(bf16[32,1024]{1,0:T(8,128)(2,1)} %get-tuple-element.46), channel_id=1, source_target_pairs={{0,15},{1,14},{2,13},{3,12},{4,11},{5,10},{6,9},{7,8},{8,7},{9,6},... | collective-permute-start | bytes 196616 | tf_op jit(solution)/shard_map/ppermute | solution.py:404
  20.9 0.0 collective-permute-done.10.refs_3_
  20.9 0.2 collective-permute-start.8
  21.1 0.0 collective-permute-done.11.refs_4_
  21.1 2.5 %collective-permute-start.9 = (bf16[32,1024]{1,0:T(8,128)(2,1)}, bf16[32,1024]{1,0:T(8,128)(2,1)S(1)}, u32[]{:S(2)}, u32[]{:S(2)}) collective-permute-start(bf16[32,1024]{1,0:T(8,128)(2,1)} %get-tuple-element.41), channel_id=1, source_target_pairs={{0,11},{1,10},{2,9},{3,8},{4,15},{5,14},{6,13},{7,12},{8,3},{9,2},... | collective-permute-start | bytes 196616 | tf_op jit(solution)/shard_map/ppermute | solution.py:404
  23.6 0.0 collective-permute-done.12.refs_5_
  23.6 4.0 %collective-permute-start = (bf16[32,1024]{1,0:T(8,128)(2,1)}, bf16[32,1024]{1,0:T(8,128)(2,1)S(1)}, u32[]{:S(2)}, u32[]{:S(2)}) collective-permute-start(bf16[32,1024]{1,0:T(8,128)(2,1)} %get-tuple-element.31), channel_id=1, source_target_pairs={{0,9},{1,8},{2,11},{3,10},{4,13},{5,12},{6,15},{7,14},{8,1},{9,0},... | collective-permute-start | bytes 196616 | tf_op jit(solution)/shard_map/ppermute | solution.py:404
  27.6 0.0 collective-permute-done.13.refs_6_
  27.6 1.1 %collective-permute-start.1 = (bf16[32,1024]{1,0:T(8,128)(2,1)}, bf16[32,1024]{1,0:T(8,128)(2,1)S(1)}, u32[]{:S(2)}, u32[]{:S(2)}) collective-permute-start(bf16[32,1024]{1,0:T(8,128)(2,1)} %get-tuple-element.32), channel_id=1, source_target_pairs={{0,12},{1,13},{2,14},{3,15},{4,8},{5,9},{6,10},{7,11},{8,4},{9,5},... | collective-permute-start | bytes 196616 | tf_op jit(solution)/shard_map/ppermute | solution.py:404
  28.7 0.0 collective-permute-done.14.refs_7_
  28.7 2.3 %collective-permute-start.2 = (bf16[32,1024]{1,0:T(8,128)(2,1)}, bf16[32,1024]{1,0:T(8,128)(2,1)S(1)}, u32[]{:S(2)}, u32[]{:S(2)}) collective-permute-start(bf16[32,1024]{1,0:T(8,128)(2,1)} %get-tuple-element.33), channel_id=1, source_target_pairs={{0,13},{1,12},{2,15},{3,14},{4,9},{5,8},{6,11},{7,10},{8,5},{9,4},... | collective-permute-start | bytes 196616 | tf_op jit(solution)/shard_map/ppermute | solution.py:404
  31.0 0.9 %collective-permute-start.3 = (bf16[32,1024]{1,0:T(8,128)(2,1)}, bf16[32,1024]{1,0:T(8,128)(2,1)S(1)}, u32[]{:S(2)}, u32[]{:S(2)}) collective-permute-start(bf16[32,1024]{1,0:T(8,128)(2,1)} %get-tuple-element.34), channel_id=1, source_target_pairs={{0,6},{1,7},{2,4},{3,5},{4,2},{5,3},{6,0},{7,1},{8,14},{9,15},{10,... | collective-permute-start | bytes 196616 | tf_op jit(solution)/shard_map/ppermute | solution.py:404
  31.9 2.0 %collective-permute-done.9.refs_2_ = bf16[32,1024]{1,0:T(8,128)(2,1)S(1)} collective-permute-done((bf16[32,1024]{1,0:T(8,128)(2,1)}, bf16[32,1024]{1,0:T(8,128)(2,1)S(1)}, u32[]{:S(2)}, u32[]{:S(2)}) %collective-permute-start.9) | collective-permute-done | bytes 65568 | tf_op jit(solution)/shard_map/ppermute | solution.py:404
  33.9 0.0 collective-permute-start.4
  33.9 2.7 %collective-permute-done.refs_0_ = bf16[32,1024]{1,0:T(8,128)(2,1)S(1)} collective-permute-done((bf16[32,1024]{1,0:T(8,128)(2,1)}, bf16[32,1024]{1,0:T(8,128)(2,1)S(1)}, u32[]{:S(2)}, u32[]{:S(2)}) %collective-permute-start) | collective-permute-done | bytes 65568 | tf_op jit(solution)/shard_map/ppermute | solution.py:404
  36.6 0.4 collective-permute-start.5
  37.0 1.5 %collective-permute-start.7 = (bf16[32,1024]{1,0:T(8,128)(2,1)}, bf16[32,1024]{1,0:T(8,128)(2,1)S(1)}, u32[]{:S(2)}, u32[]{:S(2)}) collective-permute-start(bf16[32,1024]{1,0:T(8,128)(2,1)} %get-tuple-element.38), channel_id=1, source_target_pairs={{0,1},{1,0},{2,3},{3,2},{4,5},{5,4},{6,7},{7,6},{8,9},{9,8},{10,11... | collective-permute-start | bytes 196616 | tf_op jit(solution)/shard_map/ppermute | solution.py:404
  38.5 0.8 %copy-done.2 = bf16[32,1024]{1,0:T(8,128)(2,1)S(1)} copy-done((bf16[32,1024]{1,0:T(8,128)(2,1)S(1)}, bf16[32,1024]{1,0:T(8,128)(2,1)}, u32[]{:S(2)}) %copy-start.2) | copy-done | bytes 65560
  39.3 1.1 %early_rows.1 = (bf16[256,1024]{1,0:T(8,128)(2,1)S(1)}, bf16[256,256]{1,0:T(8,128)(2,1)S(1)}, bf16[256,256]{1,0:T(8,128)(2,1)S(1)}) custom-call(bf16[1024]{0:T(1024)(128)(2,1)S(1)} %copy-done.3, bf16[1024,512]{1,0:T(8,128)(2,1)S(1)} %copy-done, bf16[1024,1024]{1,0:T(8,128)(2,1)S(1)} %copy-done.1, bf16[32,1024]{1,0:T(8,128)(2,1)S(1)} %copy-done.2, ...), custom_call_target="tpu_custom_call" | custom-call | flops 805306368 | bytes 4194304 | tf_op jit(solution)/shard_map/early_rows/pallas_call | solution.py:230
  40.5 0.2 collective-permute-done.5.refs_5_
  40.6 1.3 %collective-permute-done.6.refs_6_ = bf16[32,1024]{1,0:T(8,128)(2,1)S(1)} collective-permute-done((bf16[32,1024]{1,0:T(8,128)(2,1)}, bf16[32,1024]{1,0:T(8,128)(2,1)S(1)}, u32[]{:S(2)}, u32[]{:S(2)}) %collective-permute-start.6) | collective-permute-done | bytes 65568 | tf_op jit(solution)/shard_map/ppermute | solution.py:404
  41.9 0.7 %pairs.1 = (bf16[256,1024]{1,0:T(8,128)(2,1)S(1)}, bf16[512,256]{1,0:T(8,128)(2,1)S(1)}, bf16[512,256]{1,0:T(8,128)(2,1)S(1)}) custom-call(bf16[1024]{0:T(1024)(128)(2,1)S(1)} %copy-done.3, bf16[1024,512]{1,0:T(8,128)(2,1)S(1)} %copy-done, bf16[32,1024]{1,0:T(8,128)(2,1)S(1)} %collective-permute-done.refs_0_, ...), custom_call_target="tpu_custom_call" | custom-call | flops 268435456 | bytes 2359296 | tf_op jit(solution)/shard_map/pairs/pallas_call | solution.py:248
  42.6 2.8 %collective-permute-start.16 = (bf16[512,256]{1,0:T(8,128)(2,1)S(1)}, bf16[512,256]{1,0:T(8,128)(2,1)S(1)}, u32[]{:S(2)}, u32[]{:S(2)}) collective-permute-start(bf16[512,256]{1,0:T(8,128)(2,1)S(1)} %get-tuple-element.51.refs_0_), channel_id=1, source_target_pairs={{0,1},{1,2},{2,3},{3,4},{4,5},{5,6},{6,7},{7,8},{8,9},{9,10},{10,1... | collective-permute-start | bytes 786440 | tf_op jit(solution)/shard_map/ppermute | solution.py:27
  45.4 2.2 %collective-permute-start.15 = (bf16[512,256]{1,0:T(8,128)(2,1)S(1)}, bf16[512,256]{1,0:T(8,128)(2,1)S(1)}, u32[]{:S(2)}, u32[]{:S(2)}) collective-permute-start(bf16[512,256]{1,0:T(8,128)(2,1)S(1)} %get-tuple-element.52.refs_1_), channel_id=1, source_target_pairs={{0,1},{1,2},{2,3},{3,4},{4,5},{5,6},{6,7},{7,8},{8,9},{9,10},{10,1... | collective-permute-start | bytes 786440 | tf_op jit(solution)/shard_map/ppermute | solution.py:27
  47.7 3.2 %own_frame.1 = (bf16[512,1024]{1,0:T(8,128)(2,1)S(1)}, f32[512,1024]{1,0:T(8,128)S(1)}, f32[512,1024]{1,0:T(8,128)S(1)}, f32[512,1024]{1,0:T(8,128)S(1)}) custom-call(bf16[256,1024]{1,0:T(8,128)(2,1)S(1)} %get-tuple-element.49.normed_ref, bf16[1024,1024]{1,0:T(8,128)(2,1)S(1)} %copy-done.1, bf16[256,1024]{1,0:T(8,128)(2,1)S(1)} %get-tuple-element.50.early_ref, ...), custom_call_target="tpu_custom_call" | custom-call | flops 2147483648 | bytes 6291456 | tf_op jit(solution)/shard_map/own_frame/pallas_call | solution.py:309
  50.8 1.7 %earlier_frame.2.refs_0_ = bf16[512,512]{1,0:T(8,128)(2,1)S(1)} custom-call(bf16[512,1024]{1,0:T(8,128)(2,1)S(1)} %get-tuple-element.53.query_ref, bf16[512,256]{1,0:T(8,128)(2,1)S(1)} %collective-permute-done.16.pairs_ref, f32[512,1024]{1,0:T(8,128)S(1)} %get-tuple-element.54.sum_ref, f32[512,1024]{1,0:T(8,128)S(1)} %get-tuple-element.55.total_ref, ...), custom_call_target="tpu_custom_call" | custom-call | flops 536870912 | bytes 5242880 | tf_op jit(solution)/shard_map/earlier_frame/pallas_call | solution.py:388
  52.6 2.5 %earlier_frame.3 = bf16[512,1024]{1,0:T(8,128)(2,1)} custom-call(bf16[512,1024]{1,0:T(8,128)(2,1)S(1)} %get-tuple-element.53.query_ref, bf16[512,256]{1,0:T(8,128)(2,1)S(1)} %collective-permute-done.15.pairs_ref, f32[512,1024]{1,0:T(8,128)S(1)} %get-tuple-element.54.sum_ref, f32[512,1024]{1,0:T(8,128)S(1)} %get-tuple-element.55.total_ref, ...), custom_call_target="tpu_custom_call" | custom-call | flops 536870912 | bytes 5242880 | tf_op jit(solution)/shard_map/earlier_frame/pallas_call | solution.py:388
  (16 shorter events, 0.0 us)
Async XLA Ops:
  0.0 38.5 %copy-start = (bf16[1024,512]{1,0:T(8,128)(2,1)S(1)}, bf16[1024,512]{1,0:T(8,128)(2,1)}, u32[]{:S(2)}) copy-start(bf16[1024,512]{1,0:T(8,128)(2,1)} %w_kv_ref.3) | copy-start | bytes 3145732
  0.0 38.5 %copy-start.1 = (bf16[1024,1024]{1,0:T(8,128)(2,1)S(1)}, bf16[1024,1024]{1,0:T(8,128)(2,1)}, u32[]{:S(2)}) copy-start(bf16[1024,1024]{1,0:T(8,128)(2,1)} %w_ref.1) | copy-start | bytes 6291460
  0.0 38.5 %copy-start.3 = (bf16[1024]{0:T(1024)(128)(2,1)S(1)}, bf16[1024]{0:T(1024)(128)(2,1)}, u32[]{:S(2)}) copy-start(bf16[1024]{0:T(1024)(128)(2,1)} %gain_ref.3) | copy-start | bytes 6148
  10.5 10.5 %collective-permute-start.10 = (bf16[32,1024]{1,0:T(8,128)(2,1)}, bf16[32,1024]{1,0:T(8,128)(2,1)S(1)}, u32[]{:S(2)}, u32[]{:S(2)}) collective-permute-start(bf16[32,1024]{1,0:T(8,128)(2,1)} %get-tuple-element.42), channel_id=1, source_target_pairs={{0,8},{1,9},{2,10},{3,11},{4,12},{5,13},{6,14},{7,15},{8,0},{9,1},... | collective-permute-start | bytes 196616 | tf_op jit(solution)/shard_map/ppermute | solution.py:404
  13.7 7.5 %collective-permute-start.11 = (bf16[32,1024]{1,0:T(8,128)(2,1)}, bf16[32,1024]{1,0:T(8,128)(2,1)S(1)}, u32[]{:S(2)}, u32[]{:S(2)}) collective-permute-start(bf16[32,1024]{1,0:T(8,128)(2,1)} %get-tuple-element.43), channel_id=1, source_target_pairs={{0,4},{1,5},{2,6},{3,7},{4,0},{5,1},{6,2},{7,3},{8,12},{9,13},{10,... | collective-permute-start | bytes 196616 | tf_op jit(solution)/shard_map/ppermute | solution.py:404
  15.0 8.7 %collective-permute-start.12 = (bf16[32,1024]{1,0:T(8,128)(2,1)}, bf16[32,1024]{1,0:T(8,128)(2,1)S(1)}, u32[]{:S(2)}, u32[]{:S(2)}) collective-permute-start(bf16[32,1024]{1,0:T(8,128)(2,1)} %get-tuple-element.44), channel_id=1, source_target_pairs={{0,14},{1,15},{2,12},{3,13},{4,10},{5,11},{6,8},{7,9},{8,6},{9,7},... | collective-permute-start | bytes 196616 | tf_op jit(solution)/shard_map/ppermute | solution.py:404
  15.9 11.7 %collective-permute-start.13 = (bf16[32,1024]{1,0:T(8,128)(2,1)}, bf16[32,1024]{1,0:T(8,128)(2,1)S(1)}, u32[]{:S(2)}, u32[]{:S(2)}) collective-permute-start(bf16[32,1024]{1,0:T(8,128)(2,1)} %get-tuple-element.45), channel_id=1, source_target_pairs={{0,10},{1,11},{2,8},{3,9},{4,14},{5,15},{6,12},{7,13},{8,2},{9,3},... | collective-permute-start | bytes 196616 | tf_op jit(solution)/shard_map/ppermute | solution.py:404
  17.2 11.5 %collective-permute-start.14 = (bf16[32,1024]{1,0:T(8,128)(2,1)}, bf16[32,1024]{1,0:T(8,128)(2,1)S(1)}, u32[]{:S(2)}, u32[]{:S(2)}) collective-permute-start(bf16[32,1024]{1,0:T(8,128)(2,1)} %get-tuple-element.46), channel_id=1, source_target_pairs={{0,15},{1,14},{2,13},{3,12},{4,11},{5,10},{6,9},{7,8},{8,7},{9,6},... | collective-permute-start | bytes 196616 | tf_op jit(solution)/shard_map/ppermute | solution.py:404
  20.9 10.1 %collective-permute-start.8 = (bf16[32,1024]{1,0:T(8,128)(2,1)}, bf16[32,1024]{1,0:T(8,128)(2,1)S(1)}, u32[]{:S(2)}, u32[]{:S(2)}) collective-permute-start(bf16[32,1024]{1,0:T(8,128)(2,1)} %get-tuple-element.40), channel_id=1, source_target_pairs={{0,5},{1,4},{2,7},{3,6},{4,1},{5,0},{6,3},{7,2},{8,13},{9,12},{10,... | collective-permute-start | bytes 196616 | tf_op jit(solution)/shard_map/ppermute | solution.py:404
  21.1 12.8 %collective-permute-start.9 = (bf16[32,1024]{1,0:T(8,128)(2,1)}, bf16[32,1024]{1,0:T(8,128)(2,1)S(1)}, u32[]{:S(2)}, u32[]{:S(2)}) collective-permute-start(bf16[32,1024]{1,0:T(8,128)(2,1)} %get-tuple-element.41), channel_id=1, source_target_pairs={{0,11},{1,10},{2,9},{3,8},{4,15},{5,14},{6,13},{7,12},{8,3},{9,2},... | collective-permute-start | bytes 196616 | tf_op jit(solution)/shard_map/ppermute | solution.py:404
  23.6 13.0 %collective-permute-start = (bf16[32,1024]{1,0:T(8,128)(2,1)}, bf16[32,1024]{1,0:T(8,128)(2,1)S(1)}, u32[]{:S(2)}, u32[]{:S(2)}) collective-permute-start(bf16[32,1024]{1,0:T(8,128)(2,1)} %get-tuple-element.31), channel_id=1, source_target_pairs={{0,9},{1,8},{2,11},{3,10},{4,13},{5,12},{6,15},{7,14},{8,1},{9,0},... | collective-permute-start | bytes 196616 | tf_op jit(solution)/shard_map/ppermute | solution.py:404
  27.6 9.4 %collective-permute-start.1 = (bf16[32,1024]{1,0:T(8,128)(2,1)}, bf16[32,1024]{1,0:T(8,128)(2,1)S(1)}, u32[]{:S(2)}, u32[]{:S(2)}) collective-permute-start(bf16[32,1024]{1,0:T(8,128)(2,1)} %get-tuple-element.32), channel_id=1, source_target_pairs={{0,12},{1,13},{2,14},{3,15},{4,8},{5,9},{6,10},{7,11},{8,4},{9,5},... | collective-permute-start | bytes 196616 | tf_op jit(solution)/shard_map/ppermute | solution.py:404
  28.7 8.3 %collective-permute-start.2 = (bf16[32,1024]{1,0:T(8,128)(2,1)}, bf16[32,1024]{1,0:T(8,128)(2,1)S(1)}, u32[]{:S(2)}, u32[]{:S(2)}) collective-permute-start(bf16[32,1024]{1,0:T(8,128)(2,1)} %get-tuple-element.33), channel_id=1, source_target_pairs={{0,13},{1,12},{2,15},{3,14},{4,9},{5,8},{6,11},{7,10},{8,5},{9,4},... | collective-permute-start | bytes 196616 | tf_op jit(solution)/shard_map/ppermute | solution.py:404
  31.0 9.4 %collective-permute-start.3 = (bf16[32,1024]{1,0:T(8,128)(2,1)}, bf16[32,1024]{1,0:T(8,128)(2,1)S(1)}, u32[]{:S(2)}, u32[]{:S(2)}) collective-permute-start(bf16[32,1024]{1,0:T(8,128)(2,1)} %get-tuple-element.34), channel_id=1, source_target_pairs={{0,6},{1,7},{2,4},{3,5},{4,2},{5,3},{6,0},{7,1},{8,14},{9,15},{10,... | collective-permute-start | bytes 196616 | tf_op jit(solution)/shard_map/ppermute | solution.py:404
  33.9 6.6 %collective-permute-start.4 = (bf16[32,1024]{1,0:T(8,128)(2,1)}, bf16[32,1024]{1,0:T(8,128)(2,1)S(1)}, u32[]{:S(2)}, u32[]{:S(2)}) collective-permute-start(bf16[32,1024]{1,0:T(8,128)(2,1)} %get-tuple-element.35), channel_id=1, source_target_pairs={{0,7},{1,6},{2,5},{3,4},{4,3},{5,2},{6,1},{7,0},{8,15},{9,14},{10,... | collective-permute-start | bytes 196616 | tf_op jit(solution)/shard_map/ppermute | solution.py:404
  36.6 4.0 %collective-permute-start.5 = (bf16[32,1024]{1,0:T(8,128)(2,1)}, bf16[32,1024]{1,0:T(8,128)(2,1)S(1)}, u32[]{:S(2)}, u32[]{:S(2)}) collective-permute-start(bf16[32,1024]{1,0:T(8,128)(2,1)} %get-tuple-element.36), channel_id=1, source_target_pairs={{0,2},{1,3},{2,0},{3,1},{4,6},{5,7},{6,4},{7,5},{8,10},{9,11},{10,... | collective-permute-start | bytes 196616 | tf_op jit(solution)/shard_map/ppermute | solution.py:404
  37.0 4.9 %collective-permute-start.6 = (bf16[32,1024]{1,0:T(8,128)(2,1)}, bf16[32,1024]{1,0:T(8,128)(2,1)S(1)}, u32[]{:S(2)}, u32[]{:S(2)}) collective-permute-start(bf16[32,1024]{1,0:T(8,128)(2,1)} %get-tuple-element.37), channel_id=1, source_target_pairs={{0,3},{1,2},{2,1},{3,0},{4,7},{5,6},{6,5},{7,4},{8,11},{9,10},{10,... | collective-permute-start | bytes 196616 | tf_op jit(solution)/shard_map/ppermute | solution.py:404
  37.0 4.9 %collective-permute-start.7 = (bf16[32,1024]{1,0:T(8,128)(2,1)}, bf16[32,1024]{1,0:T(8,128)(2,1)S(1)}, u32[]{:S(2)}, u32[]{:S(2)}) collective-permute-start(bf16[32,1024]{1,0:T(8,128)(2,1)} %get-tuple-element.38), channel_id=1, source_target_pairs={{0,1},{1,0},{2,3},{3,2},{4,5},{5,4},{6,7},{7,6},{8,9},{9,8},{10,11... | collective-permute-start | bytes 196616 | tf_op jit(solution)/shard_map/ppermute | solution.py:404
  38.5 0.8 %copy-start.2 = (bf16[32,1024]{1,0:T(8,128)(2,1)S(1)}, bf16[32,1024]{1,0:T(8,128)(2,1)}, u32[]{:S(2)}) copy-start(bf16[32,1024]{1,0:T(8,128)(2,1)} %get-tuple-element.39.refs_0_) | copy-start | bytes 196612
  42.6 8.2 %collective-permute-start.16 = (bf16[512,256]{1,0:T(8,128)(2,1)S(1)}, bf16[512,256]{1,0:T(8,128)(2,1)S(1)}, u32[]{:S(2)}, u32[]{:S(2)}) collective-permute-start(bf16[512,256]{1,0:T(8,128)(2,1)S(1)} %get-tuple-element.51.refs_0_), channel_id=1, source_target_pairs={{0,1},{1,2},{2,3},{3,4},{4,5},{5,6},{6,7},{7,8},{8,9},{9,10},{10,1... | collective-permute-start | bytes 786440 | tf_op jit(solution)/shard_map/ppermute | solution.py:27
  45.4 7.1 %collective-permute-start.15 = (bf16[512,256]{1,0:T(8,128)(2,1)S(1)}, bf16[512,256]{1,0:T(8,128)(2,1)S(1)}, u32[]{:S(2)}, u32[]{:S(2)}) collective-permute-start(bf16[512,256]{1,0:T(8,128)(2,1)S(1)} %get-tuple-element.52.refs_1_), channel_id=1, source_target_pairs={{0,1},{1,2},{2,3},{3,4},{4,5},{5,6},{6,7},{7,8},{8,9},{9,10},{10,1... | collective-permute-start | bytes 786440 | tf_op jit(solution)/shard_map/ppermute | solution.py:27

commit v18 on v17

--- a/solution.py
+++ b/solution.py
@@ -14,8 +14,8 @@
 SB = 16
 SPAN = 128
 GROUPS = ((0, 4), (4, 8))
-APART = (0, 5, 11, 8, 4, 14, 10, 15, 9, 12, 13, 6, 7, 2, 3, 1)
-EARLY = SB // 2
+APART = (0, 5, 11, 9, 2, 12, 6, 8, 4, 14, 10, 15, 13, 3, 7, 1)
+EARLY = SB - 4
 
 epsilon = 1e-06
 MIB = 1 << 20

time: 55.8 us -> 54.7 us (0.980)
  waiting for transfers between devices: 6.22 us -> 2.59 us
  starting transfers between devices: 28.3 us -> 31.1 us
    ppermute x15, waiting for transfers between devices: 6.21 us -> 2.58 us  [swap(): return lax.ppermute(tile, 'tm', route)]
    ppermute x15, starting transfers between devices: 23.3 us -> 25.7 us  [swap(): return lax.ppermute(tile, 'tm', route)]
  transfers between devices with their start and end apart: 17 -> 17, of which waited for: 4 -> 1; matrix products, arithmetic and copies ran while one was open for 0% -> 0% of each run, Pallas kernels for 11% -> 12%
where the time goes in v18:
time: 54.7 us; the launch traced here: 54.5 us
  starting transfers between devices  31.1 us (57%)
  Pallas kernels  19.7 us (36%)
  waiting for transfers between devices  2.59 us (5%)
  local copies, waits for them, and re-layouts  0.85 us (2%)
    ppermute x15, starting transfers between devices, swap(): return lax.ppermute(tile, 'tm', route)  25.7 us
    pallas_call x1, Pallas kernels, mixer(): pl.pallas_call(functools.partial(mixer_kernel, state is not None), in_spe...  10.4 us
    ppermute x2, starting transfers between devices, shifted(): return lax.ppermute(block, axis, route)  5.42 us
    pallas_call x2, Pallas kernels, earlier_frame(): pl.pallas_call(functools.partial(earlier_kernel, group), compiler_params=...  4.19 us
    pallas_call x1, Pallas kernels, own_frame(): pl.pallas_call(own_kernel, out_shape=[jax.ShapeDtypeStruct((rows, width),...  3.06 us
    ppermute x15, waiting for transfers between devices, swap(): return lax.ppermute(tile, 'tm', route)  2.58 us
    pallas_call x1, Pallas kernels, make_early(): pl.pallas_call(early_kernel, out_shape=[jax.ShapeDtypeStruct((rows, w_que...  1.53 us
  transfers between devices with their start and end apart: 17, of which 1 were waited for; matrix products, arithmetic and copies ran while one was open for 0% of the time, Pallas kernels for 12%

profile of v18, /device:TPU:1, one launch (start us, length us, event | category | flops | bytes accessed | tf_op | source)
XLA Modules:
  0.0 54.5 jit_solution(4178534886631453153)
XLA Ops:
  0.0 10.4 %mixer.1 = (bf16[32,1024]{1,0:T(8,128)(2,1)}, bf16[32,1024]{1,0:T(8,128)(2,1)}, bf16[32,1024]{1,0:T(8,128)(2,1)}, bf16[32,1024]{1,0:T(8,128)(2,1)}, bf16[32,1024...) custom-call(bf16[512,1024]{1,0:T(8,128)(2,1)} %bitcast.2, ...), custom_call_target="tpu_custom_call" | custom-call | flops 3758096384 | bytes 8388608 | tf_op jit(solution)/shard_map/mixer/pallas_call | solution.py:155
  10.5 3.2 %collective-permute-start.10 = (bf16[32,1024]{1,0:T(8,128)(2,1)}, bf16[32,1024]{1,0:T(8,128)(2,1)S(1)}, u32[]{:S(2)}, u32[]{:S(2)}) collective-permute-start(bf16[32,1024]{1,0:T(8,128)(2,1)} %get-tuple-element.42), channel_id=1, source_target_pairs={{0,8},{1,9},{2,10},{3,11},{4,12},{5,13},{6,14},{7,15},{8,0},{9,1},... | collective-permute-start | bytes 196616 | tf_op jit(solution)/shard_map/ppermute | solution.py:404
  13.7 1.3 %collective-permute-start.11 = (bf16[32,1024]{1,0:T(8,128)(2,1)}, bf16[32,1024]{1,0:T(8,128)(2,1)S(1)}, u32[]{:S(2)}, u32[]{:S(2)}) collective-permute-start(bf16[32,1024]{1,0:T(8,128)(2,1)} %get-tuple-element.43), channel_id=1, source_target_pairs={{0,4},{1,5},{2,6},{3,7},{4,0},{5,1},{6,2},{7,3},{8,12},{9,13},{10,... | collective-permute-start | bytes 196616 | tf_op jit(solution)/shard_map/ppermute | solution.py:404
  15.0 0.9 %collective-permute-start.12 = (bf16[32,1024]{1,0:T(8,128)(2,1)}, bf16[32,1024]{1,0:T(8,128)(2,1)S(1)}, u32[]{:S(2)}, u32[]{:S(2)}) collective-permute-start(bf16[32,1024]{1,0:T(8,128)(2,1)} %get-tuple-element.44), channel_id=1, source_target_pairs={{0,14},{1,15},{2,12},{3,13},{4,10},{5,11},{6,8},{7,9},{8,6},{9,7},... | collective-permute-start | bytes 196616 | tf_op jit(solution)/shard_map/ppermute | solution.py:404
  15.9 1.3 %collective-permute-start.13 = (bf16[32,1024]{1,0:T(8,128)(2,1)}, bf16[32,1024]{1,0:T(8,128)(2,1)S(1)}, u32[]{:S(2)}, u32[]{:S(2)}) collective-permute-start(bf16[32,1024]{1,0:T(8,128)(2,1)} %get-tuple-element.45), channel_id=1, source_target_pairs={{0,10},{1,11},{2,8},{3,9},{4,14},{5,15},{6,12},{7,13},{8,2},{9,3},... | collective-permute-start | bytes 196616 | tf_op jit(solution)/shard_map/ppermute | solution.py:404
  17.2 3.7 %collective-permute-start.14 = (bf16[32,1024]{1,0:T(8,128)(2,1)}, bf16[32,1024]{1,0:T(8,128)(2,1)S(1)}, u32[]{:S(2)}, u32[]{:S(2)}) collective-permute-start(bf16[32,1024]{1,0:T(8,128)(2,1)} %get-tuple-element.46), channel_id=1, source_target_pairs={{0,15},{1,14},{2,13},{3,12},{4,11},{5,10},{6,9},{7,8},{8,7},{9,6},... | collective-permute-start | bytes 196616 | tf_op jit(solution)/shard_map/ppermute | solution.py:404
  20.9 0.0 collective-permute-done.10.refs_7_
  20.9 0.2 collective-permute-start.4
  21.1 0.0 collective-permute-done.11.refs_8_
  21.1 2.5 %collective-permute-start.5 = (bf16[32,1024]{1,0:T(8,128)(2,1)}, bf16[32,1024]{1,0:T(8,128)(2,1)S(1)}, u32[]{:S(2)}, u32[]{:S(2)}) collective-permute-start(bf16[32,1024]{1,0:T(8,128)(2,1)} %get-tuple-element.37), channel_id=1, source_target_pairs={{0,11},{1,10},{2,9},{3,8},{4,15},{5,14},{6,13},{7,12},{8,3},{9,2},... | collective-permute-start | bytes 196616 | tf_op jit(solution)/shard_map/ppermute | solution.py:404
  23.6 4.0 %collective-permute-start.6 = (bf16[32,1024]{1,0:T(8,128)(2,1)}, bf16[32,1024]{1,0:T(8,128)(2,1)S(1)}, u32[]{:S(2)}, u32[]{:S(2)}) collective-permute-start(bf16[32,1024]{1,0:T(8,128)(2,1)} %get-tuple-element.38), channel_id=1, source_target_pairs={{0,9},{1,8},{2,11},{3,10},{4,13},{5,12},{6,15},{7,14},{8,1},{9,0},... | collective-permute-start | bytes 196616 | tf_op jit(solution)/shard_map/ppermute | solution.py:404
  27.6 0.2 collective-permute-start.7
  27.8 0.0 collective-permute-done.14.refs_11_
  27.8 1.4 %collective-permute-start.8 = (bf16[32,1024]{1,0:T(8,128)(2,1)}, bf16[32,1024]{1,0:T(8,128)(2,1)S(1)}, u32[]{:S(2)}, u32[]{:S(2)}) collective-permute-start(bf16[32,1024]{1,0:T(8,128)(2,1)} %get-tuple-element.40), channel_id=1, source_target_pairs={{0,12},{1,13},{2,14},{3,15},{4,8},{5,9},{6,10},{7,11},{8,4},{9,5},... | collective-permute-start | bytes 196616 | tf_op jit(solution)/shard_map/ppermute | solution.py:404
  29.2 3.2 %collective-permute-start.9 = (bf16[32,1024]{1,0:T(8,128)(2,1)}, bf16[32,1024]{1,0:T(8,128)(2,1)S(1)}, u32[]{:S(2)}, u32[]{:S(2)}) collective-permute-start(bf16[32,1024]{1,0:T(8,128)(2,1)} %get-tuple-element.41), channel_id=1, source_target_pairs={{0,6},{1,7},{2,4},{3,5},{4,2},{5,3},{6,0},{7,1},{8,14},{9,15},{10,... | collective-permute-start | bytes 196616 | tf_op jit(solution)/shard_map/ppermute | solution.py:404
  32.4 0.0 collective-permute-done.5.refs_2_
  32.5 2.1 %collective-permute-start = (bf16[32,1024]{1,0:T(8,128)(2,1)}, bf16[32,1024]{1,0:T(8,128)(2,1)S(1)}, u32[]{:S(2)}, u32[]{:S(2)}) collective-permute-start(bf16[32,1024]{1,0:T(8,128)(2,1)} %get-tuple-element.31), channel_id=1, source_target_pairs={{0,13},{1,12},{2,15},{3,14},{4,9},{5,8},{6,11},{7,10},{8,5},{9,4},... | collective-permute-start | bytes 196616 | tf_op jit(solution)/shard_map/ppermute | solution.py:404
  34.6 0.0 collective-permute-done.6.refs_3_
  34.6 1.5 %collective-permute-start.1 = (bf16[32,1024]{1,0:T(8,128)(2,1)}, bf16[32,1024]{1,0:T(8,128)(2,1)S(1)}, u32[]{:S(2)}, u32[]{:S(2)}) collective-permute-start(bf16[32,1024]{1,0:T(8,128)(2,1)} %get-tuple-element.32), channel_id=1, source_target_pairs={{0,3},{1,2},{2,1},{3,0},{4,7},{5,6},{6,5},{7,4},{8,11},{9,10},{10,... | collective-permute-start | bytes 196616 | tf_op jit(solution)/shard_map/ppermute | solution.py:404
  36.1 0.0 collective-permute-done.7.refs_4_
  36.2 0.1 collective-permute-start.3
  36.2 0.0 collective-permute-done.9.refs_6_
  36.3 0.0 copy-start.3
  36.3 0.8 %copy-done.3 = bf16[32,1024]{1,0:T(8,128)(2,1)S(1)} copy-done((bf16[32,1024]{1,0:T(8,128)(2,1)S(1)}, bf16[32,1024]{1,0:T(8,128)(2,1)}, u32[]{:S(2)}) %copy-start.3) | copy-done | bytes 65560
  37.1 1.5 %early_rows.1 = (bf16[384,1024]{1,0:T(8,128)(2,1)S(1)}, bf16[384,256]{1,0:T(8,128)(2,1)S(1)}, bf16[384,256]{1,0:T(8,128)(2,1)S(1)}) custom-call(bf16[1024]{0:T(1024)(128)(2,1)S(1)} %copy-done.1, bf16[1024,512]{1,0:T(8,128)(2,1)S(1)} %copy-done, bf16[1024,1024]{1,0:T(8,128)(2,1)S(1)} %copy-done.2, bf16[32,1024]{1,0:T(8,128)(2,1)S(1)} %copy-done.3, ...), custom_call_target="tpu_custom_call" | custom-call | flops 1207959552 | bytes 4718592 | tf_op jit(solution)/shard_map/early_rows/pallas_call | solution.py:230
  38.7 2.5 %collective-permute-done.2.refs_2_ = bf16[32,1024]{1,0:T(8,128)(2,1)S(1)} collective-permute-done((bf16[32,1024]{1,0:T(8,128)(2,1)}, bf16[32,1024]{1,0:T(8,128)(2,1)S(1)}, u32[]{:S(2)}, u32[]{:S(2)}) %collective-permute-start.2) | collective-permute-done | bytes 65568 | tf_op jit(solution)/shard_map/ppermute | solution.py:404
  41.2 0.5 pairs.1
  41.7 2.1 %collective-permute-start.16 = (bf16[512,256]{1,0:T(8,128)(2,1)S(1)}, bf16[512,256]{1,0:T(8,128)(2,1)S(1)}, u32[]{:S(2)}, u32[]{:S(2)}) collective-permute-start(bf16[512,256]{1,0:T(8,128)(2,1)S(1)} %get-tuple-element.51.refs_0_), channel_id=1, source_target_pairs={{0,1},{1,2},{2,3},{3,4},{4,5},{5,6},{6,7},{7,8},{8,9},{9,10},{10,1... | collective-permute-start | bytes 786440 | tf_op jit(solution)/shard_map/ppermute | solution.py:27
  43.7 3.3 %collective-permute-start.15 = (bf16[512,256]{1,0:T(8,128)(2,1)S(1)}, bf16[512,256]{1,0:T(8,128)(2,1)S(1)}, u32[]{:S(2)}, u32[]{:S(2)}) collective-permute-start(bf16[512,256]{1,0:T(8,128)(2,1)S(1)} %get-tuple-element.52.refs_1_), channel_id=1, source_target_pairs={{0,1},{1,2},{2,3},{3,4},{4,5},{5,6},{6,7},{7,8},{8,9},{9,10},{10,1... | collective-permute-start | bytes 786440 | tf_op jit(solution)/shard_map/ppermute | solution.py:27
  47.1 3.1 %own_frame.1 = (bf16[512,1024]{1,0:T(8,128)(2,1)S(1)}, f32[512,1024]{1,0:T(8,128)S(1)}, f32[512,1024]{1,0:T(8,128)S(1)}, f32[512,1024]{1,0:T(8,128)S(1)}) custom-call(bf16[128,1024]{1,0:T(8,128)(2,1)S(1)} %get-tuple-element.49.normed_ref, bf16[1024,1024]{1,0:T(8,128)(2,1)S(1)} %copy-done.2, bf16[384,1024]{1,0:T(8,128)(2,1)S(1)} %get-tuple-element.50.early_ref, ...), custom_call_target="tpu_custom_call" | custom-call | flops 2147483648 | bytes 6291456 | tf_op jit(solution)/shard_map/own_frame/pallas_call | solution.py:309
  50.2 1.7 %earlier_frame.2.refs_0_ = bf16[512,512]{1,0:T(8,128)(2,1)S(1)} custom-call(bf16[512,1024]{1,0:T(8,128)(2,1)S(1)} %get-tuple-element.53.query_ref, bf16[512,256]{1,0:T(8,128)(2,1)S(1)} %collective-permute-done.16.pairs_ref, f32[512,1024]{1,0:T(8,128)S(1)} %get-tuple-element.54.sum_ref, f32[512,1024]{1,0:T(8,128)S(1)} %get-tuple-element.55.total_ref, ...), custom_call_target="tpu_custom_call" | custom-call | flops 536870912 | bytes 5242880 | tf_op jit(solution)/shard_map/earlier_frame/pallas_call | solution.py:388
  51.9 2.5 %earlier_frame.3 = bf16[512,1024]{1,0:T(8,128)(2,1)} custom-call(bf16[512,1024]{1,0:T(8,128)(2,1)S(1)} %get-tuple-element.53.query_ref, bf16[512,256]{1,0:T(8,128)(2,1)S(1)} %collective-permute-done.15.pairs_ref, f32[512,1024]{1,0:T(8,128)S(1)} %get-tuple-element.54.sum_ref, f32[512,1024]{1,0:T(8,128)S(1)} %get-tuple-element.55.total_ref, ...), custom_call_target="tpu_custom_call" | custom-call | flops 536870912 | bytes 5242880 | tf_op jit(solution)/shard_map/earlier_frame/pallas_call | solution.py:388
  (16 shorter events, 0.0 us)
Async XLA Ops:
  0.0 36.3 %copy-start = (bf16[1024,512]{1,0:T(8,128)(2,1)S(1)}, bf16[1024,512]{1,0:T(8,128)(2,1)}, u32[]{:S(2)}) copy-start(bf16[1024,512]{1,0:T(8,128)(2,1)} %w_kv_ref.3) | copy-start | bytes 3145732
  0.0 36.3 %copy-start.1 = (bf16[1024]{0:T(1024)(128)(2,1)S(1)}, bf16[1024]{0:T(1024)(128)(2,1)}, u32[]{:S(2)}) copy-start(bf16[1024]{0:T(1024)(128)(2,1)} %gain_ref.3) | copy-start | bytes 6148
  0.0 36.3 %copy-start.2 = (bf16[1024,1024]{1,0:T(8,128)(2,1)S(1)}, bf16[1024,1024]{1,0:T(8,128)(2,1)}, u32[]{:S(2)}) copy-start(bf16[1024,1024]{1,0:T(8,128)(2,1)} %w_ref.1) | copy-start | bytes 6291460
  10.5 10.5 %collective-permute-start.10 = (bf16[32,1024]{1,0:T(8,128)(2,1)}, bf16[32,1024]{1,0:T(8,128)(2,1)S(1)}, u32[]{:S(2)}, u32[]{:S(2)}) collective-permute-start(bf16[32,1024]{1,0:T(8,128)(2,1)} %get-tuple-element.42), channel_id=1, source_target_pairs={{0,8},{1,9},{2,10},{3,11},{4,12},{5,13},{6,14},{7,15},{8,0},{9,1},... | collective-permute-start | bytes 196616 | tf_op jit(solution)/shard_map/ppermute | solution.py:404
  13.7 7.5 %collective-permute-start.11 = (bf16[32,1024]{1,0:T(8,128)(2,1)}, bf16[32,1024]{1,0:T(8,128)(2,1)S(1)}, u32[]{:S(2)}, u32[]{:S(2)}) collective-permute-start(bf16[32,1024]{1,0:T(8,128)(2,1)} %get-tuple-element.43), channel_id=1, source_target_pairs={{0,4},{1,5},{2,6},{3,7},{4,0},{5,1},{6,2},{7,3},{8,12},{9,13},{10,... | collective-permute-start | bytes 196616 | tf_op jit(solution)/shard_map/ppermute | solution.py:404
  15.0 8.7 %collective-permute-start.12 = (bf16[32,1024]{1,0:T(8,128)(2,1)}, bf16[32,1024]{1,0:T(8,128)(2,1)S(1)}, u32[]{:S(2)}, u32[]{:S(2)}) collective-permute-start(bf16[32,1024]{1,0:T(8,128)(2,1)} %get-tuple-element.44), channel_id=1, source_target_pairs={{0,14},{1,15},{2,12},{3,13},{4,10},{5,11},{6,8},{7,9},{8,6},{9,7},... | collective-permute-start | bytes 196616 | tf_op jit(solution)/shard_map/ppermute | solution.py:404
  15.9 11.7 %collective-permute-start.13 = (bf16[32,1024]{1,0:T(8,128)(2,1)}, bf16[32,1024]{1,0:T(8,128)(2,1)S(1)}, u32[]{:S(2)}, u32[]{:S(2)}) collective-permute-start(bf16[32,1024]{1,0:T(8,128)(2,1)} %get-tuple-element.45), channel_id=1, source_target_pairs={{0,10},{1,11},{2,8},{3,9},{4,14},{5,15},{6,12},{7,13},{8,2},{9,3},... | collective-permute-start | bytes 196616 | tf_op jit(solution)/shard_map/ppermute | solution.py:404
  17.2 10.6 %collective-permute-start.14 = (bf16[32,1024]{1,0:T(8,128)(2,1)}, bf16[32,1024]{1,0:T(8,128)(2,1)S(1)}, u32[]{:S(2)}, u32[]{:S(2)}) collective-permute-start(bf16[32,1024]{1,0:T(8,128)(2,1)} %get-tuple-element.46), channel_id=1, source_target_pairs={{0,15},{1,14},{2,13},{3,12},{4,11},{5,10},{6,9},{7,8},{8,7},{9,6},... | collective-permute-start | bytes 196616 | tf_op jit(solution)/shard_map/ppermute | solution.py:404
  20.9 8.3 %collective-permute-start.4 = (bf16[32,1024]{1,0:T(8,128)(2,1)}, bf16[32,1024]{1,0:T(8,128)(2,1)S(1)}, u32[]{:S(2)}, u32[]{:S(2)}) collective-permute-start(bf16[32,1024]{1,0:T(8,128)(2,1)} %get-tuple-element.36), channel_id=1, source_target_pairs={{0,5},{1,4},{2,7},{3,6},{4,1},{5,0},{6,3},{7,2},{8,13},{9,12},{10,... | collective-permute-start | bytes 196616 | tf_op jit(solution)/shard_map/ppermute | solution.py:404
  21.1 11.4 %collective-permute-start.5 = (bf16[32,1024]{1,0:T(8,128)(2,1)}, bf16[32,1024]{1,0:T(8,128)(2,1)S(1)}, u32[]{:S(2)}, u32[]{:S(2)}) collective-permute-start(bf16[32,1024]{1,0:T(8,128)(2,1)} %get-tuple-element.37), channel_id=1, source_target_pairs={{0,11},{1,10},{2,9},{3,8},{4,15},{5,14},{6,13},{7,12},{8,3},{9,2},... | collective-permute-start | bytes 196616 | tf_op jit(solution)/shard_map/ppermute | solution.py:404
  23.6 11.0 %collective-permute-start.6 = (bf16[32,1024]{1,0:T(8,128)(2,1)}, bf16[32,1024]{1,0:T(8,128)(2,1)S(1)}, u32[]{:S(2)}, u32[]{:S(2)}) collective-permute-start(bf16[32,1024]{1,0:T(8,128)(2,1)} %get-tuple-element.38), channel_id=1, source_target_pairs={{0,9},{1,8},{2,11},{3,10},{4,13},{5,12},{6,15},{7,14},{8,1},{9,0},... | collective-permute-start | bytes 196616 | tf_op jit(solution)/shard_map/ppermute | solution.py:404
  27.6 8.6 %collective-permute-start.7 = (bf16[32,1024]{1,0:T(8,128)(2,1)}, bf16[32,1024]{1,0:T(8,128)(2,1)S(1)}, u32[]{:S(2)}, u32[]{:S(2)}) collective-permute-start(bf16[32,1024]{1,0:T(8,128)(2,1)} %get-tuple-element.39), channel_id=1, source_target_pairs={{0,2},{1,3},{2,0},{3,1},{4,6},{5,7},{6,4},{7,5},{8,10},{9,11},{10,... | collective-permute-start | bytes 196616 | tf_op jit(solution)/shard_map/ppermute | solution.py:404
  27.8 8.3 %collective-permute-start.8 = (bf16[32,1024]{1,0:T(8,128)(2,1)}, bf16[32,1024]{1,0:T(8,128)(2,1)S(1)}, u32[]{:S(2)}, u32[]{:S(2)}) collective-permute-start(bf16[32,1024]{1,0:T(8,128)(2,1)} %get-tuple-element.40), channel_id=1, source_target_pairs={{0,12},{1,13},{2,14},{3,15},{4,8},{5,9},{6,10},{7,11},{8,4},{9,5},... | collective-permute-start | bytes 196616 | tf_op jit(solution)/shard_map/ppermute | solution.py:404
  29.2 7.0 %collective-permute-start.9 = (bf16[32,1024]{1,0:T(8,128)(2,1)}, bf16[32,1024]{1,0:T(8,128)(2,1)S(1)}, u32[]{:S(2)}, u32[]{:S(2)}) collective-permute-start(bf16[32,1024]{1,0:T(8,128)(2,1)} %get-tuple-element.41), channel_id=1, source_target_pairs={{0,6},{1,7},{2,4},{3,5},{4,2},{5,3},{6,0},{7,1},{8,14},{9,15},{10,... | collective-permute-start | bytes 196616 | tf_op jit(solution)/shard_map/ppermute | solution.py:404
  32.5 6.2 %collective-permute-start = (bf16[32,1024]{1,0:T(8,128)(2,1)}, bf16[32,1024]{1,0:T(8,128)(2,1)S(1)}, u32[]{:S(2)}, u32[]{:S(2)}) collective-permute-start(bf16[32,1024]{1,0:T(8,128)(2,1)} %get-tuple-element.31), channel_id=1, source_target_pairs={{0,13},{1,12},{2,15},{3,14},{4,9},{5,8},{6,11},{7,10},{8,5},{9,4},... | collective-permute-start | bytes 196616 | tf_op jit(solution)/shard_map/ppermute | solution.py:404
  34.6 4.1 %collective-permute-start.1 = (bf16[32,1024]{1,0:T(8,128)(2,1)}, bf16[32,1024]{1,0:T(8,128)(2,1)S(1)}, u32[]{:S(2)}, u32[]{:S(2)}) collective-permute-start(bf16[32,1024]{1,0:T(8,128)(2,1)} %get-tuple-element.32), channel_id=1, source_target_pairs={{0,3},{1,2},{2,1},{3,0},{4,7},{5,6},{6,5},{7,4},{8,11},{9,10},{10,... | collective-permute-start | bytes 196616 | tf_op jit(solution)/shard_map/ppermute | solution.py:404
  36.2 5.0 %collective-permute-start.2 = (bf16[32,1024]{1,0:T(8,128)(2,1)}, bf16[32,1024]{1,0:T(8,128)(2,1)S(1)}, u32[]{:S(2)}, u32[]{:S(2)}) collective-permute-start(bf16[32,1024]{1,0:T(8,128)(2,1)} %get-tuple-element.33), channel_id=1, source_target_pairs={{0,7},{1,6},{2,5},{3,4},{4,3},{5,2},{6,1},{7,0},{8,15},{9,14},{10,... | collective-permute-start | bytes 196616 | tf_op jit(solution)/shard_map/ppermute | solution.py:404
  36.2 5.0 %collective-permute-start.3 = (bf16[32,1024]{1,0:T(8,128)(2,1)}, bf16[32,1024]{1,0:T(8,128)(2,1)S(1)}, u32[]{:S(2)}, u32[]{:S(2)}) collective-permute-start(bf16[32,1024]{1,0:T(8,128)(2,1)} %get-tuple-element.34), channel_id=1, source_target_pairs={{0,1},{1,0},{2,3},{3,2},{4,5},{5,4},{6,7},{7,6},{8,9},{9,8},{10,11... | collective-permute-start | bytes 196616 | tf_op jit(solution)/shard_map/ppermute | solution.py:404
  36.3 0.8 %copy-start.3 = (bf16[32,1024]{1,0:T(8,128)(2,1)S(1)}, bf16[32,1024]{1,0:T(8,128)(2,1)}, u32[]{:S(2)}) copy-start(bf16[32,1024]{1,0:T(8,128)(2,1)} %get-tuple-element.35.refs_0_) | copy-start | bytes 196612
  41.7 8.5 %collective-permute-start.16 = (bf16[512,256]{1,0:T(8,128)(2,1)S(1)}, bf16[512,256]{1,0:T(8,128)(2,1)S(1)}, u32[]{:S(2)}, u32[]{:S(2)}) collective-permute-start(bf16[512,256]{1,0:T(8,128)(2,1)S(1)} %get-tuple-element.51.refs_0_), channel_id=1, source_target_pairs={{0,1},{1,2},{2,3},{3,4},{4,5},{5,6},{6,7},{7,8},{8,9},{9,10},{10,1... | collective-permute-start | bytes 786440 | tf_op jit(solution)/shard_map/ppermute | solution.py:27
  43.7 8.2 %collective-permute-start.15 = (bf16[512,256]{1,0:T(8,128)(2,1)S(1)}, bf16[512,256]{1,0:T(8,128)(2,1)S(1)}, u32[]{:S(2)}, u32[]{:S(2)}) collective-permute-start(bf16[512,256]{1,0:T(8,128)(2,1)S(1)} %get-tuple-element.52.refs_1_), channel_id=1, source_target_pairs={{0,1},{1,2},{2,3},{3,4},{4,5},{5,6},{6,7},{7,8},{8,9},{9,10},{10,1... | collective-permute-start | bytes 786440 | tf_op jit(solution)/shard_map/ppermute | solution.py:27

commit v19 on v18

--- a/solution.py
+++ b/solution.py
@@ -14,7 +14,7 @@
 SB = 16
 SPAN = 128
 GROUPS = ((0, 4), (4, 8))
-APART = (0, 5, 11, 9, 2, 12, 6, 8, 4, 14, 10, 15, 13, 3, 7, 1)
+APART = (0, 5, 11, 9, 2, 12, 6, 8, 4, 14, 10, 15, 13, 7, 3, 1)
 EARLY = SB - 4
 
 epsilon = 1e-06

time: 54.7 us -> 54.7 us (level)
  transfers between devices with their start and end apart: 17 -> 17, of which waited for: 1 -> 2; matrix products, arithmetic and copies ran while one was open for 0% -> 0% of each run, Pallas kernels for 12% -> 12%
where the time goes in v19:
time: 54.7 us; the launch traced here: 54.2 us
  starting transfers between devices  31.2 us (57%)
  Pallas kernels  19.7 us (36%)
  waiting for transfers between devices  2.17 us (4%)
  local copies, waits for them, and re-layouts  0.85 us (2%)
    ppermute x15, starting transfers between devices, swap(): return lax.ppermute(tile, 'tm', route)  25.7 us
    pallas_call x1, Pallas kernels, mixer(): pl.pallas_call(functools.partial(mixer_kernel, state is not None), in_spe...  10.4 us
    ppermute x2, starting transfers between devices, shifted(): return lax.ppermute(block, axis, route)  5.5 us
    pallas_call x2, Pallas kernels, earlier_frame(): pl.pallas_call(functools.partial(earlier_kernel, group), compiler_params=...  4.19 us
    pallas_call x1, Pallas kernels, own_frame(): pl.pallas_call(own_kernel, out_shape=[jax.ShapeDtypeStruct((rows, width),...  3.06 us
    ppermute x15, waiting for transfers between devices, swap(): return lax.ppermute(tile, 'tm', route)  2.16 us
    pallas_call x1, Pallas kernels, make_early(): pl.pallas_call(early_kernel, out_shape=[jax.ShapeDtypeStruct((rows, w_que...  1.53 us
  transfers between devices with their start and end apart: 17, of which 2 were waited for; matrix products, arithmetic and copies ran while one was open for 0% of the time, Pallas kernels for 12%

profile of v19, /device:TPU:1, one launch (start us, length us, event | category | flops | bytes accessed | tf_op | source)
XLA Modules:
  0.0 54.2 jit_solution(1838065729681627060)
XLA Ops:
  0.0 10.4 %mixer.1 = (bf16[32,1024]{1,0:T(8,128)(2,1)}, bf16[32,1024]{1,0:T(8,128)(2,1)}, bf16[32,1024]{1,0:T(8,128)(2,1)}, bf16[32,1024]{1,0:T(8,128)(2,1)}, bf16[32,1024...) custom-call(bf16[512,1024]{1,0:T(8,128)(2,1)} %bitcast.2, ...), custom_call_target="tpu_custom_call" | custom-call | flops 3758096384 | bytes 8388608 | tf_op jit(solution)/shard_map/mixer/pallas_call | solution.py:155
  10.5 3.2 %collective-permute-start.10 = (bf16[32,1024]{1,0:T(8,128)(2,1)}, bf16[32,1024]{1,0:T(8,128)(2,1)S(1)}, u32[]{:S(2)}, u32[]{:S(2)}) collective-permute-start(bf16[32,1024]{1,0:T(8,128)(2,1)} %get-tuple-element.42), channel_id=1, source_target_pairs={{0,8},{1,9},{2,10},{3,11},{4,12},{5,13},{6,14},{7,15},{8,0},{9,1},... | collective-permute-start | bytes 196616 | tf_op jit(solution)/shard_map/ppermute | solution.py:404
  13.7 1.3 %collective-permute-start.11 = (bf16[32,1024]{1,0:T(8,128)(2,1)}, bf16[32,1024]{1,0:T(8,128)(2,1)S(1)}, u32[]{:S(2)}, u32[]{:S(2)}) collective-permute-start(bf16[32,1024]{1,0:T(8,128)(2,1)} %get-tuple-element.43), channel_id=1, source_target_pairs={{0,4},{1,5},{2,6},{3,7},{4,0},{5,1},{6,2},{7,3},{8,12},{9,13},{10,... | collective-permute-start | bytes 196616 | tf_op jit(solution)/shard_map/ppermute | solution.py:404
  15.0 0.9 %collective-permute-start.12 = (bf16[32,1024]{1,0:T(8,128)(2,1)}, bf16[32,1024]{1,0:T(8,128)(2,1)S(1)}, u32[]{:S(2)}, u32[]{:S(2)}) collective-permute-start(bf16[32,1024]{1,0:T(8,128)(2,1)} %get-tuple-element.44), channel_id=1, source_target_pairs={{0,14},{1,15},{2,12},{3,13},{4,10},{5,11},{6,8},{7,9},{8,6},{9,7},... | collective-permute-start | bytes 196616 | tf_op jit(solution)/shard_map/ppermute | solution.py:404
  15.9 1.3 %collective-permute-start.13 = (bf16[32,1024]{1,0:T(8,128)(2,1)}, bf16[32,1024]{1,0:T(8,128)(2,1)S(1)}, u32[]{:S(2)}, u32[]{:S(2)}) collective-permute-start(bf16[32,1024]{1,0:T(8,128)(2,1)} %get-tuple-element.45), channel_id=1, source_target_pairs={{0,10},{1,11},{2,8},{3,9},{4,14},{5,15},{6,12},{7,13},{8,2},{9,3},... | collective-permute-start | bytes 196616 | tf_op jit(solution)/shard_map/ppermute | solution.py:404
  17.2 3.7 %collective-permute-start.14 = (bf16[32,1024]{1,0:T(8,128)(2,1)}, bf16[32,1024]{1,0:T(8,128)(2,1)S(1)}, u32[]{:S(2)}, u32[]{:S(2)}) collective-permute-start(bf16[32,1024]{1,0:T(8,128)(2,1)} %get-tuple-element.46), channel_id=1, source_target_pairs={{0,15},{1,14},{2,13},{3,12},{4,11},{5,10},{6,9},{7,8},{8,7},{9,6},... | collective-permute-start | bytes 196616 | tf_op jit(solution)/shard_map/ppermute | solution.py:404
  20.9 0.2 collective-permute-start.4
  21.1 2.5 %collective-permute-start.5 = (bf16[32,1024]{1,0:T(8,128)(2,1)}, bf16[32,1024]{1,0:T(8,128)(2,1)S(1)}, u32[]{:S(2)}, u32[]{:S(2)}) collective-permute-start(bf16[32,1024]{1,0:T(8,128)(2,1)} %get-tuple-element.37), channel_id=1, source_target_pairs={{0,11},{1,10},{2,9},{3,8},{4,15},{5,14},{6,13},{7,12},{8,3},{9,2},... | collective-permute-start | bytes 196616 | tf_op jit(solution)/shard_map/ppermute | solution.py:404
  23.6 0.0 collective-permute-done.12.refs_9_
  23.6 4.0 %collective-permute-start.6 = (bf16[32,1024]{1,0:T(8,128)(2,1)}, bf16[32,1024]{1,0:T(8,128)(2,1)S(1)}, u32[]{:S(2)}, u32[]{:S(2)}) collective-permute-start(bf16[32,1024]{1,0:T(8,128)(2,1)} %get-tuple-element.38), channel_id=1, source_target_pairs={{0,9},{1,8},{2,11},{3,10},{4,13},{5,12},{6,15},{7,14},{8,1},{9,0},... | collective-permute-start | bytes 196616 | tf_op jit(solution)/shard_map/ppermute | solution.py:404
  27.6 0.0 collective-permute-done.13.refs_10_
  27.6 0.2 collective-permute-start.7
  27.8 1.4 %collective-permute-start.8 = (bf16[32,1024]{1,0:T(8,128)(2,1)}, bf16[32,1024]{1,0:T(8,128)(2,1)S(1)}, u32[]{:S(2)}, u32[]{:S(2)}) collective-permute-start(bf16[32,1024]{1,0:T(8,128)(2,1)} %get-tuple-element.40), channel_id=1, source_target_pairs={{0,12},{1,13},{2,14},{3,15},{4,8},{5,9},{6,10},{7,11},{8,4},{9,5},... | collective-permute-start | bytes 196616 | tf_op jit(solution)/shard_map/ppermute | solution.py:404
  29.2 0.0 collective-permute-done.4.refs_1_
  29.2 3.2 %collective-permute-start.9 = (bf16[32,1024]{1,0:T(8,128)(2,1)}, bf16[32,1024]{1,0:T(8,128)(2,1)S(1)}, u32[]{:S(2)}, u32[]{:S(2)}) collective-permute-start(bf16[32,1024]{1,0:T(8,128)(2,1)} %get-tuple-element.41), channel_id=1, source_target_pairs={{0,6},{1,7},{2,4},{3,5},{4,2},{5,3},{6,0},{7,1},{8,14},{9,15},{10,... | collective-permute-start | bytes 196616 | tf_op jit(solution)/shard_map/ppermute | solution.py:404
  32.4 0.0 collective-permute-done.5.refs_2_
  32.5 2.1 %collective-permute-start = (bf16[32,1024]{1,0:T(8,128)(2,1)}, bf16[32,1024]{1,0:T(8,128)(2,1)S(1)}, u32[]{:S(2)}, u32[]{:S(2)}) collective-permute-start(bf16[32,1024]{1,0:T(8,128)(2,1)} %get-tuple-element.31), channel_id=1, source_target_pairs={{0,13},{1,12},{2,15},{3,14},{4,9},{5,8},{6,11},{7,10},{8,5},{9,4},... | collective-permute-start | bytes 196616 | tf_op jit(solution)/shard_map/ppermute | solution.py:404
  34.6 0.3 collective-permute-start.1
  34.9 1.3 %collective-permute-start.2 = (bf16[32,1024]{1,0:T(8,128)(2,1)}, bf16[32,1024]{1,0:T(8,128)(2,1)S(1)}, u32[]{:S(2)}, u32[]{:S(2)}) collective-permute-start(bf16[32,1024]{1,0:T(8,128)(2,1)} %get-tuple-element.33), channel_id=1, source_target_pairs={{0,3},{1,2},{2,1},{3,0},{4,7},{5,6},{6,5},{7,4},{8,11},{9,10},{10,... | collective-permute-start | bytes 196616 | tf_op jit(solution)/shard_map/ppermute | solution.py:404
  36.3 0.0 copy-start.3
  36.3 0.8 %copy-done.3 = bf16[32,1024]{1,0:T(8,128)(2,1)S(1)} copy-done((bf16[32,1024]{1,0:T(8,128)(2,1)S(1)}, bf16[32,1024]{1,0:T(8,128)(2,1)}, u32[]{:S(2)}) %copy-start.3) | copy-done | bytes 65560
  37.1 1.5 %early_rows.1 = (bf16[384,1024]{1,0:T(8,128)(2,1)S(1)}, bf16[384,256]{1,0:T(8,128)(2,1)S(1)}, bf16[384,256]{1,0:T(8,128)(2,1)S(1)}) custom-call(bf16[1024]{0:T(1024)(128)(2,1)S(1)} %copy-done.1, bf16[1024,512]{1,0:T(8,128)(2,1)S(1)} %copy-done, bf16[1024,1024]{1,0:T(8,128)(2,1)S(1)} %copy-done.2, bf16[32,1024]{1,0:T(8,128)(2,1)S(1)} %copy-done.3, ...), custom_call_target="tpu_custom_call" | custom-call | flops 1207959552 | bytes 4718592 | tf_op jit(solution)/shard_map/early_rows/pallas_call | solution.py:230
  38.6 0.2 collective-permute-done.refs_0_
  38.8 1.9 %collective-permute-done.1.refs_1_ = bf16[32,1024]{1,0:T(8,128)(2,1)S(1)} collective-permute-done((bf16[32,1024]{1,0:T(8,128)(2,1)}, bf16[32,1024]{1,0:T(8,128)(2,1)S(1)}, u32[]{:S(2)}, u32[]{:S(2)}) %collective-permute-start.1) | collective-permute-done | bytes 65568 | tf_op jit(solution)/shard_map/ppermute | solution.py:404
  40.7 0.0 collective-permute-done.2.refs_2_
  40.7 0.0 collective-permute-done.3.refs_3_
  40.7 0.5 pairs.1
  41.2 3.3 %collective-permute-start.16 = (bf16[512,256]{1,0:T(8,128)(2,1)S(1)}, bf16[512,256]{1,0:T(8,128)(2,1)S(1)}, u32[]{:S(2)}, u32[]{:S(2)}) collective-permute-start(bf16[512,256]{1,0:T(8,128)(2,1)S(1)} %get-tuple-element.51.refs_0_), channel_id=1, source_target_pairs={{0,1},{1,2},{2,3},{3,4},{4,5},{5,6},{6,7},{7,8},{8,9},{9,10},{10,1... | collective-permute-start | bytes 786440 | tf_op jit(solution)/shard_map/ppermute | solution.py:27
  44.5 2.2 %collective-permute-start.15 = (bf16[512,256]{1,0:T(8,128)(2,1)S(1)}, bf16[512,256]{1,0:T(8,128)(2,1)S(1)}, u32[]{:S(2)}, u32[]{:S(2)}) collective-permute-start(bf16[512,256]{1,0:T(8,128)(2,1)S(1)} %get-tuple-element.52.refs_1_), channel_id=1, source_target_pairs={{0,1},{1,2},{2,3},{3,4},{4,5},{5,6},{6,7},{7,8},{8,9},{9,10},{10,1... | collective-permute-start | bytes 786440 | tf_op jit(solution)/shard_map/ppermute | solution.py:27
  46.7 3.1 %own_frame.1 = (bf16[512,1024]{1,0:T(8,128)(2,1)S(1)}, f32[512,1024]{1,0:T(8,128)S(1)}, f32[512,1024]{1,0:T(8,128)S(1)}, f32[512,1024]{1,0:T(8,128)S(1)}) custom-call(bf16[128,1024]{1,0:T(8,128)(2,1)S(1)} %get-tuple-element.49.normed_ref, bf16[1024,1024]{1,0:T(8,128)(2,1)S(1)} %copy-done.2, bf16[384,1024]{1,0:T(8,128)(2,1)S(1)} %get-tuple-element.50.early_ref, ...), custom_call_target="tpu_custom_call" | custom-call | flops 2147483648 | bytes 6291456 | tf_op jit(solution)/shard_map/own_frame/pallas_call | solution.py:309
  49.8 1.7 %earlier_frame.2.refs_0_ = bf16[512,512]{1,0:T(8,128)(2,1)S(1)} custom-call(bf16[512,1024]{1,0:T(8,128)(2,1)S(1)} %get-tuple-element.53.query_ref, bf16[512,256]{1,0:T(8,128)(2,1)S(1)} %collective-permute-done.16.pairs_ref, f32[512,1024]{1,0:T(8,128)S(1)} %get-tuple-element.54.sum_ref, f32[512,1024]{1,0:T(8,128)S(1)} %get-tuple-element.55.total_ref, ...), custom_call_target="tpu_custom_call" | custom-call | flops 536870912 | bytes 5242880 | tf_op jit(solution)/shard_map/earlier_frame/pallas_call | solution.py:388
  51.5 2.5 %earlier_frame.3 = bf16[512,1024]{1,0:T(8,128)(2,1)} custom-call(bf16[512,1024]{1,0:T(8,128)(2,1)S(1)} %get-tuple-element.53.query_ref, bf16[512,256]{1,0:T(8,128)(2,1)S(1)} %collective-permute-done.15.pairs_ref, f32[512,1024]{1,0:T(8,128)S(1)} %get-tuple-element.54.sum_ref, f32[512,1024]{1,0:T(8,128)S(1)} %get-tuple-element.55.total_ref, ...), custom_call_target="tpu_custom_call" | custom-call | flops 536870912 | bytes 5242880 | tf_op jit(solution)/shard_map/earlier_frame/pallas_call | solution.py:388
  (16 shorter events, 0.0 us)
Async XLA Ops:
  0.0 36.2 %copy-start = (bf16[1024,512]{1,0:T(8,128)(2,1)S(1)}, bf16[1024,512]{1,0:T(8,128)(2,1)}, u32[]{:S(2)}) copy-start(bf16[1024,512]{1,0:T(8,128)(2,1)} %w_kv_ref.3) | copy-start | bytes 3145732
  0.0 36.2 %copy-start.1 = (bf16[1024]{0:T(1024)(128)(2,1)S(1)}, bf16[1024]{0:T(1024)(128)(2,1)}, u32[]{:S(2)}) copy-start(bf16[1024]{0:T(1024)(128)(2,1)} %gain_ref.3) | copy-start | bytes 6148
  0.0 36.3 %copy-start.2 = (bf16[1024,1024]{1,0:T(8,128)(2,1)S(1)}, bf16[1024,1024]{1,0:T(8,128)(2,1)}, u32[]{:S(2)}) copy-start(bf16[1024,1024]{1,0:T(8,128)(2,1)} %w_ref.1) | copy-start | bytes 6291460
  10.5 10.5 %collective-permute-start.10 = (bf16[32,1024]{1,0:T(8,128)(2,1)}, bf16[32,1024]{1,0:T(8,128)(2,1)S(1)}, u32[]{:S(2)}, u32[]{:S(2)}) collective-permute-start(bf16[32,1024]{1,0:T(8,128)(2,1)} %get-tuple-element.42), channel_id=1, source_target_pairs={{0,8},{1,9},{2,10},{3,11},{4,12},{5,13},{6,14},{7,15},{8,0},{9,1},... | collective-permute-start | bytes 196616 | tf_op jit(solution)/shard_map/ppermute | solution.py:404
  13.7 7.5 %collective-permute-start.11 = (bf16[32,1024]{1,0:T(8,128)(2,1)}, bf16[32,1024]{1,0:T(8,128)(2,1)S(1)}, u32[]{:S(2)}, u32[]{:S(2)}) collective-permute-start(bf16[32,1024]{1,0:T(8,128)(2,1)} %get-tuple-element.43), channel_id=1, source_target_pairs={{0,4},{1,5},{2,6},{3,7},{4,0},{5,1},{6,2},{7,3},{8,12},{9,13},{10,... | collective-permute-start | bytes 196616 | tf_op jit(solution)/shard_map/ppermute | solution.py:404
  15.0 8.7 %collective-permute-start.12 = (bf16[32,1024]{1,0:T(8,128)(2,1)}, bf16[32,1024]{1,0:T(8,128)(2,1)S(1)}, u32[]{:S(2)}, u32[]{:S(2)}) collective-permute-start(bf16[32,1024]{1,0:T(8,128)(2,1)} %get-tuple-element.44), channel_id=1, source_target_pairs={{0,14},{1,15},{2,12},{3,13},{4,10},{5,11},{6,8},{7,9},{8,6},{9,7},... | collective-permute-start | bytes 196616 | tf_op jit(solution)/shard_map/ppermute | solution.py:404
  15.9 11.7 %collective-permute-start.13 = (bf16[32,1024]{1,0:T(8,128)(2,1)}, bf16[32,1024]{1,0:T(8,128)(2,1)S(1)}, u32[]{:S(2)}, u32[]{:S(2)}) collective-permute-start(bf16[32,1024]{1,0:T(8,128)(2,1)} %get-tuple-element.45), channel_id=1, source_target_pairs={{0,10},{1,11},{2,8},{3,9},{4,14},{5,15},{6,12},{7,13},{8,2},{9,3},... | collective-permute-start | bytes 196616 | tf_op jit(solution)/shard_map/ppermute | solution.py:404
  17.2 10.6 %collective-permute-start.14 = (bf16[32,1024]{1,0:T(8,128)(2,1)}, bf16[32,1024]{1,0:T(8,128)(2,1)S(1)}, u32[]{:S(2)}, u32[]{:S(2)}) collective-permute-start(bf16[32,1024]{1,0:T(8,128)(2,1)} %get-tuple-element.46), channel_id=1, source_target_pairs={{0,15},{1,14},{2,13},{3,12},{4,11},{5,10},{6,9},{7,8},{8,7},{9,6},... | collective-permute-start | bytes 196616 | tf_op jit(solution)/shard_map/ppermute | solution.py:404
  20.9 8.3 %collective-permute-start.4 = (bf16[32,1024]{1,0:T(8,128)(2,1)}, bf16[32,1024]{1,0:T(8,128)(2,1)S(1)}, u32[]{:S(2)}, u32[]{:S(2)}) collective-permute-start(bf16[32,1024]{1,0:T(8,128)(2,1)} %get-tuple-element.36), channel_id=1, source_target_pairs={{0,5},{1,4},{2,7},{3,6},{4,1},{5,0},{6,3},{7,2},{8,13},{9,12},{10,... | collective-permute-start | bytes 196616 | tf_op jit(solution)/shard_map/ppermute | solution.py:404
  21.1 11.4 %collective-permute-start.5 = (bf16[32,1024]{1,0:T(8,128)(2,1)}, bf16[32,1024]{1,0:T(8,128)(2,1)S(1)}, u32[]{:S(2)}, u32[]{:S(2)}) collective-permute-start(bf16[32,1024]{1,0:T(8,128)(2,1)} %get-tuple-element.37), channel_id=1, source_target_pairs={{0,11},{1,10},{2,9},{3,8},{4,15},{5,14},{6,13},{7,12},{8,3},{9,2},... | collective-permute-start | bytes 196616 | tf_op jit(solution)/shard_map/ppermute | solution.py:404
  23.6 11.0 %collective-permute-start.6 = (bf16[32,1024]{1,0:T(8,128)(2,1)}, bf16[32,1024]{1,0:T(8,128)(2,1)S(1)}, u32[]{:S(2)}, u32[]{:S(2)}) collective-permute-start(bf16[32,1024]{1,0:T(8,128)(2,1)} %get-tuple-element.38), channel_id=1, source_target_pairs={{0,9},{1,8},{2,11},{3,10},{4,13},{5,12},{6,15},{7,14},{8,1},{9,0},... | collective-permute-start | bytes 196616 | tf_op jit(solution)/shard_map/ppermute | solution.py:404
  27.6 7.3 %collective-permute-start.7 = (bf16[32,1024]{1,0:T(8,128)(2,1)}, bf16[32,1024]{1,0:T(8,128)(2,1)S(1)}, u32[]{:S(2)}, u32[]{:S(2)}) collective-permute-start(bf16[32,1024]{1,0:T(8,128)(2,1)} %get-tuple-element.39), channel_id=1, source_target_pairs={{0,2},{1,3},{2,0},{3,1},{4,6},{5,7},{6,4},{7,5},{8,10},{9,11},{10,... | collective-permute-start | bytes 196616 | tf_op jit(solution)/shard_map/ppermute | solution.py:404
  27.8 8.4 %collective-permute-start.8 = (bf16[32,1024]{1,0:T(8,128)(2,1)}, bf16[32,1024]{1,0:T(8,128)(2,1)S(1)}, u32[]{:S(2)}, u32[]{:S(2)}) collective-permute-start(bf16[32,1024]{1,0:T(8,128)(2,1)} %get-tuple-element.40), channel_id=1, source_target_pairs={{0,12},{1,13},{2,14},{3,15},{4,8},{5,9},{6,10},{7,11},{8,4},{9,5},... | collective-permute-start | bytes 196616 | tf_op jit(solution)/shard_map/ppermute | solution.py:404
  29.2 7.0 %collective-permute-start.9 = (bf16[32,1024]{1,0:T(8,128)(2,1)}, bf16[32,1024]{1,0:T(8,128)(2,1)S(1)}, u32[]{:S(2)}, u32[]{:S(2)}) collective-permute-start(bf16[32,1024]{1,0:T(8,128)(2,1)} %get-tuple-element.41), channel_id=1, source_target_pairs={{0,6},{1,7},{2,4},{3,5},{4,2},{5,3},{6,0},{7,1},{8,14},{9,15},{10,... | collective-permute-start | bytes 196616 | tf_op jit(solution)/shard_map/ppermute | solution.py:404
  32.5 6.4 %collective-permute-start = (bf16[32,1024]{1,0:T(8,128)(2,1)}, bf16[32,1024]{1,0:T(8,128)(2,1)S(1)}, u32[]{:S(2)}, u32[]{:S(2)}) collective-permute-start(bf16[32,1024]{1,0:T(8,128)(2,1)} %get-tuple-element.31), channel_id=1, source_target_pairs={{0,13},{1,12},{2,15},{3,14},{4,9},{5,8},{6,11},{7,10},{8,5},{9,4},... | collective-permute-start | bytes 196616 | tf_op jit(solution)/shard_map/ppermute | solution.py:404
  34.6 6.1 %collective-permute-start.1 = (bf16[32,1024]{1,0:T(8,128)(2,1)}, bf16[32,1024]{1,0:T(8,128)(2,1)S(1)}, u32[]{:S(2)}, u32[]{:S(2)}) collective-permute-start(bf16[32,1024]{1,0:T(8,128)(2,1)} %get-tuple-element.32), channel_id=1, source_target_pairs={{0,7},{1,6},{2,5},{3,4},{4,3},{5,2},{6,1},{7,0},{8,15},{9,14},{10,... | collective-permute-start | bytes 196616 | tf_op jit(solution)/shard_map/ppermute | solution.py:404
  34.9 5.8 %collective-permute-start.2 = (bf16[32,1024]{1,0:T(8,128)(2,1)}, bf16[32,1024]{1,0:T(8,128)(2,1)S(1)}, u32[]{:S(2)}, u32[]{:S(2)}) collective-permute-start(bf16[32,1024]{1,0:T(8,128)(2,1)} %get-tuple-element.33), channel_id=1, source_target_pairs={{0,3},{1,2},{2,1},{3,0},{4,7},{5,6},{6,5},{7,4},{8,11},{9,10},{10,... | collective-permute-start | bytes 196616 | tf_op jit(solution)/shard_map/ppermute | solution.py:404
  36.2 4.5 %collective-permute-start.3 = (bf16[32,1024]{1,0:T(8,128)(2,1)}, bf16[32,1024]{1,0:T(8,128)(2,1)S(1)}, u32[]{:S(2)}, u32[]{:S(2)}) collective-permute-start(bf16[32,1024]{1,0:T(8,128)(2,1)} %get-tuple-element.34), channel_id=1, source_target_pairs={{0,1},{1,0},{2,3},{3,2},{4,5},{5,4},{6,7},{7,6},{8,9},{9,8},{10,11... | collective-permute-start | bytes 196616 | tf_op jit(solution)/shard_map/ppermute | solution.py:404
  36.3 0.8 %copy-start.3 = (bf16[32,1024]{1,0:T(8,128)(2,1)S(1)}, bf16[32,1024]{1,0:T(8,128)(2,1)}, u32[]{:S(2)}) copy-start(bf16[32,1024]{1,0:T(8,128)(2,1)} %get-tuple-element.35.refs_0_) | copy-start | bytes 196612
  41.2 8.6 %collective-permute-start.16 = (bf16[512,256]{1,0:T(8,128)(2,1)S(1)}, bf16[512,256]{1,0:T(8,128)(2,1)S(1)}, u32[]{:S(2)}, u32[]{:S(2)}) collective-permute-start(bf16[512,256]{1,0:T(8,128)(2,1)S(1)} %get-tuple-element.51.refs_0_), channel_id=1, source_target_pairs={{0,1},{1,2},{2,3},{3,4},{4,5},{5,6},{6,7},{7,8},{8,9},{9,10},{10,1... | collective-permute-start | bytes 786440 | tf_op jit(solution)/shard_map/ppermute | solution.py:27
  44.5 7.0 %collective-permute-start.15 = (bf16[512,256]{1,0:T(8,128)(2,1)S(1)}, bf16[512,256]{1,0:T(8,128)(2,1)S(1)}, u32[]{:S(2)}, u32[]{:S(2)}) collective-permute-start(bf16[512,256]{1,0:T(8,128)(2,1)S(1)} %get-tuple-element.52.refs_1_), channel_id=1, source_target_pairs={{0,1},{1,2},{2,3},{3,4},{4,5},{5,6},{6,7},{7,8},{8,9},{9,10},{10,1... | collective-permute-start | bytes 786440 | tf_op jit(solution)/shard_map/ppermute | solution.py:27

commit v20 on v19

--- a/solution.py
+++ b/solution.py
@@ -14,7 +14,7 @@
 SB = 16
 SPAN = 128
 GROUPS = ((0, 4), (4, 8))
-APART = (0, 5, 11, 9, 2, 12, 6, 8, 4, 14, 10, 15, 13, 7, 3, 1)
+APART = (0, 5, 11, 9, 7, 12, 6, 8, 4, 14, 10, 15, 13, 2, 3, 1)
 EARLY = SB - 4
 
 epsilon = 1e-06

time: 54.7 us -> 55.1 us (level)
  starting transfers between devices: 31.2 us -> 32 us
    ppermute x15, starting transfers between devices: 25.7 us -> 27.1 us  [swap(): return lax.ppermute(tile, 'tm', route)]
    ppermute x2, starting transfers between devices: 5.5 us -> 4.86 us  [shifted(): return lax.ppermute(block, axis, route)]
  transfers between devices with their start and end apart: 17 -> 17, of which waited for: 2 -> 3; matrix products, arithmetic and copies ran while one was open for 0% -> 0% of each run, Pallas kernels for 12% -> 12%
where the time goes in v20:
time: 55.1 us; the launch traced here: 54.5 us
  starting transfers between devices  32 us (58%)
  Pallas kernels  19.7 us (36%)
  waiting for transfers between devices  1.65 us (3%)
  local copies, waits for them, and re-layouts  0.85 us (2%)
    ppermute x15, starting transfers between devices, swap(): return lax.ppermute(tile, 'tm', route)  27.1 us
    pallas_call x1, Pallas kernels, mixer(): pl.pallas_call(functools.partial(mixer_kernel, state is not None), in_spe...  10.4 us
    ppermute x2, starting transfers between devices, shifted(): return lax.ppermute(block, axis, route)  4.86 us
    pallas_call x2, Pallas kernels, earlier_frame(): pl.pallas_call(functools.partial(earlier_kernel, group), compiler_params=...  4.19 us
    pallas_call x1, Pallas kernels, own_frame(): pl.pallas_call(own_kernel, out_shape=[jax.ShapeDtypeStruct((rows, width),...  3.06 us
    ppermute x15, waiting for transfers between devices, swap(): return lax.ppermute(tile, 'tm', route)  1.64 us
    pallas_call x1, Pallas kernels, make_early(): pl.pallas_call(early_kernel, out_shape=[jax.ShapeDtypeStruct((rows, w_que...  1.54 us
  transfers between devices with their start and end apart: 17, of which 3 were waited for; matrix products, arithmetic and copies ran while one was open for 0% of the time, Pallas kernels for 12%

profile of v20, /device:TPU:1, one launch (start us, length us, event | category | flops | bytes accessed | tf_op | source)
XLA Modules:
  0.0 54.5 jit_solution(8164060671861431038)
XLA Ops:
  0.0 10.4 %mixer.1 = (bf16[32,1024]{1,0:T(8,128)(2,1)}, bf16[32,1024]{1,0:T(8,128)(2,1)}, bf16[32,1024]{1,0:T(8,128)(2,1)}, bf16[32,1024]{1,0:T(8,128)(2,1)}, bf16[32,1024...) custom-call(bf16[512,1024]{1,0:T(8,128)(2,1)} %bitcast.2, ...), custom_call_target="tpu_custom_call" | custom-call | flops 3758096384 | bytes 8388608 | tf_op jit(solution)/shard_map/mixer/pallas_call | solution.py:155
  10.5 3.2 %collective-permute-start.10 = (bf16[32,1024]{1,0:T(8,128)(2,1)}, bf16[32,1024]{1,0:T(8,128)(2,1)S(1)}, u32[]{:S(2)}, u32[]{:S(2)}) collective-permute-start(bf16[32,1024]{1,0:T(8,128)(2,1)} %get-tuple-element.42), channel_id=1, source_target_pairs={{0,8},{1,9},{2,10},{3,11},{4,12},{5,13},{6,14},{7,15},{8,0},{9,1},... | collective-permute-start | bytes 196616 | tf_op jit(solution)/shard_map/ppermute | solution.py:404
  13.7 1.3 %collective-permute-start.11 = (bf16[32,1024]{1,0:T(8,128)(2,1)}, bf16[32,1024]{1,0:T(8,128)(2,1)S(1)}, u32[]{:S(2)}, u32[]{:S(2)}) collective-permute-start(bf16[32,1024]{1,0:T(8,128)(2,1)} %get-tuple-element.43), channel_id=1, source_target_pairs={{0,4},{1,5},{2,6},{3,7},{4,0},{5,1},{6,2},{7,3},{8,12},{9,13},{10,... | collective-permute-start | bytes 196616 | tf_op jit(solution)/shard_map/ppermute | solution.py:404
  15.0 0.9 %collective-permute-start.12 = (bf16[32,1024]{1,0:T(8,128)(2,1)}, bf16[32,1024]{1,0:T(8,128)(2,1)S(1)}, u32[]{:S(2)}, u32[]{:S(2)}) collective-permute-start(bf16[32,1024]{1,0:T(8,128)(2,1)} %get-tuple-element.44), channel_id=1, source_target_pairs={{0,14},{1,15},{2,12},{3,13},{4,10},{5,11},{6,8},{7,9},{8,6},{9,7},... | collective-permute-start | bytes 196616 | tf_op jit(solution)/shard_map/ppermute | solution.py:404
  15.9 1.3 %collective-permute-start.13 = (bf16[32,1024]{1,0:T(8,128)(2,1)}, bf16[32,1024]{1,0:T(8,128)(2,1)S(1)}, u32[]{:S(2)}, u32[]{:S(2)}) collective-permute-start(bf16[32,1024]{1,0:T(8,128)(2,1)} %get-tuple-element.45), channel_id=1, source_target_pairs={{0,10},{1,11},{2,8},{3,9},{4,14},{5,15},{6,12},{7,13},{8,2},{9,3},... | collective-permute-start | bytes 196616 | tf_op jit(solution)/shard_map/ppermute | solution.py:404
  17.2 3.7 %collective-permute-start.14 = (bf16[32,1024]{1,0:T(8,128)(2,1)}, bf16[32,1024]{1,0:T(8,128)(2,1)S(1)}, u32[]{:S(2)}, u32[]{:S(2)}) collective-permute-start(bf16[32,1024]{1,0:T(8,128)(2,1)} %get-tuple-element.46), channel_id=1, source_target_pairs={{0,15},{1,14},{2,13},{3,12},{4,11},{5,10},{6,9},{7,8},{8,7},{9,6},... | collective-permute-start | bytes 196616 | tf_op jit(solution)/shard_map/ppermute | solution.py:404
  20.9 0.2 collective-permute-start.4
  21.1 2.5 %collective-permute-start.5 = (bf16[32,1024]{1,0:T(8,128)(2,1)}, bf16[32,1024]{1,0:T(8,128)(2,1)S(1)}, u32[]{:S(2)}, u32[]{:S(2)}) collective-permute-start(bf16[32,1024]{1,0:T(8,128)(2,1)} %get-tuple-element.37), channel_id=1, source_target_pairs={{0,11},{1,10},{2,9},{3,8},{4,15},{5,14},{6,13},{7,12},{8,3},{9,2},... | collective-permute-start | bytes 196616 | tf_op jit(solution)/shard_map/ppermute | solution.py:404
  23.6 0.0 collective-permute-done.12.refs_9_
  23.6 4.0 %collective-permute-start.6 = (bf16[32,1024]{1,0:T(8,128)(2,1)}, bf16[32,1024]{1,0:T(8,128)(2,1)S(1)}, u32[]{:S(2)}, u32[]{:S(2)}) collective-permute-start(bf16[32,1024]{1,0:T(8,128)(2,1)} %get-tuple-element.38), channel_id=1, source_target_pairs={{0,9},{1,8},{2,11},{3,10},{4,13},{5,12},{6,15},{7,14},{8,1},{9,0},... | collective-permute-start | bytes 196616 | tf_op jit(solution)/shard_map/ppermute | solution.py:404
  27.6 0.0 collective-permute-start.7
  27.6 0.0 collective-permute-done.14.refs_11_
  27.6 1.1 %collective-permute-start.8 = (bf16[32,1024]{1,0:T(8,128)(2,1)}, bf16[32,1024]{1,0:T(8,128)(2,1)S(1)}, u32[]{:S(2)}, u32[]{:S(2)}) collective-permute-start(bf16[32,1024]{1,0:T(8,128)(2,1)} %get-tuple-element.40), channel_id=1, source_target_pairs={{0,12},{1,13},{2,14},{3,15},{4,8},{5,9},{6,10},{7,11},{8,4},{9,5},... | collective-permute-start | bytes 196616 | tf_op jit(solution)/shard_map/ppermute | solution.py:404
  28.7 0.0 collective-permute-done.4.refs_1_
  28.7 3.7 %collective-permute-start.9 = (bf16[32,1024]{1,0:T(8,128)(2,1)}, bf16[32,1024]{1,0:T(8,128)(2,1)S(1)}, u32[]{:S(2)}, u32[]{:S(2)}) collective-permute-start(bf16[32,1024]{1,0:T(8,128)(2,1)} %get-tuple-element.41), channel_id=1, source_target_pairs={{0,6},{1,7},{2,4},{3,5},{4,2},{5,3},{6,0},{7,1},{8,14},{9,15},{10,... | collective-permute-start | bytes 196616 | tf_op jit(solution)/shard_map/ppermute | solution.py:404
  32.5 0.6 %collective-permute-done.5.refs_2_ = bf16[32,1024]{1,0:T(8,128)(2,1)S(1)} collective-permute-done((bf16[32,1024]{1,0:T(8,128)(2,1)}, bf16[32,1024]{1,0:T(8,128)(2,1)S(1)}, u32[]{:S(2)}, u32[]{:S(2)}) %collective-permute-start.5) | collective-permute-done | bytes 65568 | tf_op jit(solution)/shard_map/ppermute | solution.py:404
  33.1 1.6 %collective-permute-start = (bf16[32,1024]{1,0:T(8,128)(2,1)}, bf16[32,1024]{1,0:T(8,128)(2,1)S(1)}, u32[]{:S(2)}, u32[]{:S(2)}) collective-permute-start(bf16[32,1024]{1,0:T(8,128)(2,1)} %get-tuple-element.31), channel_id=1, source_target_pairs={{0,13},{1,12},{2,15},{3,14},{4,9},{5,8},{6,11},{7,10},{8,5},{9,4},... | collective-permute-start | bytes 196616 | tf_op jit(solution)/shard_map/ppermute | solution.py:404
  34.7 1.2 %collective-permute-start.1 = (bf16[32,1024]{1,0:T(8,128)(2,1)}, bf16[32,1024]{1,0:T(8,128)(2,1)S(1)}, u32[]{:S(2)}, u32[]{:S(2)}) collective-permute-start(bf16[32,1024]{1,0:T(8,128)(2,1)} %get-tuple-element.32), channel_id=1, source_target_pairs={{0,2},{1,3},{2,0},{3,1},{4,6},{5,7},{6,4},{7,5},{8,10},{9,11},{10,... | collective-permute-start | bytes 196616 | tf_op jit(solution)/shard_map/ppermute | solution.py:404
  35.9 0.4 collective-permute-done.7.refs_4_
  36.3 2.3 %collective-permute-start.2 = (bf16[32,1024]{1,0:T(8,128)(2,1)}, bf16[32,1024]{1,0:T(8,128)(2,1)S(1)}, u32[]{:S(2)}, u32[]{:S(2)}) collective-permute-start(bf16[32,1024]{1,0:T(8,128)(2,1)} %get-tuple-element.33), channel_id=1, source_target_pairs={{0,3},{1,2},{2,1},{3,0},{4,7},{5,6},{6,5},{7,4},{8,11},{9,10},{10,... | collective-permute-start | bytes 196616 | tf_op jit(solution)/shard_map/ppermute | solution.py:404
  38.6 0.0 collective-permute-done.8.refs_5_
  38.6 0.0 collective-permute-start.3
  38.7 0.0 copy-start.3
  38.7 0.8 %copy-done.3 = bf16[32,1024]{1,0:T(8,128)(2,1)S(1)} copy-done((bf16[32,1024]{1,0:T(8,128)(2,1)S(1)}, bf16[32,1024]{1,0:T(8,128)(2,1)}, u32[]{:S(2)}) %copy-start.3) | copy-done | bytes 65560
  39.5 1.5 %early_rows.1 = (bf16[384,1024]{1,0:T(8,128)(2,1)S(1)}, bf16[384,256]{1,0:T(8,128)(2,1)S(1)}, bf16[384,256]{1,0:T(8,128)(2,1)S(1)}) custom-call(bf16[1024]{0:T(1024)(128)(2,1)S(1)} %copy-done.1, bf16[1024,512]{1,0:T(8,128)(2,1)S(1)} %copy-done, bf16[1024,1024]{1,0:T(8,128)(2,1)S(1)} %copy-done.2, bf16[32,1024]{1,0:T(8,128)(2,1)S(1)} %copy-done.3, ...), custom_call_target="tpu_custom_call" | custom-call | flops 1207959552 | bytes 4718592 | tf_op jit(solution)/shard_map/early_rows/pallas_call | solution.py:230
  41.1 0.6 %collective-permute-done.2.refs_2_ = bf16[32,1024]{1,0:T(8,128)(2,1)S(1)} collective-permute-done((bf16[32,1024]{1,0:T(8,128)(2,1)}, bf16[32,1024]{1,0:T(8,128)(2,1)S(1)}, u32[]{:S(2)}, u32[]{:S(2)}) %collective-permute-start.2) | collective-permute-done | bytes 65568 | tf_op jit(solution)/shard_map/ppermute | solution.py:404
  41.7 0.5 pairs.1
  42.2 2.8 %collective-permute-start.16 = (bf16[512,256]{1,0:T(8,128)(2,1)S(1)}, bf16[512,256]{1,0:T(8,128)(2,1)S(1)}, u32[]{:S(2)}, u32[]{:S(2)}) collective-permute-start(bf16[512,256]{1,0:T(8,128)(2,1)S(1)} %get-tuple-element.51.refs_0_), channel_id=1, source_target_pairs={{0,1},{1,2},{2,3},{3,4},{4,5},{5,6},{6,7},{7,8},{8,9},{9,10},{10,1... | collective-permute-start | bytes 786440 | tf_op jit(solution)/shard_map/ppermute | solution.py:27
  44.9 2.1 %collective-permute-start.15 = (bf16[512,256]{1,0:T(8,128)(2,1)S(1)}, bf16[512,256]{1,0:T(8,128)(2,1)S(1)}, u32[]{:S(2)}, u32[]{:S(2)}) collective-permute-start(bf16[512,256]{1,0:T(8,128)(2,1)S(1)} %get-tuple-element.52.refs_1_), channel_id=1, source_target_pairs={{0,1},{1,2},{2,3},{3,4},{4,5},{5,6},{6,7},{7,8},{8,9},{9,10},{10,1... | collective-permute-start | bytes 786440 | tf_op jit(solution)/shard_map/ppermute | solution.py:27
  47.0 3.1 %own_frame.1 = (bf16[512,1024]{1,0:T(8,128)(2,1)S(1)}, f32[512,1024]{1,0:T(8,128)S(1)}, f32[512,1024]{1,0:T(8,128)S(1)}, f32[512,1024]{1,0:T(8,128)S(1)}) custom-call(bf16[128,1024]{1,0:T(8,128)(2,1)S(1)} %get-tuple-element.49.normed_ref, bf16[1024,1024]{1,0:T(8,128)(2,1)S(1)} %copy-done.2, bf16[384,1024]{1,0:T(8,128)(2,1)S(1)} %get-tuple-element.50.early_ref, ...), custom_call_target="tpu_custom_call" | custom-call | flops 2147483648 | bytes 6291456 | tf_op jit(solution)/shard_map/own_frame/pallas_call | solution.py:309
  50.1 1.7 %earlier_frame.2.refs_0_ = bf16[512,512]{1,0:T(8,128)(2,1)S(1)} custom-call(bf16[512,1024]{1,0:T(8,128)(2,1)S(1)} %get-tuple-element.53.query_ref, bf16[512,256]{1,0:T(8,128)(2,1)S(1)} %collective-permute-done.16.pairs_ref, f32[512,1024]{1,0:T(8,128)S(1)} %get-tuple-element.54.sum_ref, f32[512,1024]{1,0:T(8,128)S(1)} %get-tuple-element.55.total_ref, ...), custom_call_target="tpu_custom_call" | custom-call | flops 536870912 | bytes 5242880 | tf_op jit(solution)/shard_map/earlier_frame/pallas_call | solution.py:388
  51.9 2.5 %earlier_frame.3 = bf16[512,1024]{1,0:T(8,128)(2,1)} custom-call(bf16[512,1024]{1,0:T(8,128)(2,1)S(1)} %get-tuple-element.53.query_ref, bf16[512,256]{1,0:T(8,128)(2,1)S(1)} %collective-permute-done.15.pairs_ref, f32[512,1024]{1,0:T(8,128)S(1)} %get-tuple-element.54.sum_ref, f32[512,1024]{1,0:T(8,128)S(1)} %get-tuple-element.55.total_ref, ...), custom_call_target="tpu_custom_call" | custom-call | flops 536870912 | bytes 5242880 | tf_op jit(solution)/shard_map/earlier_frame/pallas_call | solution.py:388
  (16 shorter events, 0.0 us)
Async XLA Ops:
  0.0 38.6 %copy-start = (bf16[1024,512]{1,0:T(8,128)(2,1)S(1)}, bf16[1024,512]{1,0:T(8,128)(2,1)}, u32[]{:S(2)}) copy-start(bf16[1024,512]{1,0:T(8,128)(2,1)} %w_kv_ref.3) | copy-start | bytes 3145732
  0.0 38.7 %copy-start.1 = (bf16[1024]{0:T(1024)(128)(2,1)S(1)}, bf16[1024]{0:T(1024)(128)(2,1)}, u32[]{:S(2)}) copy-start(bf16[1024]{0:T(1024)(128)(2,1)} %gain_ref.3) | copy-start | bytes 6148
  0.0 38.7 %copy-start.2 = (bf16[1024,1024]{1,0:T(8,128)(2,1)S(1)}, bf16[1024,1024]{1,0:T(8,128)(2,1)}, u32[]{:S(2)}) copy-start(bf16[1024,1024]{1,0:T(8,128)(2,1)} %w_ref.1) | copy-start | bytes 6291460
  10.5 10.5 %collective-permute-start.10 = (bf16[32,1024]{1,0:T(8,128)(2,1)}, bf16[32,1024]{1,0:T(8,128)(2,1)S(1)}, u32[]{:S(2)}, u32[]{:S(2)}) collective-permute-start(bf16[32,1024]{1,0:T(8,128)(2,1)} %get-tuple-element.42), channel_id=1, source_target_pairs={{0,8},{1,9},{2,10},{3,11},{4,12},{5,13},{6,14},{7,15},{8,0},{9,1},... | collective-permute-start | bytes 196616 | tf_op jit(solution)/shard_map/ppermute | solution.py:404
  13.7 7.5 %collective-permute-start.11 = (bf16[32,1024]{1,0:T(8,128)(2,1)}, bf16[32,1024]{1,0:T(8,128)(2,1)S(1)}, u32[]{:S(2)}, u32[]{:S(2)}) collective-permute-start(bf16[32,1024]{1,0:T(8,128)(2,1)} %get-tuple-element.43), channel_id=1, source_target_pairs={{0,4},{1,5},{2,6},{3,7},{4,0},{5,1},{6,2},{7,3},{8,12},{9,13},{10,... | collective-permute-start | bytes 196616 | tf_op jit(solution)/shard_map/ppermute | solution.py:404
  15.0 8.7 %collective-permute-start.12 = (bf16[32,1024]{1,0:T(8,128)(2,1)}, bf16[32,1024]{1,0:T(8,128)(2,1)S(1)}, u32[]{:S(2)}, u32[]{:S(2)}) collective-permute-start(bf16[32,1024]{1,0:T(8,128)(2,1)} %get-tuple-element.44), channel_id=1, source_target_pairs={{0,14},{1,15},{2,12},{3,13},{4,10},{5,11},{6,8},{7,9},{8,6},{9,7},... | collective-permute-start | bytes 196616 | tf_op jit(solution)/shard_map/ppermute | solution.py:404
  15.9 11.7 %collective-permute-start.13 = (bf16[32,1024]{1,0:T(8,128)(2,1)}, bf16[32,1024]{1,0:T(8,128)(2,1)S(1)}, u32[]{:S(2)}, u32[]{:S(2)}) collective-permute-start(bf16[32,1024]{1,0:T(8,128)(2,1)} %get-tuple-element.45), channel_id=1, source_target_pairs={{0,10},{1,11},{2,8},{3,9},{4,14},{5,15},{6,12},{7,13},{8,2},{9,3},... | collective-permute-start | bytes 196616 | tf_op jit(solution)/shard_map/ppermute | solution.py:404
  17.2 10.4 %collective-permute-start.14 = (bf16[32,1024]{1,0:T(8,128)(2,1)}, bf16[32,1024]{1,0:T(8,128)(2,1)S(1)}, u32[]{:S(2)}, u32[]{:S(2)}) collective-permute-start(bf16[32,1024]{1,0:T(8,128)(2,1)} %get-tuple-element.46), channel_id=1, source_target_pairs={{0,15},{1,14},{2,13},{3,12},{4,11},{5,10},{6,9},{7,8},{8,7},{9,6},... | collective-permute-start | bytes 196616 | tf_op jit(solution)/shard_map/ppermute | solution.py:404
  20.9 7.8 %collective-permute-start.4 = (bf16[32,1024]{1,0:T(8,128)(2,1)}, bf16[32,1024]{1,0:T(8,128)(2,1)S(1)}, u32[]{:S(2)}, u32[]{:S(2)}) collective-permute-start(bf16[32,1024]{1,0:T(8,128)(2,1)} %get-tuple-element.36), channel_id=1, source_target_pairs={{0,5},{1,4},{2,7},{3,6},{4,1},{5,0},{6,3},{7,2},{8,13},{9,12},{10,... | collective-permute-start | bytes 196616 | tf_op jit(solution)/shard_map/ppermute | solution.py:404
  21.1 11.9 %collective-permute-start.5 = (bf16[32,1024]{1,0:T(8,128)(2,1)}, bf16[32,1024]{1,0:T(8,128)(2,1)S(1)}, u32[]{:S(2)}, u32[]{:S(2)}) collective-permute-start(bf16[32,1024]{1,0:T(8,128)(2,1)} %get-tuple-element.37), channel_id=1, source_target_pairs={{0,11},{1,10},{2,9},{3,8},{4,15},{5,14},{6,13},{7,12},{8,3},{9,2},... | collective-permute-start | bytes 196616 | tf_op jit(solution)/shard_map/ppermute | solution.py:404
  23.6 11.1 %collective-permute-start.6 = (bf16[32,1024]{1,0:T(8,128)(2,1)}, bf16[32,1024]{1,0:T(8,128)(2,1)S(1)}, u32[]{:S(2)}, u32[]{:S(2)}) collective-permute-start(bf16[32,1024]{1,0:T(8,128)(2,1)} %get-tuple-element.38), channel_id=1, source_target_pairs={{0,9},{1,8},{2,11},{3,10},{4,13},{5,12},{6,15},{7,14},{8,1},{9,0},... | collective-permute-start | bytes 196616 | tf_op jit(solution)/shard_map/ppermute | solution.py:404
  27.6 8.7 %collective-permute-start.7 = (bf16[32,1024]{1,0:T(8,128)(2,1)}, bf16[32,1024]{1,0:T(8,128)(2,1)S(1)}, u32[]{:S(2)}, u32[]{:S(2)}) collective-permute-start(bf16[32,1024]{1,0:T(8,128)(2,1)} %get-tuple-element.39), channel_id=1, source_target_pairs={{0,7},{1,6},{2,5},{3,4},{4,3},{5,2},{6,1},{7,0},{8,15},{9,14},{10,... | collective-permute-start | bytes 196616 | tf_op jit(solution)/shard_map/ppermute | solution.py:404
  27.6 11.0 %collective-permute-start.8 = (bf16[32,1024]{1,0:T(8,128)(2,1)}, bf16[32,1024]{1,0:T(8,128)(2,1)S(1)}, u32[]{:S(2)}, u32[]{:S(2)}) collective-permute-start(bf16[32,1024]{1,0:T(8,128)(2,1)} %get-tuple-element.40), channel_id=1, source_target_pairs={{0,12},{1,13},{2,14},{3,15},{4,8},{5,9},{6,10},{7,11},{8,4},{9,5},... | collective-permute-start | bytes 196616 | tf_op jit(solution)/shard_map/ppermute | solution.py:404
  28.7 9.9 %collective-permute-start.9 = (bf16[32,1024]{1,0:T(8,128)(2,1)}, bf16[32,1024]{1,0:T(8,128)(2,1)S(1)}, u32[]{:S(2)}, u32[]{:S(2)}) collective-permute-start(bf16[32,1024]{1,0:T(8,128)(2,1)} %get-tuple-element.41), channel_id=1, source_target_pairs={{0,6},{1,7},{2,4},{3,5},{4,2},{5,3},{6,0},{7,1},{8,14},{9,15},{10,... | collective-permute-start | bytes 196616 | tf_op jit(solution)/shard_map/ppermute | solution.py:404
  33.1 8.0 %collective-permute-start = (bf16[32,1024]{1,0:T(8,128)(2,1)}, bf16[32,1024]{1,0:T(8,128)(2,1)S(1)}, u32[]{:S(2)}, u32[]{:S(2)}) collective-permute-start(bf16[32,1024]{1,0:T(8,128)(2,1)} %get-tuple-element.31), channel_id=1, source_target_pairs={{0,13},{1,12},{2,15},{3,14},{4,9},{5,8},{6,11},{7,10},{8,5},{9,4},... | collective-permute-start | bytes 196616 | tf_op jit(solution)/shard_map/ppermute | solution.py:404
  34.7 6.4 %collective-permute-start.1 = (bf16[32,1024]{1,0:T(8,128)(2,1)}, bf16[32,1024]{1,0:T(8,128)(2,1)S(1)}, u32[]{:S(2)}, u32[]{:S(2)}) collective-permute-start(bf16[32,1024]{1,0:T(8,128)(2,1)} %get-tuple-element.32), channel_id=1, source_target_pairs={{0,2},{1,3},{2,0},{3,1},{4,6},{5,7},{6,4},{7,5},{8,10},{9,11},{10,... | collective-permute-start | bytes 196616 | tf_op jit(solution)/shard_map/ppermute | solution.py:404
  36.3 5.4 %collective-permute-start.2 = (bf16[32,1024]{1,0:T(8,128)(2,1)}, bf16[32,1024]{1,0:T(8,128)(2,1)S(1)}, u32[]{:S(2)}, u32[]{:S(2)}) collective-permute-start(bf16[32,1024]{1,0:T(8,128)(2,1)} %get-tuple-element.33), channel_id=1, source_target_pairs={{0,3},{1,2},{2,1},{3,0},{4,7},{5,6},{6,5},{7,4},{8,11},{9,10},{10,... | collective-permute-start | bytes 196616 | tf_op jit(solution)/shard_map/ppermute | solution.py:404
  38.6 3.1 %collective-permute-start.3 = (bf16[32,1024]{1,0:T(8,128)(2,1)}, bf16[32,1024]{1,0:T(8,128)(2,1)S(1)}, u32[]{:S(2)}, u32[]{:S(2)}) collective-permute-start(bf16[32,1024]{1,0:T(8,128)(2,1)} %get-tuple-element.34), channel_id=1, source_target_pairs={{0,1},{1,0},{2,3},{3,2},{4,5},{5,4},{6,7},{7,6},{8,9},{9,8},{10,11... | collective-permute-start | bytes 196616 | tf_op jit(solution)/shard_map/ppermute | solution.py:404
  38.7 0.8 %copy-start.3 = (bf16[32,1024]{1,0:T(8,128)(2,1)S(1)}, bf16[32,1024]{1,0:T(8,128)(2,1)}, u32[]{:S(2)}) copy-start(bf16[32,1024]{1,0:T(8,128)(2,1)} %get-tuple-element.35.refs_0_) | copy-start | bytes 196612
  42.2 7.9 %collective-permute-start.16 = (bf16[512,256]{1,0:T(8,128)(2,1)S(1)}, bf16[512,256]{1,0:T(8,128)(2,1)S(1)}, u32[]{:S(2)}, u32[]{:S(2)}) collective-permute-start(bf16[512,256]{1,0:T(8,128)(2,1)S(1)} %get-tuple-element.51.refs_0_), channel_id=1, source_target_pairs={{0,1},{1,2},{2,3},{3,4},{4,5},{5,6},{6,7},{7,8},{8,9},{9,10},{10,1... | collective-permute-start | bytes 786440 | tf_op jit(solution)/shard_map/ppermute | solution.py:27
  44.9 6.9 %collective-permute-start.15 = (bf16[512,256]{1,0:T(8,128)(2,1)S(1)}, bf16[512,256]{1,0:T(8,128)(2,1)S(1)}, u32[]{:S(2)}, u32[]{:S(2)}) collective-permute-start(bf16[512,256]{1,0:T(8,128)(2,1)S(1)} %get-tuple-element.52.refs_1_), channel_id=1, source_target_pairs={{0,1},{1,2},{2,3},{3,4},{4,5},{5,6},{6,7},{7,8},{8,9},{9,10},{10,1... | collective-permute-start | bytes 786440 | tf_op jit(solution)/shard_map/ppermute | solution.py:27

commit v21 on v20

--- a/solution.py
+++ b/solution.py
@@ -14,7 +14,7 @@
 SB = 16
 SPAN = 128
 GROUPS = ((0, 4), (4, 8))
-APART = (0, 5, 11, 9, 7, 12, 6, 8, 4, 14, 10, 15, 13, 2, 3, 1)
+APART = (0, 5, 11, 9, 2, 12, 6, 4, 8, 14, 10, 15, 13, 3, 7, 1)
 EARLY = SB - 4
 
 epsilon = 1e-06

time: 55.1 us -> 55.2 us (level)
  waiting for transfers between devices: 1.65 us -> 3.27 us
  starting transfers between devices: 32 us -> 30.9 us
    ppermute x15, starting transfers between devices: 27.1 us -> 25.3 us  [swap(): return lax.ppermute(tile, 'tm', route)]
    ppermute x15, waiting for transfers between devices: 1.64 us -> 3.26 us  [swap(): return lax.ppermute(tile, 'tm', route)]
    ppermute x2, starting transfers between devices: 4.86 us -> 5.67 us  [shifted(): return lax.ppermute(block, axis, route)]
  transfers between devices with their start and end apart: 17 -> 17, of which waited for: 3 -> 2; matrix products, arithmetic and copies ran while one was open for 0% -> 0% of each run, Pallas kernels for 12% -> 11%
where the time goes in v21:
time: 55.2 us; the launch traced here: 55 us
  starting transfers between devices  30.9 us (56%)
  Pallas kernels  19.7 us (36%)
  waiting for transfers between devices  3.27 us (6%)
  local copies, waits for them, and re-layouts  0.85 us (2%)
    ppermute x15, starting transfers between devices, swap(): return lax.ppermute(tile, 'tm', route)  25.3 us
    pallas_call x1, Pallas kernels, mixer(): pl.pallas_call(functools.partial(mixer_kernel, state is not None), in_spe...  10.4 us
    ppermute x2, starting transfers between devices, shifted(): return lax.ppermute(block, axis, route)  5.67 us
    pallas_call x2, Pallas kernels, earlier_frame(): pl.pallas_call(functools.partial(earlier_kernel, group), compiler_params=...  4.19 us
    ppermute x15, waiting for transfers between devices, swap(): return lax.ppermute(tile, 'tm', route)  3.26 us
    pallas_call x1, Pallas kernels, own_frame(): pl.pallas_call(own_kernel, out_shape=[jax.ShapeDtypeStruct((rows, width),...  3.05 us
    pallas_call x1, Pallas kernels, make_early(): pl.pallas_call(early_kernel, out_shape=[jax.ShapeDtypeStruct((rows, w_que...  1.54 us
  transfers between devices with their start and end apart: 17, of which 2 were waited for; matrix products, arithmetic and copies ran while one was open for 0% of the time, Pallas kernels for 11%

profile of v21, /device:TPU:1, one launch (start us, length us, event | category | flops | bytes accessed | tf_op | source)
XLA Modules:
  0.0 55.0 jit_solution(4138959429406330137)
XLA Ops:
  0.0 10.4 %mixer.1 = (bf16[32,1024]{1,0:T(8,128)(2,1)}, bf16[32,1024]{1,0:T(8,128)(2,1)}, bf16[32,1024]{1,0:T(8,128)(2,1)}, bf16[32,1024]{1,0:T(8,128)(2,1)}, bf16[32,1024...) custom-call(bf16[512,1024]{1,0:T(8,128)(2,1)} %bitcast.2, ...), custom_call_target="tpu_custom_call" | custom-call | flops 3758096384 | bytes 8388608 | tf_op jit(solution)/shard_map/mixer/pallas_call | solution.py:155
  10.5 2.2 %collective-permute-start.10 = (bf16[32,1024]{1,0:T(8,128)(2,1)}, bf16[32,1024]{1,0:T(8,128)(2,1)S(1)}, u32[]{:S(2)}, u32[]{:S(2)}) collective-permute-start(bf16[32,1024]{1,0:T(8,128)(2,1)} %get-tuple-element.42), channel_id=1, source_target_pairs={{0,4},{1,5},{2,6},{3,7},{4,0},{5,1},{6,2},{7,3},{8,12},{9,13},{10,... | collective-permute-start | bytes 196616 | tf_op jit(solution)/shard_map/ppermute | solution.py:404
  12.6 2.3 %collective-permute-start.11 = (bf16[32,1024]{1,0:T(8,128)(2,1)}, bf16[32,1024]{1,0:T(8,128)(2,1)S(1)}, u32[]{:S(2)}, u32[]{:S(2)}) collective-permute-start(bf16[32,1024]{1,0:T(8,128)(2,1)} %get-tuple-element.43), channel_id=1, source_target_pairs={{0,8},{1,9},{2,10},{3,11},{4,12},{5,13},{6,14},{7,15},{8,0},{9,1},... | collective-permute-start | bytes 196616 | tf_op jit(solution)/shard_map/ppermute | solution.py:404
  15.0 0.9 %collective-permute-start.12 = (bf16[32,1024]{1,0:T(8,128)(2,1)}, bf16[32,1024]{1,0:T(8,128)(2,1)S(1)}, u32[]{:S(2)}, u32[]{:S(2)}) collective-permute-start(bf16[32,1024]{1,0:T(8,128)(2,1)} %get-tuple-element.44), channel_id=1, source_target_pairs={{0,14},{1,15},{2,12},{3,13},{4,10},{5,11},{6,8},{7,9},{8,6},{9,7},... | collective-permute-start | bytes 196616 | tf_op jit(solution)/shard_map/ppermute | solution.py:404
  15.9 1.3 %collective-permute-start.13 = (bf16[32,1024]{1,0:T(8,128)(2,1)}, bf16[32,1024]{1,0:T(8,128)(2,1)S(1)}, u32[]{:S(2)}, u32[]{:S(2)}) collective-permute-start(bf16[32,1024]{1,0:T(8,128)(2,1)} %get-tuple-element.45), channel_id=1, source_target_pairs={{0,10},{1,11},{2,8},{3,9},{4,14},{5,15},{6,12},{7,13},{8,2},{9,3},... | collective-permute-start | bytes 196616 | tf_op jit(solution)/shard_map/ppermute | solution.py:404
  17.2 3.7 %collective-permute-start.14 = (bf16[32,1024]{1,0:T(8,128)(2,1)}, bf16[32,1024]{1,0:T(8,128)(2,1)S(1)}, u32[]{:S(2)}, u32[]{:S(2)}) collective-permute-start(bf16[32,1024]{1,0:T(8,128)(2,1)} %get-tuple-element.46), channel_id=1, source_target_pairs={{0,15},{1,14},{2,13},{3,12},{4,11},{5,10},{6,9},{7,8},{8,7},{9,6},... | collective-permute-start | bytes 196616 | tf_op jit(solution)/shard_map/ppermute | solution.py:404
  20.9 0.0 collective-permute-done.10.refs_7_
  20.9 0.2 collective-permute-start.4
  21.1 2.5 %collective-permute-start.5 = (bf16[32,1024]{1,0:T(8,128)(2,1)}, bf16[32,1024]{1,0:T(8,128)(2,1)S(1)}, u32[]{:S(2)}, u32[]{:S(2)}) collective-permute-start(bf16[32,1024]{1,0:T(8,128)(2,1)} %get-tuple-element.37), channel_id=1, source_target_pairs={{0,11},{1,10},{2,9},{3,8},{4,15},{5,14},{6,13},{7,12},{8,3},{9,2},... | collective-permute-start | bytes 196616 | tf_op jit(solution)/shard_map/ppermute | solution.py:404
  23.6 0.0 collective-permute-done.12.refs_9_
  23.6 5.0 %collective-permute-start.6 = (bf16[32,1024]{1,0:T(8,128)(2,1)}, bf16[32,1024]{1,0:T(8,128)(2,1)S(1)}, u32[]{:S(2)}, u32[]{:S(2)}) collective-permute-start(bf16[32,1024]{1,0:T(8,128)(2,1)} %get-tuple-element.38), channel_id=1, source_target_pairs={{0,9},{1,8},{2,11},{3,10},{4,13},{5,12},{6,15},{7,14},{8,1},{9,0},... | collective-permute-start | bytes 196616 | tf_op jit(solution)/shard_map/ppermute | solution.py:404
  28.6 0.0 collective-permute-done.13.refs_10_
  28.6 0.1 collective-permute-start.7
  28.7 1.2 %collective-permute-start.8 = (bf16[32,1024]{1,0:T(8,128)(2,1)}, bf16[32,1024]{1,0:T(8,128)(2,1)S(1)}, u32[]{:S(2)}, u32[]{:S(2)}) collective-permute-start(bf16[32,1024]{1,0:T(8,128)(2,1)} %get-tuple-element.40), channel_id=1, source_target_pairs={{0,12},{1,13},{2,14},{3,15},{4,8},{5,9},{6,10},{7,11},{8,4},{9,5},... | collective-permute-start | bytes 196616 | tf_op jit(solution)/shard_map/ppermute | solution.py:404
  29.9 0.0 collective-permute-done.4.refs_1_
  29.9 1.8 %collective-permute-start.9 = (bf16[32,1024]{1,0:T(8,128)(2,1)}, bf16[32,1024]{1,0:T(8,128)(2,1)S(1)}, u32[]{:S(2)}, u32[]{:S(2)}) collective-permute-start(bf16[32,1024]{1,0:T(8,128)(2,1)} %get-tuple-element.41), channel_id=1, source_target_pairs={{0,6},{1,7},{2,4},{3,5},{4,2},{5,3},{6,0},{7,1},{8,14},{9,15},{10,... | collective-permute-start | bytes 196616 | tf_op jit(solution)/shard_map/ppermute | solution.py:404
  31.7 1.8 %collective-permute-done.5.refs_2_ = bf16[32,1024]{1,0:T(8,128)(2,1)S(1)} collective-permute-done((bf16[32,1024]{1,0:T(8,128)(2,1)}, bf16[32,1024]{1,0:T(8,128)(2,1)S(1)}, u32[]{:S(2)}, u32[]{:S(2)}) %collective-permute-start.5) | collective-permute-done | bytes 65568 | tf_op jit(solution)/shard_map/ppermute | solution.py:404
  33.4 1.4 %collective-permute-start = (bf16[32,1024]{1,0:T(8,128)(2,1)}, bf16[32,1024]{1,0:T(8,128)(2,1)S(1)}, u32[]{:S(2)}, u32[]{:S(2)}) collective-permute-start(bf16[32,1024]{1,0:T(8,128)(2,1)} %get-tuple-element.31), channel_id=1, source_target_pairs={{0,13},{1,12},{2,15},{3,14},{4,9},{5,8},{6,11},{7,10},{8,5},{9,4},... | collective-permute-start | bytes 196616 | tf_op jit(solution)/shard_map/ppermute | solution.py:404
  34.8 1.2 %collective-permute-start.1 = (bf16[32,1024]{1,0:T(8,128)(2,1)}, bf16[32,1024]{1,0:T(8,128)(2,1)S(1)}, u32[]{:S(2)}, u32[]{:S(2)}) collective-permute-start(bf16[32,1024]{1,0:T(8,128)(2,1)} %get-tuple-element.32), channel_id=1, source_target_pairs={{0,3},{1,2},{2,1},{3,0},{4,7},{5,6},{6,5},{7,4},{8,11},{9,10},{10,... | collective-permute-start | bytes 196616 | tf_op jit(solution)/shard_map/ppermute | solution.py:404
  36.0 0.0 collective-permute-done.8.refs_5_
  36.0 1.5 %collective-permute-start.3 = (bf16[32,1024]{1,0:T(8,128)(2,1)}, bf16[32,1024]{1,0:T(8,128)(2,1)S(1)}, u32[]{:S(2)}, u32[]{:S(2)}) collective-permute-start(bf16[32,1024]{1,0:T(8,128)(2,1)} %get-tuple-element.34), channel_id=1, source_target_pairs={{0,1},{1,0},{2,3},{3,2},{4,5},{5,4},{6,7},{7,6},{8,9},{9,8},{10,11... | collective-permute-start | bytes 196616 | tf_op jit(solution)/shard_map/ppermute | solution.py:404
  37.5 0.0 copy-start.3
  37.5 0.8 %copy-done.3 = bf16[32,1024]{1,0:T(8,128)(2,1)S(1)} copy-done((bf16[32,1024]{1,0:T(8,128)(2,1)S(1)}, bf16[32,1024]{1,0:T(8,128)(2,1)}, u32[]{:S(2)}) %copy-start.3) | copy-done | bytes 65560
  38.4 1.5 %early_rows.1 = (bf16[384,1024]{1,0:T(8,128)(2,1)S(1)}, bf16[384,256]{1,0:T(8,128)(2,1)S(1)}, bf16[384,256]{1,0:T(8,128)(2,1)S(1)}) custom-call(bf16[1024]{0:T(1024)(128)(2,1)S(1)} %copy-done.1, bf16[1024,512]{1,0:T(8,128)(2,1)S(1)} %copy-done, bf16[1024,1024]{1,0:T(8,128)(2,1)S(1)} %copy-done.2, bf16[32,1024]{1,0:T(8,128)(2,1)S(1)} %copy-done.3, ...), custom_call_target="tpu_custom_call" | custom-call | flops 1207959552 | bytes 4718592 | tf_op jit(solution)/shard_map/early_rows/pallas_call | solution.py:230
  39.9 1.5 %collective-permute-done.2.refs_2_ = bf16[32,1024]{1,0:T(8,128)(2,1)S(1)} collective-permute-done((bf16[32,1024]{1,0:T(8,128)(2,1)}, bf16[32,1024]{1,0:T(8,128)(2,1)S(1)}, u32[]{:S(2)}, u32[]{:S(2)}) %collective-permute-start.2) | collective-permute-done | bytes 65568 | tf_op jit(solution)/shard_map/ppermute | solution.py:404
  41.4 0.5 pairs.1
  41.9 2.2 %collective-permute-start.16 = (bf16[512,256]{1,0:T(8,128)(2,1)S(1)}, bf16[512,256]{1,0:T(8,128)(2,1)S(1)}, u32[]{:S(2)}, u32[]{:S(2)}) collective-permute-start(bf16[512,256]{1,0:T(8,128)(2,1)S(1)} %get-tuple-element.51.refs_0_), channel_id=1, source_target_pairs={{0,1},{1,2},{2,3},{3,4},{4,5},{5,6},{6,7},{7,8},{8,9},{9,10},{10,1... | collective-permute-start | bytes 786440 | tf_op jit(solution)/shard_map/ppermute | solution.py:27
  44.1 3.4 %collective-permute-start.15 = (bf16[512,256]{1,0:T(8,128)(2,1)S(1)}, bf16[512,256]{1,0:T(8,128)(2,1)S(1)}, u32[]{:S(2)}, u32[]{:S(2)}) collective-permute-start(bf16[512,256]{1,0:T(8,128)(2,1)S(1)} %get-tuple-element.52.refs_1_), channel_id=1, source_target_pairs={{0,1},{1,2},{2,3},{3,4},{4,5},{5,6},{6,7},{7,8},{8,9},{9,10},{10,1... | collective-permute-start | bytes 786440 | tf_op jit(solution)/shard_map/ppermute | solution.py:27
  47.6 3.1 %own_frame.1 = (bf16[512,1024]{1,0:T(8,128)(2,1)S(1)}, f32[512,1024]{1,0:T(8,128)S(1)}, f32[512,1024]{1,0:T(8,128)S(1)}, f32[512,1024]{1,0:T(8,128)S(1)}) custom-call(bf16[128,1024]{1,0:T(8,128)(2,1)S(1)} %get-tuple-element.49.normed_ref, bf16[1024,1024]{1,0:T(8,128)(2,1)S(1)} %copy-done.2, bf16[384,1024]{1,0:T(8,128)(2,1)S(1)} %get-tuple-element.50.early_ref, ...), custom_call_target="tpu_custom_call" | custom-call | flops 2147483648 | bytes 6291456 | tf_op jit(solution)/shard_map/own_frame/pallas_call | solution.py:309
  50.6 0.0 collective-permute-done.16.pairs_ref
  50.6 1.7 %earlier_frame.2.refs_0_ = bf16[512,512]{1,0:T(8,128)(2,1)S(1)} custom-call(bf16[512,1024]{1,0:T(8,128)(2,1)S(1)} %get-tuple-element.53.query_ref, bf16[512,256]{1,0:T(8,128)(2,1)S(1)} %collective-permute-done.16.pairs_ref, f32[512,1024]{1,0:T(8,128)S(1)} %get-tuple-element.54.sum_ref, f32[512,1024]{1,0:T(8,128)S(1)} %get-tuple-element.55.total_ref, ...), custom_call_target="tpu_custom_call" | custom-call | flops 536870912 | bytes 5242880 | tf_op jit(solution)/shard_map/earlier_frame/pallas_call | solution.py:388
  52.4 2.5 %earlier_frame.3 = bf16[512,1024]{1,0:T(8,128)(2,1)} custom-call(bf16[512,1024]{1,0:T(8,128)(2,1)S(1)} %get-tuple-element.53.query_ref, bf16[512,256]{1,0:T(8,128)(2,1)S(1)} %collective-permute-done.15.pairs_ref, f32[512,1024]{1,0:T(8,128)S(1)} %get-tuple-element.54.sum_ref, f32[512,1024]{1,0:T(8,128)S(1)} %get-tuple-element.55.total_ref, ...), custom_call_target="tpu_custom_call" | custom-call | flops 536870912 | bytes 5242880 | tf_op jit(solution)/shard_map/earlier_frame/pallas_call | solution.py:388
  (16 shorter events, 0.0 us)
Async XLA Ops:
  0.0 37.5 %copy-start = (bf16[1024,512]{1,0:T(8,128)(2,1)S(1)}, bf16[1024,512]{1,0:T(8,128)(2,1)}, u32[]{:S(2)}) copy-start(bf16[1024,512]{1,0:T(8,128)(2,1)} %w_kv_ref.3) | copy-start | bytes 3145732
  0.0 37.5 %copy-start.1 = (bf16[1024]{0:T(1024)(128)(2,1)S(1)}, bf16[1024]{0:T(1024)(128)(2,1)}, u32[]{:S(2)}) copy-start(bf16[1024]{0:T(1024)(128)(2,1)} %gain_ref.3) | copy-start | bytes 6148
  0.0 37.5 %copy-start.2 = (bf16[1024,1024]{1,0:T(8,128)(2,1)S(1)}, bf16[1024,1024]{1,0:T(8,128)(2,1)}, u32[]{:S(2)}) copy-start(bf16[1024,1024]{1,0:T(8,128)(2,1)} %w_ref.1) | copy-start | bytes 6291460
  10.5 10.5 %collective-permute-start.10 = (bf16[32,1024]{1,0:T(8,128)(2,1)}, bf16[32,1024]{1,0:T(8,128)(2,1)S(1)}, u32[]{:S(2)}, u32[]{:S(2)}) collective-permute-start(bf16[32,1024]{1,0:T(8,128)(2,1)} %get-tuple-element.42), channel_id=1, source_target_pairs={{0,4},{1,5},{2,6},{3,7},{4,0},{5,1},{6,2},{7,3},{8,12},{9,13},{10,... | collective-permute-start | bytes 196616 | tf_op jit(solution)/shard_map/ppermute | solution.py:404
  12.6 8.5 %collective-permute-start.11 = (bf16[32,1024]{1,0:T(8,128)(2,1)}, bf16[32,1024]{1,0:T(8,128)(2,1)S(1)}, u32[]{:S(2)}, u32[]{:S(2)}) collective-permute-start(bf16[32,1024]{1,0:T(8,128)(2,1)} %get-tuple-element.43), channel_id=1, source_target_pairs={{0,8},{1,9},{2,10},{3,11},{4,12},{5,13},{6,14},{7,15},{8,0},{9,1},... | collective-permute-start | bytes 196616 | tf_op jit(solution)/shard_map/ppermute | solution.py:404
  15.0 8.7 %collective-permute-start.12 = (bf16[32,1024]{1,0:T(8,128)(2,1)}, bf16[32,1024]{1,0:T(8,128)(2,1)S(1)}, u32[]{:S(2)}, u32[]{:S(2)}) collective-permute-start(bf16[32,1024]{1,0:T(8,128)(2,1)} %get-tuple-element.44), channel_id=1, source_target_pairs={{0,14},{1,15},{2,12},{3,13},{4,10},{5,11},{6,8},{7,9},{8,6},{9,7},... | collective-permute-start | bytes 196616 | tf_op jit(solution)/shard_map/ppermute | solution.py:404
  15.9 12.8 %collective-permute-start.13 = (bf16[32,1024]{1,0:T(8,128)(2,1)}, bf16[32,1024]{1,0:T(8,128)(2,1)S(1)}, u32[]{:S(2)}, u32[]{:S(2)}) collective-permute-start(bf16[32,1024]{1,0:T(8,128)(2,1)} %get-tuple-element.45), channel_id=1, source_target_pairs={{0,10},{1,11},{2,8},{3,9},{4,14},{5,15},{6,12},{7,13},{8,2},{9,3},... | collective-permute-start | bytes 196616 | tf_op jit(solution)/shard_map/ppermute | solution.py:404
  17.2 11.5 %collective-permute-start.14 = (bf16[32,1024]{1,0:T(8,128)(2,1)}, bf16[32,1024]{1,0:T(8,128)(2,1)S(1)}, u32[]{:S(2)}, u32[]{:S(2)}) collective-permute-start(bf16[32,1024]{1,0:T(8,128)(2,1)} %get-tuple-element.46), channel_id=1, source_target_pairs={{0,15},{1,14},{2,13},{3,12},{4,11},{5,10},{6,9},{7,8},{8,7},{9,6},... | collective-permute-start | bytes 196616 | tf_op jit(solution)/shard_map/ppermute | solution.py:404
  20.9 8.9 %collective-permute-start.4 = (bf16[32,1024]{1,0:T(8,128)(2,1)}, bf16[32,1024]{1,0:T(8,128)(2,1)S(1)}, u32[]{:S(2)}, u32[]{:S(2)}) collective-permute-start(bf16[32,1024]{1,0:T(8,128)(2,1)} %get-tuple-element.36), channel_id=1, source_target_pairs={{0,5},{1,4},{2,7},{3,6},{4,1},{5,0},{6,3},{7,2},{8,13},{9,12},{10,... | collective-permute-start | bytes 196616 | tf_op jit(solution)/shard_map/ppermute | solution.py:404
  21.1 12.3 %collective-permute-start.5 = (bf16[32,1024]{1,0:T(8,128)(2,1)}, bf16[32,1024]{1,0:T(8,128)(2,1)S(1)}, u32[]{:S(2)}, u32[]{:S(2)}) collective-permute-start(bf16[32,1024]{1,0:T(8,128)(2,1)} %get-tuple-element.37), channel_id=1, source_target_pairs={{0,11},{1,10},{2,9},{3,8},{4,15},{5,14},{6,13},{7,12},{8,3},{9,2},... | collective-permute-start | bytes 196616 | tf_op jit(solution)/shard_map/ppermute | solution.py:404
  23.6 11.2 %collective-permute-start.6 = (bf16[32,1024]{1,0:T(8,128)(2,1)}, bf16[32,1024]{1,0:T(8,128)(2,1)S(1)}, u32[]{:S(2)}, u32[]{:S(2)}) collective-permute-start(bf16[32,1024]{1,0:T(8,128)(2,1)} %get-tuple-element.38), channel_id=1, source_target_pairs={{0,9},{1,8},{2,11},{3,10},{4,13},{5,12},{6,15},{7,14},{8,1},{9,0},... | collective-permute-start | bytes 196616 | tf_op jit(solution)/shard_map/ppermute | solution.py:404
  28.6 7.4 %collective-permute-start.7 = (bf16[32,1024]{1,0:T(8,128)(2,1)}, bf16[32,1024]{1,0:T(8,128)(2,1)S(1)}, u32[]{:S(2)}, u32[]{:S(2)}) collective-permute-start(bf16[32,1024]{1,0:T(8,128)(2,1)} %get-tuple-element.39), channel_id=1, source_target_pairs={{0,2},{1,3},{2,0},{3,1},{4,6},{5,7},{6,4},{7,5},{8,10},{9,11},{10,... | collective-permute-start | bytes 196616 | tf_op jit(solution)/shard_map/ppermute | solution.py:404
  28.7 7.3 %collective-permute-start.8 = (bf16[32,1024]{1,0:T(8,128)(2,1)}, bf16[32,1024]{1,0:T(8,128)(2,1)S(1)}, u32[]{:S(2)}, u32[]{:S(2)}) collective-permute-start(bf16[32,1024]{1,0:T(8,128)(2,1)} %get-tuple-element.40), channel_id=1, source_target_pairs={{0,12},{1,13},{2,14},{3,15},{4,8},{5,9},{6,10},{7,11},{8,4},{9,5},... | collective-permute-start | bytes 196616 | tf_op jit(solution)/shard_map/ppermute | solution.py:404
  29.9 7.7 %collective-permute-start.9 = (bf16[32,1024]{1,0:T(8,128)(2,1)}, bf16[32,1024]{1,0:T(8,128)(2,1)S(1)}, u32[]{:S(2)}, u32[]{:S(2)}) collective-permute-start(bf16[32,1024]{1,0:T(8,128)(2,1)} %get-tuple-element.41), channel_id=1, source_target_pairs={{0,6},{1,7},{2,4},{3,5},{4,2},{5,3},{6,0},{7,1},{8,14},{9,15},{10,... | collective-permute-start | bytes 196616 | tf_op jit(solution)/shard_map/ppermute | solution.py:404
  33.4 6.5 %collective-permute-start = (bf16[32,1024]{1,0:T(8,128)(2,1)}, bf16[32,1024]{1,0:T(8,128)(2,1)S(1)}, u32[]{:S(2)}, u32[]{:S(2)}) collective-permute-start(bf16[32,1024]{1,0:T(8,128)(2,1)} %get-tuple-element.31), channel_id=1, source_target_pairs={{0,13},{1,12},{2,15},{3,14},{4,9},{5,8},{6,11},{7,10},{8,5},{9,4},... | collective-permute-start | bytes 196616 | tf_op jit(solution)/shard_map/ppermute | solution.py:404
  34.8 5.1 %collective-permute-start.1 = (bf16[32,1024]{1,0:T(8,128)(2,1)}, bf16[32,1024]{1,0:T(8,128)(2,1)S(1)}, u32[]{:S(2)}, u32[]{:S(2)}) collective-permute-start(bf16[32,1024]{1,0:T(8,128)(2,1)} %get-tuple-element.32), channel_id=1, source_target_pairs={{0,3},{1,2},{2,1},{3,0},{4,7},{5,6},{6,5},{7,4},{8,11},{9,10},{10,... | collective-permute-start | bytes 196616 | tf_op jit(solution)/shard_map/ppermute | solution.py:404
  36.0 5.4 %collective-permute-start.2 = (bf16[32,1024]{1,0:T(8,128)(2,1)}, bf16[32,1024]{1,0:T(8,128)(2,1)S(1)}, u32[]{:S(2)}, u32[]{:S(2)}) collective-permute-start(bf16[32,1024]{1,0:T(8,128)(2,1)} %get-tuple-element.33), channel_id=1, source_target_pairs={{0,7},{1,6},{2,5},{3,4},{4,3},{5,2},{6,1},{7,0},{8,15},{9,14},{10,... | collective-permute-start | bytes 196616 | tf_op jit(solution)/shard_map/ppermute | solution.py:404
  36.0 5.4 %collective-permute-start.3 = (bf16[32,1024]{1,0:T(8,128)(2,1)}, bf16[32,1024]{1,0:T(8,128)(2,1)S(1)}, u32[]{:S(2)}, u32[]{:S(2)}) collective-permute-start(bf16[32,1024]{1,0:T(8,128)(2,1)} %get-tuple-element.34), channel_id=1, source_target_pairs={{0,1},{1,0},{2,3},{3,2},{4,5},{5,4},{6,7},{7,6},{8,9},{9,8},{10,11... | collective-permute-start | bytes 196616 | tf_op jit(solution)/shard_map/ppermute | solution.py:404
  37.5 0.8 %copy-start.3 = (bf16[32,1024]{1,0:T(8,128)(2,1)S(1)}, bf16[32,1024]{1,0:T(8,128)(2,1)}, u32[]{:S(2)}) copy-start(bf16[32,1024]{1,0:T(8,128)(2,1)} %get-tuple-element.35.refs_0_) | copy-start | bytes 196612
  41.9 8.7 %collective-permute-start.16 = (bf16[512,256]{1,0:T(8,128)(2,1)S(1)}, bf16[512,256]{1,0:T(8,128)(2,1)S(1)}, u32[]{:S(2)}, u32[]{:S(2)}) collective-permute-start(bf16[512,256]{1,0:T(8,128)(2,1)S(1)} %get-tuple-element.51.refs_0_), channel_id=1, source_target_pairs={{0,1},{1,2},{2,3},{3,4},{4,5},{5,6},{6,7},{7,8},{8,9},{9,10},{10,1... | collective-permute-start | bytes 786440 | tf_op jit(solution)/shard_map/ppermute | solution.py:27
  44.1 8.2 %collective-permute-start.15 = (bf16[512,256]{1,0:T(8,128)(2,1)S(1)}, bf16[512,256]{1,0:T(8,128)(2,1)S(1)}, u32[]{:S(2)}, u32[]{:S(2)}) collective-permute-start(bf16[512,256]{1,0:T(8,128)(2,1)S(1)} %get-tuple-element.52.refs_1_), channel_id=1, source_target_pairs={{0,1},{1,2},{2,3},{3,4},{4,5},{5,6},{6,7},{7,8},{8,9},{9,10},{10,1... | collective-permute-start | bytes 786440 | tf_op jit(solution)/shard_map/ppermute | solution.py:27

commit v22 on v21

--- a/solution.py
+++ b/solution.py
@@ -14,7 +14,7 @@
 SB = 16
 SPAN = 128
 GROUPS = ((0, 4), (4, 8))
-APART = (0, 5, 11, 9, 2, 12, 6, 4, 8, 14, 10, 15, 13, 3, 7, 1)
+APART = (0, 5, 11, 9, 2, 12, 6, 8, 14, 4, 10, 15, 13, 3, 7, 1)
 EARLY = SB - 4
 
 epsilon = 1e-06

time: 55.2 us -> 54.9 us (level)
  transfers between devices with their start and end apart: 17 -> 17, of which waited for: 2 -> 2; matrix products, arithmetic and copies ran while one was open for 0% -> 0% of each run, Pallas kernels for 11% -> 12%
where the time goes in v22:
time: 54.9 us; the launch traced here: 54.7 us
  starting transfers between devices  30.5 us (56%)
  Pallas kernels  19.7 us (36%)
  waiting for transfers between devices  3.45 us (6%)
  local copies, waits for them, and re-layouts  0.85 us (2%)
    ppermute x15, starting transfers between devices, swap(): return lax.ppermute(tile, 'tm', route)  24.8 us
    pallas_call x1, Pallas kernels, mixer(): pl.pallas_call(functools.partial(mixer_kernel, state is not None), in_spe...  10.4 us
    ppermute x2, starting transfers between devices, shifted(): return lax.ppermute(block, axis, route)  5.63 us
    pallas_call x2, Pallas kernels, earlier_frame(): pl.pallas_call(functools.partial(earlier_kernel, group), compiler_params=...  4.19 us
    ppermute x15, waiting for transfers between devices, swap(): return lax.ppermute(tile, 'tm', route)  3.44 us
    pallas_call x1, Pallas kernels, own_frame(): pl.pallas_call(own_kernel, out_shape=[jax.ShapeDtypeStruct((rows, width),...  3.06 us
    pallas_call x1, Pallas kernels, make_early(): pl.pallas_call(early_kernel, out_shape=[jax.ShapeDtypeStruct((rows, w_que...  1.53 us
  transfers between devices with their start and end apart: 17, of which 2 were waited for; matrix products, arithmetic and copies ran while one was open for 0% of the time, Pallas kernels for 12%

profile of v22, /device:TPU:1, one launch (start us, length us, event | category | flops | bytes accessed | tf_op | source)
XLA Modules:
  0.0 54.7 jit_solution(16617430269613103321)
XLA Ops:
  0.0 10.4 %mixer.1 = (bf16[32,1024]{1,0:T(8,128)(2,1)}, bf16[32,1024]{1,0:T(8,128)(2,1)}, bf16[32,1024]{1,0:T(8,128)(2,1)}, bf16[32,1024]{1,0:T(8,128)(2,1)}, bf16[32,1024...) custom-call(bf16[512,1024]{1,0:T(8,128)(2,1)} %bitcast.2, ...), custom_call_target="tpu_custom_call" | custom-call | flops 3758096384 | bytes 8388608 | tf_op jit(solution)/shard_map/mixer/pallas_call | solution.py:155
  10.5 3.2 %collective-permute-start.10 = (bf16[32,1024]{1,0:T(8,128)(2,1)}, bf16[32,1024]{1,0:T(8,128)(2,1)S(1)}, u32[]{:S(2)}, u32[]{:S(2)}) collective-permute-start(bf16[32,1024]{1,0:T(8,128)(2,1)} %get-tuple-element.42), channel_id=1, source_target_pairs={{0,8},{1,9},{2,10},{3,11},{4,12},{5,13},{6,14},{7,15},{8,0},{9,1},... | collective-permute-start | bytes 196616 | tf_op jit(solution)/shard_map/ppermute | solution.py:404
  13.7 2.0 %collective-permute-start.11 = (bf16[32,1024]{1,0:T(8,128)(2,1)}, bf16[32,1024]{1,0:T(8,128)(2,1)S(1)}, u32[]{:S(2)}, u32[]{:S(2)}) collective-permute-start(bf16[32,1024]{1,0:T(8,128)(2,1)} %get-tuple-element.43), channel_id=1, source_target_pairs={{0,14},{1,15},{2,12},{3,13},{4,10},{5,11},{6,8},{7,9},{8,6},{9,7},... | collective-permute-start | bytes 196616 | tf_op jit(solution)/shard_map/ppermute | solution.py:404
  15.7 2.4 %collective-permute-start.13 = (bf16[32,1024]{1,0:T(8,128)(2,1)}, bf16[32,1024]{1,0:T(8,128)(2,1)S(1)}, u32[]{:S(2)}, u32[]{:S(2)}) collective-permute-start(bf16[32,1024]{1,0:T(8,128)(2,1)} %get-tuple-element.45), channel_id=1, source_target_pairs={{0,10},{1,11},{2,8},{3,9},{4,14},{5,15},{6,12},{7,13},{8,2},{9,3},... | collective-permute-start | bytes 196616 | tf_op jit(solution)/shard_map/ppermute | solution.py:404
  18.1 3.7 %collective-permute-start.14 = (bf16[32,1024]{1,0:T(8,128)(2,1)}, bf16[32,1024]{1,0:T(8,128)(2,1)S(1)}, u32[]{:S(2)}, u32[]{:S(2)}) collective-permute-start(bf16[32,1024]{1,0:T(8,128)(2,1)} %get-tuple-element.46), channel_id=1, source_target_pairs={{0,15},{1,14},{2,13},{3,12},{4,11},{5,10},{6,9},{7,8},{8,7},{9,6},... | collective-permute-start | bytes 196616 | tf_op jit(solution)/shard_map/ppermute | solution.py:404
  21.8 0.0 collective-permute-done.11.refs_8_
  21.8 5.0 %collective-permute-start.5 = (bf16[32,1024]{1,0:T(8,128)(2,1)}, bf16[32,1024]{1,0:T(8,128)(2,1)S(1)}, u32[]{:S(2)}, u32[]{:S(2)}) collective-permute-start(bf16[32,1024]{1,0:T(8,128)(2,1)} %get-tuple-element.37), channel_id=1, source_target_pairs={{0,11},{1,10},{2,9},{3,8},{4,15},{5,14},{6,13},{7,12},{8,3},{9,2},... | collective-permute-start | bytes 196616 | tf_op jit(solution)/shard_map/ppermute | solution.py:404
  26.8 0.0 collective-permute-done.12.refs_9_
  26.8 0.7 %collective-permute-start.6 = (bf16[32,1024]{1,0:T(8,128)(2,1)}, bf16[32,1024]{1,0:T(8,128)(2,1)S(1)}, u32[]{:S(2)}, u32[]{:S(2)}) collective-permute-start(bf16[32,1024]{1,0:T(8,128)(2,1)} %get-tuple-element.38), channel_id=1, source_target_pairs={{0,9},{1,8},{2,11},{3,10},{4,13},{5,12},{6,15},{7,14},{8,1},{9,0},... | collective-permute-start | bytes 196616 | tf_op jit(solution)/shard_map/ppermute | solution.py:404
  27.5 1.2 %collective-permute-start.7 = (bf16[32,1024]{1,0:T(8,128)(2,1)}, bf16[32,1024]{1,0:T(8,128)(2,1)S(1)}, u32[]{:S(2)}, u32[]{:S(2)}) collective-permute-start(bf16[32,1024]{1,0:T(8,128)(2,1)} %get-tuple-element.39), channel_id=1, source_target_pairs={{0,2},{1,3},{2,0},{3,1},{4,6},{5,7},{6,4},{7,5},{8,10},{9,11},{10,... | collective-permute-start | bytes 196616 | tf_op jit(solution)/shard_map/ppermute | solution.py:404
  28.8 0.0 collective-permute-done.14.refs_11_
  28.8 0.2 collective-permute-start.8
  29.0 0.0 collective-permute-done.4.refs_1_
  29.0 1.8 %collective-permute-start.9 = (bf16[32,1024]{1,0:T(8,128)(2,1)}, bf16[32,1024]{1,0:T(8,128)(2,1)S(1)}, u32[]{:S(2)}, u32[]{:S(2)}) collective-permute-start(bf16[32,1024]{1,0:T(8,128)(2,1)} %get-tuple-element.41), channel_id=1, source_target_pairs={{0,6},{1,7},{2,4},{3,5},{4,2},{5,3},{6,0},{7,1},{8,14},{9,15},{10,... | collective-permute-start | bytes 196616 | tf_op jit(solution)/shard_map/ppermute | solution.py:404
  30.8 1.1 %collective-permute-done.5.refs_2_ = bf16[32,1024]{1,0:T(8,128)(2,1)S(1)} collective-permute-done((bf16[32,1024]{1,0:T(8,128)(2,1)}, bf16[32,1024]{1,0:T(8,128)(2,1)S(1)}, u32[]{:S(2)}, u32[]{:S(2)}) %collective-permute-start.5) | collective-permute-done | bytes 65568 | tf_op jit(solution)/shard_map/ppermute | solution.py:404
  31.9 1.6 %collective-permute-start = (bf16[32,1024]{1,0:T(8,128)(2,1)}, bf16[32,1024]{1,0:T(8,128)(2,1)S(1)}, u32[]{:S(2)}, u32[]{:S(2)}) collective-permute-start(bf16[32,1024]{1,0:T(8,128)(2,1)} %get-tuple-element.31), channel_id=1, source_target_pairs={{0,13},{1,12},{2,15},{3,14},{4,9},{5,8},{6,11},{7,10},{8,5},{9,4},... | collective-permute-start | bytes 196616 | tf_op jit(solution)/shard_map/ppermute | solution.py:404
  33.5 2.7 %collective-permute-start.1 = (bf16[32,1024]{1,0:T(8,128)(2,1)}, bf16[32,1024]{1,0:T(8,128)(2,1)S(1)}, u32[]{:S(2)}, u32[]{:S(2)}) collective-permute-start(bf16[32,1024]{1,0:T(8,128)(2,1)} %get-tuple-element.32), channel_id=1, source_target_pairs={{0,3},{1,2},{2,1},{3,0},{4,7},{5,6},{6,5},{7,4},{8,11},{9,10},{10,... | collective-permute-start | bytes 196616 | tf_op jit(solution)/shard_map/ppermute | solution.py:404
  36.2 0.2 collective-permute-start.3
  36.4 0.0 collective-permute-done.9.refs_6_
  36.4 0.0 copy-start.3
  36.5 0.8 %copy-done.3 = bf16[32,1024]{1,0:T(8,128)(2,1)S(1)} copy-done((bf16[32,1024]{1,0:T(8,128)(2,1)S(1)}, bf16[32,1024]{1,0:T(8,128)(2,1)}, u32[]{:S(2)}) %copy-start.3) | copy-done | bytes 65560
  37.3 1.5 %early_rows.1 = (bf16[384,1024]{1,0:T(8,128)(2,1)S(1)}, bf16[384,256]{1,0:T(8,128)(2,1)S(1)}, bf16[384,256]{1,0:T(8,128)(2,1)S(1)}) custom-call(bf16[1024]{0:T(1024)(128)(2,1)S(1)} %copy-done.1, bf16[1024,512]{1,0:T(8,128)(2,1)S(1)} %copy-done, bf16[1024,1024]{1,0:T(8,128)(2,1)S(1)} %copy-done.2, bf16[32,1024]{1,0:T(8,128)(2,1)S(1)} %copy-done.3, ...), custom_call_target="tpu_custom_call" | custom-call | flops 1207959552 | bytes 4718592 | tf_op jit(solution)/shard_map/early_rows/pallas_call | solution.py:230
  38.8 0.0 collective-permute-done.refs_0_
  38.8 2.3 %collective-permute-done.2.refs_2_ = bf16[32,1024]{1,0:T(8,128)(2,1)S(1)} collective-permute-done((bf16[32,1024]{1,0:T(8,128)(2,1)}, bf16[32,1024]{1,0:T(8,128)(2,1)S(1)}, u32[]{:S(2)}, u32[]{:S(2)}) %collective-permute-start.2) | collective-permute-done | bytes 65568 | tf_op jit(solution)/shard_map/ppermute | solution.py:404
  41.2 0.0 collective-permute-done.3.refs_3_
  41.2 0.5 pairs.1
  41.6 2.0 %collective-permute-start.16 = (bf16[512,256]{1,0:T(8,128)(2,1)S(1)}, bf16[512,256]{1,0:T(8,128)(2,1)S(1)}, u32[]{:S(2)}, u32[]{:S(2)}) collective-permute-start(bf16[512,256]{1,0:T(8,128)(2,1)S(1)} %get-tuple-element.51.refs_0_), channel_id=1, source_target_pairs={{0,1},{1,2},{2,3},{3,4},{4,5},{5,6},{6,7},{7,8},{8,9},{9,10},{10,1... | collective-permute-start | bytes 786440 | tf_op jit(solution)/shard_map/ppermute | solution.py:27
  43.7 3.6 %collective-permute-start.15 = (bf16[512,256]{1,0:T(8,128)(2,1)S(1)}, bf16[512,256]{1,0:T(8,128)(2,1)S(1)}, u32[]{:S(2)}, u32[]{:S(2)}) collective-permute-start(bf16[512,256]{1,0:T(8,128)(2,1)S(1)} %get-tuple-element.52.refs_1_), channel_id=1, source_target_pairs={{0,1},{1,2},{2,3},{3,4},{4,5},{5,6},{6,7},{7,8},{8,9},{9,10},{10,1... | collective-permute-start | bytes 786440 | tf_op jit(solution)/shard_map/ppermute | solution.py:27
  47.3 3.1 %own_frame.1 = (bf16[512,1024]{1,0:T(8,128)(2,1)S(1)}, f32[512,1024]{1,0:T(8,128)S(1)}, f32[512,1024]{1,0:T(8,128)S(1)}, f32[512,1024]{1,0:T(8,128)S(1)}) custom-call(bf16[128,1024]{1,0:T(8,128)(2,1)S(1)} %get-tuple-element.49.normed_ref, bf16[1024,1024]{1,0:T(8,128)(2,1)S(1)} %copy-done.2, bf16[384,1024]{1,0:T(8,128)(2,1)S(1)} %get-tuple-element.50.early_ref, ...), custom_call_target="tpu_custom_call" | custom-call | flops 2147483648 | bytes 6291456 | tf_op jit(solution)/shard_map/own_frame/pallas_call | solution.py:309
  50.3 0.0 collective-permute-done.16.pairs_ref
  50.4 1.7 %earlier_frame.2.refs_0_ = bf16[512,512]{1,0:T(8,128)(2,1)S(1)} custom-call(bf16[512,1024]{1,0:T(8,128)(2,1)S(1)} %get-tuple-element.53.query_ref, bf16[512,256]{1,0:T(8,128)(2,1)S(1)} %collective-permute-done.16.pairs_ref, f32[512,1024]{1,0:T(8,128)S(1)} %get-tuple-element.54.sum_ref, f32[512,1024]{1,0:T(8,128)S(1)} %get-tuple-element.55.total_ref, ...), custom_call_target="tpu_custom_call" | custom-call | flops 536870912 | bytes 5242880 | tf_op jit(solution)/shard_map/earlier_frame/pallas_call | solution.py:388
  52.1 2.5 %earlier_frame.3 = bf16[512,1024]{1,0:T(8,128)(2,1)} custom-call(bf16[512,1024]{1,0:T(8,128)(2,1)S(1)} %get-tuple-element.53.query_ref, bf16[512,256]{1,0:T(8,128)(2,1)S(1)} %collective-permute-done.15.pairs_ref, f32[512,1024]{1,0:T(8,128)S(1)} %get-tuple-element.54.sum_ref, f32[512,1024]{1,0:T(8,128)S(1)} %get-tuple-element.55.total_ref, ...), custom_call_target="tpu_custom_call" | custom-call | flops 536870912 | bytes 5242880 | tf_op jit(solution)/shard_map/earlier_frame/pallas_call | solution.py:388
  (16 shorter events, 0.0 us)
Async XLA Ops:
  0.0 36.4 %copy-start = (bf16[1024,512]{1,0:T(8,128)(2,1)S(1)}, bf16[1024,512]{1,0:T(8,128)(2,1)}, u32[]{:S(2)}) copy-start(bf16[1024,512]{1,0:T(8,128)(2,1)} %w_kv_ref.3) | copy-start | bytes 3145732
  0.0 36.4 %copy-start.1 = (bf16[1024]{0:T(1024)(128)(2,1)S(1)}, bf16[1024]{0:T(1024)(128)(2,1)}, u32[]{:S(2)}) copy-start(bf16[1024]{0:T(1024)(128)(2,1)} %gain_ref.3) | copy-start | bytes 6148
  0.0 36.4 %copy-start.2 = (bf16[1024,1024]{1,0:T(8,128)(2,1)S(1)}, bf16[1024,1024]{1,0:T(8,128)(2,1)}, u32[]{:S(2)}) copy-start(bf16[1024,1024]{1,0:T(8,128)(2,1)} %w_ref.1) | copy-start | bytes 6291460
  10.5 11.4 %collective-permute-start.10 = (bf16[32,1024]{1,0:T(8,128)(2,1)}, bf16[32,1024]{1,0:T(8,128)(2,1)S(1)}, u32[]{:S(2)}, u32[]{:S(2)}) collective-permute-start(bf16[32,1024]{1,0:T(8,128)(2,1)} %get-tuple-element.42), channel_id=1, source_target_pairs={{0,8},{1,9},{2,10},{3,11},{4,12},{5,13},{6,14},{7,15},{8,0},{9,1},... | collective-permute-start | bytes 196616 | tf_op jit(solution)/shard_map/ppermute | solution.py:404
  13.7 8.2 %collective-permute-start.11 = (bf16[32,1024]{1,0:T(8,128)(2,1)}, bf16[32,1024]{1,0:T(8,128)(2,1)S(1)}, u32[]{:S(2)}, u32[]{:S(2)}) collective-permute-start(bf16[32,1024]{1,0:T(8,128)(2,1)} %get-tuple-element.43), channel_id=1, source_target_pairs={{0,14},{1,15},{2,12},{3,13},{4,10},{5,11},{6,8},{7,9},{8,6},{9,7},... | collective-permute-start | bytes 196616 | tf_op jit(solution)/shard_map/ppermute | solution.py:404
  15.7 11.1 %collective-permute-start.12 = (bf16[32,1024]{1,0:T(8,128)(2,1)}, bf16[32,1024]{1,0:T(8,128)(2,1)S(1)}, u32[]{:S(2)}, u32[]{:S(2)}) collective-permute-start(bf16[32,1024]{1,0:T(8,128)(2,1)} %get-tuple-element.44), channel_id=1, source_target_pairs={{0,4},{1,5},{2,6},{3,7},{4,0},{5,1},{6,2},{7,3},{8,12},{9,13},{10,... | collective-permute-start | bytes 196616 | tf_op jit(solution)/shard_map/ppermute | solution.py:404
  15.7 11.8 %collective-permute-start.13 = (bf16[32,1024]{1,0:T(8,128)(2,1)}, bf16[32,1024]{1,0:T(8,128)(2,1)S(1)}, u32[]{:S(2)}, u32[]{:S(2)}) collective-permute-start(bf16[32,1024]{1,0:T(8,128)(2,1)} %get-tuple-element.45), channel_id=1, source_target_pairs={{0,10},{1,11},{2,8},{3,9},{4,14},{5,15},{6,12},{7,13},{8,2},{9,3},... | collective-permute-start | bytes 196616 | tf_op jit(solution)/shard_map/ppermute | solution.py:404
  18.1 10.7 %collective-permute-start.14 = (bf16[32,1024]{1,0:T(8,128)(2,1)}, bf16[32,1024]{1,0:T(8,128)(2,1)S(1)}, u32[]{:S(2)}, u32[]{:S(2)}) collective-permute-start(bf16[32,1024]{1,0:T(8,128)(2,1)} %get-tuple-element.46), channel_id=1, source_target_pairs={{0,15},{1,14},{2,13},{3,12},{4,11},{5,10},{6,9},{7,8},{8,7},{9,6},... | collective-permute-start | bytes 196616 | tf_op jit(solution)/shard_map/ppermute | solution.py:404
  21.8 7.2 %collective-permute-start.4 = (bf16[32,1024]{1,0:T(8,128)(2,1)}, bf16[32,1024]{1,0:T(8,128)(2,1)S(1)}, u32[]{:S(2)}, u32[]{:S(2)}) collective-permute-start(bf16[32,1024]{1,0:T(8,128)(2,1)} %get-tuple-element.36), channel_id=1, source_target_pairs={{0,5},{1,4},{2,7},{3,6},{4,1},{5,0},{6,3},{7,2},{8,13},{9,12},{10,... | collective-permute-start | bytes 196616 | tf_op jit(solution)/shard_map/ppermute | solution.py:404
  21.8 10.1 %collective-permute-start.5 = (bf16[32,1024]{1,0:T(8,128)(2,1)}, bf16[32,1024]{1,0:T(8,128)(2,1)S(1)}, u32[]{:S(2)}, u32[]{:S(2)}) collective-permute-start(bf16[32,1024]{1,0:T(8,128)(2,1)} %get-tuple-element.37), channel_id=1, source_target_pairs={{0,11},{1,10},{2,9},{3,8},{4,15},{5,14},{6,13},{7,12},{8,3},{9,2},... | collective-permute-start | bytes 196616 | tf_op jit(solution)/shard_map/ppermute | solution.py:404
  26.8 6.6 %collective-permute-start.6 = (bf16[32,1024]{1,0:T(8,128)(2,1)}, bf16[32,1024]{1,0:T(8,128)(2,1)S(1)}, u32[]{:S(2)}, u32[]{:S(2)}) collective-permute-start(bf16[32,1024]{1,0:T(8,128)(2,1)} %get-tuple-element.38), channel_id=1, source_target_pairs={{0,9},{1,8},{2,11},{3,10},{4,13},{5,12},{6,15},{7,14},{8,1},{9,0},... | collective-permute-start | bytes 196616 | tf_op jit(solution)/shard_map/ppermute | solution.py:404
  27.5 8.7 %collective-permute-start.7 = (bf16[32,1024]{1,0:T(8,128)(2,1)}, bf16[32,1024]{1,0:T(8,128)(2,1)S(1)}, u32[]{:S(2)}, u32[]{:S(2)}) collective-permute-start(bf16[32,1024]{1,0:T(8,128)(2,1)} %get-tuple-element.39), channel_id=1, source_target_pairs={{0,2},{1,3},{2,0},{3,1},{4,6},{5,7},{6,4},{7,5},{8,10},{9,11},{10,... | collective-permute-start | bytes 196616 | tf_op jit(solution)/shard_map/ppermute | solution.py:404
  28.8 7.4 %collective-permute-start.8 = (bf16[32,1024]{1,0:T(8,128)(2,1)}, bf16[32,1024]{1,0:T(8,128)(2,1)S(1)}, u32[]{:S(2)}, u32[]{:S(2)}) collective-permute-start(bf16[32,1024]{1,0:T(8,128)(2,1)} %get-tuple-element.40), channel_id=1, source_target_pairs={{0,12},{1,13},{2,14},{3,15},{4,8},{5,9},{6,10},{7,11},{8,4},{9,5},... | collective-permute-start | bytes 196616 | tf_op jit(solution)/shard_map/ppermute | solution.py:404
  29.0 7.4 %collective-permute-start.9 = (bf16[32,1024]{1,0:T(8,128)(2,1)}, bf16[32,1024]{1,0:T(8,128)(2,1)S(1)}, u32[]{:S(2)}, u32[]{:S(2)}) collective-permute-start(bf16[32,1024]{1,0:T(8,128)(2,1)} %get-tuple-element.41), channel_id=1, source_target_pairs={{0,6},{1,7},{2,4},{3,5},{4,2},{5,3},{6,0},{7,1},{8,14},{9,15},{10,... | collective-permute-start | bytes 196616 | tf_op jit(solution)/shard_map/ppermute | solution.py:404
  31.9 6.9 %collective-permute-start = (bf16[32,1024]{1,0:T(8,128)(2,1)}, bf16[32,1024]{1,0:T(8,128)(2,1)S(1)}, u32[]{:S(2)}, u32[]{:S(2)}) collective-permute-start(bf16[32,1024]{1,0:T(8,128)(2,1)} %get-tuple-element.31), channel_id=1, source_target_pairs={{0,13},{1,12},{2,15},{3,14},{4,9},{5,8},{6,11},{7,10},{8,5},{9,4},... | collective-permute-start | bytes 196616 | tf_op jit(solution)/shard_map/ppermute | solution.py:404
  33.5 5.4 %collective-permute-start.1 = (bf16[32,1024]{1,0:T(8,128)(2,1)}, bf16[32,1024]{1,0:T(8,128)(2,1)S(1)}, u32[]{:S(2)}, u32[]{:S(2)}) collective-permute-start(bf16[32,1024]{1,0:T(8,128)(2,1)} %get-tuple-element.32), channel_id=1, source_target_pairs={{0,3},{1,2},{2,1},{3,0},{4,7},{5,6},{6,5},{7,4},{8,11},{9,10},{10,... | collective-permute-start | bytes 196616 | tf_op jit(solution)/shard_map/ppermute | solution.py:404
  36.2 5.0 %collective-permute-start.2 = (bf16[32,1024]{1,0:T(8,128)(2,1)}, bf16[32,1024]{1,0:T(8,128)(2,1)S(1)}, u32[]{:S(2)}, u32[]{:S(2)}) collective-permute-start(bf16[32,1024]{1,0:T(8,128)(2,1)} %get-tuple-element.33), channel_id=1, source_target_pairs={{0,7},{1,6},{2,5},{3,4},{4,3},{5,2},{6,1},{7,0},{8,15},{9,14},{10,... | collective-permute-start | bytes 196616 | tf_op jit(solution)/shard_map/ppermute | solution.py:404
  36.2 5.0 %collective-permute-start.3 = (bf16[32,1024]{1,0:T(8,128)(2,1)}, bf16[32,1024]{1,0:T(8,128)(2,1)S(1)}, u32[]{:S(2)}, u32[]{:S(2)}) collective-permute-start(bf16[32,1024]{1,0:T(8,128)(2,1)} %get-tuple-element.34), channel_id=1, source_target_pairs={{0,1},{1,0},{2,3},{3,2},{4,5},{5,4},{6,7},{7,6},{8,9},{9,8},{10,11... | collective-permute-start | bytes 196616 | tf_op jit(solution)/shard_map/ppermute | solution.py:404
  36.4 0.8 %copy-start.3 = (bf16[32,1024]{1,0:T(8,128)(2,1)S(1)}, bf16[32,1024]{1,0:T(8,128)(2,1)}, u32[]{:S(2)}) copy-start(bf16[32,1024]{1,0:T(8,128)(2,1)} %get-tuple-element.35.refs_0_) | copy-start | bytes 196612
  41.6 8.7 %collective-permute-start.16 = (bf16[512,256]{1,0:T(8,128)(2,1)S(1)}, bf16[512,256]{1,0:T(8,128)(2,1)S(1)}, u32[]{:S(2)}, u32[]{:S(2)}) collective-permute-start(bf16[512,256]{1,0:T(8,128)(2,1)S(1)} %get-tuple-element.51.refs_0_), channel_id=1, source_target_pairs={{0,1},{1,2},{2,3},{3,4},{4,5},{5,6},{6,7},{7,8},{8,9},{9,10},{10,1... | collective-permute-start | bytes 786440 | tf_op jit(solution)/shard_map/ppermute | solution.py:27
  43.7 8.4 %collective-permute-start.15 = (bf16[512,256]{1,0:T(8,128)(2,1)S(1)}, bf16[512,256]{1,0:T(8,128)(2,1)S(1)}, u32[]{:S(2)}, u32[]{:S(2)}) collective-permute-start(bf16[512,256]{1,0:T(8,128)(2,1)S(1)} %get-tuple-element.52.refs_1_), channel_id=1, source_target_pairs={{0,1},{1,2},{2,3},{3,4},{4,5},{5,6},{6,7},{7,8},{8,9},{9,10},{10,1... | collective-permute-start | bytes 786440 | tf_op jit(solution)/shard_map/ppermute | solution.py:27
